TPU v7x, 32 devices: a whole 2x2x4 slice. The times are simulated.
32 devices in a mesh: dp: 8 (over z, x), seq: 4 (over y, core).
Axes of the slice: x: 2, y: 2, z: 4, core: 2. Of those that a mesh axis runs over, the one named last changes fastest.
Arguments:
- tokens: bfloat16 [4, 32, 256, 512], P(None, 'dp', 'seq'), may hold values from -6 to 6
- cotangent: bfloat16 [4, 32, 256, 512], P(None, 'dp', 'seq'), may hold values from -6 to 6
- lengths: int32 [4, 32], P(None, 'dp'), may hold values from 64 to 250, as said below
- attn_w: float32 [512, 2048], P('dp'), may hold values from -1.06066017 to 1.06066017
- attn_m: float32 [512, 2048], P('dp'), may hold values from -0.0009765625 to 0.0009765625
- attn_v: float32 [512, 2048], P('dp'), may hold values from 1.5868744e-10 to 2.538999e-09
- mlp_w: float32 [2, 512, 2048], P(None, 'dp'), may hold values from -0.25 to 0.25
- mlp_m: float32 [2, 512, 2048], P(None, 'dp'), may hold values from -0.0009765625 to 0.0009765625
- mlp_v: float32 [2, 512, 2048], P(None, 'dp'), may hold values from 1.5868744e-10 to 2.538999e-09
- vec_w: float32 [10, 512], P(None, 'dp'), may hold values from -1 to 3.2
- vec_m: float32 [10, 512], P(None, 'dp'), may hold values from -0.0009765625 to 0.0009765625
- vec_v: float32 [10, 512], P(None, 'dp'), may hold values from 1.5868744e-10 to 2.538999e-09
Outputs:
- output: bfloat16 [4, 32, 256, 512], P(None, 'dp', 'seq')
- input_grad: bfloat16 [4, 32, 256, 512], P(None, 'dp', 'seq')
- attn_w_new: float32 [512, 2048], P('dp')
- attn_m_new: float32 [512, 2048], P('dp')
- attn_v_new: float32 [512, 2048], P('dp')
- mlp_w_new: float32 [2, 512, 2048], P(None, 'dp')
- mlp_m_new: float32 [2, 512, 2048], P(None, 'dp')
- mlp_v_new: float32 [2, 512, 2048], P(None, 'dp')
- vec_w_new: float32 [10, 512], P(None, 'dp')
- vec_m_new: float32 [10, 512], P(None, 'dp')
- vec_v_new: float32 [10, 512], P(None, 'dp')
- grad_norm: float32 [], replicated
Inputs may be any that keep to these rules, and one draw needn't show every extreme that they name: `lengths`: each length is 64, 128 or 250; among the 4 rows of one index of dp in each micro-batch at least one has 250.
All inputs are finite; a program needn't handle non-finite values.
Results may differ from a plain program's by a relative error of at most 0.018.
The roundings to bfloat16 on the way count: a program that leaves them out, or rounds other values in their place, can miss the bound.
Values may be sent and summed in bfloat16 or wider, within the bound.
No kernel may reach another device: no remote copies, remote signals or barrier semaphores. Data moves between devices by JAX's collectives and lax.ppermute only.
A program may use at most 128 MiB of HBM per device.

v0:
```python
import math

import jax
import jax.numpy as jnp
from jax import lax
from jax.sharding import PartitionSpec as P

HEADS = 8
ADAM_STEP = 10


CLIP_NORM = 1.0
BETA_ONE = 0.9
BETA_TWO = 0.999
LEARN_RATE = 0.08
VEC_RATE = 0.4
WEIGHT_DECAY = 0.01
ADAM_EPS = 1e-08
NORM_EPS = 1e-05


def layer_norm(values, gain, shift):
    center = values - jnp.mean(values, axis=-1, keepdims=True)
    spread = jnp.mean(center * center, axis=-1, keepdims=True)
    return center * lax.rsqrt(spread + NORM_EPS) * gain + shift


def exact_gelu(values):
    return jax.nn.gelu(values, approximate=False)


def adam_update(weight, moment, second, grad, decay, rate):
    moment_new = BETA_ONE * moment + (1.0 - BETA_ONE) * grad
    second_new = BETA_TWO * second + (1.0 - BETA_TWO) * grad * grad
    first_hat = moment_new / (1.0 - BETA_ONE**ADAM_STEP)
    second_hat = second_new / (1.0 - BETA_TWO**ADAM_STEP)
    weight_new = weight - rate * (first_hat / (jnp.sqrt(second_hat) + ADAM_EPS) + decay * weight)
    return (weight_new, moment_new, second_new)


def same_value(value):
    return value


def layer_pass(
    x_float, grad_y_low, row_lengths, params, spread_qkv, gather_attn, spread_grad, gather_grad
):
    (
        w_qkv,
        w_out,
        w_up,
        w_down,
        gain_one,
        shift_one,
        gain_two,
        shift_two,
        bias_out,
        bias_down,
        bias_up,
    ) = params
    row_count, part_slots, model_width = x_float.shape
    head_size = model_width // HEADS
    score_scale = 1.0 / math.sqrt(head_size)
    h_one_f, norm_one_pull = jax.vjp(layer_norm, x_float, gain_one, shift_one)
    h_one = h_one_f.astype(jnp.bfloat16)
    qkv_local = jnp.einsum("rpd,de->rpe", h_one, w_qkv, preferred_element_type=jnp.float32).astype(
        jnp.bfloat16
    )
    qkv_local = qkv_local.reshape(row_count, part_slots, 3, model_width)
    qkv_heads = spread_qkv(qkv_local)
    slot_count = qkv_heads.shape[1]
    local_width = qkv_heads.shape[3]
    heads_dev = local_width // head_size
    slot_ids = jnp.arange(slot_count, dtype=jnp.int32)
    queries = qkv_heads[:, :, 0].reshape(row_count, slot_count, heads_dev, head_size)
    keys_h = qkv_heads[:, :, 1].reshape(row_count, slot_count, heads_dev, head_size)
    values_h = qkv_heads[:, :, 2].reshape(row_count, slot_count, heads_dev, head_size)
    valid = slot_ids[None, :] < row_lengths[:, None]
    key_mask = valid[:, None, None, :]
    scores = (
        jnp.einsum("rqhc,rkhc->rhqk", queries, keys_h, preferred_element_type=jnp.float32)
        * score_scale
    )
    scores = jnp.where(key_mask, scores, -1e30)
    row_max = jnp.max(scores, axis=-1, keepdims=True)
    shifted = jnp.exp(scores - row_max)
    log_total = row_max + jnp.log(jnp.sum(shifted, axis=-1, keepdims=True))
    probs_low = jnp.exp(scores - log_total).astype(jnp.bfloat16)
    attended = jnp.einsum(
        "rhqk,rkhc->rqhc", probs_low, values_h, preferred_element_type=jnp.float32
    )
    attended = attended.astype(jnp.bfloat16).reshape(row_count, slot_count, local_width)
    features = gather_attn(attended)
    x_one = (
        x_float
        + jnp.einsum("rpd,de->rpe", features, w_out, preferred_element_type=jnp.float32)
        + bias_out
    )
    h_two_f, norm_two_pull = jax.vjp(layer_norm, x_one, gain_two, shift_two)
    h_two = h_two_f.astype(jnp.bfloat16)
    up_pre = jnp.einsum("rpd,df->rpf", h_two, w_up, preferred_element_type=jnp.float32) + bias_up
    act_f, gelu_pull = jax.vjp(exact_gelu, up_pre)
    act = act_f.astype(jnp.bfloat16)
    result = (
        x_one
        + jnp.einsum("rpf,df->rpd", act, w_down, preferred_element_type=jnp.float32)
        + bias_down
    )
    grad_y = grad_y_low.astype(jnp.float32)
    grad_wdown = jnp.einsum("rpd,rpf->df", grad_y_low, act, preferred_element_type=jnp.float32)
    bdown_term = jnp.sum(grad_y, axis=(0, 1))
    grad_act = jnp.einsum("rpd,df->rpf", grad_y_low, w_down, preferred_element_type=jnp.float32)
    grad_up_pre = gelu_pull(grad_act)[0].astype(jnp.bfloat16)
    grad_wup = jnp.einsum("rpd,rpf->df", h_two, grad_up_pre, preferred_element_type=jnp.float32)
    grad_bup = jnp.sum(grad_up_pre.astype(jnp.float32), axis=(0, 1))
    grad_h_two = jnp.einsum("rpf,df->rpd", grad_up_pre, w_up, preferred_element_type=jnp.float32)
    grad_x_one, grad_g_two, grad_s_two = norm_two_pull(grad_h_two)
    grad_x_one = grad_x_one + grad_y
    grad_attn_out = grad_x_one.astype(jnp.bfloat16)
    grad_wout = jnp.einsum(
        "rpd,rpe->de", features, grad_attn_out, preferred_element_type=jnp.float32
    )
    bout_term = jnp.sum(grad_attn_out.astype(jnp.float32), axis=(0, 1))
    grad_feat = jnp.einsum(
        "rpe,de->rpd", grad_attn_out, w_out, preferred_element_type=jnp.float32
    ).astype(jnp.bfloat16)
    grad_heads = spread_grad(grad_feat)
    grad_heads = grad_heads.reshape(row_count, slot_count, heads_dev, head_size)
    again_scores = (
        jnp.einsum("rqhc,rkhc->rhqk", queries, keys_h, preferred_element_type=jnp.float32)
        * score_scale
    )
    again_scores = jnp.where(key_mask, again_scores, -1e30)
    probs_again = jnp.exp(again_scores - log_total)
    grad_probs = jnp.einsum(
        "rqhc,rkhc->rhqk", grad_heads, values_h, preferred_element_type=jnp.float32
    )
    inner = jnp.sum(probs_again * grad_probs, axis=-1, keepdims=True)
    grad_scores = (probs_again * (grad_probs - inner)).astype(jnp.bfloat16)
    grad_queries = (
        jnp.einsum("rhqk,rkhc->rqhc", grad_scores, keys_h, preferred_element_type=jnp.float32)
        * score_scale
    )
    grad_keys = (
        jnp.einsum("rhqk,rqhc->rkhc", grad_scores, queries, preferred_element_type=jnp.float32)
        * score_scale
    )
    grad_values = jnp.einsum(
        "rhqk,rqhc->rkhc",
        probs_again.astype(jnp.bfloat16),
        grad_heads,
        preferred_element_type=jnp.float32,
    )
    grad_qkv_heads = jnp.stack([grad_queries, grad_keys, grad_values], axis=2)
    grad_qkv_heads = grad_qkv_heads.reshape(row_count, slot_count, 3, local_width).astype(
        jnp.bfloat16
    )
    grad_qkv_local = gather_grad(grad_qkv_heads)
    grad_qkv_local = grad_qkv_local.reshape(row_count, part_slots, 3 * model_width)
    grad_wqkv = jnp.einsum("rpd,rpe->de", h_one, grad_qkv_local, preferred_element_type=jnp.float32)
    grad_h_one = jnp.einsum(
        "rpe,de->rpd", grad_qkv_local, w_qkv, preferred_element_type=jnp.float32
    )
    grad_x_ln, grad_g_one, grad_s_one = norm_one_pull(grad_h_one)
    input_piece = (grad_x_ln + grad_x_one).astype(jnp.bfloat16)
    small_terms = jnp.stack([grad_g_one, grad_s_one, grad_g_two, grad_s_two, bout_term, bdown_term])
    return (
        result.astype(jnp.bfloat16),
        input_piece,
        (grad_wqkv, grad_wout, grad_wup, grad_wdown, small_terms, grad_bup),
    )


def on_device(
    tokens, cotangent, lengths, attn_w, attn_m, attn_v, mlp_w, mlp_m, mlp_v, vec_w, vec_m, vec_v
):
    attn_all, mlp_all, vec_all = (
        lax.all_gather(attn_w.astype(jnp.bfloat16), "dp", axis=0, tiled=True),
        lax.all_gather(mlp_w.astype(jnp.bfloat16), "dp", axis=1, tiled=True),
        lax.all_gather(vec_w.astype(jnp.bfloat16), "dp", axis=1, tiled=True),
    )
    model_width = attn_all.shape[0]
    vec_float = vec_all.astype(jnp.float32)
    params = (
        attn_all[:, : 3 * model_width],
        attn_all[:, 3 * model_width :],
        mlp_all[0],
        mlp_all[1],
        vec_float[0],
        vec_float[1],
        vec_float[2],
        vec_float[3],
        vec_float[4],
        vec_float[5],
        vec_float[6:].reshape(-1),
    )
    micro_count, row_count, part_slots, _ = tokens.shape
    seq_count = lax.axis_size("seq")
    flat_count = micro_count * row_count
    per_device = flat_count // seq_count
    moved_tokens, moved_cot = (
        lax.all_to_all(
            tokens.reshape(flat_count, part_slots, model_width),
            "seq",
            split_axis=0,
            concat_axis=1,
            tiled=True,
        ),
        lax.all_to_all(
            cotangent.reshape(flat_count, part_slots, model_width),
            "seq",
            split_axis=0,
            concat_axis=1,
            tiled=True,
        ),
    )
    row_lengths = lax.dynamic_slice_in_dim(
        lengths.reshape(-1), lax.axis_index("seq") * per_device, per_device
    )
    result, input_piece, totals = layer_pass(
        moved_tokens.astype(jnp.float32),
        moved_cot,
        row_lengths,
        params,
        same_value,
        same_value,
        same_value,
        same_value,
    )
    back_result, back_grad = (
        lax.all_to_all(result, "seq", split_axis=1, concat_axis=0, tiled=True),
        lax.all_to_all(input_piece, "seq", split_axis=1, concat_axis=0, tiled=True),
    )
    output = back_result.reshape(tokens.shape)
    input_grad = back_grad.reshape(tokens.shape)
    grad_wqkv, grad_wout, grad_wup, grad_wdown, grad_small, grad_bup = totals
    attn_total = jnp.concatenate([grad_wqkv, grad_wout], axis=1)
    mlp_total = jnp.stack([grad_wup, grad_wdown])
    vec_total = jnp.concatenate([grad_small, grad_bup.reshape(-1, model_width)], axis=0)
    attn_rows = attn_w.shape[0]
    mlp_rows = mlp_w.shape[1]
    vec_cols = vec_w.shape[1]
    attn_sum, mlp_sum, vec_sum = lax.psum((attn_total, mlp_total, vec_total), ("dp", "seq"))
    square_total = (
        jnp.sum(attn_sum * attn_sum) + jnp.sum(mlp_sum * mlp_sum) + jnp.sum(vec_sum * vec_sum)
    )
    position = lax.axis_index("dp")
    attn_grad = lax.dynamic_slice_in_dim(attn_sum, position * attn_rows, attn_rows, 0)
    mlp_grad = lax.dynamic_slice_in_dim(mlp_sum, position * mlp_rows, mlp_rows, 1)
    vec_grad = lax.dynamic_slice_in_dim(vec_sum, position * vec_cols, vec_cols, 1)
    grad_norm = jnp.sqrt(square_total)
    clip_factor = CLIP_NORM / jnp.maximum(grad_norm, CLIP_NORM)
    attn_new = adam_update(
        attn_w, attn_m, attn_v, attn_grad * clip_factor, WEIGHT_DECAY, LEARN_RATE
    )
    mlp_new = adam_update(mlp_w, mlp_m, mlp_v, mlp_grad * clip_factor, WEIGHT_DECAY, LEARN_RATE)
    vec_new = adam_update(vec_w, vec_m, vec_v, vec_grad * clip_factor, 0.0, VEC_RATE)
    return (
        output,
        input_grad,
        attn_new[0],
        attn_new[1],
        attn_new[2],
        mlp_new[0],
        mlp_new[1],
        mlp_new[2],
        vec_new[0],
        vec_new[1],
        vec_new[2],
        grad_norm,
    )


def solution(mesh):
    placed = (
        P(None, "dp", "seq", None),
        P(None, "dp", "seq", None),
        P(None, "dp"),
        P("dp", None),
        P("dp", None),
        P("dp", None),
        P(None, "dp", None),
        P(None, "dp", None),
        P(None, "dp", None),
        P(None, "dp"),
        P(None, "dp"),
        P(None, "dp"),
    )
    return jax.shard_map(
        on_device,
        mesh=mesh,
        in_specs=placed,
        out_specs=(
            P(None, "dp", "seq", None),
            P(None, "dp", "seq", None),
            P("dp", None),
            P("dp", None),
            P("dp", None),
            P(None, "dp", None),
            P(None, "dp", None),
            P(None, "dp", None),
            P(None, "dp"),
            P(None, "dp"),
            P(None, "dp"),
            P(),
        ),
        check_vma=False,
    )
```

profile of v0, /device:TPU:0, one launch (start us, length us, event | category | flops | bytes accessed | tf_op | source)
XLA Modules:
  0.0 476.8 jit_solution(13071424087077795501)
XLA Ops:
  7.2 1.8 convert_element_type.95
  9.1 2.1 convert_element_type.101
  11.2 4.3 all-to-all-start
  15.5 31.5 %all-gather = bf16[8,64,10]{1,2,0:T(8,128)(2,1)S(1)} all-gather(bf16[1,64,10]{1,2,0:T(8,128)(2,1)S(1)} %convert_bitcast_fusion.1), channel_id=1, replica_groups=mesh['dp'=8,'seq'=4] {'dp'}, dimensions={0}, use_global_device_ids=true | all-gather | bytes 11520 | tf_op jit(solution)/shard_map/all_gather | solution.py:180
  47.4 3.5 all-to-all-start.2
  51.3 0.5 multiply_reduce_fusion.8
  51.9 13.4 %all-to-all-done.2 = bf16[16,64,512]{2,1,0:T(8,128)(2,1)S(1)} async-done(((bf16[16,64,512]{2,1,0:T(8,128)(2,1)}), bf16[16,64,512]{2,1,0:T(8,128)(2,1)S(1)}, u32[]{:S(2)}, u32[]{:S(2)}) %all-to-all-start.2) | async-done | bytes 1048608 | tf_op jit(solution)/shard_map/all_to_all | solution.py:209
  65.5 0.9 copy-done.6
  66.9 1.4 add_convert_fusion.4
  68.3 5.2 %convolution_convert_fusion = bf16[4,256,1536]{2,1,0:T(8,128)(2,1)} fusion(bf16[4,256,512]{2,1,0:T(8,128)(2,1)} %add_convert_fusion.4, bf16[512,2048]{1,0:T(8,128)(2,1)} %all-gather.4.cloned.1.call-done), kind=kOutput, calls=%fused_computation.33 | convolution fusion | flops 1612185600 | bytes 5767168 | tf_op jit(solution)/shard_map/rpd,de->rpe/dot_general | solution.py:66
  73.5 5.0 %copy.102 = bf16[4,256,1536]{1,2,0:T(8,128)(2,1)} copy(bf16[4,256,1536]{2,1,0:T(8,128)(2,1)} %convolution_convert_fusion) | data formatting | bytes 6291456 | tf_op jit(solution)/shard_map/convert_element_type | solution.py:66
  78.4 2.1 fusion.35
  80.5 2.1 fusion.6
  82.7 2.0 exponential_reduce_fusion
  84.7 1.2 copy-done
  85.9 2.2 convolution_convert_fusion.2
  88.1 2.2 fusion.37
  90.4 1.3 copy-done.1
  91.7 0.4 multiply_reduce_fusion.7
  92.1 45.4 %all-gather.6.cloned.1.call-done = bf16[2,512,2048]{2,1,0:T(8,128)(2,1)} async-done(((bf16[2,64,2048]{2,1,0:T(8,128)(2,1)}), bf16[2,512,2048]{2,1,0:T(8,128)(2,1)}) %all-gather.6.cloned.1.call-update) | async-done | bytes 4194320 | tf_op jit(solution)/shard_map/all_gather | solution.py:179
  137.6 6.7 %fusion.10 = (u8[256,2048]{1,0:T(8,128)(4,1)S(1)}, u8[256,2048]{1,0:T(8,128)(4,1)S(1)}, f32[4,256,2048]{2,1,0:T(8,128)S(1)}) fusion(f32[2048]{0:T(1024)S(1)} %bitcast.186, bf16[2,512,2048]{2,1,0:T(8,128)(2,1)} %all-gather.6.cloned.1.call-done, f32[4,256,512]{2,1,0:T(8,128)} %copy-done.1, f32[512]{0:T(512)S(1)} %bitcast.197, f32[512]{0:T(512)S(1)} %bitcast.193, ...), kind=kOutput, calls=%fused_computation.62 | convolution fusion | flops 2178416640 | bytes 13651968 | tf_op jit(solution)/shard_map/rpd,df->rpf/dot_general | solution.py:101
  144.3 20.1 %multiply_convert_fusion.1 = (bf16[4,256,2048]{2,1,0:T(8,128)(2,1)}, f32[4,256,2048]{2,1,0:T(8,128)S(1)}) fusion(f32[4,256,2048]{2,1,0:T(8,128)S(1)} %get-tuple-element.51, f32[2048]{0:T(1024)S(1)} %bitcast.187, u8[256,2048]{1,0:T(8,128)(4,1)S(1)} %get-tuple-element.13, u8[256,2048]{1,0:T(8,128)(4,1)S(1)} %get-tuple-element.12), kind=kLoop, calls=%fused_computation.13 | loop fusion | flops 148897792 | bytes 22028288 | tf_op jit(solution)/shard_map/convert_element_type | solution.py:103
  164.4 7.3 %convert_reduce_fusion = (f32[2048]{0:T(1024)S(1)}, bf16[4,256,2048]{2,1,0:T(8,128)(2,1)S(1)}) fusion(f32[4,256,2048]{2,1,0:T(8,128)S(1)} %get-tuple-element.37, bf16[4,256,512]{2,1,0:T(8,128)(2,1)S(1)} %bitcast.161, bf16[2,512,2048]{2,1,0:T(8,128)(2,1)} %all-gather.6.cloned.1.call-done, f32[4,256,2048]{2,1,0:T(8,128)S(1)} %get-tuple-element.51, ...), kind=kOutput, calls=%fused_computation.8 | convolution fusion | flops 2183133184 | bytes 24133632 | tf_op jit(solution)/shard_map/rpd,df->rpf/dot_general | solution.py:112
  171.8 4.5 convolution_bitcast_fusion.2
  176.3 2.9 multiply_reduce_fusion.3
  179.2 0.8 fusion.33
  180.0 1.3 copy-done.3
  181.3 0.5 convert_reduce_fusion.2
  181.8 1.7 convolution_bitcast_fusion.3
  183.5 2.7 convolution_convert_fusion.3
  186.2 2.3 copy.108
  188.5 6.7 %convolution_convert_fusion.1 = bf16[4,8,64,256]{3,2,1,0:T(8,128)(2,1)} fusion(bf16[4,256,8,64]{1,3,2,0:T(8,128)(2,1)} %bitcast.169, f32[4,8,256,256]{2,3,1,0:T(8,128)} %copy-done, f32[4,8,256]{2,1,0:T(8,128)S(1)} %log_add_fusion, pred[4,256]{1,0:T(4,128)(4,1)S(1)} %iota_compare_fusion), kind=kOutput, calls=%fused_computation.68 | convolution fusion | flops 277348352 | bytes 10519552 | tf_op jit(solution)/shard_map/rhqk,rqhc->rkhc/dot_general | solution.py:148
  195.2 5.7 %multiply_reduce_fusion.1 = (f32[4,8,256]{2,1,0:T(8,128)S(1)}, f32[4,8,256,256]{2,3,1,0:T(8,128)S(1)}) fusion(f32[4,8,256,256]{2,3,1,0:T(8,128)} %copy-done, f32[4,8,256]{2,1,0:T(8,128)S(1)} %log_add_fusion, pred[4,256]{1,0:T(4,128)(4,1)S(1)} %iota_compare_fusion, bf16[4,256,8,64]{1,3,2,0:T(8,128)(2,1)S(1)} %bitcast.170, ...), kind=kOutput, calls=%fused_computation.11 | convolution fusion | flops 278913024 | bytes 18940928 | tf_op jit(solution)/shard_map/rqhc,rkhc->rhqk/dot_general | solution.py:135
  200.9 2.6 multiply_convert_fusion
  203.5 1.4 multiply_convert_fusion.2
  204.9 0.8 multiply_convert_fusion.3
  205.7 1.3 copy-done.13
  207.1 2.5 convolution_bitcast_fusion.1
  209.6 0.3 pad_maximum_fusion.2
  210.0 0.8 copy-done.20
  210.8 1.8 convolution_bitcast_fusion
  212.7 0.6 copy-done.5
  213.2 3.8 pad_maximum_fusion
  217.1 2.3 pad_maximum_fusion.1
  219.4 5.8 %add_convert_fusion.2 = bf16[4,256,512]{2,1,0:T(8,128)(2,1)S(1)} fusion(f32[4,256,512]{2,1,0:T(8,128)} %copy-done.1, bf16[4,256,2048]{2,1,0:T(8,128)(2,1)} %get-tuple-element.36, bf16[2,512,2048]{2,1,0:T(8,128)(2,1)} %all-gather.6.cloned.1.call-done, f32[512]{0:T(512)S(1)} %bitcast.204), kind=kOutput, calls=%fused_computation.56 | convolution fusion | flops 2149056512 | bytes 9439232 | tf_op jit(solution)/shard_map/rpf,df->rpd/dot_general | solution.py:106
  225.2 1.8 copy.105
  227.0 4.5 all-to-all-start.1
  231.5 4.7 fusion.28
  236.1 1.3 multiply_reduce_fusion.4
  237.4 0.3 copy-done.4
  237.7 1.3 add_convert_fusion.1
  239.0 1.8 copy.116
  240.8 9.4 %all-to-all-done.1 = bf16[4,256,512]{2,0,1:T(4,128)(2,1)} async-done(((bf16[4,256,512]{2,0,1:T(4,128)(2,1)}), bf16[4,256,512]{2,0,1:T(4,128)(2,1)}, u32[]{:S(2)}, u32[]{:S(2)}) %all-to-all-start.1) | async-done | bytes 1048608 | tf_op jit(solution)/shard_map/all_to_all | solution.py:231
  250.2 3.5 all-to-all-start.3
  254.1 58.1 %psum.23 = f32[10,512]{1,0:T(8,128)S(1)} all-reduce(f32[10,512]{1,0:T(8,128)S(1)} %concatenate.9), channel_id=1, replica_groups=mesh['dp'=8,'seq'=4] {'dp','seq'}, use_global_device_ids=true, to_apply=%region_22.23 | all-reduce | flops 5120 | bytes 40960 | tf_op jit(solution)/shard_map/psum | solution.py:243
  312.2 0.6 multiply_reduce_fusion.9
  312.8 2.4 copy.147
  315.2 1.2 copy.146
  316.4 135.3 %all-reduce.3.cloned.1.call-done = (f32[512,2048]{1,0:T(8,128)}, f32[2,512,2048]{2,1,0:T(8,128)}) async-done(((f32[512,2048]{1,0:T(8,128)}, f32[2,512,2048]{2,1,0:T(8,128)}), (f32[512,2048]{1,0:T(8,128)}, f32[2,512,2048]{2,1,0:T(8,128)})) %all-reduce.3.cloned.1.call-update) | async-done | bytes 12582928 | tf_op jit(solution)/shard_map/psum | solution.py:243
  451.8 6.3 %multiply_reduce_fusion = f32[]{:T(128)} fusion(f32[2,512,2048]{2,1,0:T(8,128)} %get-tuple-element.22), kind=kLoop, calls=%fused_computation.9 | loop fusion | flops 4194303 | bytes 8388612 | tf_op jit(solution)/shard_map/reduce_sum | solution.py:245
  458.1 1.7 multiply_reduce_fusion.2
  461.9 3.8 multiply_subtract_fusion
  465.8 2.5 multiply_subtract_fusion.1
  468.3 0.7 multiply_subtract_fusion.2
  (102 shorter events, 2.1 us)
Async XLA Ops:
  7.2 8.3 %copy-start.28 = (f32[10,64]{1,0:T(8,128)S(1)}, f32[10,64]{1,0:T(8,128)}, u32[]{:S(2)}) copy-start(f32[10,64]{1,0:T(8,128)} %param.21) | copy-start | bytes 7684
  7.2 39.8 %copy-start.31 = (s32[4,4]{1,0:T(4,128)S(1)}, s32[4,4]{1,0:T(4,128)}, u32[]{:S(2)}) copy-start(s32[4,4]{1,0:T(4,128)} %param.14) | copy-start | bytes 196
  7.2 61.1 %all-gather.4.cloned.1.call-start = ((), (), s32[]{:S(2)}) async-start(), calls=%async_computation.4 | async-start | bytes 2359296 | tf_op jit(solution)/shard_map/all_gather | solution.py:178
  9.0 128.5 %all-gather.6.cloned.1.call-start = ((), (), s32[]{:S(2)}) async-start(), calls=%async_computation.5 | async-start | bytes 4718592 | tf_op jit(solution)/shard_map/all_gather | solution.py:179
  11.2 36.2 %all-to-all-start = ((bf16[16,64,512]{2,1,0:T(8,128)(2,1)}), bf16[16,64,512]{2,1,0:T(8,128)(2,1)S(1)}, u32[]{:S(2)}, u32[]{:S(2)}) async-start(bf16[16,64,512]{2,1,0:T(8,128)(2,1)} %bitcast.178), calls=%async_computation | async-start | bytes 2097152 | tf_op jit(solution)/shard_map/all_to_all | solution.py:202
  47.4 18.0 %all-to-all-start.2 = ((bf16[16,64,512]{2,1,0:T(8,128)(2,1)}), bf16[16,64,512]{2,1,0:T(8,128)(2,1)S(1)}, u32[]{:S(2)}, u32[]{:S(2)}) async-start(bf16[16,64,512]{2,1,0:T(8,128)(2,1)} %bitcast.28), calls=%async_computation.2 | async-start | bytes 2097152 | tf_op jit(solution)/shard_map/all_to_all | solution.py:209
  50.9 400.8 %all-reduce.3.cloned.1.call-start = ((), (), s32[]{:S(2)}) async-start(), calls=%async_computation.6 | async-start | bytes 25165824 | tf_op jit(solution)/shard_map/psum | solution.py:243
  65.4 1.0 copy-start.6
  80.5 2.2 copy-start.8
  80.5 2.2 copy-start.10
  80.5 4.2 copy-start.15
  82.7 3.2 copy-start
  88.1 4.0 copy-start.22
  90.3 1.4 copy-start.1
  164.4 7.3 %copy-start.2 = (f32[4,256,512]{2,1,0:T(8,128)S(1)}, f32[4,256,512]{2,1,0:T(8,128)}, u32[]{:S(2)}) copy-start(f32[4,256,512]{2,1,0:T(8,128)} %copy-done.1) | copy-start | bytes 6291460
  171.8 4.5 copy-start.32
  179.2 2.6 copy-start.23
  180.0 1.3 copy-start.3
  188.5 6.7 %copy-start.14 = (bf16[4,256,512]{1,2,0:T(8,128)(2,1)S(1)}, bf16[4,256,512]{1,2,0:T(8,128)(2,1)}, u32[]{:S(2)}) copy-start(bf16[4,256,512]{1,2,0:T(8,128)(2,1)} %copy.108) | copy-start | bytes 3145732
  188.5 6.7 %copy-start.16 = (bf16[4,256,1,512]{1,3,2,0:T(8,128)(2,1)S(1)}, bf16[4,256,1,512]{1,3,2,0:T(8,128)(2,1)}, u32[]{:S(2)}) copy-start(bf16[4,256,1,512]{1,3,2,0:T(8,128)(2,1)} %copy-done.15) | copy-start | bytes 3145732
  188.5 12.4 %slice-start = ((s8[8388608]{0:T(1024)(128)(4,1)}), s8[4194304]{0:T(1024)(128)(4,1)S(1)}, s32[]{:S(2)}) async-start(s8[8388608]{0:T(1024)(128)(4,1)} %bitcast.156), calls=%async_computation.7 | async-start | bytes 8388608
  195.2 5.7 %slice-start.1 = ((s8[8388608]{0:T(1024)(128)(4,1)}), s8[4194304]{0:T(1024)(128)(4,1)S(1)}, s32[]{:S(2)}) async-start(s8[8388608]{0:T(1024)(128)(4,1)} %bitcast.156), calls=%async_computation.8 | async-start | bytes 8388608
  200.9 2.6 copy-start.11
  203.5 1.4 copy-start.9
  204.9 2.2 copy-start.13
  207.1 2.6 copy-start.24
  209.6 1.2 copy-start.20
  210.0 2.7 copy-start.18
  210.8 2.4 copy-start.5
  213.2 3.8 copy-start.25
  227.0 23.2 %all-to-all-start.1 = ((bf16[4,256,512]{2,0,1:T(4,128)(2,1)}), bf16[4,256,512]{2,0,1:T(4,128)(2,1)}, u32[]{:S(2)}, u32[]{:S(2)}) async-start(bf16[4,256,512]{2,0,1:T(4,128)(2,1)} %copy.105), calls=%async_computation.1 | async-start | bytes 2097152 | tf_op jit(solution)/shard_map/all_to_all | solution.py:231
  236.1 1.6 copy-start.4
  239.0 14.7 %copy-start.7 = (bf16[16,64,512]{2,1,0:T(8,128)(2,1)S(1)}, bf16[16,64,512]{2,1,0:T(8,128)(2,1)}, u32[]{:S(2)}) copy-start(bf16[16,64,512]{2,1,0:T(8,128)(2,1)} %copy-done.6) | copy-start | bytes 3145732
  250.2 65.1 %all-to-all-start.3 = ((bf16[4,256,512]{2,0,1:T(4,128)(2,1)}), bf16[4,256,512]{2,0,1:T(4,128)(2,1)S(1)}, u32[]{:S(2)}, u32[]{:S(2)}) async-start(bf16[4,256,512]{2,0,1:T(4,128)(2,1)} %copy.116), calls=%async_computation.3 | async-start | bytes 2097152 | tf_op jit(solution)/shard_map/all_to_all | solution.py:232
  451.8 6.3 %copy-start.12 = (f32[512,2048]{1,0:T(8,128)S(1)}, f32[512,2048]{1,0:T(8,128)}, u32[]{:S(2)}) copy-start(f32[512,2048]{1,0:T(8,128)} %get-tuple-element.21) | copy-start | bytes 12582916
  458.1 3.8 copy-start.17
  458.1 3.8 copy-start.21
  459.8 6.0 %copy-start.19 = (f32[64,2048]{1,0:T(8,128)S(1)}, f32[64,2048]{1,0:T(8,128)}, u32[]{:S(2)}) copy-start(f32[64,2048]{1,0:T(8,128)} %param.15) | copy-start | bytes 1572868
  459.8 6.0 %copy-start.26 = (f32[64,2048]{1,0:T(8,128)S(1)}, f32[64,2048]{1,0:T(8,128)}, u32[]{:S(2)}) copy-start(f32[64,2048]{1,0:T(8,128)} %param.16) | copy-start | bytes 1572868
  461.9 3.9 copy-start.27
  461.9 6.3 %copy-start.29 = (f32[10,64]{1,0:T(8,128)S(1)}, f32[10,64]{1,0:T(8,128)}, u32[]{:S(2)}) copy-start(f32[10,64]{1,0:T(8,128)} %param.22) | copy-start | bytes 7684
  461.9 6.3 %copy-start.30 = (f32[10,64]{1,0:T(8,128)S(1)}, f32[10,64]{1,0:T(8,128)}, u32[]{:S(2)}) copy-start(f32[10,64]{1,0:T(8,128)} %param.23) | copy-start | bytes 7684
Sparse Core Ops, SparseCore 0:
  10.7 52.2 all-gather.3
  65.8 71.7 all-gather.5
  219.5 232.2 all-reduce.2
where the time goes:
time: 481 us; the launch traced here: 477 us
  waiting for transfers between devices  204 us (42%)
  blocking collectives  89.6 us (19%)
  matrix products  67 us (14%)
  other arithmetic  57.5 us (12%)
  local copies, waits for them, and re-layouts  25.3 us (5%)
  between operations  17.8 us (4%)
  starting transfers between devices  15.9 us (3%)
    psum x1, waiting for transfers between devices, on_device(): lax.psum((attn_total, mlp_total, vec_total), ('dp', 'seq'))  135 us
    psum x1, blocking collectives, on_device(): lax.psum((attn_total, mlp_total, vec_total), ('dp', 'seq'))  58.1 us
    all_gather x1, waiting for transfers between devices, on_device(): lax.all_gather(mlp_w.astype(jnp.bfloat16), 'dp', axis=1, tiled=True)  45.4 us
    all_gather x1, blocking collectives, on_device(): lax.all_gather(vec_w.astype(jnp.bfloat16), 'dp', axis=1, tiled=True)  31.5 us
    convert_element_type x1, other arithmetic, layer_pass(): act = act_f.astype(jnp.bfloat16)  20.1 us
    all_to_all x1, waiting for transfers between devices, on_device(): lax.all_to_all(cotangent.reshape(flat_count, part_slots, model_width), 's...  13.4 us
  transfers between devices with their start and end apart: 7, of which 4 were waited for; matrix products, arithmetic and copies ran while one was open for 10% of the time, Pallas kernels for 0%

commit v1 on v0

--- a/solution.py
+++ b/solution.py
@@ -43,7 +43,7 @@
 
 
 def layer_pass(
-    x_float, grad_y_low, row_lengths, params, spread_qkv, gather_attn, spread_grad, gather_grad
+    slot_ids, x_float, grad_y_low, row_lengths, params, spread_qkv, gather_attn, spread_grad, gather_grad
 ):
     (
         w_qkv,
@@ -71,7 +71,6 @@
     slot_count = qkv_heads.shape[1]
     local_width = qkv_heads.shape[3]
     heads_dev = local_width // head_size
-    slot_ids = jnp.arange(slot_count, dtype=jnp.int32)
     queries = qkv_heads[:, :, 0].reshape(row_count, slot_count, heads_dev, head_size)
     keys_h = qkv_heads[:, :, 1].reshape(row_count, slot_count, heads_dev, head_size)
     values_h = qkv_heads[:, :, 2].reshape(row_count, slot_count, heads_dev, head_size)
@@ -171,21 +170,100 @@
     )
 
 
+def swap(value, axis):
+    return lax.ppermute(value, axis, [(0, 1), (1, 0)])
+
+
+def ordered(own, other, index, axis):
+    first = jnp.where(index == 0, own, other)
+    second = jnp.where(index == 0, other, own)
+    return jnp.stack([first, second], axis)
+
+
+def from_seq(pieces, axes):
+    perm = [(j, j) for j in range(4)]
+    out = []
+    for k in range(4):
+        if k == 0:
+            out.append(pieces[0])
+        else:
+            out.append(lax.ppermute(pieces[k], axes, [(j, j ^ k) for j in range(4)]))
+    return out
+
+
+def gather_rows(shard, lo, core):
+    hi_count = lax.axis_size("hi")
+    rows, cols = shard.shape
+    half = lax.dynamic_slice_in_dim(shard, core * (rows // 2), rows // 2, 0)
+    spread = jnp.broadcast_to(half[None], (hi_count, rows // 2, cols))
+    own = lax.all_to_all(spread, "hi", 0, 0)
+    other = swap(own, "lo")
+    own_far = swap(own, "core")
+    other_far = swap(other, "core")
+    near = ordered(own, other, lo, 1)
+    far = ordered(own_far, other_far, lo, 1)
+    whole = ordered(near, far, core, 2)
+    return whole.reshape(hi_count * 2 * rows, cols)
+
+
+def reduce_rows(total, y, core):
+    hi_count = lax.axis_size("hi")
+    width, cols = total.shape
+    rows = width // (2 * hi_count)
+    half = cols // 2
+    quarter = half // 2
+    keep = lax.dynamic_slice_in_dim(total, core * half, half, 1)
+    send = lax.dynamic_slice_in_dim(total, (1 - core) * half, half, 1)
+    got = swap(send.astype(jnp.bfloat16), "core")
+    part = (keep + got.astype(jnp.float32)).astype(jnp.bfloat16)
+    part = part.reshape(hi_count, 2, rows, 2, quarter).transpose(1, 3, 0, 2, 4)
+    part = part.reshape(4, hi_count, rows, quarter)
+    part = lax.all_to_all(part, ("lo", "y"), 0, 0)
+    part = jnp.sum(part.astype(jnp.float32), axis=0).astype(jnp.bfloat16)
+    part = lax.all_to_all(part, "hi", 0, 0)
+    part = jnp.sum(part.astype(jnp.float32), axis=0).astype(jnp.bfloat16)
+    other = swap(part, "y")
+    mine = ordered(part, other, y, 1).reshape(rows, half)
+    far = swap(mine, "core")
+    whole = ordered(mine, far, core, 1).reshape(rows, cols)
+    return whole.astype(jnp.float32)
+
+
 def on_device(
     tokens, cotangent, lengths, attn_w, attn_m, attn_v, mlp_w, mlp_m, mlp_v, vec_w, vec_m, vec_v
 ):
-    attn_all, mlp_all, vec_all = (
-        lax.all_gather(attn_w.astype(jnp.bfloat16), "dp", axis=0, tiled=True),
-        lax.all_gather(mlp_w.astype(jnp.bfloat16), "dp", axis=1, tiled=True),
-        lax.all_gather(vec_w.astype(jnp.bfloat16), "dp", axis=1, tiled=True),
-    )
-    model_width = attn_all.shape[0]
+    lo = lax.axis_index("lo")
+    y = lax.axis_index("y")
+    core = lax.axis_index("core")
+    me = y * 2 + core
+    seq_axes = ("y", "core")
+    model_width = tokens.shape[-1]
+    vec_low = vec_w.astype(jnp.bfloat16)
+    attn_low = attn_w.astype(jnp.bfloat16)
+    mlp_low = mlp_w.astype(jnp.bfloat16)
+    micro_count, row_count, part_slots, _ = tokens.shape
+    flat_count = micro_count * row_count
+    seq_count = 4
+    per_device = flat_count // seq_count
+    flat_tokens = tokens.reshape(seq_count, per_device, part_slots, model_width)
+    flat_cot = cotangent.reshape(seq_count, per_device, part_slots, model_width)
+
+    def pick(stack, k):
+        return lax.dynamic_index_in_dim(stack, me ^ k, 0, keepdims=False)
+
+    moved_tokens = from_seq([pick(flat_tokens, k) for k in range(4)], seq_axes)
+    w_qkv = gather_rows(attn_low[:, : 3 * model_width], lo, core)
+    vec_all = lax.all_gather(vec_low, ("hi", "lo"), axis=1, tiled=True)
+    w_out = gather_rows(attn_low[:, 3 * model_width :], lo, core)
+    moved_cot = from_seq([pick(flat_cot, k) for k in range(4)], seq_axes)
+    w_up = gather_rows(mlp_low[0], lo, core)
+    w_down = gather_rows(mlp_low[1], lo, core)
     vec_float = vec_all.astype(jnp.float32)
     params = (
-        attn_all[:, : 3 * model_width],
-        attn_all[:, 3 * model_width :],
-        mlp_all[0],
-        mlp_all[1],
+        w_qkv,
+        w_out,
+        w_up,
+        w_down,
         vec_float[0],
         vec_float[1],
         vec_float[2],
@@ -194,32 +272,15 @@
         vec_float[5],
         vec_float[6:].reshape(-1),
     )
-    micro_count, row_count, part_slots, _ = tokens.shape
-    seq_count = lax.axis_size("seq")
-    flat_count = micro_count * row_count
-    per_device = flat_count // seq_count
-    moved_tokens, moved_cot = (
-        lax.all_to_all(
-            tokens.reshape(flat_count, part_slots, model_width),
-            "seq",
-            split_axis=0,
-            concat_axis=1,
-            tiled=True,
-        ),
-        lax.all_to_all(
-            cotangent.reshape(flat_count, part_slots, model_width),
-            "seq",
-            split_axis=0,
-            concat_axis=1,
-            tiled=True,
-        ),
-    )
-    row_lengths = lax.dynamic_slice_in_dim(
-        lengths.reshape(-1), lax.axis_index("seq") * per_device, per_device
-    )
+    row_lengths = lax.dynamic_slice_in_dim(lengths.reshape(-1), me * per_device, per_device)
+    slot_ids = jnp.concatenate(
+        [(me ^ k) * part_slots + jnp.arange(part_slots, dtype=jnp.int32) for k in range(4)]
+    )
+    x_float = jnp.concatenate(moved_tokens, axis=1).astype(jnp.float32)
     result, input_piece, totals = layer_pass(
-        moved_tokens.astype(jnp.float32),
-        moved_cot,
+        slot_ids,
+        x_float,
+        jnp.concatenate(moved_cot, axis=1),
         row_lengths,
         params,
         same_value,
@@ -227,82 +288,56 @@
         same_value,
         same_value,
     )
-    back_result, back_grad = (
-        lax.all_to_all(result, "seq", split_axis=1, concat_axis=0, tiled=True),
-        lax.all_to_all(input_piece, "seq", split_axis=1, concat_axis=0, tiled=True),
-    )
-    output = back_result.reshape(tokens.shape)
-    input_grad = back_grad.reshape(tokens.shape)
+
+    def send_back(value):
+        parts = [value[:, k * part_slots : (k + 1) * part_slots] for k in range(4)]
+        parts = from_seq(parts, seq_axes)
+        pairs = [ordered(parts[0], parts[1], core, 0), ordered(parts[2], parts[3], core, 0)]
+        return ordered(pairs[0], pairs[1], y, 0).reshape(tokens.shape)
+
+    output = send_back(result)
+    input_grad = send_back(input_piece)
     grad_wqkv, grad_wout, grad_wup, grad_wdown, grad_small, grad_bup = totals
-    attn_total = jnp.concatenate([grad_wqkv, grad_wout], axis=1)
-    mlp_total = jnp.stack([grad_wup, grad_wdown])
     vec_total = jnp.concatenate([grad_small, grad_bup.reshape(-1, model_width)], axis=0)
-    attn_rows = attn_w.shape[0]
-    mlp_rows = mlp_w.shape[1]
+    vec_rows = vec_total.shape[0]
     vec_cols = vec_w.shape[1]
-    attn_sum, mlp_sum, vec_sum = lax.psum((attn_total, mlp_total, vec_total), ("dp", "seq"))
-    square_total = (
-        jnp.sum(attn_sum * attn_sum) + jnp.sum(mlp_sum * mlp_sum) + jnp.sum(vec_sum * vec_sum)
-    )
-    position = lax.axis_index("dp")
-    attn_grad = lax.dynamic_slice_in_dim(attn_sum, position * attn_rows, attn_rows, 0)
-    mlp_grad = lax.dynamic_slice_in_dim(mlp_sum, position * mlp_rows, mlp_rows, 1)
-    vec_grad = lax.dynamic_slice_in_dim(vec_sum, position * vec_cols, vec_cols, 1)
-    grad_norm = jnp.sqrt(square_total)
+    down_sum = reduce_rows(grad_wdown, y, core)
+    up_sum = reduce_rows(grad_wup, y, core)
+    attn_sum = reduce_rows(jnp.concatenate([grad_wqkv, grad_wout], axis=1), y, core)
+    vec_flat = jnp.pad(vec_total.reshape(vec_rows, -1, vec_cols).transpose(1, 0, 2), ((0, 0), (0, 6), (0, 0)))
+    vec_sum = reduce_rows(vec_flat.reshape(-1, vec_cols * 2), y, core)
+    vec_sum = vec_sum.reshape(16, vec_cols)[:vec_rows]
+    square = jnp.sum(attn_sum * attn_sum) + jnp.sum(up_sum * up_sum)
+    square = square + jnp.sum(down_sum * down_sum) + jnp.sum(vec_sum * vec_sum)
+    dp_count = lax.axis_size(("hi", "lo"))
+    squares = lax.all_to_all(jnp.full((dp_count, 8, 128), square), ("hi", "lo"), 0, 0)
+    grad_norm = jnp.sqrt(jnp.sum(squares[:, 0, 0]))
     clip_factor = CLIP_NORM / jnp.maximum(grad_norm, CLIP_NORM)
+    mlp_sum = jnp.stack([up_sum, down_sum])
     attn_new = adam_update(
-        attn_w, attn_m, attn_v, attn_grad * clip_factor, WEIGHT_DECAY, LEARN_RATE
-    )
-    mlp_new = adam_update(mlp_w, mlp_m, mlp_v, mlp_grad * clip_factor, WEIGHT_DECAY, LEARN_RATE)
-    vec_new = adam_update(vec_w, vec_m, vec_v, vec_grad * clip_factor, 0.0, VEC_RATE)
-    return (
-        output,
-        input_grad,
-        attn_new[0],
-        attn_new[1],
-        attn_new[2],
-        mlp_new[0],
-        mlp_new[1],
-        mlp_new[2],
-        vec_new[0],
-        vec_new[1],
-        vec_new[2],
-        grad_norm,
-    )
+        attn_w, attn_m, attn_v, attn_sum * clip_factor, WEIGHT_DECAY, LEARN_RATE
+    )
+    mlp_new = adam_update(mlp_w, mlp_m, mlp_v, mlp_sum * clip_factor, WEIGHT_DECAY, LEARN_RATE)
+    vec_new = adam_update(vec_w, vec_m, vec_v, vec_sum * clip_factor, 0.0, VEC_RATE)
+    return (output, input_grad, *attn_new, *mlp_new, *vec_new, grad_norm)
 
 
 def solution(mesh):
-    placed = (
-        P(None, "dp", "seq", None),
-        P(None, "dp", "seq", None),
-        P(None, "dp"),
-        P("dp", None),
-        P("dp", None),
-        P("dp", None),
-        P(None, "dp", None),
-        P(None, "dp", None),
-        P(None, "dp", None),
-        P(None, "dp"),
-        P(None, "dp"),
-        P(None, "dp"),
-    )
+    dp_count = mesh.shape["dp"]
+    seq_count = mesh.shape["seq"]
+    fine = jax.sharding.Mesh(
+        mesh.devices.reshape(dp_count // 2, 2, seq_count // 2, 2), ("hi", "lo", "y", "core")
+    )
+    dp = ("hi", "lo")
+    seq = ("y", "core")
+    acts = P(None, dp, seq, None)
+    attn = P(dp, None)
+    mlp = P(None, dp, None)
+    vec = P(None, dp)
     return jax.shard_map(
         on_device,
-        mesh=mesh,
-        in_specs=placed,
-        out_specs=(
-            P(None, "dp", "seq", None),
-            P(None, "dp", "seq", None),
-            P("dp", None),
-            P("dp", None),
-            P("dp", None),
-            P(None, "dp", None),
-            P(None, "dp", None),
-            P(None, "dp", None),
-            P(None, "dp"),
-            P(None, "dp"),
-            P(None, "dp"),
-            P(),
-        ),
+        mesh=fine,
+        in_specs=(acts, acts, P(None, dp), attn, attn, attn, mlp, mlp, mlp, vec, vec, vec),
+        out_specs=(acts, acts, attn, attn, attn, mlp, mlp, mlp, vec, vec, vec, P()),
         check_vma=False,
     )

time: 481 us -> 371 us (0.77)
  waiting for transfers between devices: 204 us -> 64.9 us
  starting transfers between devices: 15.9 us -> 77.7 us
  blocking collectives: 89.6 us -> 30.9 us
  local copies, waits for them, and re-layouts: 25.3 us -> 48.2 us
  other arithmetic: 57.5 us -> 74.2 us
  between operations: 17.8 us -> 6.78 us
    psum x1 -> x0, waiting for transfers between devices: 135 us -> none  [on_device(): lax.psum((attn_total, mlp_total, vec_total), ('dp', 'seq'))]
    psum x1 -> x0, blocking collectives: 58.1 us -> none  [on_device(): lax.psum((attn_total, mlp_total, vec_total), ('dp', 'seq'))]
    all_gather x2 -> x0, waiting for transfers between devices: 45.4 us -> none  [the longest x1 45.4 us: on_device(): lax.all_gather(mlp_w.astype(jnp.bfloat16), 'dp', axis=1, tiled=True)]
    all_to_all x4 -> x13, starting transfers between devices: 15.8 us -> 53.1 us  [the longest x4 17.3 us: reduce_rows(): part = lax.all_to_all(part, 'hi', 0, 0)]
    ppermute x0 -> x36, starting transfers between devices: none -> 24.6 us  [the longest x24 17.1 us: swap(): return lax.ppermute(value, axis, [(0, 1), (1, 0)])]
    ppermute x0 -> x36, waiting for transfers between devices: none -> 23.9 us  [the longest x24 21.6 us: swap(): return lax.ppermute(value, axis, [(0, 1), (1, 0)])]
    all_to_all x4 -> x13, waiting for transfers between devices: 22.9 us -> 41 us  [the longest x4 20.3 us: gather_rows(): own = lax.all_to_all(spread, 'hi', 0, 0)]
    reshape x1 -> x13, local copies, waits for them, and re-layouts: 0.01 us -> 12.3 us  [the longest x8 12.1 us: reduce_rows(): part = part.reshape(hi_count, 2, rows, 2, quarter).transpose(1, 3, 0, 2, 4)]
  transfers between devices with their start and end apart: 7 -> 49, of which waited for: 4 -> 16; matrix products, arithmetic and copies ran while one was open for 10% -> 33% of each run, Pallas kernels for 0% -> 0%
where the time goes in v1:
time: 371 us; the launch traced here: 367 us
  starting transfers between devices  77.7 us (21%)
  other arithmetic  74.2 us (20%)
  waiting for transfers between devices  64.9 us (17%)
  matrix products  64 us (17%)
  local copies, waits for them, and re-layouts  48.2 us (13%)
  blocking collectives  30.9 us (8%)
  between operations  6.78 us (2%)
    all_gather x1, blocking collectives, on_device(): vec_all = lax.all_gather(vec_low, ('hi', 'lo'), axis=1, tiled=True)  30.9 us
    ppermute x24, waiting for transfers between devices, swap(): return lax.ppermute(value, axis, [(0, 1), (1, 0)])  21.6 us
    all_to_all x4, waiting for transfers between devices, gather_rows(): own = lax.all_to_all(spread, 'hi', 0, 0)  20.3 us
    convert_element_type x1, other arithmetic, layer_pass(): act = act_f.astype(jnp.bfloat16)  20.3 us
    all_to_all x4, starting transfers between devices, reduce_rows(): part = lax.all_to_all(part, 'hi', 0, 0)  17.3 us
    ppermute x24, starting transfers between devices, swap(): return lax.ppermute(value, axis, [(0, 1), (1, 0)])  17.1 us
    all_to_all x4, starting transfers between devices, gather_rows(): own = lax.all_to_all(spread, 'hi', 0, 0)  16.7 us
    another operation x28, other arithmetic, ordered(): return jnp.stack([first, second], axis)  16.3 us
  transfers between devices with their start and end apart: 49, of which 16 were waited for; matrix products, arithmetic and copies ran while one was open for 33% of the time, Pallas kernels for 0%

profile of v1, /device:TPU:0, one launch (start us, length us, event | category | flops | bytes accessed | tf_op | source)
XLA Modules:
  0.0 366.7 jit_solution(4877091724063768601)
XLA Ops:
  0.7 2.1 dynamic-slice_bitcast_fusion.7
  3.3 2.6 collective-permute-start.1
  6.7 5.1 %all-to-all-start.1 = ((bf16[4,32,512]{2,1,0:T(8,128)(2,1)}), bf16[4,32,512]{2,1,0:T(8,128)(2,1)S(1)}, u32[]{:S(2)}, u32[]{:S(2)}) async-start(bf16[4,32,512]{2,1,0:T(8,128)(2,1)} %broadcast_in_dim.72), calls=%async_computation.1 | async-start | bytes 262144 | tf_op jit(solution)/shard_map/all_to_all | solution.py:199
  11.7 2.2 dynamic-slice_bitcast_fusion.3
  15.6 30.9 %all-gather = bf16[8,64,10]{1,2,0:T(8,128)(2,1)S(1)} all-gather(bf16[1,64,10]{1,2,0:T(8,128)(2,1)S(1)} %convert_bitcast_fusion), channel_id=1, replica_groups=mesh['hi'=4,'lo'=2,'y'=2,'core'=2] {'hi','lo'}, dimensions={0}, use_global_device_ids=true | all-gather | bytes 11520 | tf_op jit(solution)/shard_map/all_gather | solution.py:256
  47.6 3.5 all-to-all-start
  51.4 8.5 %all-to-all-done = bf16[4,32,1536]{2,1,0:T(8,128)(2,1)S(1)} async-done(((bf16[4,32,1536]{2,1,0:T(8,128)(2,1)}), bf16[4,32,1536]{2,1,0:T(8,128)(2,1)S(1)}, u32[]{:S(2)}, u32[]{:S(2)}) %all-to-all-start) | async-done | bytes 393248 | tf_op jit(solution)/shard_map/all_to_all | solution.py:199
  60.8 4.1 %all-to-all-start.2 = ((bf16[4,32,2048]{2,1,0:T(8,128)(2,1)}), bf16[4,32,2048]{2,1,0:T(8,128)(2,1)}, u32[]{:S(2)}, u32[]{:S(2)}) async-start(bf16[4,32,2048]{2,1,0:T(8,128)(2,1)} %broadcast_in_dim.74), calls=%async_computation.2 | async-start | bytes 1048576 | tf_op jit(solution)/shard_map/all_to_all | solution.py:199
  65.1 2.7 collective-permute-start.6
  68.7 6.5 %all-to-all-done.2 = bf16[4,32,2048]{2,1,0:T(8,128)(2,1)} async-done(((bf16[4,32,2048]{2,1,0:T(8,128)(2,1)}), bf16[4,32,2048]{2,1,0:T(8,128)(2,1)}, u32[]{:S(2)}, u32[]{:S(2)}) %all-to-all-start.2) | async-done | bytes 524320 | tf_op jit(solution)/shard_map/all_to_all | solution.py:199
  76.1 4.0 %all-to-all-start.3 = ((bf16[4,32,2048]{2,1,0:T(8,128)(2,1)}), bf16[4,32,2048]{2,1,0:T(8,128)(2,1)S(1)}, u32[]{:S(2)}, u32[]{:S(2)}) async-start(bf16[4,32,2048]{2,1,0:T(8,128)(2,1)} %broadcast_in_dim.76), calls=%async_computation.3 | async-start | bytes 1048576 | tf_op jit(solution)/shard_map/all_to_all | solution.py:199
  80.2 2.7 collective-permute-start.3
  85.1 5.2 %all-to-all-done.3 = bf16[4,32,2048]{2,1,0:T(8,128)(2,1)S(1)} async-done(((bf16[4,32,2048]{2,1,0:T(8,128)(2,1)}), bf16[4,32,2048]{2,1,0:T(8,128)(2,1)S(1)}, u32[]{:S(2)}, u32[]{:S(2)}) %all-to-all-start.3) | async-done | bytes 524320 | tf_op jit(solution)/shard_map/all_to_all | solution.py:199
  90.3 2.5 collective-permute-done.3
  96.7 7.5 %collective-permute-done.9 = bf16[4,32,2048]{2,1,0:T(8,128)(2,1)} collective-permute-done((bf16[4,32,2048]{2,1,0:T(8,128)(2,1)}, bf16[4,32,2048]{2,1,0:T(8,128)(2,1)}, u32[]{:S(2)}, u32[]{:S(2)}) %collective-permute-start.9) | collective-permute-done | bytes 524320 | tf_op jit(solution)/shard_map/ppermute | solution.py:174
  104.2 2.2 select_bitcast_fusion.7
  106.5 8.7 %collective-permute-done.12 = bf16[4,32,2048]{2,1,0:T(8,128)(2,1)S(1)} collective-permute-done((bf16[4,32,2048]{2,1,0:T(8,128)(2,1)S(1)}, bf16[4,32,2048]{2,1,0:T(8,128)(2,1)S(1)}, u32[]{:S(2)}, u32[]{:S(2)}) %collective-permute-start.12) | collective-permute-done | bytes 524320 | tf_op jit(solution)/shard_map/ppermute | solution.py:174
  118.6 3.3 convolution_convert_fusion
  121.9 3.2 copy.277
  125.4 2.1 fusion.6
  127.5 2.0 exponential_reduce_fusion
  130.8 2.2 convolution_convert_fusion.1
  137.3 4.4 %fusion.26 = (u8[256,2048]{1,0:T(8,128)(4,1)S(1)}, u8[256,2048]{1,0:T(8,128)(4,1)S(1)}, f32[4,256,2048]{2,1,0:T(8,128)S(1)}) fusion(f32[2048]{0:T(1024)S(1)} %bitcast.271, bf16[512,2048,1]{1,0,2:T(8,128)(2,1)S(1)} %bitcast.252, f32[4,256,512]{2,1,0:T(8,128)S(1)} %get-tuple-element.115, f32[512]{0:T(512)S(1)} %bitcast.278, f32[512]{0:T(512)S(1)} %bitcast.274, ...), kind=kOutput, calls=%fused_computation.76 | convolution fusion | flops 2178416640 | bytes 13651968 | tf_op jit(solution)/shard_map/rpd,df->rpf/dot_general | solution.py:100
  141.7 20.3 %multiply_convert_fusion.1 = (bf16[4,256,2048]{2,1,0:T(8,128)(2,1)}, f32[4,256,2048]{2,1,0:T(8,128)S(1)}) fusion(f32[4,256,2048]{2,1,0:T(8,128)S(1)} %get-tuple-element.116, f32[2048]{0:T(1024)S(1)} %bitcast.272, u8[256,2048]{1,0:T(8,128)(4,1)S(1)} %get-tuple-element.13, u8[256,2048]{1,0:T(8,128)(4,1)S(1)} %get-tuple-element.12), kind=kLoop, calls=%fused_computation.11 | loop fusion | flops 148897792 | bytes 22028288 | tf_op jit(solution)/shard_map/convert_element_type | solution.py:102
  165.1 7.0 %convert_reduce_fusion = (f32[2048]{0:T(1024)S(1)}, bf16[4,256,2048]{2,1,0:T(8,128)(2,1)S(1)}) fusion(f32[4,256,2048]{2,1,0:T(8,128)S(1)} %get-tuple-element.35, bf16[512,2048,1]{1,0,2:T(8,128)(2,1)} %bitcast.250, bf16[4,64,512]{2,1,0:T(8,128)(2,1)} %collective-permute-done.20, bf16[4,64,512]{2,1,0:T(8,128)(2,1)} %collective-permute-done.19, ...), kind=kOutput, calls=%fused_computation.7 | convolution fusion | flops 2187327488 | bytes 24133632 | tf_op jit(solution)/shard_map/rpd,df->rpf/dot_general | solution.py:111
  172.1 6.0 %multiply_reduce_fusion.1 = (f32[512]{0:T(512)S(1)}, f32[4,256]{1,0:T(4,128)S(1)}, f32[512]{0:T(512)S(1)}, f32[4,256,512]{2,1,0:T(8,128)S(1)}) fusion(f32[4,256,512]{2,1,0:T(8,128)S(1)} %get-tuple-element.115, f32[4,256]{1,0:T(4,128)S(1)} %fusion.42, f32[4,256]{1,0:T(4,128)S(1)} %broadcast_multiply_fusion, f32[512]{0:T(512)S(1)} %bitcast.275, ...), kind=kOutput, calls=%fused_computation.65 | convolution fusion | flops 2151675904 | bytes 10504192 | tf_op jit(solution)/shard_map/rpf,df->rpd/dot_general | solution.py:115
  178.9 2.2 convert_reduce_fusion.3
  185.6 7.0 %multiply_reduce_fusion = (f32[4,8,256]{2,1,0:T(8,128)S(1)}, f32[4,8,256,256]{2,3,1,0:T(8,128)S(1)}) fusion(f32[4,8,256,256]{2,3,1,0:T(8,128)} %copy-done, f32[4,8,256]{2,1,0:T(8,128)S(1)} %log_add_fusion, pred[4,256]{1,0:T(4,128)(4,1)S(1)} %broadcast_compare_fusion, bf16[4,256,8,64]{1,3,2,0:T(8,128)(2,1)S(1)} %bitcast.240, bf16[4,256,8,64]{1,3,2,0:T(8,128)(2,1)} %bitcast.243), kind=kOutput, calls=%fused_computation.9 | convolution fusion | flops 278913024 | bytes 18940928 | tf_op jit(solution)/shard_map/rqhc,rkhc->rhqk/dot_general | solution.py:134
  192.6 2.6 multiply_convert_fusion
  197.8 2.1 fusion.35
  200.0 4.7 %convolution_bitcast_fusion.2 = f32[512,2048]{1,0:T(8,128)} fusion(bf16[4,256,2048]{2,1,0:T(8,128)(2,1)S(1)} %copy-done.9, f32[4,256,512]{2,1,0:T(8,128)S(1)} %get-tuple-element.115, f32[512]{0:T(512)S(1)} %bitcast.279, f32[512]{0:T(512)S(1)} %bitcast.277, f32[4,256]{1,0:T(4,128)S(1)} %fusion.42, f32[4,256]{1,0:T(4,128)S(1)} %broadcast_multiply_fusion), kind=kOutput, calls=%fused_computation.37 | convolution fusion | flops 2150105088 | bytes 10498048 | tf_op jit(solution)/shard_map/rpd,rpf->df/dot_general | solution.py:113
  207.1 2.3 fusion.47
  213.5 2.7 dynamic-slice_convert_fusion.1
  216.4 4.9 %convolution_bitcast_fusion.1 = f32[512,2048]{1,0:T(8,128)S(1)} fusion(bf16[4,256,2048]{2,1,0:T(8,128)(2,1)} %get-tuple-element.34, bf16[4,64,512]{2,1,0:T(8,128)(2,1)} %collective-permute-done.20, bf16[4,64,512]{2,1,0:T(8,128)(2,1)} %collective-permute-done.19, bf16[4,64,512]{2,1,0:T(8,128)(2,1)} %collective-permute-done.18, ...), kind=kOutput, calls=%fused_computation.36 | convolution fusion | flops 2151677952 | bytes 9437184 | tf_op jit(solution)/shard_map/rpd,rpf->df/dot_general | solution.py:109
  225.7 3.2 all-to-all-start.10
  228.9 5.7 %convolution_bitcast_fusion = f32[512,1536]{1,0:T(8,128)} fusion(bf16[4,256,1536]{1,2,0:T(8,128)(2,1)} %bitcast.248, f32[512]{0:T(512)S(1)} %bitcast.287, f32[512]{0:T(512)S(1)} %bitcast.283, f32[4,256]{1,0:T(4,128)S(1)} %fusion.41, f32[4,256]{1,0:T(4,128)S(1)} %broadcast_multiply_fusion.1, bf16[4,64,512]{2,1,0:T(8,128)(2,1)S(1)} %copy-done.23, ...), kind=kOutput, calls=%fused_computation.35 | convolution fusion | flops 1617428480 | bytes 7352320 | tf_op jit(solution)/shard_map/rpd,rpe->de/dot_general | solution.py:159
  235.4 5.1 %all-to-all-start.11 = ((bf16[4,2,128]{2,1,0:T(2,128)(2,1)}), bf16[4,2,128]{2,1,0:T(2,128)(2,1)S(1)}, u32[]{:S(2)}, u32[]{:S(2)}) async-start(bf16[4,2,128]{2,1,0:T(2,128)(2,1)} %reshape.1021), calls=%async_computation.11 | async-start | bytes 4096 | tf_op jit(solution)/shard_map/all_to_all | solution.py:223
  240.5 2.3 add_convert_fusion.2
  244.3 2.4 copy.305
  246.8 4.2 %all-to-all-start.6 = ((bf16[4,4,64,512]{3,2,1,0:T(8,128)(2,1)}), bf16[4,4,64,512]{3,2,1,0:T(8,128)(2,1)}, u32[]{:S(2)}, u32[]{:S(2)}) async-start(bf16[4,4,64,512]{3,2,1,0:T(8,128)(2,1)} %bitcast.94), calls=%async_computation.6 | async-start | bytes 2097152 | tf_op jit(solution)/shard_map/all_to_all | solution.py:221
  251.1 2.4 convolution_bitcast_fusion.3
  255.1 2.3 add_convert_fusion.1
  258.9 2.4 copy.308
  261.3 3.8 %all-to-all-done.6 = bf16[4,4,64,512]{3,2,1,0:T(8,128)(2,1)} async-done(((bf16[4,4,64,512]{3,2,1,0:T(8,128)(2,1)}), bf16[4,4,64,512]{3,2,1,0:T(8,128)(2,1)}, u32[]{:S(2)}, u32[]{:S(2)}) %all-to-all-start.6) | async-done | bytes 1048608 | tf_op jit(solution)/shard_map/all_to_all | solution.py:221
  265.1 4.2 %all-to-all-start.8 = ((bf16[4,4,64,512]{3,2,1,0:T(8,128)(2,1)}), bf16[4,4,64,512]{3,2,1,0:T(8,128)(2,1)}, u32[]{:S(2)}, u32[]{:S(2)}) async-start(bf16[4,4,64,512]{3,2,1,0:T(8,128)(2,1)} %bitcast.101), calls=%async_computation.8 | async-start | bytes 2097152 | tf_op jit(solution)/shard_map/all_to_all | solution.py:221
  269.3 3.2 add_convert_fusion.3
  273.4 2.0 collective-permute-start.34
  275.4 2.5 fusion.24
  279.5 2.4 copy.302
  283.2 3.7 %all-to-all-start.4 = ((bf16[4,4,64,512]{3,2,1,0:T(8,128)(2,1)}), bf16[4,4,64,512]{3,2,1,0:T(8,128)(2,1)S(1)}, u32[]{:S(2)}, u32[]{:S(2)}) async-start(bf16[4,4,64,512]{3,2,1,0:T(8,128)(2,1)} %bitcast.244), calls=%async_computation.4 | async-start | bytes 2097152 | tf_op jit(solution)/shard_map/all_to_all | solution.py:221
  286.9 5.2 %add_convert_fusion.4 = bf16[4,256,512]{2,1,0:T(8,128)(2,1)S(1)} fusion(f32[4,256,512]{2,1,0:T(8,128)S(1)} %get-tuple-element.115, bf16[4,256,2048]{2,1,0:T(8,128)(2,1)} %get-tuple-element.34, bf16[512,2048,1]{1,0,2:T(8,128)(2,1)} %bitcast.251, f32[512]{0:T(512)S(1)} %bitcast.285), kind=kOutput, calls=%fused_computation.72 | convolution fusion | flops 2149056512 | bytes 9439232 | tf_op jit(solution)/shard_map/rpf,df->rpd/dot_general | solution.py:105
  297.8 2.2 reduce_sum.339
  300.7 4.8 %all-to-all-start.7 = ((bf16[4,64,512]{2,1,0:T(8,128)(2,1)}), bf16[4,64,512]{2,1,0:T(8,128)(2,1)S(1)}, u32[]{:S(2)}, u32[]{:S(2)}) async-start(bf16[4,64,512]{2,1,0:T(8,128)(2,1)} %reduce_sum.339), calls=%async_computation.7 | async-start | bytes 524288 | tf_op jit(solution)/shard_map/all_to_all | solution.py:223
  308.7 2.2 reduce_sum.342
  310.8 3.1 all-to-all-done.7
  313.9 4.0 %all-to-all-start.9 = ((bf16[4,64,512]{2,1,0:T(8,128)(2,1)}), bf16[4,64,512]{2,1,0:T(8,128)(2,1)}, u32[]{:S(2)}, u32[]{:S(2)}) async-start(bf16[4,64,512]{2,1,0:T(8,128)(2,1)} %reduce_sum.342), calls=%async_computation.9 | async-start | bytes 524288 | tf_op jit(solution)/shard_map/all_to_all | solution.py:223
  319.2 2.3 collective-permute-done.17
  324.2 2.3 all-to-all-done.9
  326.5 3.4 all-to-all-start.5
  335.3 3.7 %all-to-all-done.5 = bf16[4,64,512]{2,1,0:T(8,128)(2,1)S(1)} async-done(((bf16[4,64,512]{2,1,0:T(8,128)(2,1)}), bf16[4,64,512]{2,1,0:T(8,128)(2,1)S(1)}, u32[]{:S(2)}, u32[]{:S(2)}) %all-to-all-start.5) | async-done | bytes 262176 | tf_op jit(solution)/shard_map/all_to_all | solution.py:223
  340.8 2.6 collective-permute-done.25
  349.2 3.7 %all-to-all-start.12 = ((f32[8,8,128]{2,1,0:T(8,128)}), f32[8,8,128]{2,1,0:T(8,128)S(1)}, u32[]{:S(2)}, u32[]{:S(2)}) async-start(f32[8,8,128]{2,1,0:T(8,128)} %broadcast_in_dim.81), calls=%async_computation.12 | async-start | bytes 65536 | tf_op jit(solution)/shard_map/all_to_all | solution.py:313
  353.9 5.7 %all-to-all-done.12 = f32[8,8,128]{2,1,0:T(8,128)S(1)} async-done(((f32[8,8,128]{2,1,0:T(8,128)}), f32[8,8,128]{2,1,0:T(8,128)S(1)}, u32[]{:S(2)}, u32[]{:S(2)}) %all-to-all-start.12) | async-done | bytes 32800 | tf_op jit(solution)/shard_map/all_to_all | solution.py:313
  363.2 2.3 multiply_subtract_fusion
  (334 shorter events, 80.6 us)
Async XLA Ops:
  2.8 12.7 %copy-start.53 = (f32[10,64]{1,0:T(8,128)S(1)}, f32[10,64]{1,0:T(8,128)}, u32[]{:S(2)}) copy-start(f32[10,64]{1,0:T(8,128)} %param.21) | copy-start | bytes 7684
  2.8 62.2 %collective-permute-start = (bf16[4,64,512]{2,1,0:T(8,128)(2,1)}, bf16[4,64,512]{2,1,0:T(8,128)(2,1)S(1)}, u32[]{:S(2)}, u32[]{:S(2)}) collective-permute-start(bf16[4,64,512]{2,1,0:T(8,128)(2,1)} %get-tuple-element.71), channel_id=1, source_target_pairs={{0,1},{1,0},{2,3},{3,2},{4,5},{5,4},{6,7},{7,6},{8,9},{9,8},{10,11... | collective-permute-start | bytes 786440 | tf_op jit(solution)/shard_map/ppermute | solution.py:190
  3.3 61.8 %collective-permute-start.1 = (bf16[4,64,512]{2,1,0:T(8,128)(2,1)}, bf16[4,64,512]{2,1,0:T(8,128)(2,1)S(1)}, u32[]{:S(2)}, u32[]{:S(2)}) collective-permute-start(bf16[4,64,512]{2,1,0:T(8,128)(2,1)} %get-tuple-element.73), channel_id=1, source_target_pairs={{0,2},{1,3},{2,0},{3,1},{4,6},{5,7},{6,4},{7,5},{8,10},{9,11},{10,... | collective-permute-start | bytes 786440 | tf_op jit(solution)/shard_map/ppermute | solution.py:190
  5.8 61.9 %collective-permute-start.2 = (bf16[4,64,512]{2,1,0:T(8,128)(2,1)}, bf16[4,64,512]{2,1,0:T(8,128)(2,1)S(1)}, u32[]{:S(2)}, u32[]{:S(2)}) collective-permute-start(bf16[4,64,512]{2,1,0:T(8,128)(2,1)} %get-tuple-element.72), channel_id=1, source_target_pairs={{0,3},{1,2},{2,1},{3,0},{4,7},{5,6},{6,5},{7,4},{8,11},{9,10},{10,... | collective-permute-start | bytes 786440 | tf_op jit(solution)/shard_map/ppermute | solution.py:190
  5.9 40.7 %copy-start.12 = (f32[2,64,2048]{2,1,0:T(8,128)S(1)}, f32[2,64,2048]{2,1,0:T(8,128)}, u32[]{:S(2)}) copy-start(f32[2,64,2048]{2,1,0:T(8,128)} %param.18) | copy-start | bytes 3145732
  6.7 40.1 %all-to-all-start.1 = ((bf16[4,32,512]{2,1,0:T(8,128)(2,1)}), bf16[4,32,512]{2,1,0:T(8,128)(2,1)S(1)}, u32[]{:S(2)}, u32[]{:S(2)}) async-start(bf16[4,32,512]{2,1,0:T(8,128)(2,1)} %broadcast_in_dim.72), calls=%async_computation.1 | async-start | bytes 262144 | tf_op jit(solution)/shard_map/all_to_all | solution.py:199
  14.0 151.1 %collective-permute-start.18 = (bf16[4,64,512]{2,1,0:T(8,128)(2,1)}, bf16[4,64,512]{2,1,0:T(8,128)(2,1)}, u32[]{:S(2)}, u32[]{:S(2)}) collective-permute-start(bf16[4,64,512]{2,1,0:T(8,128)(2,1)} %get-tuple-element.55), channel_id=1, source_target_pairs={{0,1},{1,0},{2,3},{3,2},{4,5},{5,4},{6,7},{7,6},{8,9},{9,8},{10,11... | collective-permute-start | bytes 786440 | tf_op jit(solution)/shard_map/ppermute | solution.py:190
  14.0 151.1 %collective-permute-start.19 = (bf16[4,64,512]{2,1,0:T(8,128)(2,1)}, bf16[4,64,512]{2,1,0:T(8,128)(2,1)}, u32[]{:S(2)}, u32[]{:S(2)}) collective-permute-start(bf16[4,64,512]{2,1,0:T(8,128)(2,1)} %get-tuple-element.57), channel_id=1, source_target_pairs={{0,2},{1,3},{2,0},{3,1},{4,6},{5,7},{6,4},{7,5},{8,10},{9,11},{10,... | collective-permute-start | bytes 786440 | tf_op jit(solution)/shard_map/ppermute | solution.py:190
  47.6 12.3 %all-to-all-start = ((bf16[4,32,1536]{2,1,0:T(8,128)(2,1)}), bf16[4,32,1536]{2,1,0:T(8,128)(2,1)S(1)}, u32[]{:S(2)}, u32[]{:S(2)}) async-start(bf16[4,32,1536]{2,1,0:T(8,128)(2,1)} %broadcast_in_dim.38), calls=%async_computation | async-start | bytes 786432 | tf_op jit(solution)/shard_map/all_to_all | solution.py:199
  60.8 14.5 %all-to-all-start.2 = ((bf16[4,32,2048]{2,1,0:T(8,128)(2,1)}), bf16[4,32,2048]{2,1,0:T(8,128)(2,1)}, u32[]{:S(2)}, u32[]{:S(2)}) async-start(bf16[4,32,2048]{2,1,0:T(8,128)(2,1)} %broadcast_in_dim.74), calls=%async_computation.2 | async-start | bytes 1048576 | tf_op jit(solution)/shard_map/all_to_all | solution.py:199
  65.0 52.4 %copy-start.15 = (bf16[4,64,512]{2,1,0:T(8,128)(2,1)}, bf16[4,64,512]{2,1,0:T(8,128)(2,1)S(1)}, u32[]{:S(2)}) copy-start(bf16[4,64,512]{2,1,0:T(8,128)(2,1)S(1)} %collective-permute-done) | copy-start | bytes 786436
  65.0 100.1 %collective-permute-start.20 = (bf16[4,64,512]{2,1,0:T(8,128)(2,1)}, bf16[4,64,512]{2,1,0:T(8,128)(2,1)}, u32[]{:S(2)}, u32[]{:S(2)}) collective-permute-start(bf16[4,64,512]{2,1,0:T(8,128)(2,1)} %get-tuple-element.56), channel_id=1, source_target_pairs={{0,3},{1,2},{2,1},{3,0},{4,7},{5,6},{6,5},{7,4},{8,11},{9,10},{10,... | collective-permute-start | bytes 786440 | tf_op jit(solution)/shard_map/ppermute | solution.py:190
  65.0 52.4 %copy-start.18 = (bf16[4,64,512]{2,1,0:T(8,128)(2,1)}, bf16[4,64,512]{2,1,0:T(8,128)(2,1)S(1)}, u32[]{:S(2)}) copy-start(bf16[4,64,512]{2,1,0:T(8,128)(2,1)S(1)} %collective-permute-done.1) | copy-start | bytes 786436
  65.1 15.1 %collective-permute-start.6 = (bf16[4,32,512]{2,1,0:T(8,128)(2,1)S(1)}, bf16[4,32,512]{2,1,0:T(8,128)(2,1)S(1)}, u32[]{:S(2)}, u32[]{:S(2)}) collective-permute-start(bf16[4,32,512]{2,1,0:T(8,128)(2,1)S(1)} %all-to-all-done.1), channel_id=1, source_target_pairs={{0,4},{4,0},{1,5},{5,1},{2,6},{6,2},{3,7},{7,3},{8,12},{12,8},{9,1... | collective-permute-start | bytes 393224 | tf_op jit(solution)/shard_map/ppermute | solution.py:174
  67.7 49.7 %copy-start.21 = (bf16[4,64,512]{2,1,0:T(8,128)(2,1)}, bf16[4,64,512]{2,1,0:T(8,128)(2,1)S(1)}, u32[]{:S(2)}) copy-start(bf16[4,64,512]{2,1,0:T(8,128)(2,1)S(1)} %collective-permute-done.2) | copy-start | bytes 786436
  67.7 12.5 %collective-permute-start.7 = (bf16[4,32,512]{2,1,0:T(8,128)(2,1)S(1)}, bf16[4,32,512]{2,1,0:T(8,128)(2,1)S(1)}, u32[]{:S(2)}, u32[]{:S(2)}) collective-permute-start(bf16[4,32,512]{2,1,0:T(8,128)(2,1)S(1)} %all-to-all-done.1), channel_id=1, source_target_pairs={{0,1},{1,0},{2,3},{3,2},{4,5},{5,4},{6,7},{7,6},{8,9},{9,8},{10,11... | collective-permute-start | bytes 393224 | tf_op jit(solution)/shard_map/ppermute | solution.py:174
  76.1 14.2 %all-to-all-start.3 = ((bf16[4,32,2048]{2,1,0:T(8,128)(2,1)}), bf16[4,32,2048]{2,1,0:T(8,128)(2,1)S(1)}, u32[]{:S(2)}, u32[]{:S(2)}) async-start(bf16[4,32,2048]{2,1,0:T(8,128)(2,1)} %broadcast_in_dim.76), calls=%async_computation.3 | async-start | bytes 1048576 | tf_op jit(solution)/shard_map/all_to_all | solution.py:199
  80.1 2.8 collective-permute-start.8
  80.2 12.6 %collective-permute-start.3 = (bf16[4,32,1536]{2,1,0:T(8,128)(2,1)S(1)}, bf16[4,32,1536]{2,1,0:T(8,128)(2,1)S(1)}, u32[]{:S(2)}, u32[]{:S(2)}) collective-permute-start(bf16[4,32,1536]{2,1,0:T(8,128)(2,1)S(1)} %all-to-all-done), channel_id=1, source_target_pairs={{0,4},{4,0},{1,5},{5,1},{2,6},{6,2},{3,7},{7,3},{8,12},{12,8},{9,1... | collective-permute-start | bytes 1179656 | tf_op jit(solution)/shard_map/ppermute | solution.py:174
  83.0 21.2 %collective-permute-start.9 = (bf16[4,32,2048]{2,1,0:T(8,128)(2,1)}, bf16[4,32,2048]{2,1,0:T(8,128)(2,1)}, u32[]{:S(2)}, u32[]{:S(2)}) collective-permute-start(bf16[4,32,2048]{2,1,0:T(8,128)(2,1)} %all-to-all-done.2), channel_id=1, source_target_pairs={{0,4},{4,0},{1,5},{5,1},{2,6},{6,2},{3,7},{7,3},{8,12},{12,8},{9,1... | collective-permute-start | bytes 1572872 | tf_op jit(solution)/shard_map/ppermute | solution.py:174
  90.3 25.9 %copy-start.34 = (bf16[4,32,2048]{2,1,0:T(8,128)(2,1)}, bf16[4,32,2048]{2,1,0:T(8,128)(2,1)S(1)}, u32[]{:S(2)}) copy-start(bf16[4,32,2048]{2,1,0:T(8,128)(2,1)S(1)} %all-to-all-done.3) | copy-start | bytes 1572868
  93.6 21.5 %collective-permute-start.12 = (bf16[4,32,2048]{2,1,0:T(8,128)(2,1)S(1)}, bf16[4,32,2048]{2,1,0:T(8,128)(2,1)S(1)}, u32[]{:S(2)}, u32[]{:S(2)}) collective-permute-start(bf16[4,32,2048]{2,1,0:T(8,128)(2,1)S(1)} %all-to-all-done.3), channel_id=1, source_target_pairs={{0,4},{4,0},{1,5},{5,1},{2,6},{6,2},{3,7},{7,3},{8,12},{12,8},{9,1... | collective-permute-start | bytes 1572872 | tf_op jit(solution)/shard_map/ppermute | solution.py:174
  95.6 19.6 %copy-start.52 = (bf16[4,32,1536]{2,1,0:T(8,128)(2,1)S(1)}, bf16[4,32,1536]{2,1,0:T(8,128)(2,1)}, u32[]{:S(2)}) copy-start(bf16[4,32,1536]{2,1,0:T(8,128)(2,1)} %copy-done.51) | copy-start | bytes 1179652
  104.2 12.1 %collective-permute-start.4 = (bf16[4,32,1536]{2,1,0:T(8,128)(2,1)S(1)}, bf16[4,32,1536]{2,1,0:T(8,128)(2,1)S(1)}, u32[]{:S(2)}, u32[]{:S(2)}) collective-permute-start(bf16[4,32,1536]{2,1,0:T(8,128)(2,1)S(1)} %all-to-all-done), channel_id=1, source_target_pairs={{0,1},{1,0},{2,3},{3,2},{4,5},{5,4},{6,7},{7,6},{8,9},{9,8},{10,11... | collective-permute-start | bytes 1179656 | tf_op jit(solution)/shard_map/ppermute | solution.py:174
  115.1 1.7 collective-permute-start.5
  116.3 18.2 %collective-permute-start.10 = (bf16[4,32,2048]{2,1,0:T(8,128)(2,1)}, bf16[4,32,2048]{2,1,0:T(8,128)(2,1)}, u32[]{:S(2)}, u32[]{:S(2)}) collective-permute-start(bf16[4,32,2048]{2,1,0:T(8,128)(2,1)} %all-to-all-done.2), channel_id=1, source_target_pairs={{0,1},{1,0},{2,3},{3,2},{4,5},{5,4},{6,7},{7,6},{8,9},{9,8},{10,11... | collective-permute-start | bytes 1572872 | tf_op jit(solution)/shard_map/ppermute | solution.py:174
  116.9 18.5 %collective-permute-start.11 = (bf16[4,32,2048]{2,1,0:T(8,128)(2,1)}, bf16[4,32,2048]{2,1,0:T(8,128)(2,1)}, u32[]{:S(2)}, u32[]{:S(2)}) collective-permute-start(bf16[4,32,2048]{2,1,0:T(8,128)(2,1)} %collective-permute-done.9), channel_id=1, source_target_pairs={{0,1},{1,0},{2,3},{3,2},{4,5},{5,4},{6,7},{7,6},{8,9},{9,8},{10,11... | collective-permute-start | bytes 1572872 | tf_op jit(solution)/shard_map/ppermute | solution.py:174
  135.0 27.0 %collective-permute-start.13 = (bf16[4,32,2048]{2,1,0:T(8,128)(2,1)S(1)}, bf16[4,32,2048]{2,1,0:T(8,128)(2,1)S(1)}, u32[]{:S(2)}, u32[]{:S(2)}) collective-permute-start(bf16[4,32,2048]{2,1,0:T(8,128)(2,1)S(1)} %copy-done.35), channel_id=1, source_target_pairs={{0,1},{1,0},{2,3},{3,2},{4,5},{5,4},{6,7},{7,6},{8,9},{9,8},{10,11... | collective-permute-start | bytes 1572872 | tf_op jit(solution)/shard_map/ppermute | solution.py:174
  135.4 26.6 %collective-permute-start.14 = (bf16[4,32,2048]{2,1,0:T(8,128)(2,1)S(1)}, bf16[4,32,2048]{2,1,0:T(8,128)(2,1)S(1)}, u32[]{:S(2)}, u32[]{:S(2)}) collective-permute-start(bf16[4,32,2048]{2,1,0:T(8,128)(2,1)S(1)} %copy-done.48), channel_id=1, source_target_pairs={{0,1},{1,0},{2,3},{3,2},{4,5},{5,4},{6,7},{7,6},{8,9},{9,8},{10,11... | collective-permute-start | bytes 1572872 | tf_op jit(solution)/shard_map/ppermute | solution.py:174
  185.5 7.0 %slice-start = ((s8[8388608]{0:T(1024)(128)(4,1)}), s8[4194304]{0:T(1024)(128)(4,1)S(1)}, s32[]{:S(2)}) async-start(s8[8388608]{0:T(1024)(128)(4,1)} %bitcast.233), calls=%async_computation.13 | async-start | bytes 8388608
  185.6 7.0 %slice-start.1 = ((s8[8388608]{0:T(1024)(128)(4,1)}), s8[4194304]{0:T(1024)(128)(4,1)S(1)}, s32[]{:S(2)}) async-start(s8[8388608]{0:T(1024)(128)(4,1)} %bitcast.233), calls=%async_computation.14 | async-start | bytes 8388608
  213.2 11.6 %collective-permute-start.33 = (bf16[64,64]{1,0:T(8,128)(2,1)S(1)}, bf16[64,64]{1,0:T(8,128)(2,1)S(1)}, u32[]{:S(2)}, u32[]{:S(2)}) collective-permute-start(bf16[64,64]{1,0:T(8,128)(2,1)S(1)} %dynamic-slice_convert_fusion.2), channel_id=1, source_target_pairs={{0,1},{1,0},{2,3},{3,2},{4,5},{5,4},{6,7},{7,6},{8,9},{9,8},{10,11... | collective-permute-start | bytes 24584 | tf_op jit(solution)/shard_map/ppermute | solution.py:174
  216.3 24.2 %collective-permute-start.27 = (bf16[512,1024]{1,0:T(8,128)(2,1)}, bf16[512,1024]{1,0:T(8,128)(2,1)}, u32[]{:S(2)}, u32[]{:S(2)}) collective-permute-start(bf16[512,1024]{1,0:T(8,128)(2,1)} %dynamic-slice_convert_fusion.1), channel_id=1, source_target_pairs={{0,1},{1,0},{2,3},{3,2},{4,5},{5,4},{6,7},{7,6},{8,9},{9,8},{10,11... | collective-permute-start | bytes 3145736 | tf_op jit(solution)/shard_map/ppermute | solution.py:174
  224.4 30.6 %collective-permute-start.30 = (bf16[512,1024]{1,0:T(8,128)(2,1)}, bf16[512,1024]{1,0:T(8,128)(2,1)}, u32[]{:S(2)}, u32[]{:S(2)}) collective-permute-start(bf16[512,1024]{1,0:T(8,128)(2,1)} %dynamic-slice_convert_fusion), channel_id=1, source_target_pairs={{0,1},{1,0},{2,3},{3,2},{4,5},{5,4},{6,7},{7,6},{8,9},{9,8},{10,11... | collective-permute-start | bytes 3145736 | tf_op jit(solution)/shard_map/ppermute | solution.py:174
  225.7 9.0 %all-to-all-start.10 = ((bf16[4,2,512]{2,1,0:T(2,128)(2,1)}), bf16[4,2,512]{2,1,0:T(2,128)(2,1)S(1)}, u32[]{:S(2)}, u32[]{:S(2)}) async-start(bf16[4,2,512]{2,1,0:T(2,128)(2,1)} %reshape.1019), calls=%async_computation.10 | async-start | bytes 16384 | tf_op jit(solution)/shard_map/all_to_all | solution.py:221
  235.4 11.4 %all-to-all-start.11 = ((bf16[4,2,128]{2,1,0:T(2,128)(2,1)}), bf16[4,2,128]{2,1,0:T(2,128)(2,1)S(1)}, u32[]{:S(2)}, u32[]{:S(2)}) async-start(bf16[4,2,128]{2,1,0:T(2,128)(2,1)} %reshape.1021), calls=%async_computation.11 | async-start | bytes 4096 | tf_op jit(solution)/shard_map/all_to_all | solution.py:223
  246.8 18.3 %all-to-all-start.6 = ((bf16[4,4,64,512]{3,2,1,0:T(8,128)(2,1)}), bf16[4,4,64,512]{3,2,1,0:T(8,128)(2,1)}, u32[]{:S(2)}, u32[]{:S(2)}) async-start(bf16[4,4,64,512]{3,2,1,0:T(8,128)(2,1)} %bitcast.94), calls=%async_computation.6 | async-start | bytes 2097152 | tf_op jit(solution)/shard_map/all_to_all | solution.py:221
  255.0 20.4 %collective-permute-start.24 = (bf16[512,1024]{1,0:T(8,128)(2,1)}, bf16[512,1024]{1,0:T(8,128)(2,1)}, u32[]{:S(2)}, u32[]{:S(2)}) collective-permute-start(bf16[512,1024]{1,0:T(8,128)(2,1)} %fusion.21), channel_id=1, source_target_pairs={{0,1},{1,0},{2,3},{3,2},{4,5},{5,4},{6,7},{7,6},{8,9},{9,8},{10,11... | collective-permute-start | bytes 3145736 | tf_op jit(solution)/shard_map/ppermute | solution.py:174
  265.1 18.1 %all-to-all-start.8 = ((bf16[4,4,64,512]{3,2,1,0:T(8,128)(2,1)}), bf16[4,4,64,512]{3,2,1,0:T(8,128)(2,1)}, u32[]{:S(2)}, u32[]{:S(2)}) async-start(bf16[4,4,64,512]{3,2,1,0:T(8,128)(2,1)} %bitcast.101), calls=%async_computation.8 | async-start | bytes 2097152 | tf_op jit(solution)/shard_map/all_to_all | solution.py:221
  273.3 20.5 %collective-permute-start.21 = (bf16[4,64,512]{2,1,0:T(8,128)(2,1)}, bf16[4,64,512]{2,1,0:T(8,128)(2,1)S(1)}, u32[]{:S(2)}, u32[]{:S(2)}) collective-permute-start(bf16[4,64,512]{2,1,0:T(8,128)(2,1)} %slice.121), channel_id=1, source_target_pairs={{0,1},{1,0},{2,3},{3,2},{4,5},{5,4},{6,7},{7,6},{8,9},{9,8},{10,11... | collective-permute-start | bytes 786440 | tf_op jit(solution)/shard_map/ppermute | solution.py:190
  273.4 19.8 %collective-permute-start.34 = (bf16[8,32]{1,0:T(8,128)(2,1)S(1)}, bf16[8,32]{1,0:T(8,128)(2,1)S(1)}, u32[]{:S(2)}, u32[]{:S(2)}) collective-permute-start(bf16[8,32]{1,0:T(8,128)(2,1)S(1)} %reduce_sum.353), channel_id=1, source_target_pairs={{0,2},{2,0},{1,3},{3,1},{4,6},{6,4},{5,7},{7,5},{8,10},{10,8},{9,1... | collective-permute-start | bytes 1544 | tf_op jit(solution)/shard_map/ppermute | solution.py:174
  283.2 17.6 %all-to-all-start.4 = ((bf16[4,4,64,512]{3,2,1,0:T(8,128)(2,1)}), bf16[4,4,64,512]{3,2,1,0:T(8,128)(2,1)S(1)}, u32[]{:S(2)}, u32[]{:S(2)}) async-start(bf16[4,4,64,512]{3,2,1,0:T(8,128)(2,1)} %bitcast.244), calls=%async_computation.4 | async-start | bytes 2097152 | tf_op jit(solution)/shard_map/all_to_all | solution.py:221
  293.1 13.1 %copy-start.40 = (bf16[4,256,512]{2,1,0:T(8,128)(2,1)S(1)}, bf16[4,256,512]{2,1,0:T(8,128)(2,1)}, u32[]{:S(2)}) copy-start(bf16[4,256,512]{2,1,0:T(8,128)(2,1)} %copy-done.39) | copy-start | bytes 3145732
  293.1 13.1 %collective-permute-start.15 = (bf16[4,64,512]{2,1,0:T(8,128)(2,1)S(1)}, bf16[4,64,512]{2,1,0:T(8,128)(2,1)}, u32[]{:S(2)}, u32[]{:S(2)}) collective-permute-start(bf16[4,64,512]{2,1,0:T(8,128)(2,1)S(1)} %slice.117), channel_id=1, source_target_pairs={{0,1},{1,0},{2,3},{3,2},{4,5},{5,4},{6,7},{7,6},{8,9},{9,8},{10,11... | collective-permute-start | bytes 786440 | tf_op jit(solution)/shard_map/ppermute | solution.py:190
  293.3 12.2 %collective-permute-start.35 = (bf16[8,64]{1,0:T(8,128)(2,1)S(1)}, bf16[8,64]{1,0:T(8,128)(2,1)S(1)}, u32[]{:S(2)}, u32[]{:S(2)}) collective-permute-start(bf16[8,64]{1,0:T(8,128)(2,1)S(1)} %reshape.1007), channel_id=1, source_target_pairs={{0,1},{1,0},{2,3},{3,2},{4,5},{5,4},{6,7},{7,6},{8,9},{9,8},{10,11... | collective-permute-start | bytes 3080 | tf_op jit(solution)/shard_map/ppermute | solution.py:174
  295.8 22.2 %collective-permute-start.22 = (bf16[4,64,512]{2,1,0:T(8,128)(2,1)}, bf16[4,64,512]{2,1,0:T(8,128)(2,1)}, u32[]{:S(2)}, u32[]{:S(2)}) collective-permute-start(bf16[4,64,512]{2,1,0:T(8,128)(2,1)} %get-tuple-element.53), channel_id=1, source_target_pairs={{0,2},{1,3},{2,0},{3,1},{4,6},{5,7},{6,4},{7,5},{8,10},{9,11},{10,... | collective-permute-start | bytes 786440 | tf_op jit(solution)/shard_map/ppermute | solution.py:190
  297.8 20.2 %collective-permute-start.23 = (bf16[4,64,512]{2,1,0:T(8,128)(2,1)}, bf16[4,64,512]{2,1,0:T(8,128)(2,1)}, u32[]{:S(2)}, u32[]{:S(2)}) collective-permute-start(bf16[4,64,512]{2,1,0:T(8,128)(2,1)} %get-tuple-element.52), channel_id=1, source_target_pairs={{0,3},{1,2},{2,1},{3,0},{4,7},{5,6},{6,5},{7,4},{8,11},{9,10},{10,... | collective-permute-start | bytes 786440 | tf_op jit(solution)/shard_map/ppermute | solution.py:190
  300.7 13.2 %all-to-all-start.7 = ((bf16[4,64,512]{2,1,0:T(8,128)(2,1)}), bf16[4,64,512]{2,1,0:T(8,128)(2,1)S(1)}, u32[]{:S(2)}, u32[]{:S(2)}) async-start(bf16[4,64,512]{2,1,0:T(8,128)(2,1)} %reduce_sum.339), calls=%async_computation.7 | async-start | bytes 524288 | tf_op jit(solution)/shard_map/all_to_all | solution.py:223
  308.0 11.2 %collective-permute-start.16 = (bf16[4,64,512]{2,1,0:T(8,128)(2,1)}, bf16[4,64,512]{2,1,0:T(8,128)(2,1)}, u32[]{:S(2)}, u32[]{:S(2)}) collective-permute-start(bf16[4,64,512]{2,1,0:T(8,128)(2,1)} %get-tuple-element.61), channel_id=1, source_target_pairs={{0,2},{1,3},{2,0},{3,1},{4,6},{5,7},{6,4},{7,5},{8,10},{9,11},{10,... | collective-permute-start | bytes 786440 | tf_op jit(solution)/shard_map/ppermute | solution.py:190
  308.6 12.9 %collective-permute-start.17 = (bf16[4,64,512]{2,1,0:T(8,128)(2,1)}, bf16[4,64,512]{2,1,0:T(8,128)(2,1)}, u32[]{:S(2)}, u32[]{:S(2)}) collective-permute-start(bf16[4,64,512]{2,1,0:T(8,128)(2,1)} %get-tuple-element.60), channel_id=1, source_target_pairs={{0,3},{1,2},{2,1},{3,0},{4,7},{5,6},{6,5},{7,4},{8,11},{9,10},{10,... | collective-permute-start | bytes 786440 | tf_op jit(solution)/shard_map/ppermute | solution.py:190
  313.9 12.6 %all-to-all-start.9 = ((bf16[4,64,512]{2,1,0:T(8,128)(2,1)}), bf16[4,64,512]{2,1,0:T(8,128)(2,1)}, u32[]{:S(2)}, u32[]{:S(2)}) async-start(bf16[4,64,512]{2,1,0:T(8,128)(2,1)} %reduce_sum.342), calls=%async_computation.9 | async-start | bytes 524288 | tf_op jit(solution)/shard_map/all_to_all | solution.py:223
  326.5 12.6 %all-to-all-start.5 = ((bf16[4,64,512]{2,1,0:T(8,128)(2,1)}), bf16[4,64,512]{2,1,0:T(8,128)(2,1)S(1)}, u32[]{:S(2)}, u32[]{:S(2)}) async-start(bf16[4,64,512]{2,1,0:T(8,128)(2,1)} %reduce_sum.336), calls=%async_computation.5 | async-start | bytes 524288 | tf_op jit(solution)/shard_map/all_to_all | solution.py:223
  331.1 8.9 %collective-permute-start.28 = (bf16[64,512]{1,0:T(8,128)(2,1)S(1)}, bf16[64,512]{1,0:T(8,128)(2,1)S(1)}, u32[]{:S(2)}, u32[]{:S(2)}) collective-permute-start(bf16[64,512]{1,0:T(8,128)(2,1)S(1)} %reduce_sum.340), channel_id=1, source_target_pairs={{0,2},{2,0},{1,3},{3,1},{4,6},{6,4},{5,7},{7,5},{8,10},{10,8},{9,1... | collective-permute-start | bytes 196616 | tf_op jit(solution)/shard_map/ppermute | solution.py:174
  334.9 5.3 %collective-permute-start.31 = (bf16[64,512]{1,0:T(8,128)(2,1)S(1)}, bf16[64,512]{1,0:T(8,128)(2,1)S(1)}, u32[]{:S(2)}, u32[]{:S(2)}) collective-permute-start(bf16[64,512]{1,0:T(8,128)(2,1)S(1)} %reduce_sum.343), channel_id=1, source_target_pairs={{0,2},{2,0},{1,3},{3,1},{4,6},{6,4},{5,7},{7,5},{8,10},{10,8},{9,1... | collective-permute-start | bytes 196616 | tf_op jit(solution)/shard_map/ppermute | solution.py:174
  339.1 4.3 %collective-permute-start.25 = (bf16[64,512]{1,0:T(8,128)(2,1)S(1)}, bf16[64,512]{1,0:T(8,128)(2,1)S(1)}, u32[]{:S(2)}, u32[]{:S(2)}) collective-permute-start(bf16[64,512]{1,0:T(8,128)(2,1)S(1)} %reduce_sum.337), channel_id=1, source_target_pairs={{0,2},{2,0},{1,3},{3,1},{4,6},{6,4},{5,7},{7,5},{8,10},{10,8},{9,1... | collective-permute-start | bytes 196616 | tf_op jit(solution)/shard_map/ppermute | solution.py:174
  340.1 3.5 collective-permute-start.29
  340.3 3.3 collective-permute-start.32
  343.5 1.7 collective-permute-start.26
  349.2 10.4 %all-to-all-start.12 = ((f32[8,8,128]{2,1,0:T(8,128)}), f32[8,8,128]{2,1,0:T(8,128)S(1)}, u32[]{:S(2)}, u32[]{:S(2)}) async-start(f32[8,8,128]{2,1,0:T(8,128)} %broadcast_in_dim.81), calls=%async_computation.12 | async-start | bytes 65536 | tf_op jit(solution)/shard_map/all_to_all | solution.py:313
  352.9 8.1 %copy-start.54 = (f32[10,64]{1,0:T(8,128)S(1)}, f32[10,64]{1,0:T(8,128)}, u32[]{:S(2)}) copy-start(f32[10,64]{1,0:T(8,128)} %param.22) | copy-start | bytes 7684
  352.9 8.1 %copy-start.55 = (f32[10,64]{1,0:T(8,128)S(1)}, f32[10,64]{1,0:T(8,128)}, u32[]{:S(2)}) copy-start(f32[10,64]{1,0:T(8,128)} %param.23) | copy-start | bytes 7684
  352.9 8.8 %copy-start.33 = (f32[64,2048]{1,0:T(8,128)S(1)}, f32[64,2048]{1,0:T(8,128)}, u32[]{:S(2)}) copy-start(f32[64,2048]{1,0:T(8,128)} %param.15) | copy-start | bytes 1572868
  352.9 8.8 %copy-start.45 = (f32[64,2048]{1,0:T(8,128)S(1)}, f32[64,2048]{1,0:T(8,128)}, u32[]{:S(2)}) copy-start(f32[64,2048]{1,0:T(8,128)} %param.16) | copy-start | bytes 1572868
  353.0 8.8 %copy-start.46 = (f32[64,2048]{1,0:T(8,128)S(1)}, f32[64,2048]{1,0:T(8,128)}, u32[]{:S(2)}) copy-start(f32[64,2048]{1,0:T(8,128)} %param.17) | copy-start | bytes 1572868
  (45 other events, 108.5 us)

commit v2 on v1

v2 whole, which is shorter than its diff:
```python
import functools
import math

import jax
import jax.numpy as jnp
from jax import lax
from jax.experimental import pallas as pl
from jax.experimental.pallas import tpu as pltpu
from jax.sharding import PartitionSpec as P

HEADS = 8
ADAM_STEP = 10
CLIP_NORM = 1.0
BETA_ONE = 0.9
BETA_TWO = 0.999
LEARN_RATE = 0.08
VEC_RATE = 0.4
WEIGHT_DECAY = 0.01
ADAM_EPS = 1e-08
NORM_EPS = 1e-05
VMEM_BYTES = 60 * 1024 * 1024

TAIL_SCALE = 0.4 / math.sqrt(2.0)
TAIL = (
    0.2256758631446491,
    0.22566953041000726,
    0.2078437638365498,
    0.16853459369628254,
    0.1414582080030511,
    -0.005661972621845868,
    0.1691478544806666,
    -0.18293913558029784,
    0.05027141967490775,
)
F32 = jnp.float32
BF16 = jnp.bfloat16
ANY = pl.BlockSpec(memory_space=pl.ANY)
SMEM = pl.BlockSpec(memory_space=pltpu.SMEM)


def nt_dot(left, right):
    return lax.dot_general(left, right, (((1,), (1,)), ((), ())), preferred_element_type=F32)


def nn_dot(left, right):
    return jnp.dot(left, right, preferred_element_type=F32)


def centered(values):
    center = values - jnp.mean(values, axis=-1, keepdims=True)
    spread = jnp.mean(center * center, axis=-1, keepdims=True)
    scale = lax.rsqrt(spread + NORM_EPS)
    return center * scale, scale


def norm_back(unit, scale, grad):
    mean_grad = jnp.mean(grad, axis=-1, keepdims=True)
    mean_both = jnp.mean(grad * unit, axis=-1, keepdims=True)
    return scale * (grad - mean_grad - unit * mean_both)


def gelu_and_slope(up):
    size = jnp.abs(up)
    t = 1.0 / (1.0 + TAIL_SCALE * size)
    poly = jnp.full_like(t, TAIL[-1])
    for coef in TAIL[-2::-1]:
        poly = poly * t + coef
    bell = jnp.exp(-0.5 * up * up)
    tail = 0.5 * (t * poly) * bell
    share = jnp.where(up >= 0, 1.0 - tail, tail)
    return up * share, share + up * (bell * (1.0 / math.sqrt(2.0 * math.pi)))


def placements(pieces, jobs, place, sems):
    lo = place[0]
    core = place[1]
    copies = []
    for i, piece in enumerate(pieces):
        lo_at = lo if i % 2 == 0 else 1 - lo
        core_at = core if i < 2 else 1 - core
        hi_count, rows, _ = piece.shape
        for h in range(hi_count):
            row = pl.multiple_of(((h * 2 + lo_at) * 2 + core_at) * rows, rows)
            for column, width, target in jobs:
                copies.append(
                    pltpu.make_async_copy(
                        piece.at[h, :, pl.ds(column, width)],
                        target.at[pl.ds(row, rows), :],
                        sems.at[len(copies)],
                    )
                )
    return copies


def dp_placements(pieces, target, place, sems):
    copies = []
    for i, piece in enumerate(pieces):
        core_at = place[1] if i == 0 else 1 - place[1]
        dp_count, rows, _ = piece.shape
        for d in range(dp_count):
            row = pl.multiple_of((d * 2 + core_at) * rows, rows)
            copies.append(
                pltpu.make_async_copy(
                    piece.at[d], target.at[pl.ds(row, rows), :], sems.at[len(copies)]
                )
            )
    return copies


def head_masks(width):
    lane = lax.broadcasted_iota(jnp.int32, (1, width), 1)
    first = jnp.where(lane < width // 2, 1.0, 0.0)
    return first.astype(BF16), (1.0 - first).astype(BF16)


def fill_bias(place, lengths, row, bias):
    part = bias.shape[0] // 4
    for k in range(4):
        base = (place[2] ^ k) * part
        slot = lax.broadcasted_iota(jnp.int32, (part, bias.shape[1]), 0) + base
        bias[k * part : (k + 1) * part, :] = jnp.where(slot < lengths[row], 0.0, -1e30)


def qkv_body(place, x0, x1, x2, x3, p0, p1, p2, p3, vec, h_out, qkv_out, w_qkv, sems):
    row = pl.program_id(0)
    width = vec.shape[1]
    copies = placements((p0, p1, p2, p3), [(0, 3 * width, w_qkv)], place, sems)

    @pl.when(row == 0)
    def _():
        for copy in copies:
            copy.start()

    x = jnp.concatenate([ref[0] for ref in (x0, x1, x2, x3)], axis=0).astype(F32)
    unit, _ = centered(x)
    h = (unit * vec[0:1] + vec[1:2]).astype(BF16)
    h_out[...] = h

    @pl.when(row == 0)
    def _():
        for copy in copies:
            copy.wait()

    q = nn_dot(h, w_qkv[:, :width]).astype(BF16)
    qkv_out[:, :width] = q * jnp.asarray(1.0 / math.sqrt(width // HEADS), BF16)
    qkv_out[:, width:] = nn_dot(h, w_qkv[:, width:]).astype(BF16)


def attend_body(place, lengths, qkv, attn_out, lse_out, bias):
    row = pl.program_id(0)
    width = attn_out.shape[1]
    pair = 2 * (width // HEADS)
    fill_bias(place, lengths, row, bias)
    masks = head_masks(pair)
    for p in range(HEADS // 2):
        at = p * pair
        qp = qkv[:, at : at + pair]
        kp = qkv[:, width + at : width + at + pair]
        v_turned = qkv[:, 2 * width + at : 2 * width + at + pair].T
        outs = []
        for i in range(2):
            scores = nt_dot(kp, qp * masks[i]) + bias[...]
            top = jnp.max(scores, axis=0, keepdims=True)
            grown = jnp.exp(scores - top)
            total = jnp.sum(grown, axis=0, keepdims=True)
            lse_out[0, 2 * p + i : 2 * p + i + 1, :] = top + jnp.log(total)
            probs = (grown * (1.0 / total)).astype(BF16)
            outs.append(nn_dot(v_turned[i * (pair // 2) : (i + 1) * (pair // 2)], probs))
        attn_out[:, at : at + pair] = jnp.concatenate(outs, axis=0).T.astype(BF16)


def up_body(
    place, x0, x1, x2, x3, attn, p0, p1, p2, p3, vec,
    x_one_out, h_out, act_out, slope_out, w_out, w_up, sems,
):
    row = pl.program_id(0)
    width = vec.shape[1]
    hidden = w_up.shape[1]
    jobs = [(0, width, w_out), (width, hidden, w_up)]
    copies = placements((p0, p1, p2, p3), jobs, place, sems)

    @pl.when(row == 0)
    def _():
        for copy in copies:
            copy.start()
        for copy in copies:
            copy.wait()

    x = jnp.concatenate([ref[0] for ref in (x0, x1, x2, x3)], axis=0).astype(F32)
    x_one = x + (nn_dot(attn[...], w_out[...]) + vec[4:5])
    x_one_out[...] = x_one
    unit, _ = centered(x_one)
    h = (unit * vec[2:3] + vec[3:4]).astype(BF16)
    h_out[...] = h
    for j in range(hidden // width):
        columns = slice(j * width, (j + 1) * width)
        up = nn_dot(h, w_up[:, columns]) + vec[6 + j : 7 + j]
        act, slope = gelu_and_slope(up)
        act_out[:, columns] = act.astype(BF16)
        slope_out[:, columns] = slope.astype(BF16)


def write_parts(parts, half, y, column, value, dims):
    hi_count, lo_count, rows = dims
    quarter = value.shape[1]
    value = value.astype(BF16)
    for h in range(hi_count):
        for lo in range(lo_count):
            at = (h * lo_count + lo) * rows
            parts[half, lo, y, h, :, column : column + quarter] = value[at : at + rows]


def send_parts(parts, keep, send, core, sems):
    copies = [
        pltpu.make_async_copy(parts.at[core], keep, sems.at[0]),
        pltpu.make_async_copy(parts.at[1 - core], send, sems.at[1]),
    ]
    for copy in copies:
        copy.start()
    for copy in copies:
        copy.wait()


def down_grad_body(dims, place, act, d0, d1, d2, d3, keep, send, dy_turned, parts, sems):
    part = d0.shape[1]
    for r in range(d0.shape[0]):
        for k, ref in enumerate((d0, d1, d2, d3)):
            at = (r * 4 + k) * part
            if k % 2 == 0:
                both = jnp.concatenate([ref[r], (d1, d3)[k // 2][r]], axis=0)
                dy_turned[:, at : at + 2 * part] = both.T
    quarter = act.shape[1] // 4
    for half in range(2):
        for y in range(2):
            at = (half * 2 + y) * quarter
            value = nn_dot(dy_turned[...], act[:, at : at + quarter])
            write_parts(parts, half, y, 0, value, dims)
    send_parts(parts, keep, send, place[3], sems)


def down_body(
    place, x_one, act, slope, d0, d1, d2, d3,
    b0, b1, b2, b3, c0, c1, vec,
    o0, o1, o2, o3, dx_out, dattn_out, dup_out, dao_out, vec_out,
    w_out, w_up, w_down, up_sems, down_sems,
):
    row = pl.program_id(0)
    width = vec.shape[1]
    hidden = w_up.shape[1]
    slots = x_one.shape[0]
    up_copies = placements((b0, b1, b2, b3), [(0, width, w_out), (width, hidden, w_up)], place, up_sems)
    down_copies = dp_placements((c0, c1), w_down, place, down_sems)

    @pl.when(row == 0)
    def _():
        vec_out[...] = jnp.zeros_like(vec_out)
        for copy in down_copies + up_copies:
            copy.start()
        for copy in down_copies + up_copies:
            copy.wait()

    dy = jnp.concatenate([ref[0] for ref in (d0, d1, d2, d3)], axis=0)
    dy_float = dy.astype(F32)
    result = (x_one[...] + (nt_dot(act[...], w_down[...]) + vec[5:6])).astype(BF16)
    part = slots // 4
    for k, out in enumerate((o0, o1, o2, o3)):
        out[0] = result[k * part : (k + 1) * part]
    for j in range(hidden // width):
        columns = slice(j * width, (j + 1) * width)
        dact = nn_dot(dy, w_down[:, columns])
        dup = (slope[:, columns].astype(F32) * dact).astype(BF16)
        dup_out[:, columns] = dup
        vec_out[6 + j : 7 + j] += jnp.sum(dup.astype(F32), axis=0, keepdims=True)
    dh = nt_dot(dup_out[...], w_up[...])
    unit, scale = centered(x_one[...])
    vec_out[2:3] += jnp.sum(dh * unit, axis=0, keepdims=True)
    vec_out[3:4] += jnp.sum(dh, axis=0, keepdims=True)
    dx = dy_float + norm_back(unit, scale, dh * vec[2:3])
    dx_out[...] = dx
    dao = dx.astype(BF16)
    dao_out[...] = dao
    vec_out[4:5] += jnp.sum(dao.astype(F32), axis=0, keepdims=True)
    vec_out[5:6] += jnp.sum(dy_float, axis=0, keepdims=True)
    dattn_out[...] = nt_dot(dao, w_out[...]).astype(BF16)


def up_grad_body(dims, place, h_two, dup, attn, dao, keep, send, turned, parts, sems):
    turned[...] = h_two[...].T
    quarter = dup.shape[1] // 4
    small = dao.shape[1] // 4
    for half in range(2):
        for y in range(2):
            at = (half * 2 + y) * quarter
            value = nn_dot(turned[...], dup[:, at : at + quarter])
            write_parts(parts, half, y, 0, value, dims)
    turned[...] = attn[...].T
    for half in range(2):
        for y in range(2):
            at = (half * 2 + y) * small
            value = nn_dot(turned[...], dao[:, at : at + small])
            write_parts(parts, half, y, quarter, value, dims)
    send_parts(parts, keep, send, place[3], sems)


def scores_back_body(place, lengths, qkv, lse, dattn, dqkv, bias):
    row = pl.program_id(0) + place[4]
    width = dattn.shape[1]
    pair = 2 * (width // HEADS)
    score_scale = 1.0 / math.sqrt(width // HEADS)
    fill_bias(place, lengths, row, bias)
    masks = head_masks(pair)
    for p in range(HEADS // 2):
        at = p * pair
        qp = qkv[:, at : at + pair]
        kp = qkv[:, width + at : width + at + pair]
        vp = qkv[:, 2 * width + at : 2 * width + at + pair]
        gp = dattn[:, at : at + pair]
        k_turned = kp.T
        probs_list, ds_list, dq_list, q_list, g_list = [], [], [], [], []
        for i in range(2):
            qh = qp * masks[i]
            gh = gp * masks[i]
            scores = nt_dot(kp, qh) + bias[...]
            probs = jnp.exp(scores - lse[0, 2 * p + i : 2 * p + i + 1, :])
            dprobs = nt_dot(vp, gh)
            inner = jnp.sum(probs * dprobs, axis=0, keepdims=True)
            ds = (probs * (dprobs - inner)).astype(BF16)
            dq_list.append(nn_dot(k_turned[i * (pair // 2) : (i + 1) * (pair // 2)], ds))
            probs_list.append(probs.astype(BF16))
            ds_list.append(ds)
            q_list.append(qh)
            g_list.append(gh)
        dq = jnp.concatenate(dq_list, axis=0).T * score_scale
        dk = nn_dot(jnp.concatenate(ds_list, axis=1), jnp.concatenate(q_list, axis=0))
        dv = nn_dot(jnp.concatenate(probs_list, axis=1), jnp.concatenate(g_list, axis=0))
        dqkv[:, at : at + pair] = dq.astype(BF16)
        dqkv[:, width + at : width + at + pair] = dk.astype(BF16)
        dqkv[:, 2 * width + at : 2 * width + at + pair] = dv.astype(BF16)


def qkv_grad_body(dims, place, h_one, g0, g1, keep, send, turned, parts, sems):
    turned[...] = h_one[...].T
    count = g0.shape[0]
    quarter = g0.shape[1] // 4
    for half in range(2):
        for y in range(2):
            at = (half * 2 + y) * quarter
            value = nn_dot(turned[:, :count], g0[:, at : at + quarter])
            value = value + nn_dot(turned[:, count:], g1[:, at : at + quarter])
            write_parts(parts, half, y, 0, value, dims)
    send_parts(parts, keep, send, place[3], sems)


def input_body(
    place, g0, g1, x0, x1, x2, x3, dx, p0, p1, p2, p3, vec, o0, o1, o2, o3, vec_out, w_qkv, sems
):
    row = pl.program_id(0)
    width = vec.shape[1]
    slots = dx.shape[0]
    copies = placements((p0, p1, p2, p3), [(0, 3 * width, w_qkv)], place, sems)

    @pl.when(row == 0)
    def _():
        vec_out[...] = jnp.zeros_like(vec_out)
        for copy in copies:
            copy.start()
        for copy in copies:
            copy.wait()

    first = row < pl.num_programs(0) // 2
    dqkv = jnp.where(first, g0[...], g1[...])
    dh = nt_dot(dqkv, w_qkv[...])
    x = jnp.concatenate([ref[0] for ref in (x0, x1, x2, x3)], axis=0).astype(F32)
    unit, scale = centered(x)
    vec_out[0:1] += jnp.sum(dh * unit, axis=0, keepdims=True)
    vec_out[1:2] += jnp.sum(dh, axis=0, keepdims=True)
    grad = (dx[...] + norm_back(unit, scale, dh * vec[0:1])).astype(BF16)
    part = slots // 4
    for k, out in enumerate((o0, o1, o2, o3)):
        out[0] = grad[k * part : (k + 1) * part]


def shape_of(dims, dtype):
    return jax.ShapeDtypeStruct(dims, dtype)


def rows_spec(rows, cols):
    return pl.BlockSpec((rows, cols), lambda r: (r, 0))


def whole_spec(shape):
    return pl.BlockSpec(shape, lambda r: (0,) * len(shape))


def call(body, grid, in_specs, out_specs, out_shape, scratch, cost, name):
    return pl.pallas_call(
        body,
        grid=(grid,),
        in_specs=in_specs,
        out_specs=out_specs,
        out_shape=out_shape,
        scratch_shapes=scratch,
        compiler_params=pltpu.CompilerParams(
            vmem_limit_bytes=VMEM_BYTES, dimension_semantics=("arbitrary",)
        ),
        cost_estimate=pl.CostEstimate(
            flops=int(cost * 1e9), bytes_accessed=int(cost * 2e6), transcendentals=0
        ),
        name=name,
    )


def swap(value, axis):
    return lax.ppermute(value, axis, [(0, 1), (1, 0)])


def ordered(own, other, index, axis):
    first = jnp.where(index == 0, own, other)
    second = jnp.where(index == 0, other, own)
    return jnp.stack([first, second], axis)


def from_seq(pieces):
    moved = [pieces[0]]
    for k in range(1, 4):
        moved.append(lax.ppermute(pieces[k], ("y", "core"), [(j, j ^ k) for j in range(4)]))
    return moved


def spread_hi(half):
    hi_count = lax.axis_size("hi")
    spread = jnp.broadcast_to(half[None], (hi_count, *half.shape))
    return lax.all_to_all(spread, "hi", 0, 0)


def share(own):
    other = swap(own, "lo")
    return [own, other, swap(own, "core"), swap(other, "core")]


def settle(pieces, lo, core, groups=4):
    near = ordered(pieces[0], pieces[1], lo, 1)
    far = ordered(pieces[2], pieces[3], lo, 1)
    whole = ordered(near, far, core, 2)
    cols = whole.shape[-1]
    whole = whole.reshape(groups, 2, 2, -1, cols)
    return [whole[:, 0, 0], whole[:, 1, 0], whole[:, 0, 1], whole[:, 1, 1]]


def add_pair(keep, got):
    return (keep.astype(F32) + got.astype(F32)).astype(BF16)


def spread_plane(part):
    part = part.reshape(4, *part.shape[2:])
    return lax.all_to_all(part, ("lo", "y"), 0, 0)


def total(part):
    return jnp.sum(part.astype(F32), axis=0).astype(BF16)


def to_all(mine):
    side = swap(mine, "y")
    return [mine, side, swap(mine, "core"), swap(side, "core")]


def after(value, *others):
    return lax.optimization_barrier((value, *others))[0]


def in_columns(pieces, y, core):
    near = ordered(pieces[0], pieces[1], y, 1)
    far = ordered(pieces[2], pieces[3], y, 1)
    both = ordered(near, far, core, 1)
    return both.reshape(both.shape[0], -1).astype(F32)


def adam_update(weight, moment, second, grad, decay, rate):
    moment_new = BETA_ONE * moment + (1.0 - BETA_ONE) * grad
    second_new = BETA_TWO * second + (1.0 - BETA_TWO) * grad * grad
    first_hat = moment_new / (1.0 - BETA_ONE**ADAM_STEP)
    second_hat = second_new / (1.0 - BETA_TWO**ADAM_STEP)
    weight_new = weight - rate * (first_hat / (jnp.sqrt(second_hat) + ADAM_EPS) + decay * weight)
    return (weight_new, moment_new, second_new)


def on_device(
    tokens, cotangent, lengths, attn_w, attn_m, attn_v, mlp_w, mlp_m, mlp_v, vec_w, vec_m, vec_v
):
    lo = lax.axis_index("lo")
    y = lax.axis_index("y")
    core = lax.axis_index("core")
    hi_count = lax.axis_size("hi")
    me = y * 2 + core
    micro_count, row_count, part, width = tokens.shape
    hidden = mlp_w.shape[2]
    shard = attn_w.shape[0]
    slots = 4 * part
    rows = micro_count * row_count // 4
    count = rows * slots
    vec_rows, vec_cols = vec_w.shape
    half_rows = shard // 2
    fits = half_rows % 16 == 0

    flat_tokens = tokens.reshape(4, rows, part, width)
    flat_cot = cotangent.reshape(4, rows, part, width)

    def pick(stack, k):
        return lax.dynamic_index_in_dim(stack, me ^ k, 0, keepdims=False)

    def half_of(value):
        return lax.dynamic_slice_in_dim(value, core * half_rows, half_rows, 0)

    xs = from_seq([pick(flat_tokens, k) for k in range(4)])
    lanes = 128
    ride = jnp.pad(vec_w.reshape(-1), (0, half_rows * lanes - vec_w.size)).reshape(half_rows, lanes)
    first_half = jnp.concatenate([half_of(attn_w[:, : 3 * width]), ride], axis=1).astype(BF16)
    qkv_own = spread_hi(first_half)
    up_half = jnp.concatenate([half_of(attn_w[:, 3 * width :]), half_of(mlp_w[0])], axis=1)
    up_half, down_half, qkv_own = lax.optimization_barrier(
        (up_half.astype(BF16), half_of(mlp_w[1]).astype(BF16), qkv_own)
    )
    qkv_pieces = share(qkv_own)
    up_own = spread_hi(up_half)
    down_own = lax.all_gather(down_half, ("hi", "lo"), axis=0)
    vec_all = ordered(qkv_pieces[0][:, :, 3 * width :], qkv_pieces[1][:, :, 3 * width :], lo, 1)
    vec_all = vec_all.reshape(2 * hi_count, -1)[:, : vec_w.size].reshape(-1, vec_rows, vec_cols)
    vec_all = vec_all.transpose(1, 0, 2).reshape(vec_rows, width)
    vec_float = jnp.pad(vec_all.astype(F32), ((0, 16 - vec_rows), (0, 0)))

    if fits:
        place = jnp.stack([lo, core, me, core, 0 * lo]).astype(jnp.int32)
        dims = (hi_count, 2, shard)
    else:
        qkv_pieces = settle(qkv_pieces, lo, core)
        place = jnp.stack([0 * lo, 0 * lo, me, core, 0 * lo]).astype(jnp.int32)
        dims = (1, 1, width)
    row_lengths = lax.dynamic_slice_in_dim(lengths.reshape(-1), me * rows, rows)

    slot_spec = pl.BlockSpec((1, part, width), lambda r: (r, 0, 0))
    vec_spec = whole_spec((16, width))
    lse_spec = pl.BlockSpec((1, HEADS, slots), lambda r: (r, 0, 0))
    wide = rows_spec(slots, hidden)
    narrow = rows_spec(slots, width)
    triple = rows_spec(slots, 3 * width)
    n_piece = 4 * qkv_pieces[0].shape[0]
    dma = pltpu.SemaphoreType.DMA
    h_one, qkv = call(
        qkv_body,
        rows,
        [SMEM, *[slot_spec] * 4, *[ANY] * 4, vec_spec],
        [narrow, triple],
        [shape_of((count, width), BF16), shape_of((count, 3 * width), BF16)],
        [pltpu.VMEM((width, 3 * width), BF16), dma((n_piece,))],
        7,
        "qkv",
    )(place, *xs, *qkv_pieces, vec_float)

    cot, qkv, up_own = lax.optimization_barrier((flat_cot, qkv, up_own))
    dys = from_seq([pick(cot, k) for k in range(4)])
    up_pieces = share(up_own)
    attn, lse = call(
        attend_body,
        rows,
        [SMEM, SMEM, triple],
        [narrow, lse_spec],
        [shape_of((count, width), BF16), shape_of((rows, HEADS, slots), F32)],
        [pltpu.VMEM((slots, slots), F32)],
        12,
        "attend",
    )(place, row_lengths, qkv)

    if not fits:
        up_pieces = settle(up_pieces, lo, core)
    x_one, h_two, act, slope = call(
        up_body,
        rows,
        [SMEM, *[slot_spec] * 4, narrow, *[ANY] * 4, vec_spec],
        [narrow, narrow, wide, wide],
        [
            shape_of((count, width), F32),
            shape_of((count, width), BF16),
            shape_of((count, hidden), BF16),
            shape_of((count, hidden), BF16),
        ],
        [pltpu.VMEM((width, width), BF16), pltpu.VMEM((width, hidden), BF16), dma((2 * n_piece,))],
        17,
        "up",
    )(place, *xs, attn, *up_pieces, vec_float)

    def parts_shape(quarter):
        return (dims[1], 2, dims[0], dims[2], quarter)

    def grad_call(body, args, quarter, scratch, cost, name):
        shape = parts_shape(quarter)
        return call(
            functools.partial(body, dims),
            1,
            [SMEM, *[whole_spec(a.shape) for a in args]],
            [ANY, ANY],
            [shape_of(shape, BF16)] * 2,
            [scratch, pltpu.VMEM((2, *shape), BF16), dma((2,))],
            cost,
            name,
        )(place, *args)

    def in_dp_order(value):
        if fits:
            return value
        value = value.reshape(2, hi_count, 2, shard, value.shape[-1])
        return value.transpose(2, 0, 1, 3, 4)

    turned = pltpu.VMEM((width, count), BF16)
    down_keep, down_send = grad_call(
        down_grad_body, [act, *dys], hidden // 4, turned, 4, "down_grad"
    )
    down_got = swap(down_send, "core")
    down_far = swap(down_own, "core")
    down_pieces = [down_own, down_far]
    if not fits:
        whole = ordered(down_own, down_far, core, 1).reshape(8, 2, -1, hidden)
        down_pieces = [whole[:, 0], whole[:, 1]]
    n_down = 2 * down_pieces[0].shape[0]
    outs = call(
        down_body,
        rows,
        [SMEM, narrow, wide, wide, *[slot_spec] * 4, *[ANY] * 6, vec_spec],
        [*[slot_spec] * 4, narrow, narrow, wide, narrow, vec_spec],
        [
            *[shape_of((rows, part, width), BF16)] * 4,
            shape_of((count, width), F32),
            shape_of((count, width), BF16),
            shape_of((count, hidden), BF16),
            shape_of((count, width), BF16),
            shape_of((16, width), F32),
        ],
        [
            pltpu.VMEM((width, width), BF16),
            pltpu.VMEM((width, hidden), BF16),
            pltpu.VMEM((width, hidden), BF16),
            dma((2 * n_piece,)),
            dma((n_down,)),
        ],
        18,
        "down",
    )(place, x_one, act, slope, *dys, *up_pieces, *down_pieces, vec_float)
    results, (dx, dattn, dup, dao, vec_mlp) = outs[:4], outs[4:]
    down_part = in_dp_order(add_pair(down_keep, down_got))
    down_part = down_part.reshape(4, *down_part.shape[2:])
    down_part = lax.psum_scatter(down_part, ("lo", "y"), scatter_dimension=0)
    down_mine = lax.psum_scatter(down_part, "hi", scatter_dimension=0)

    up_keep, up_send = grad_call(
        up_grad_body, [h_two, dup, attn, dao], hidden // 4 + width // 4, turned, 6, "up_grad"
    )
    up_got = swap(up_send, "core")

    def scores_back(qkv, half):
        base = half * (rows // 2)
        return call(
            scores_back_body,
            rows // 2,
            [
                SMEM,
                SMEM,
                pl.BlockSpec((slots, 3 * width), lambda r: (r + base, 0)),
                pl.BlockSpec((1, HEADS, slots), lambda r: (r + base, 0, 0)),
                pl.BlockSpec((slots, width), lambda r: (r + base, 0)),
            ],
            triple,
            shape_of((count // 2, 3 * width), BF16),
            [pltpu.VMEM((slots, slots), F32)],
            8,
            "scores_back",
        )(place.at[4].set(base), row_lengths, qkv, lse, dattn)

    grad_first = scores_back(after(qkv, up_send), 0)
    up_part = in_dp_order(add_pair(up_keep, up_got))
    up_part, grad_first = lax.optimization_barrier((up_part, grad_first))
    up_part = spread_plane(up_part)
    grad_last = scores_back(after(qkv, grad_first), 1)
    qkv_keep, qkv_send = grad_call(
        qkv_grad_body, [h_one, grad_first, grad_last], 3 * width // 4, turned, 4, "qkv_grad"
    )
    qkv_got = swap(qkv_send, "core")
    outs = call(
        input_body,
        rows,
        [
            SMEM,
            pl.BlockSpec((slots, 3 * width), lambda r: (jnp.minimum(r, rows // 2 - 1), 0)),
            pl.BlockSpec((slots, 3 * width), lambda r: (jnp.maximum(r - rows // 2, 0), 0)),
            *[slot_spec] * 4,
            narrow,
            *[ANY] * 4,
            vec_spec,
        ],
        [*[slot_spec] * 4, vec_spec],
        [*[shape_of((rows, part, width), BF16)] * 4, shape_of((16, width), F32)],
        [pltpu.VMEM((width, 3 * width), BF16), dma((n_piece,))],
        6,
        "input_grad",
    )(place, grad_first, after(grad_last, qkv_send), *xs, dx, *qkv_pieces, vec_float)
    input_parts, vec_attn = outs[:4], outs[4]

    def send_back(parts):
        parts = from_seq(parts)
        pairs = [ordered(parts[0], parts[1], core, 0), ordered(parts[2], parts[3], core, 0)]
        return ordered(pairs[0], pairs[1], y, 0).reshape(tokens.shape)

    extra_rows = 8
    quarter = 3 * width // 4
    vec_total = (vec_attn + vec_mlp)[:vec_rows].reshape(vec_rows, hi_count, 2, vec_cols)
    vec_total = vec_total.transpose(2, 1, 0, 3).reshape(2, hi_count, -1)
    vec_total = jnp.pad(
        vec_total, ((0, 0), (0, 0), (0, extra_rows * quarter - vec_total.shape[-1]))
    )
    vec_total = vec_total.reshape(2, 1, hi_count, extra_rows, quarter).astype(BF16)
    vec_total = jnp.broadcast_to(vec_total, (2, 2, *vec_total.shape[2:]))
    qkv_part = in_dp_order(add_pair(qkv_keep, qkv_got))
    qkv_part = jnp.concatenate([qkv_part, vec_total], axis=3)
    up_part, qkv_part = lax.optimization_barrier((up_part, qkv_part))
    qkv_part = spread_plane(qkv_part)
    up_mine = total(lax.all_to_all(total(up_part), "hi", 0, 0))
    qkv_mine = total(lax.all_to_all(total(qkv_part), "hi", 0, 0))
    mlp_pieces = to_all(jnp.concatenate([up_mine, down_mine], axis=1))
    qkv_mine, *_ = lax.optimization_barrier((qkv_mine, *mlp_pieces[:1]))
    attn_pieces = to_all(qkv_mine)
    output = send_back(results)
    input_grad = send_back(input_parts)

    vec_sum = attn_pieces[0][shard:].astype(F32) + attn_pieces[2][shard:].astype(F32)
    vec_sum = vec_sum.reshape(-1)[: vec_rows * vec_cols].reshape(vec_rows, vec_cols)
    up_at = hidden // 4
    out_at = up_at + width // 4
    up_sum = in_columns([p[:, :up_at] for p in mlp_pieces], y, core)
    out_sum = in_columns([p[:, up_at:out_at] for p in mlp_pieces], y, core)
    down_sum = in_columns([p[:, out_at:] for p in mlp_pieces], y, core)
    qkv_sum = in_columns([p[:shard] for p in attn_pieces], y, core)
    attn_sum = jnp.concatenate([qkv_sum, out_sum], axis=1)
    mlp_sum = jnp.stack([up_sum, down_sum])
    square = jnp.sum(attn_sum * attn_sum) + jnp.sum(mlp_sum * mlp_sum) + jnp.sum(vec_sum * vec_sum)
    dp_count = 2 * hi_count
    squares = lax.all_to_all(jnp.full((dp_count, 8, 128), square), ("hi", "lo"), 0, 0)
    grad_norm = jnp.sqrt(jnp.sum(squares[:, 0, 0]))
    clip_factor = CLIP_NORM / jnp.maximum(grad_norm, CLIP_NORM)
    attn_new = adam_update(
        attn_w, attn_m, attn_v, attn_sum * clip_factor, WEIGHT_DECAY, LEARN_RATE
    )
    mlp_new = adam_update(mlp_w, mlp_m, mlp_v, mlp_sum * clip_factor, WEIGHT_DECAY, LEARN_RATE)
    vec_new = adam_update(vec_w, vec_m, vec_v, vec_sum * clip_factor, 0.0, VEC_RATE)
    return (output, input_grad, *attn_new, *mlp_new, *vec_new, grad_norm)


def solution(mesh):
    dp_count = mesh.shape["dp"]
    seq_count = mesh.shape["seq"]
    fine = jax.sharding.Mesh(
        mesh.devices.reshape(dp_count // 2, 2, seq_count // 2, 2), ("hi", "lo", "y", "core")
    )
    dp = ("hi", "lo")
    seq = ("y", "core")
    acts = P(None, dp, seq, None)
    attn = P(dp, None)
    mlp = P(None, dp, None)
    vec = P(None, dp)
    return jax.shard_map(
        on_device,
        mesh=fine,
        in_specs=(acts, acts, P(None, dp), attn, attn, attn, mlp, mlp, mlp, vec, vec, vec),
        out_specs=(acts, acts, attn, attn, attn, mlp, mlp, mlp, vec, vec, vec, P()),
        check_vma=False,
    )
```

time: 371 us -> 282 us (0.76)
  Pallas kernels: 0 us -> 98.5 us
  matrix products: 64 us -> 0 us
  other arithmetic: 74.2 us -> 38 us
  starting transfers between devices: 77.7 us -> 43 us
  local copies, waits for them, and re-layouts: 48.2 us -> 14.7 us
  blocking collectives: 30.9 us -> 0 us
  between operations: 6.78 us -> 20 us
    pallas_call x0 -> x10, Pallas kernels: none -> 98.5 us  [the longest x3 20 us: grad_call(): call(functools.partial(body, dims), 1, [SMEM, *[whole_spec(a.shape) for a...]
    dot_general x18 -> x0, matrix products: 64 us -> none  [the longest x1 6.99 us: layer_pass(): jnp.einsum('rqhc,rkhc->rhqk', grad_heads, values_h, preferred_element_typ...]
    all_gather x1 -> x0, blocking collectives: 30.9 us -> none  [on_device(): vec_all = lax.all_gather(vec_low, ('hi', 'lo'), axis=1, tiled=True)]
    convert_element_type x12 -> x3, other arithmetic: 35 us -> 6.77 us  [add_pair(): return (keep.astype(F32) + got.astype(F32)).astype(BF16)]
    all_to_all x12 -> x6, starting transfers between devices: 49.4 us -> 24.1 us  [the longest x2 9.8 us: spread_hi(): return lax.all_to_all(spread, 'hi', 0, 0)]
    reshape x14 -> x5, local copies, waits for them, and re-layouts: 12.4 us -> 0.37 us  [the longest x2 0.11 us: on_device(): (vec_attn + vec_mlp)[:vec_rows].reshape(vec_rows, hi_count, 2, vec_cols)]
    reduce_sum x19 -> x7, other arithmetic: 16.9 us -> 5.04 us  [the longest x4 1.92 us: total(): return jnp.sum(part.astype(F32), axis=0).astype(BF16)]
    ppermute x24 -> x16, starting transfers between devices: 17.1 us -> 6.25 us  [swap(): return lax.ppermute(value, axis, [(0, 1), (1, 0)])]
  transfers between devices with their start and end apart: 49 -> 38, of which waited for: 16 -> 11; matrix products, arithmetic and copies ran while one was open for 33% -> 13% of each run, Pallas kernels for 0% -> 35%
where the time goes in v2:
time: 282 us; the launch traced here: 280 us
  Pallas kernels  98.5 us (35%)
  waiting for transfers between devices  65.9 us (23%)
  starting transfers between devices  43 us (15%)
  other arithmetic  38 us (13%)
  between operations  20 us (7%)
  local copies, waits for them, and re-layouts  14.7 us (5%)
    ppermute x16, waiting for transfers between devices, swap(): return lax.ppermute(value, axis, [(0, 1), (1, 0)])  20.6 us
    pallas_call x3, Pallas kernels, grad_call(): call(functools.partial(body, dims), 1, [SMEM, *[whole_spec(a.shape) for a...  20 us
    pallas_call x1, Pallas kernels, on_device(): call(up_body, rows, [SMEM, *[slot_spec] * 4, narrow, *[ANY] * 4, vec_spec...  18 us
    pallas_call x2, Pallas kernels, scores_back(): call(scores_back_body, rows // 2, [SMEM, SMEM, pl.BlockSpec((slots, 3 * w...  16.1 us
    pallas_call x1, Pallas kernels, on_device(): call(down_body, rows, [SMEM, narrow, wide, wide, *[slot_spec] * 4, *[ANY]...  15.9 us
    all_to_all x2, waiting for transfers between devices, spread_hi(): return lax.all_to_all(spread, 'hi', 0, 0)  14.4 us
    pallas_call x1, Pallas kernels, on_device(): call(attend_body, rows, [SMEM, SMEM, triple], [narrow, lse_spec], [shape_...  13.4 us
    another operation x18, other arithmetic, ordered(): return jnp.stack([first, second], axis)  12.1 us
  transfers between devices with their start and end apart: 38, of which 11 were waited for; matrix products, arithmetic and copies ran while one was open for 13% of the time, Pallas kernels for 35%

profile of v2, /device:TPU:0, one launch (start us, length us, event | category | flops | bytes accessed | tf_op | source)
XLA Modules:
  0.0 280.1 jit_solution(322870762099508102)
XLA Ops:
  8.0 0.8 convert.43
  8.9 1.0 slice.107
  10.0 0.8 broadcast_in_dim.8
  10.8 6.3 %all-to-all-start = ((bf16[4,32,1664]{2,1,0:T(8,128)(2,1)}), bf16[4,32,1664]{2,1,0:T(8,128)(2,1)S(1)}, u32[]{:S(2)}, u32[]{:S(2)}) async-start(bf16[4,32,1664]{2,1,0:T(8,128)(2,1)} %broadcast_in_dim.8), calls=%async_computation | async-start | bytes 851968 | tf_op jit(solution)/shard_map/all_to_all | solution.py:433
  17.1 0.9 slice.104
  18.8 10.7 %all-to-all-done.p0 = bf16[4,32,1664]{2,1,0:T(8,128)(2,1)S(1)} async-done(((bf16[4,32,1664]{2,1,0:T(8,128)(2,1)}), bf16[4,32,1664]{2,1,0:T(8,128)(2,1)S(1)}, u32[]{:S(2)}, u32[]{:S(2)}) %all-to-all-start) | async-done | bytes 426016 | tf_op jit(solution)/shard_map/all_to_all | solution.py:433
  29.5 1.5 collective-permute-start.3
  31.0 0.9 dynamic-slice_bitcast_fusion.4
  31.9 1.5 collective-permute-start.1
  34.6 0.9 broadcast_in_dim.9
  35.5 3.5 %all-to-all-start.1 = ((bf16[4,32,2560]{2,1,0:T(8,128)(2,1)}), bf16[4,32,2560]{2,1,0:T(8,128)(2,1)S(1)}, u32[]{:S(2)}, u32[]{:S(2)}) async-start(bf16[4,32,2560]{2,1,0:T(8,128)(2,1)} %broadcast_in_dim.9), calls=%async_computation.1 | async-start | bytes 1310720 | tf_op jit(solution)/shard_map/all_to_all | solution.py:433
  40.4 0.8 select_bitcast_fusion.21
  42.0 4.1 %collective-permute-done.2.x3 = bf16[4,64,512]{2,1,0:T(8,128)(2,1)} collective-permute-done((bf16[4,64,512]{2,1,0:T(8,128)(2,1)S(1)}, bf16[4,64,512]{2,1,0:T(8,128)(2,1)}, u32[]{:S(2)}, u32[]{:S(2)}) %collective-permute-start.2) | collective-permute-done | bytes 262176 | tf_op jit(solution)/shard_map/ppermute | solution.py:426
  47.7 7.1 %qkv.1 = (bf16[1024,512]{1,0:T(8,128)(2,1)}, bf16[1024,1536]{1,0:T(8,128)(2,1)}) custom-call(s32[5]{0:T(128)} %stack.171.place, bf16[4,64,512]{2,1,0:T(8,128)(2,1)} %get-tuple-element.141.x0, bf16[4,64,512]{2,1,0:T(8,128)(2,1)} %collective-permute-done.x1, bf16[4,64,512]{2,1,0:T(8,128)(2,1)} %collective-permute-done.1.x2, ...), custom_call_target="tpu_custom_call" | custom-call | flops 7000000000 | bytes 14000000 | tf_op jit(solution)/shard_map/qkv/pallas_call | solution.py:549
  54.8 3.8 %all-to-all-done.1.p0.b0 = bf16[4,32,2560]{2,1,0:T(8,128)(2,1)S(1)} async-done(((bf16[4,32,2560]{2,1,0:T(8,128)(2,1)}), bf16[4,32,2560]{2,1,0:T(8,128)(2,1)S(1)}, u32[]{:S(2)}, u32[]{:S(2)}) %all-to-all-start.1) | async-done | bytes 655392 | tf_op jit(solution)/shard_map/all_to_all | solution.py:433
  59.7 0.8 dynamic-slice_bitcast_fusion
  61.0 1.7 collective-permute-start.10
  62.7 17.2 %collective-permute-done.6.p1.b1 = bf16[4,32,2560]{2,1,0:T(8,128)(2,1)} collective-permute-done((bf16[4,32,2560]{2,1,0:T(8,128)(2,1)S(1)}, bf16[4,32,2560]{2,1,0:T(8,128)(2,1)}, u32[]{:S(2)}, u32[]{:S(2)}) %collective-permute-start.6) | collective-permute-done | bytes 655392 | tf_op jit(solution)/shard_map/ppermute | solution.py:414
  79.8 13.4 %attend.1 = (bf16[1024,512]{1,0:T(8,128)(2,1)}, f32[4,8,256]{2,1,0:T(8,128)}) custom-call(s32[5]{0:T(128)} %stack.171.place, s32[4]{0:T(128)} %dynamic_slice.46.lengths, bf16[1024,1536]{1,0:T(8,128)(2,1)} %get-tuple-element.102.qkv), custom_call_target="tpu_custom_call" | custom-call | flops 12000000000 | bytes 24000000 | tf_op jit(solution)/shard_map/attend/pallas_call | solution.py:563
  93.9 0.8 copy-done.25
  94.7 18.0 %up.1 = (f32[1024,512]{1,0:T(8,128)}, bf16[1024,512]{1,0:T(8,128)(2,1)}, bf16[1024,2048]{1,0:T(8,128)(2,1)}, bf16[1024,2048]{1,0:T(8,128)(2,1)}) custom-call(s32[5]{0:T(128)} %stack.171.place, bf16[4,64,512]{2,1,0:T(8,128)(2,1)} %get-tuple-element.141.x0, bf16[4,64,512]{2,1,0:T(8,128)(2,1)} %collective-permute-done.x1, ...), custom_call_target="tpu_custom_call" | custom-call | flops 16999999488 | bytes 34000000 | tf_op jit(solution)/shard_map/up/pallas_call | solution.py:576
  113.4 6.2 %down_grad.1 = (bf16[2,2,4,64,512]{4,3,2,1,0:T(8,128)(2,1)}, bf16[2,2,4,64,512]{4,3,2,1,0:T(8,128)(2,1)}) custom-call(s32[5]{0:T(128)} %stack.171.place, bf16[1024,2048]{1,0:T(8,128)(2,1)} %get-tuple-element.85.act, bf16[4,64,512]{2,1,0:T(8,128)(2,1)} %get-tuple-element.136.d0, bf16[4,64,512]{2,1,0:T(8,128)(2,1)} %copy-done.28, ...), custom_call_target="tpu_custom_call" | custom-call | flops 4000000000 | bytes 8000000 | tf_op jit(solution)/shard_map/down_grad/pallas_call | solution.py:597
  119.7 15.9 %down.1 = (bf16[4,64,512]{2,1,0:T(8,128)(2,1)}, bf16[4,64,512]{2,1,0:T(8,128)(2,1)}, bf16[4,64,512]{2,1,0:T(8,128)(2,1)}, bf16[4,64,512]{2,1,0:T(8,128)(2,1)}, f...) custom-call(s32[5]{0:T(128)} %stack.171.place, ...), custom_call_target="tpu_custom_call" | custom-call | flops 17999998976 | bytes 36000000 | tf_op jit(solution)/shard_map/down/pallas_call | solution.py:625
  135.6 8.1 %up_grad.1 = (bf16[2,2,4,64,640]{4,3,2,1,0:T(8,128)(2,1)}, bf16[2,2,4,64,640]{4,3,2,1,0:T(8,128)(2,1)}) custom-call(s32[5]{0:T(128)} %stack.171.place, bf16[1024,512]{1,0:T(8,128)(2,1)} %get-tuple-element.93.h_two, bf16[1024,2048]{1,0:T(8,128)(2,1)} %get-tuple-element.94.dup, bf16[1024,512]{1,0:T(8,128)(2,1)} %get-tuple-element.82.attn, ...), custom_call_target="tpu_custom_call" | custom-call | flops 6000000000 | bytes 12000000 | tf_op jit(solution)/shard_map/up_grad/pallas_call | solution.py:597
  144.4 1.9 collective-permute-start.14
  146.4 8.1 %scores_back.2.g0 = bf16[512,1536]{1,0:T(8,128)(2,1)} custom-call(s32[5]{0:T(128)} %copy-done.30, s32[4]{0:T(128)} %dynamic_slice.46.lengths, bf16[1024,1536]{1,0:T(8,128)(2,1)} %get-tuple-element.102.qkv, f32[4,8,256]{2,1,0:T(8,128)} %get-tuple-element.99.lse, bf16[1024,512]{1,0:T(8,128)(2,1)} %get-tuple-element.100.dattn), custom_call_target="tpu_custom_call" | custom-call | flops 8000000000 | bytes 16000000 | tf_op jit(solution)/shard_map/scores_back/pallas_call | solution.py:661
  154.5 1.0 copy-done.4
  155.5 2.6 add_convert_fusion.1
  158.2 2.8 %add_convert_fusion = bf16[2,2,4,64,640]{4,3,2,1,0:T(8,128)(2,1)} fusion(bf16[2,2,4,64,640]{4,3,2,1,0:T(8,128)(2,1)} %collective-permute-done.16, bf16[2,2,4,64,640]{4,3,2,1,0:T(8,128)(2,1)S(1)} %copy-done.1), kind=kLoop, calls=%fused_computation | loop fusion | flops 2621440 | bytes 3932160 | tf_op jit(solution)/shard_map/convert_element_type | solution.py:451
  161.0 8.0 %scores_back.3.g1 = bf16[512,1536]{1,0:T(8,128)(2,1)} custom-call(s32[5]{0:T(128)} %copy-done.29, s32[4]{0:T(128)} %dynamic_slice.46.lengths, bf16[1024,1536]{1,0:T(8,128)(2,1)} %get-tuple-element.102.qkv, f32[4,8,256]{2,1,0:T(8,128)} %get-tuple-element.99.lse, bf16[1024,512]{1,0:T(8,128)(2,1)} %get-tuple-element.100.dattn), custom_call_target="tpu_custom_call" | custom-call | flops 8000000000 | bytes 16000000 | tf_op jit(solution)/shard_map/scores_back/pallas_call | solution.py:661
  169.0 5.7 %qkv_grad.1 = (bf16[2,2,4,64,384]{4,3,2,1,0:T(8,128)(2,1)}, bf16[2,2,4,64,384]{4,3,2,1,0:T(8,128)(2,1)}) custom-call(s32[5]{0:T(128)} %stack.171.place, bf16[1024,512]{1,0:T(8,128)(2,1)} %get-tuple-element.103.h_one, bf16[512,1536]{1,0:T(8,128)(2,1)} %scores_back.2.g0, bf16[512,1536]{1,0:T(8,128)(2,1)} %scores_back.3.g1), custom_call_target="tpu_custom_call" | custom-call | flops 4000000000 | bytes 8000000 | tf_op jit(solution)/shard_map/qkv_grad/pallas_call | solution.py:597
  175.0 3.6 %all-to-all-start.2 = ((bf16[4,4,64,640]{3,2,1,0:T(8,128)(2,1)}), bf16[4,4,64,640]{3,2,1,0:T(8,128)(2,1)S(1)}, u32[]{:S(2)}, u32[]{:S(2)}) async-start(bf16[4,4,64,640]{3,2,1,0:T(8,128)(2,1)} %bitcast.28), calls=%async_computation.2 | async-start | bytes 2621440 | tf_op jit(solution)/shard_map/all_to_all | solution.py:456
  178.6 7.9 %input_grad.1 = (bf16[4,64,512]{2,1,0:T(8,128)(2,1)}, bf16[4,64,512]{2,1,0:T(8,128)(2,1)}, bf16[4,64,512]{2,1,0:T(8,128)(2,1)}, bf16[4,64,512]{2,1,0:T(8,128)(2,1)}, f32[16,512]{1,0:T(8,128)}) custom-call(s32[5]{0:T(128)} %stack.171.place, bf16[512,1536]{1,0:T(8,128)(2,1)} %scores_back.2.g0, bf16[512,1536]{1,0:T(8,128)(2,1)} %scores_back.3.g1, ...), custom_call_target="tpu_custom_call" | custom-call | flops 6000000000 | bytes 12000000 | tf_op jit(solution)/shard_map/input_grad/pallas_call | solution.py:687
  186.5 2.0 collective-permute-start.18
  188.6 0.8 fusion.10
  189.7 1.4 add_convert_fusion.2
  191.1 1.0 pad_maximum_fusion.2
  192.1 4.6 %all-to-all-done.2 = bf16[4,4,64,640]{3,2,1,0:T(8,128)(2,1)S(1)} async-done(((bf16[4,4,64,640]{3,2,1,0:T(8,128)(2,1)}), bf16[4,4,64,640]{3,2,1,0:T(8,128)(2,1)S(1)}, u32[]{:S(2)}, u32[]{:S(2)}) %all-to-all-start.2) | async-done | bytes 1310752 | tf_op jit(solution)/shard_map/all_to_all | solution.py:456
  196.7 1.0 reduce_sum.86
  197.7 3.7 %all-to-all-start.5 = ((bf16[4,64,640]{2,1,0:T(8,128)(2,1)}), bf16[4,64,640]{2,1,0:T(8,128)(2,1)S(1)}, u32[]{:S(2)}, u32[]{:S(2)}) async-start(bf16[4,64,640]{2,1,0:T(8,128)(2,1)} %reduce_sum.86), calls=%async_computation.5 | async-start | bytes 655360 | tf_op jit(solution)/shard_map/all_to_all | solution.py:725
  201.4 1.8 select_bitcast_fusion.7
  203.3 1.9 select_bitcast_fusion.5
  205.2 6.5 %all-to-all-done.5 = bf16[4,64,640]{2,1,0:T(8,128)(2,1)S(1)} async-done(((bf16[4,64,640]{2,1,0:T(8,128)(2,1)}), bf16[4,64,640]{2,1,0:T(8,128)(2,1)S(1)}, u32[]{:S(2)}, u32[]{:S(2)}) %all-to-all-start.5) | async-done | bytes 327712 | tf_op jit(solution)/shard_map/all_to_all | solution.py:725
  211.8 3.5 %all-to-all-start.3 = ((bf16[4,4,72,384]{3,2,1,0:T(8,128)(2,1)}), bf16[4,4,72,384]{3,2,1,0:T(8,128)(2,1)S(1)}, u32[]{:S(2)}, u32[]{:S(2)}) async-start(bf16[4,4,72,384]{3,2,1,0:T(8,128)(2,1)} %bitcast.30), calls=%async_computation.3 | async-start | bytes 1769472 | tf_op jit(solution)/shard_map/all_to_all | solution.py:456
  215.3 1.8 select_bitcast_fusion.1
  217.1 0.8 select_bitcast_fusion.3
  218.0 6.3 %reduce-scatter.5.cloned.1.call-done = bf16[1,64,512]{2,1,0:T(8,128)(2,1)} async-done(((bf16[4,64,512]{2,1,0:T(8,128)(2,1)}), bf16[1,64,512]{2,1,0:T(8,128)(2,1)}) %reduce-scatter.5.cloned.1.call-update) | async-done | bytes 65552 | tf_op jit(solution)/shard_map/reduce_scatter | solution.py:652
  224.3 1.5 pad_maximum_fusion.13
  225.8 1.5 collective-permute-start.25
  227.3 2.5 broadcast_select_fusion.1
  229.7 0.8 reduce_sum.84
  230.6 3.5 %all-to-all-start.4 = ((bf16[4,72,384]{2,1,0:T(8,128)(2,1)}), bf16[4,72,384]{2,1,0:T(8,128)(2,1)S(1)}, u32[]{:S(2)}, u32[]{:S(2)}) async-start(bf16[4,72,384]{2,1,0:T(8,128)(2,1)} %reduce_sum.84), calls=%async_computation.4 | async-start | bytes 442368 | tf_op jit(solution)/shard_map/all_to_all | solution.py:726
  234.1 2.1 pad_maximum_fusion
  236.8 0.9 select_bitcast_fusion.15
  237.7 2.9 %all-to-all-done.4 = bf16[4,72,384]{2,1,0:T(8,128)(2,1)S(1)} async-done(((bf16[4,72,384]{2,1,0:T(8,128)(2,1)}), bf16[4,72,384]{2,1,0:T(8,128)(2,1)S(1)}, u32[]{:S(2)}, u32[]{:S(2)}) %all-to-all-start.4) | async-done | bytes 221216 | tf_op jit(solution)/shard_map/all_to_all | solution.py:726
  241.9 2.9 %collective-permute-done.22 = bf16[72,384]{1,0:T(8,128)(2,1)S(1)} collective-permute-done((bf16[72,384]{1,0:T(8,128)(2,1)S(1)}, bf16[72,384]{1,0:T(8,128)(2,1)S(1)}, u32[]{:S(2)}, u32[]{:S(2)}) %collective-permute-start.22) | collective-permute-done | bytes 55328 | tf_op jit(solution)/shard_map/ppermute | solution.py:414
  247.4 0.9 fusion.2
  248.7 1.6 fusion.6
  253.0 4.2 %all-to-all-start.6 = ((f32[8,8,128]{2,1,0:T(8,128)}), f32[8,8,128]{2,1,0:T(8,128)S(1)}, u32[]{:S(2)}, u32[]{:S(2)}) async-start(f32[8,8,128]{2,1,0:T(8,128)} %broadcast_in_dim.11), calls=%async_computation.7 | async-start | bytes 65536 | tf_op jit(solution)/shard_map/all_to_all | solution.py:745
  257.2 1.1 pad_maximum_fusion.1
  258.2 5.6 %all-to-all-done.6 = f32[8,8,128]{2,1,0:T(8,128)S(1)} async-done(((f32[8,8,128]{2,1,0:T(8,128)}), f32[8,8,128]{2,1,0:T(8,128)S(1)}, u32[]{:S(2)}, u32[]{:S(2)}) %all-to-all-start.6) | async-done | bytes 32800 | tf_op jit(solution)/shard_map/all_to_all | solution.py:745
  265.2 2.7 multiply_subtract_fusion.1
  267.9 2.2 multiply_subtract_fusion
  270.2 1.3 multiply_subtract_fusion.2
  (173 shorter events, 16.5 us)
Async XLA Ops:
  8.0 10.0 %copy-start = (f32[2,64,2048]{2,1,0:T(8,128)S(1)}, f32[2,64,2048]{2,1,0:T(8,128)}, u32[]{:S(2)}) copy-start(f32[2,64,2048]{2,1,0:T(8,128)} %param.22) | copy-start | bytes 3145732
  10.0 21.0 %copy-start.5 = (bf16[4,4,64,512]{3,2,1,0:T(8,128)(2,1)S(1)}, bf16[4,4,64,512]{3,2,1,0:T(8,128)(2,1)}, u32[]{:S(2)}) copy-start(bf16[4,4,64,512]{3,2,1,0:T(8,128)(2,1)} %param.16) | copy-start | bytes 3145732
  10.8 18.7 %all-to-all-start = ((bf16[4,32,1664]{2,1,0:T(8,128)(2,1)}), bf16[4,32,1664]{2,1,0:T(8,128)(2,1)S(1)}, u32[]{:S(2)}, u32[]{:S(2)}) async-start(bf16[4,32,1664]{2,1,0:T(8,128)(2,1)} %broadcast_in_dim.8), calls=%async_computation | async-start | bytes 851968 | tf_op jit(solution)/shard_map/all_to_all | solution.py:433
  29.5 10.9 %copy-start.14 = (bf16[4,32,1664]{2,1,0:T(8,128)(2,1)}, bf16[4,32,1664]{2,1,0:T(8,128)(2,1)S(1)}, u32[]{:S(2)}) copy-start(bf16[4,32,1664]{2,1,0:T(8,128)(2,1)S(1)} %all-to-all-done.p0) | copy-start | bytes 1277956
  29.5 10.9 %collective-permute-start.3 = (bf16[4,32,1664]{2,1,0:T(8,128)(2,1)S(1)}, bf16[4,32,1664]{2,1,0:T(8,128)(2,1)}, u32[]{:S(2)}, u32[]{:S(2)}) collective-permute-start(bf16[4,32,1664]{2,1,0:T(8,128)(2,1)S(1)} %all-to-all-done.p0), channel_id=1, source_target_pairs={{0,4},{4,0},{1,5},{5,1},{2,6},{6,2},{3,7},{7,3},{8,12},{12,8},{9,1... | collective-permute-start | bytes 1277960 | tf_op jit(solution)/shard_map/ppermute | solution.py:414
  31.9 10.2 %collective-permute-start = (bf16[4,64,512]{2,1,0:T(8,128)(2,1)}, bf16[4,64,512]{2,1,0:T(8,128)(2,1)}, u32[]{:S(2)}, u32[]{:S(2)}) collective-permute-start(bf16[4,64,512]{2,1,0:T(8,128)(2,1)} %get-tuple-element.140), channel_id=1, source_target_pairs={{0,1},{1,0},{2,3},{3,2},{4,5},{5,4},{6,7},{7,6},{8,9},{9,8},{10,11... | collective-permute-start | bytes 786440 | tf_op jit(solution)/shard_map/ppermute | solution.py:426
  31.9 10.2 %collective-permute-start.1 = (bf16[4,64,512]{2,1,0:T(8,128)(2,1)}, bf16[4,64,512]{2,1,0:T(8,128)(2,1)}, u32[]{:S(2)}, u32[]{:S(2)}) collective-permute-start(bf16[4,64,512]{2,1,0:T(8,128)(2,1)} %get-tuple-element.142), channel_id=1, source_target_pairs={{0,2},{1,3},{2,0},{3,1},{4,6},{5,7},{6,4},{7,5},{8,10},{9,11},{10,... | collective-permute-start | bytes 786440 | tf_op jit(solution)/shard_map/ppermute | solution.py:426
  33.4 12.7 %collective-permute-start.2 = (bf16[4,64,512]{2,1,0:T(8,128)(2,1)S(1)}, bf16[4,64,512]{2,1,0:T(8,128)(2,1)}, u32[]{:S(2)}, u32[]{:S(2)}) collective-permute-start(bf16[4,64,512]{2,1,0:T(8,128)(2,1)S(1)} %get-tuple-element.139), channel_id=1, source_target_pairs={{0,3},{1,2},{2,1},{3,0},{4,7},{5,6},{6,5},{7,4},{8,11},{9,10},{10,... | collective-permute-start | bytes 786440 | tf_op jit(solution)/shard_map/ppermute | solution.py:426
  34.3 11.8 %collective-permute-start.4 = (bf16[4,32,1664]{2,1,0:T(8,128)(2,1)S(1)}, bf16[4,32,1664]{2,1,0:T(8,128)(2,1)S(1)}, u32[]{:S(2)}, u32[]{:S(2)}) collective-permute-start(bf16[4,32,1664]{2,1,0:T(8,128)(2,1)S(1)} %all-to-all-done.p0), channel_id=1, source_target_pairs={{0,1},{1,0},{2,3},{3,2},{4,5},{5,4},{6,7},{7,6},{8,9},{9,8},{10,11... | collective-permute-start | bytes 1277960 | tf_op jit(solution)/shard_map/ppermute | solution.py:414
  35.5 23.1 %all-to-all-start.1 = ((bf16[4,32,2560]{2,1,0:T(8,128)(2,1)}), bf16[4,32,2560]{2,1,0:T(8,128)(2,1)S(1)}, u32[]{:S(2)}, u32[]{:S(2)}) async-start(bf16[4,32,2560]{2,1,0:T(8,128)(2,1)} %broadcast_in_dim.9), calls=%async_computation.1 | async-start | bytes 1310720 | tf_op jit(solution)/shard_map/all_to_all | solution.py:433
  39.0 54.3 %all-gather.3.cloned.1.call-start = ((), (), s32[]{:S(2)}) async-start(), calls=%async_computation.10 | async-start | bytes 1179648 | tf_op jit(solution)/shard_map/all_gather | solution.py:526
  39.7 163.5 %reduce-scatter.7.cloned.1.call-start = ((), (), s32[]{:S(2)}) async-start(), calls=%async_computation.11 | async-start | bytes 1310720
  40.4 5.8 %collective-permute-start.5 = (bf16[4,32,1664]{2,1,0:T(8,128)(2,1)}, bf16[4,32,1664]{2,1,0:T(8,128)(2,1)S(1)}, u32[]{:S(2)}, u32[]{:S(2)}) collective-permute-start(bf16[4,32,1664]{2,1,0:T(8,128)(2,1)} %collective-permute-done.3.p1), channel_id=1, source_target_pairs={{0,1},{1,0},{2,3},{3,2},{4,5},{5,4},{6,7},{7,6},{8,9},{9,8},{10,11... | collective-permute-start | bytes 1277960 | tf_op jit(solution)/shard_map/ppermute | solution.py:414
  47.6 11.3 %copy-start.23 = (s32[4,4]{1,0:T(4,128)S(1)}, s32[4,4]{1,0:T(4,128)}, u32[]{:S(2)}) copy-start(s32[4,4]{1,0:T(4,128)} %param.18) | copy-start | bytes 196
  47.7 12.0 %copy-start.6 = (bf16[4,4,64,512]{3,2,1,0:T(8,128)(2,1)S(1)}, bf16[4,4,64,512]{3,2,1,0:T(8,128)(2,1)}, u32[]{:S(2)}) copy-start(bf16[4,4,64,512]{3,2,1,0:T(8,128)(2,1)} %param.17) | copy-start | bytes 3145732
  58.6 34.7 %copy-start.12 = (bf16[4,32,2560]{2,1,0:T(8,128)(2,1)}, bf16[4,32,2560]{2,1,0:T(8,128)(2,1)S(1)}, u32[]{:S(2)}) copy-start(bf16[4,32,2560]{2,1,0:T(8,128)(2,1)S(1)} %all-to-all-done.1.p0.b0) | copy-start | bytes 1966084
  58.6 21.2 %collective-permute-start.6 = (bf16[4,32,2560]{2,1,0:T(8,128)(2,1)S(1)}, bf16[4,32,2560]{2,1,0:T(8,128)(2,1)}, u32[]{:S(2)}, u32[]{:S(2)}) collective-permute-start(bf16[4,32,2560]{2,1,0:T(8,128)(2,1)S(1)} %all-to-all-done.1.p0.b0), channel_id=1, source_target_pairs={{0,4},{4,0},{1,5},{5,1},{2,6},{6,2},{3,7},{7,3},{8,12},{12,8},{9,1... | collective-permute-start | bytes 1966088 | tf_op jit(solution)/shard_map/ppermute | solution.py:414
  59.7 33.6 %collective-permute-start.7 = (bf16[4,32,2560]{2,1,0:T(8,128)(2,1)S(1)}, bf16[4,32,2560]{2,1,0:T(8,128)(2,1)}, u32[]{:S(2)}, u32[]{:S(2)}) collective-permute-start(bf16[4,32,2560]{2,1,0:T(8,128)(2,1)S(1)} %all-to-all-done.1.p0.b0), channel_id=1, source_target_pairs={{0,1},{1,0},{2,3},{3,2},{4,5},{5,4},{6,7},{7,6},{8,9},{9,8},{10,11... | collective-permute-start | bytes 1966088 | tf_op jit(solution)/shard_map/ppermute | solution.py:414
  60.4 52.2 %collective-permute-start.9 = (bf16[4,64,512]{2,1,0:T(8,128)(2,1)S(1)}, bf16[4,64,512]{2,1,0:T(8,128)(2,1)S(1)}, u32[]{:S(2)}, u32[]{:S(2)}) collective-permute-start(bf16[4,64,512]{2,1,0:T(8,128)(2,1)S(1)} %get-tuple-element.135), channel_id=1, source_target_pairs={{0,1},{1,0},{2,3},{3,2},{4,5},{5,4},{6,7},{7,6},{8,9},{9,8},{10,11... | collective-permute-start | bytes 786440 | tf_op jit(solution)/shard_map/ppermute | solution.py:426
  61.0 51.7 %collective-permute-start.10 = (bf16[4,64,512]{2,1,0:T(8,128)(2,1)S(1)}, bf16[4,64,512]{2,1,0:T(8,128)(2,1)}, u32[]{:S(2)}, u32[]{:S(2)}) collective-permute-start(bf16[4,64,512]{2,1,0:T(8,128)(2,1)S(1)} %get-tuple-element.134), channel_id=1, source_target_pairs={{0,2},{1,3},{2,0},{3,1},{4,6},{5,7},{6,4},{7,5},{8,10},{9,11},{10,... | collective-permute-start | bytes 786440 | tf_op jit(solution)/shard_map/ppermute | solution.py:426
  62.6 50.1 %collective-permute-start.11 = (bf16[4,64,512]{2,1,0:T(8,128)(2,1)S(1)}, bf16[4,64,512]{2,1,0:T(8,128)(2,1)}, u32[]{:S(2)}, u32[]{:S(2)}) collective-permute-start(bf16[4,64,512]{2,1,0:T(8,128)(2,1)S(1)} %get-tuple-element.133), channel_id=1, source_target_pairs={{0,3},{1,2},{2,1},{3,0},{4,7},{5,6},{6,5},{7,4},{8,11},{9,10},{10,... | collective-permute-start | bytes 786440 | tf_op jit(solution)/shard_map/ppermute | solution.py:426
  79.8 14.1 %collective-permute-start.8 = (bf16[4,32,2560]{2,1,0:T(8,128)(2,1)}, bf16[4,32,2560]{2,1,0:T(8,128)(2,1)S(1)}, u32[]{:S(2)}, u32[]{:S(2)}) collective-permute-start(bf16[4,32,2560]{2,1,0:T(8,128)(2,1)} %collective-permute-done.6.p1.b1), channel_id=1, source_target_pairs={{0,1},{1,0},{2,3},{3,2},{4,5},{5,4},{6,7},{7,6},{8,9},{9,8},{10,11... | collective-permute-start | bytes 1966088 | tf_op jit(solution)/shard_map/ppermute | solution.py:414
  93.3 26.4 %collective-permute-start.12 = (bf16[8,32,2048]{2,1,0:T(8,128)(2,1)}, bf16[8,32,2048]{2,1,0:T(8,128)(2,1)}, u32[]{:S(2)}, u32[]{:S(2)}) collective-permute-start(bf16[8,32,2048]{2,1,0:T(8,128)(2,1)} %bitcast.106), channel_id=1, source_target_pairs={{0,1},{1,0},{2,3},{3,2},{4,5},{5,4},{6,7},{7,6},{8,9},{9,8},{10,11... | collective-permute-start | bytes 3145736 | tf_op jit(solution)/shard_map/ppermute | solution.py:414
  119.6 34.9 %collective-permute-start.21 = (bf16[2,2,4,64,512]{4,3,2,1,0:T(8,128)(2,1)}, bf16[2,2,4,64,512]{4,3,2,1,0:T(8,128)(2,1)S(1)}, u32[]{:S(2)}, u32[]{:S(2)}) collective-permute-start(bf16[2,2,4,64,512]{4,3,2,1,0:T(8,128)(2,1)} %get-tuple-element.118), channel_id=1, source_target_pairs={{0,1},{1,0},{2,3},{3,2},{4,5},{5,4},{6,7},{7,6},{8,9},{9,8},{10,11... | collective-permute-start | bytes 3145736 | tf_op jit(solution)/shard_map/ppermute | solution.py:414
  135.6 8.6 %copy-start.24 = (s32[5]{0:T(128)S(1)}, s32[5]{0:T(128)}, u32[]{:S(2)}) copy-start(s32[5]{0:T(128)} %stack.171.place) | copy-start | bytes 64
  143.7 14.4 %collective-permute-start.16 = (bf16[2,2,4,64,640]{4,3,2,1,0:T(8,128)(2,1)}, bf16[2,2,4,64,640]{4,3,2,1,0:T(8,128)(2,1)}, u32[]{:S(2)}, u32[]{:S(2)}) collective-permute-start(bf16[2,2,4,64,640]{4,3,2,1,0:T(8,128)(2,1)} %get-tuple-element.97), channel_id=1, source_target_pairs={{0,1},{1,0},{2,3},{3,2},{4,5},{5,4},{6,7},{7,6},{8,9},{9,8},{10,11... | collective-permute-start | bytes 3932168 | tf_op jit(solution)/shard_map/ppermute | solution.py:414
  144.3 2.1 copy-start.30
  144.3 10.2 %copy-start.29 = (s32[5]{0:T(128)}, s32[5]{0:T(128)S(1)}, u32[]{:S(2)}) copy-start(s32[5]{0:T(128)S(1)} %constant_dynamic-update-slice_fusion.place) | copy-start | bytes 64
  144.3 57.1 %collective-permute-start.13 = (bf16[4,64,512]{2,1,0:T(8,128)(2,1)}, bf16[4,64,512]{2,1,0:T(8,128)(2,1)}, u32[]{:S(2)}, u32[]{:S(2)}) collective-permute-start(bf16[4,64,512]{2,1,0:T(8,128)(2,1)} %get-tuple-element.90), channel_id=1, source_target_pairs={{0,1},{1,0},{2,3},{3,2},{4,5},{5,4},{6,7},{7,6},{8,9},{9,8},{10,11... | collective-permute-start | bytes 786440 | tf_op jit(solution)/shard_map/ppermute | solution.py:426
  144.4 58.8 %collective-permute-start.14 = (bf16[4,64,512]{2,1,0:T(8,128)(2,1)}, bf16[4,64,512]{2,1,0:T(8,128)(2,1)}, u32[]{:S(2)}, u32[]{:S(2)}) collective-permute-start(bf16[4,64,512]{2,1,0:T(8,128)(2,1)} %get-tuple-element.91), channel_id=1, source_target_pairs={{0,2},{1,3},{2,0},{3,1},{4,6},{5,7},{6,4},{7,5},{8,10},{9,11},{10,... | collective-permute-start | bytes 786440 | tf_op jit(solution)/shard_map/ppermute | solution.py:426
  146.3 56.9 %collective-permute-start.15 = (bf16[4,64,512]{2,1,0:T(8,128)(2,1)}, bf16[4,64,512]{2,1,0:T(8,128)(2,1)}, u32[]{:S(2)}, u32[]{:S(2)}) collective-permute-start(bf16[4,64,512]{2,1,0:T(8,128)(2,1)} %get-tuple-element.92), channel_id=1, source_target_pairs={{0,3},{1,2},{2,1},{3,0},{4,7},{5,6},{6,5},{7,4},{8,11},{9,10},{10,... | collective-permute-start | bytes 786440 | tf_op jit(solution)/shard_map/ppermute | solution.py:426
  146.4 9.1 %copy-start.3 = (bf16[2,2,4,64,512]{4,3,2,1,0:T(8,128)(2,1)S(1)}, bf16[2,2,4,64,512]{4,3,2,1,0:T(8,128)(2,1)}, u32[]{:S(2)}) copy-start(bf16[2,2,4,64,512]{4,3,2,1,0:T(8,128)(2,1)} %get-tuple-element.117) | copy-start | bytes 3145732
  154.5 1.0 copy-start.4
  155.5 2.7 copy-start.1
  174.7 14.9 %collective-permute-start.20 = (bf16[2,2,4,64,384]{4,3,2,1,0:T(8,128)(2,1)}, bf16[2,2,4,64,384]{4,3,2,1,0:T(8,128)(2,1)}, u32[]{:S(2)}, u32[]{:S(2)}) collective-permute-start(bf16[2,2,4,64,384]{4,3,2,1,0:T(8,128)(2,1)} %get-tuple-element.104), channel_id=1, source_target_pairs={{0,1},{1,0},{2,3},{3,2},{4,5},{5,4},{6,7},{7,6},{8,9},{9,8},{10,11... | collective-permute-start | bytes 2359304 | tf_op jit(solution)/shard_map/ppermute | solution.py:414
  175.0 21.7 %all-to-all-start.2 = ((bf16[4,4,64,640]{3,2,1,0:T(8,128)(2,1)}), bf16[4,4,64,640]{3,2,1,0:T(8,128)(2,1)S(1)}, u32[]{:S(2)}, u32[]{:S(2)}) async-start(bf16[4,4,64,640]{3,2,1,0:T(8,128)(2,1)} %bitcast.28), calls=%async_computation.2 | async-start | bytes 2621440 | tf_op jit(solution)/shard_map/all_to_all | solution.py:456
  178.6 10.0 %copy-start.20 = (f32[16,512]{1,0:T(8,128)S(1)}, f32[16,512]{1,0:T(8,128)}, u32[]{:S(2)}) copy-start(f32[16,512]{1,0:T(8,128)} %get-tuple-element.114) | copy-start | bytes 98308
  178.6 11.1 %copy-start.9 = (bf16[2,2,4,64,384]{4,3,2,1,0:T(8,128)(2,1)S(1)}, bf16[2,2,4,64,384]{4,3,2,1,0:T(8,128)(2,1)}, u32[]{:S(2)}) copy-start(bf16[2,2,4,64,384]{4,3,2,1,0:T(8,128)(2,1)} %get-tuple-element.112) | copy-start | bytes 2359300
  186.5 28.8 %collective-permute-start.18 = (bf16[4,64,512]{2,1,0:T(8,128)(2,1)}, bf16[4,64,512]{2,1,0:T(8,128)(2,1)S(1)}, u32[]{:S(2)}, u32[]{:S(2)}) collective-permute-start(bf16[4,64,512]{2,1,0:T(8,128)(2,1)} %get-tuple-element.109), channel_id=1, source_target_pairs={{0,2},{1,3},{2,0},{3,1},{4,6},{5,7},{6,4},{7,5},{8,10},{9,11},{10,... | collective-permute-start | bytes 786440 | tf_op jit(solution)/shard_map/ppermute | solution.py:426
  189.6 25.7 %collective-permute-start.19 = (bf16[4,64,512]{2,1,0:T(8,128)(2,1)}, bf16[4,64,512]{2,1,0:T(8,128)(2,1)}, u32[]{:S(2)}, u32[]{:S(2)}) collective-permute-start(bf16[4,64,512]{2,1,0:T(8,128)(2,1)} %get-tuple-element.110), channel_id=1, source_target_pairs={{0,3},{1,2},{2,1},{3,0},{4,7},{5,6},{6,5},{7,4},{8,11},{9,10},{10,... | collective-permute-start | bytes 786440 | tf_op jit(solution)/shard_map/ppermute | solution.py:426
  191.1 10.4 %copy-start.16 = (bf16[4,64,512]{2,1,0:T(8,128)(2,1)S(1)}, bf16[4,64,512]{2,1,0:T(8,128)(2,1)}, u32[]{:S(2)}) copy-start(bf16[4,64,512]{2,1,0:T(8,128)(2,1)} %get-tuple-element.89) | copy-start | bytes 786436
  197.7 14.1 %all-to-all-start.5 = ((bf16[4,64,640]{2,1,0:T(8,128)(2,1)}), bf16[4,64,640]{2,1,0:T(8,128)(2,1)S(1)}, u32[]{:S(2)}, u32[]{:S(2)}) async-start(bf16[4,64,640]{2,1,0:T(8,128)(2,1)} %reduce_sum.86), calls=%async_computation.5 | async-start | bytes 655360 | tf_op jit(solution)/shard_map/all_to_all | solution.py:725
  201.4 22.9 %reduce-scatter.5.cloned.1.call-start = ((), (), s32[]{:S(2)}) async-start(), calls=%async_computation.9 | async-start | bytes 327680 | tf_op jit(solution)/shard_map/reduce_scatter | solution.py:652
  203.2 13.9 %collective-permute-start.17 = (bf16[4,64,512]{2,1,0:T(8,128)(2,1)}, bf16[4,64,512]{2,1,0:T(8,128)(2,1)S(1)}, u32[]{:S(2)}, u32[]{:S(2)}) collective-permute-start(bf16[4,64,512]{2,1,0:T(8,128)(2,1)} %get-tuple-element.108), channel_id=1, source_target_pairs={{0,1},{1,0},{2,3},{3,2},{4,5},{5,4},{6,7},{7,6},{8,9},{9,8},{10,11... | collective-permute-start | bytes 786440 | tf_op jit(solution)/shard_map/ppermute | solution.py:426
  203.3 13.8 %copy-start.17 = (bf16[4,64,512]{2,1,0:T(8,128)(2,1)S(1)}, bf16[4,64,512]{2,1,0:T(8,128)(2,1)}, u32[]{:S(2)}) copy-start(bf16[4,64,512]{2,1,0:T(8,128)(2,1)} %get-tuple-element.107) | copy-start | bytes 786436
  211.8 18.0 %all-to-all-start.3 = ((bf16[4,4,72,384]{3,2,1,0:T(8,128)(2,1)}), bf16[4,4,72,384]{3,2,1,0:T(8,128)(2,1)S(1)}, u32[]{:S(2)}, u32[]{:S(2)}) async-start(bf16[4,4,72,384]{3,2,1,0:T(8,128)(2,1)} %bitcast.30), calls=%async_computation.3 | async-start | bytes 1769472 | tf_op jit(solution)/shard_map/all_to_all | solution.py:456
  218.0 9.3 %copy-start.10 = (bf16[64,640]{1,0:T(8,128)(2,1)}, bf16[64,640]{1,0:T(8,128)(2,1)S(1)}, u32[]{:S(2)}) copy-start(bf16[64,640]{1,0:T(8,128)(2,1)S(1)} %reduce_sum.87) | copy-start | bytes 245764
  225.8 10.4 %collective-permute-start.25 = (bf16[64,1152]{1,0:T(8,128)(2,1)}, bf16[64,1152]{1,0:T(8,128)(2,1)}, u32[]{:S(2)}, u32[]{:S(2)}) collective-permute-start(bf16[64,1152]{1,0:T(8,128)(2,1)} %pad_maximum_fusion.13), channel_id=1, source_target_pairs={{0,2},{2,0},{1,3},{3,1},{4,6},{6,4},{5,7},{7,5},{8,10},{10,8},{9,1... | collective-permute-start | bytes 442376 | tf_op jit(solution)/shard_map/ppermute | solution.py:414
  230.6 6.2 %copy-start.11 = (bf16[64,640]{1,0:T(8,128)(2,1)S(1)}, bf16[64,640]{1,0:T(8,128)(2,1)}, u32[]{:S(2)}) copy-start(bf16[64,640]{1,0:T(8,128)(2,1)} %copy-done.10) | copy-start | bytes 245764
  230.6 6.2 %copy-start.15 = (bf16[1,64,512]{2,1,0:T(8,128)(2,1)S(1)}, bf16[1,64,512]{2,1,0:T(8,128)(2,1)}, u32[]{:S(2)}) copy-start(bf16[1,64,512]{2,1,0:T(8,128)(2,1)} %reduce-scatter.5.cloned.1.call-done) | copy-start | bytes 196612
  230.6 9.9 %all-to-all-start.4 = ((bf16[4,72,384]{2,1,0:T(8,128)(2,1)}), bf16[4,72,384]{2,1,0:T(8,128)(2,1)S(1)}, u32[]{:S(2)}, u32[]{:S(2)}) async-start(bf16[4,72,384]{2,1,0:T(8,128)(2,1)} %reduce_sum.84), calls=%async_computation.4 | async-start | bytes 442368 | tf_op jit(solution)/shard_map/all_to_all | solution.py:726
  236.2 9.3 %collective-permute-start.26 = (bf16[64,1152]{1,0:T(8,128)(2,1)}, bf16[64,1152]{1,0:T(8,128)(2,1)S(1)}, u32[]{:S(2)}, u32[]{:S(2)}) collective-permute-start(bf16[64,1152]{1,0:T(8,128)(2,1)} %pad_maximum_fusion.13), channel_id=1, source_target_pairs={{0,1},{1,0},{2,3},{3,2},{4,5},{5,4},{6,7},{7,6},{8,9},{9,8},{10,11... | collective-permute-start | bytes 442376 | tf_op jit(solution)/shard_map/ppermute | solution.py:414
  236.2 9.3 %collective-permute-start.27 = (bf16[64,1152]{1,0:T(8,128)(2,1)}, bf16[64,1152]{1,0:T(8,128)(2,1)S(1)}, u32[]{:S(2)}, u32[]{:S(2)}) collective-permute-start(bf16[64,1152]{1,0:T(8,128)(2,1)} %collective-permute-done.25), channel_id=1, source_target_pairs={{0,1},{1,0},{2,3},{3,2},{4,5},{5,4},{6,7},{7,6},{8,9},{9,8},{10,11... | collective-permute-start | bytes 442376 | tf_op jit(solution)/shard_map/ppermute | solution.py:414
  240.6 4.2 %collective-permute-start.22 = (bf16[72,384]{1,0:T(8,128)(2,1)S(1)}, bf16[72,384]{1,0:T(8,128)(2,1)S(1)}, u32[]{:S(2)}, u32[]{:S(2)}) collective-permute-start(bf16[72,384]{1,0:T(8,128)(2,1)S(1)} %reduce_sum.85), channel_id=1, source_target_pairs={{0,2},{2,0},{1,3},{3,1},{4,6},{6,4},{5,7},{7,5},{8,10},{10,8},{9,1... | collective-permute-start | bytes 165896 | tf_op jit(solution)/shard_map/ppermute | solution.py:414
  241.9 2.9 %collective-permute-start.23 = (bf16[72,384]{1,0:T(8,128)(2,1)S(1)}, bf16[72,384]{1,0:T(8,128)(2,1)S(1)}, u32[]{:S(2)}, u32[]{:S(2)}) collective-permute-start(bf16[72,384]{1,0:T(8,128)(2,1)S(1)} %reduce_sum.85), channel_id=1, source_target_pairs={{0,1},{1,0},{2,3},{3,2},{4,5},{5,4},{6,7},{7,6},{8,9},{9,8},{10,11... | collective-permute-start | bytes 165896 | tf_op jit(solution)/shard_map/ppermute | solution.py:414
  244.8 3.5 %collective-permute-start.24 = (bf16[72,384]{1,0:T(8,128)(2,1)S(1)}, bf16[72,384]{1,0:T(8,128)(2,1)S(1)}, u32[]{:S(2)}, u32[]{:S(2)}) collective-permute-start(bf16[72,384]{1,0:T(8,128)(2,1)S(1)} %collective-permute-done.22), channel_id=1, source_target_pairs={{0,1},{1,0},{2,3},{3,2},{4,5},{5,4},{6,7},{7,6},{8,9},{9,8},{10,11... | collective-permute-start | bytes 165896 | tf_op jit(solution)/shard_map/ppermute | solution.py:414
  248.3 16.8 %copy-start.2 = (f32[64,2048]{1,0:T(8,128)S(1)}, f32[64,2048]{1,0:T(8,128)}, u32[]{:S(2)}) copy-start(f32[64,2048]{1,0:T(8,128)} %param.19) | copy-start | bytes 1572868
  248.7 16.5 %copy-start.13 = (bf16[64,512]{1,0:T(8,128)(2,1)S(1)}, bf16[64,512]{1,0:T(8,128)(2,1)}, u32[]{:S(2)}) copy-start(bf16[64,512]{1,0:T(8,128)(2,1)} %convert_element_type.124) | copy-start | bytes 196612
  253.0 10.9 %all-to-all-start.6 = ((f32[8,8,128]{2,1,0:T(8,128)}), f32[8,8,128]{2,1,0:T(8,128)S(1)}, u32[]{:S(2)}, u32[]{:S(2)}) async-start(f32[8,8,128]{2,1,0:T(8,128)} %broadcast_in_dim.11), calls=%async_computation.7 | async-start | bytes 65536 | tf_op jit(solution)/shard_map/all_to_all | solution.py:745
  258.2 9.7 %copy-start.7 = (f32[2,64,2048]{2,1,0:T(8,128)S(1)}, f32[2,64,2048]{2,1,0:T(8,128)}, u32[]{:S(2)}) copy-start(f32[2,64,2048]{2,1,0:T(8,128)} %param.23) | copy-start | bytes 3145732
  265.2 2.7 copy-start.8
  267.9 2.2 copy-start.19
  267.9 2.2 copy-start.21
  267.9 2.2 copy-start.22
  (5 other events, 3.7 us)
Sparse Core Ops, SparseCore 0:
  42.5 43.1 all-gather.2
Sparse Core Ops, SparseCore 1:
  158.2 26.8 reduce-scatter.6
  204.2 20.1 reduce-scatter.4

commit v3 on v2

--- a/solution.py
+++ b/solution.py
@@ -146,8 +146,9 @@
     qkv_out[:, width:] = nn_dot(h, w_qkv[:, width:]).astype(BF16)
 
 
-def attend_body(place, lengths, qkv, attn_out, lse_out, bias):
-    row = pl.program_id(0)
+def attend_body(place, lengths, qkv, *refs):
+    attn_out, lse_out, bias = refs[-3:]
+    row = pl.program_id(0) + place[4]
     width = attn_out.shape[1]
     pair = 2 * (width // HEADS)
     fill_bias(place, lengths, row, bias)
@@ -210,11 +211,18 @@
             parts[half, lo, y, h, :, column : column + quarter] = value[at : at + rows]
 
 
-def send_parts(parts, keep, send, core, sems):
-    copies = [
-        pltpu.make_async_copy(parts.at[core], keep, sems.at[0]),
-        pltpu.make_async_copy(parts.at[1 - core], send, sems.at[1]),
-    ]
+def send_parts(parts, keep, send, place, sems):
+    core = place[3]
+    copies = []
+    for i in range(parts.shape[1]):
+        for j in range(2):
+            lo_at, y_at = (place[5] ^ i, place[6] ^ j)
+            for half, target in ((core, keep), (1 - core, send)):
+                copies.append(
+                    pltpu.make_async_copy(
+                        parts.at[half, lo_at, y_at], target.at[i, j], sems.at[len(copies)]
+                    )
+                )
     for copy in copies:
         copy.start()
     for copy in copies:
@@ -235,14 +243,15 @@
             at = (half * 2 + y) * quarter
             value = nn_dot(dy_turned[...], act[:, at : at + quarter])
             write_parts(parts, half, y, 0, value, dims)
-    send_parts(parts, keep, send, place[3], sems)
+    send_parts(parts, keep, send, place, sems)
 
 
 def down_body(
-    place, x_one, act, slope, d0, d1, d2, d3,
+    dims, place, x_one, h_two, attn, act, slope, d0, d1, d2, d3,
     b0, b1, b2, b3, c0, c1, vec,
-    o0, o1, o2, o3, dx_out, dattn_out, dup_out, dao_out, vec_out,
-    w_out, w_up, w_down, up_sems, down_sems,
+    o0, o1, o2, o3, dx_out, dattn_out, vec_out, keep, send,
+    w_out, w_up, w_down, h_turned, attn_turned, dup_all, dao_all, parts,
+    up_sems, down_sems, out_sems,
 ):
     row = pl.program_id(0)
     width = vec.shape[1]
@@ -259,8 +268,11 @@
         for copy in down_copies + up_copies:
             copy.wait()
 
+    here = pl.ds(pl.multiple_of(row * slots, slots), slots)
     dy = jnp.concatenate([ref[0] for ref in (d0, d1, d2, d3)], axis=0)
     dy_float = dy.astype(F32)
+    h_turned[:, here] = h_two[...].T
+    attn_turned[:, here] = attn[...].T
     result = (x_one[...] + (nt_dot(act[...], w_down[...]) + vec[5:6])).astype(BF16)
     part = slots // 4
     for k, out in enumerate((o0, o1, o2, o3)):
@@ -269,45 +281,52 @@
         columns = slice(j * width, (j + 1) * width)
         dact = nn_dot(dy, w_down[:, columns])
         dup = (slope[:, columns].astype(F32) * dact).astype(BF16)
-        dup_out[:, columns] = dup
+        dup_all[here, columns] = dup
         vec_out[6 + j : 7 + j] += jnp.sum(dup.astype(F32), axis=0, keepdims=True)
-    dh = nt_dot(dup_out[...], w_up[...])
+    dh = nt_dot(dup_all[here, :], w_up[...])
     unit, scale = centered(x_one[...])
     vec_out[2:3] += jnp.sum(dh * unit, axis=0, keepdims=True)
     vec_out[3:4] += jnp.sum(dh, axis=0, keepdims=True)
     dx = dy_float + norm_back(unit, scale, dh * vec[2:3])
     dx_out[...] = dx
     dao = dx.astype(BF16)
-    dao_out[...] = dao
+    dao_all[here, :] = dao
     vec_out[4:5] += jnp.sum(dao.astype(F32), axis=0, keepdims=True)
     vec_out[5:6] += jnp.sum(dy_float, axis=0, keepdims=True)
     dattn_out[...] = nt_dot(dao, w_out[...]).astype(BF16)
 
-
-def up_grad_body(dims, place, h_two, dup, attn, dao, keep, send, turned, parts, sems):
-    turned[...] = h_two[...].T
-    quarter = dup.shape[1] // 4
-    small = dao.shape[1] // 4
-    for half in range(2):
-        for y in range(2):
-            at = (half * 2 + y) * quarter
-            value = nn_dot(turned[...], dup[:, at : at + quarter])
-            write_parts(parts, half, y, 0, value, dims)
-    turned[...] = attn[...].T
-    for half in range(2):
-        for y in range(2):
-            at = (half * 2 + y) * small
-            value = nn_dot(turned[...], dao[:, at : at + small])
-            write_parts(parts, half, y, quarter, value, dims)
-    send_parts(parts, keep, send, place[3], sems)
-
-
-def scores_back_body(place, lengths, qkv, lse, dattn, dqkv, bias):
-    row = pl.program_id(0) + place[4]
-    width = dattn.shape[1]
+    @pl.when(row == pl.num_programs(0) - 1)
+    def _():
+        quarter = hidden // 4
+        small = width // 4
+        for half in range(2):
+            for y in range(2):
+                at = (half * 2 + y) * quarter
+                value = nn_dot(h_turned[...], dup_all[:, at : at + quarter])
+                write_parts(parts, half, y, 0, value, dims)
+                at = (half * 2 + y) * small
+                value = nn_dot(attn_turned[...], dao_all[:, at : at + small])
+                write_parts(parts, half, y, quarter, value, dims)
+        send_parts(parts, keep, send, place, out_sems)
+
+
+def back_rows(
+    place, lengths, qkv, lse, dattn, xs, dx, pieces, vec, outs, dqkv, vec_out, w_qkv, bias, sems
+):
+    step = pl.program_id(0)
+    width = vec.shape[1]
+    slots = qkv.shape[0]
     pair = 2 * (width // HEADS)
     score_scale = 1.0 / math.sqrt(width // HEADS)
-    fill_bias(place, lengths, row, bias)
+    copies = placements(pieces, [(0, 3 * width, w_qkv)], place, sems)
+
+    @pl.when(step == 0)
+    def _():
+        vec_out[...] = jnp.zeros_like(vec_out)
+        for copy in copies:
+            copy.start()
+
+    fill_bias(place, lengths, step + place[4], bias)
     masks = head_masks(pair)
     for p in range(HEADS // 2):
         at = p * pair
@@ -337,47 +356,173 @@
         dqkv[:, width + at : width + at + pair] = dk.astype(BF16)
         dqkv[:, 2 * width + at : 2 * width + at + pair] = dv.astype(BF16)
 
-
-def qkv_grad_body(dims, place, h_one, g0, g1, keep, send, turned, parts, sems):
-    turned[...] = h_one[...].T
-    count = g0.shape[0]
-    quarter = g0.shape[1] // 4
-    for half in range(2):
-        for y in range(2):
-            at = (half * 2 + y) * quarter
-            value = nn_dot(turned[:, :count], g0[:, at : at + quarter])
-            value = value + nn_dot(turned[:, count:], g1[:, at : at + quarter])
-            write_parts(parts, half, y, 0, value, dims)
-    send_parts(parts, keep, send, place[3], sems)
-
-
-def input_body(
-    place, g0, g1, x0, x1, x2, x3, dx, p0, p1, p2, p3, vec, o0, o1, o2, o3, vec_out, w_qkv, sems
-):
-    row = pl.program_id(0)
-    width = vec.shape[1]
-    slots = dx.shape[0]
-    copies = placements((p0, p1, p2, p3), [(0, 3 * width, w_qkv)], place, sems)
-
-    @pl.when(row == 0)
+    @pl.when(step == 0)
     def _():
-        vec_out[...] = jnp.zeros_like(vec_out)
-        for copy in copies:
-            copy.start()
         for copy in copies:
             copy.wait()
 
-    first = row < pl.num_programs(0) // 2
-    dqkv = jnp.where(first, g0[...], g1[...])
-    dh = nt_dot(dqkv, w_qkv[...])
-    x = jnp.concatenate([ref[0] for ref in (x0, x1, x2, x3)], axis=0).astype(F32)
+    dh = nt_dot(dqkv[...], w_qkv[...])
+    x = jnp.concatenate([ref[0] for ref in xs], axis=0).astype(F32)
     unit, scale = centered(x)
     vec_out[0:1] += jnp.sum(dh * unit, axis=0, keepdims=True)
     vec_out[1:2] += jnp.sum(dh, axis=0, keepdims=True)
     grad = (dx[...] + norm_back(unit, scale, dh * vec[0:1])).astype(BF16)
     part = slots // 4
-    for k, out in enumerate((o0, o1, o2, o3)):
+    for k, out in enumerate(outs):
         out[0] = grad[k * part : (k + 1) * part]
+
+
+def back_first_body(
+    place, lengths, qkv, lse, dattn, x0, x1, x2, x3, dx, p0, p1, p2, p3, vec,
+    o0, o1, o2, o3, dqkv_out, vec_out, w_qkv, bias, sems,
+):
+    back_rows(
+        place, lengths, qkv, lse, dattn, (x0, x1, x2, x3), dx, (p0, p1, p2, p3), vec,
+        (o0, o1, o2, o3), dqkv_out, vec_out, w_qkv, bias, sems,
+    )
+
+
+def back_last_body(
+    dims, place, lengths, qkv, lse, dattn, x0, x1, x2, x3, dx, p0, p1, p2, p3, vec, h_one, before,
+    u0, u1, u2, u3,
+    o0, o1, o2, o3, vec_out, keep, send, dqkv, w_qkv, bias, h_turned, parts, sems, out_sems,
+):
+    step = pl.program_id(0)
+    slots = qkv.shape[0]
+    here = pl.ds(pl.multiple_of(step * slots, slots), slots)
+    back_rows(
+        place, lengths, qkv, lse, dattn, (x0, x1, x2, x3), dx, (p0, p1, p2, p3), vec,
+        (o0, o1, o2, o3), dqkv.at[here], vec_out, w_qkv, bias, sems,
+    )
+
+    @pl.when(step == pl.num_programs(0) - 1)
+    def _():
+        count = before.shape[0]
+        h_turned[...] = h_one[...].T
+        quarter = before.shape[1] // 4
+        for half in range(2):
+            for y in range(2):
+                at = (half * 2 + y) * quarter
+                value = nn_dot(h_turned[:, :count], before[:, at : at + quarter])
+                value = value + nn_dot(h_turned[:, count:], dqkv[:, at : at + quarter])
+                write_parts(parts, half, y, 0, value, dims)
+        send_parts(parts, keep, send, place, out_sems)
+
+
+def add_body(with_vec, *refs):
+    if with_vec:
+        keep, got, *vecs = refs[:-4]
+    else:
+        keep, got = refs[:-4]
+    outs = refs[-4:]
+    rows = keep.shape[2]
+    for k, out in enumerate(outs):
+        value = (keep[k].astype(F32) + got[k].astype(F32)).astype(BF16)
+        if not with_vec:
+            out[...] = value
+            continue
+        out[:, :rows, :] = value
+        out[:, rows:, :] = jnp.zeros((out.shape[0], 16, out.shape[2]), BF16)
+        sums = vecs[0][...]
+        for vec in vecs[1:]:
+            sums = sums + vec[...]
+        lanes = sums.shape[1] // out.shape[0]
+        for h in range(out.shape[0]):
+            out[h, rows:, :lanes] = sums[:, h * lanes : (h + 1) * lanes].astype(BF16)
+
+
+def collect_body(place, p0, p1, p2, p3, out):
+    for k, piece in enumerate((p0, p1, p2, p3)):
+        out[place[2] ^ k] = piece[...]
+
+
+def in_order(values, place):
+    core, y = place[3], place[7]
+    near = (jnp.where(y == 0, values[0], values[1]), jnp.where(y == 0, values[1], values[0]))
+    far = (jnp.where(y == 0, values[2], values[3]), jnp.where(y == 0, values[3], values[2]))
+    first = (jnp.where(core == 0, near[0], far[0]), jnp.where(core == 0, near[1], far[1]))
+    second = (jnp.where(core == 0, far[0], near[0]), jnp.where(core == 0, far[1], near[1]))
+    return (*first, *second)
+
+
+def vec_sums(a0, a2, place, shard):
+    lanes = 128
+    own = a0[shard:, :lanes].astype(F32)
+    far = a2[shard:, :lanes].astype(F32)
+    both = own + far
+    lane = lax.broadcasted_iota(jnp.int32, both.shape, 1) // (lanes // 2)
+    return jnp.where(lane == place[8], both, 0.0)
+
+
+def square_body(place, m0, m1, m2, m3, a0, a1, a2, a3, out):
+    shard = m0.shape[0]
+    values = []
+    for mlp, attn in ((m0, a0), (m1, a1), (m2, a2), (m3, a3)):
+        big = mlp[...].astype(F32)
+        small = attn[:shard].astype(F32)
+        values.append(jnp.sum(big * big) + jnp.sum(small * small))
+    vec = vec_sums(a0, a2, place, shard)
+    first, second, third, fourth = in_order(values, place)
+    value = ((first + second) + (third + fourth)) + jnp.sum(vec * vec)
+    out[...] = jnp.full(out.shape, value, F32)
+
+
+def adam_parts(weight, moment, second, grad, decay, rate):
+    moment_new = BETA_ONE * moment + (1.0 - BETA_ONE) * grad
+    second_new = BETA_TWO * second + (1.0 - BETA_TWO) * grad * grad
+    first_hat = moment_new * (1.0 / (1.0 - BETA_ONE**ADAM_STEP))
+    second_hat = second_new * (1.0 / (1.0 - BETA_TWO**ADAM_STEP))
+    step = first_hat / (jnp.sqrt(second_hat) + ADAM_EPS)
+    return weight - rate * (step + decay * weight), moment_new, second_new
+
+
+def adam_body(
+    place, squares, m0, m1, m2, m3, a0, a1, a2, a3,
+    attn_w, attn_m, attn_v, mlp_w, mlp_m, mlp_v, vec_w, vec_m, vec_v,
+    norm_out, attn_wo, attn_mo, attn_vo, mlp_wo, mlp_mo, mlp_vo, vec_wo, vec_mo, vec_vo,
+):
+    shard = m0.shape[0]
+    hidden = mlp_w.shape[2]
+    quarter = hidden // 4
+    wide = a0.shape[1]
+    small = m0.shape[1] - 2 * quarter
+    value = squares[0]
+    for d in range(1, squares.shape[0]):
+        value = value + squares[d]
+    norm = jnp.sqrt(value)
+    norm_out[...] = norm[0:1, 0:1]
+    factor = (CLIP_NORM / jnp.maximum(norm, CLIP_NORM))[0:1, 0:1]
+    rows, cols = vec_w.shape
+    vec = vec_sums(a0, a2, place, shard)
+    grad = (vec[:rows, :cols] + vec[:rows, cols : 2 * cols]) * factor
+    parts = adam_parts(vec_w[...], vec_m[...], vec_v[...], grad, 0.0, VEC_RATE)
+    for new, new_value in zip((vec_wo, vec_mo, vec_vo), parts):
+        new[...] = new_value
+    core, y = place[3], place[7]
+    olds = (attn_w, attn_m, attn_v)
+    news = (attn_wo, attn_mo, attn_vo)
+    mlp_olds = (mlp_w, mlp_m, mlp_v)
+    mlp_news = (mlp_wo, mlp_mo, mlp_vo)
+    for i, (mlp, attn) in enumerate(((m0, a0), (m1, a1), (m2, a2), (m3, a3))):
+        side = (core if i < 2 else 1 - core) * 2 + (y if i % 2 == 0 else 1 - y)
+
+        def columns(base, size, side=side):
+            return pl.ds(pl.multiple_of(base + side * size, 128), size)
+
+        at = columns(0, wide)
+        grad = attn[:shard].astype(F32) * factor
+        for new, new_value in zip(news, adam_parts(*[o[:, at] for o in olds], grad, WEIGHT_DECAY, LEARN_RATE)):
+            new[:, at] = new_value
+        at = columns(4 * wide, small)
+        grad = mlp[:, quarter : quarter + small].astype(F32) * factor
+        for new, new_value in zip(news, adam_parts(*[o[:, at] for o in olds], grad, WEIGHT_DECAY, LEARN_RATE)):
+            new[:, at] = new_value
+        at = columns(0, quarter)
+        for j, start in ((0, 0), (1, quarter + small)):
+            grad = mlp[:, start : start + quarter].astype(F32) * factor
+            parts = adam_parts(*[o[j, :, at] for o in mlp_olds], grad, WEIGHT_DECAY, LEARN_RATE)
+            for new, new_value in zip(mlp_news, parts):
+                new[j, :, at] = new_value
 
 
 def shape_of(dims, dtype):
@@ -392,7 +537,7 @@
     return pl.BlockSpec(shape, lambda r: (0,) * len(shape))
 
 
-def call(body, grid, in_specs, out_specs, out_shape, scratch, cost, name):
+def call(body, grid, in_specs, out_specs, out_shape, scratch, cost, name, aliases=None):
     return pl.pallas_call(
         body,
         grid=(grid,),
@@ -400,6 +545,7 @@
         out_specs=out_specs,
         out_shape=out_shape,
         scratch_shapes=scratch,
+        input_output_aliases=aliases or {},
         compiler_params=pltpu.CompilerParams(
             vmem_limit_bytes=VMEM_BYTES, dimension_semantics=("arbitrary",)
         ),
@@ -518,11 +664,11 @@
     first_half = jnp.concatenate([half_of(attn_w[:, : 3 * width]), ride], axis=1).astype(BF16)
     qkv_own = spread_hi(first_half)
     up_half = jnp.concatenate([half_of(attn_w[:, 3 * width :]), half_of(mlp_w[0])], axis=1)
-    up_half, down_half, qkv_own = lax.optimization_barrier(
-        (up_half.astype(BF16), half_of(mlp_w[1]).astype(BF16), qkv_own)
-    )
-    qkv_pieces = share(qkv_own)
-    up_own = spread_hi(up_half)
+    up_own = spread_hi(after(up_half.astype(BF16), qkv_own))
+    qkv_own, xs[3] = lax.optimization_barrier((qkv_own, xs[3]))
+    qkv_other = swap(qkv_own, "lo")
+    qkv_pieces = [qkv_own, qkv_other, swap(qkv_own, "core"), swap(qkv_other, "core")]
+    down_half = after(half_of(mlp_w[1]).astype(BF16), up_own)
     down_own = lax.all_gather(down_half, ("hi", "lo"), axis=0)
     vec_all = ordered(qkv_pieces[0][:, :, 3 * width :], qkv_pieces[1][:, :, 3 * width :], lo, 1)
     vec_all = vec_all.reshape(2 * hi_count, -1)[:, : vec_w.size].reshape(-1, vec_rows, vec_cols)
@@ -530,12 +676,15 @@
     vec_float = jnp.pad(vec_all.astype(F32), ((0, 16 - vec_rows), (0, 0)))
 
     if fits:
-        place = jnp.stack([lo, core, me, core, 0 * lo]).astype(jnp.int32)
+        places = [lo, core, me, core, 0 * lo, lo, y, y, lo]
         dims = (hi_count, 2, shard)
     else:
         qkv_pieces = settle(qkv_pieces, lo, core)
-        place = jnp.stack([0 * lo, 0 * lo, me, core, 0 * lo]).astype(jnp.int32)
+        places = [0 * lo, 0 * lo, me, core, 0 * lo, 0 * lo, 0 * lo, y, lo]
         dims = (1, 1, width)
+    place = jnp.stack(places).astype(jnp.int32)
+    flat = jnp.stack([*places[:5], 0 * lo, 0 * lo]).astype(jnp.int32)
+    later = place.at[4].set(rows // 2)
     row_lengths = lax.dynamic_slice_in_dim(lengths.reshape(-1), me * rows, rows)
 
     slot_spec = pl.BlockSpec((1, part, width), lambda r: (r, 0, 0))
@@ -559,18 +708,29 @@
 
     cot, qkv, up_own = lax.optimization_barrier((flat_cot, qkv, up_own))
     dys = from_seq([pick(cot, k) for k in range(4)])
-    up_pieces = share(up_own)
-    attn, lse = call(
-        attend_body,
-        rows,
-        [SMEM, SMEM, triple],
-        [narrow, lse_spec],
-        [shape_of((count, width), BF16), shape_of((rows, HEADS, slots), F32)],
-        [pltpu.VMEM((slots, slots), F32)],
-        12,
-        "attend",
-    )(place, row_lengths, qkv)
-
+    up_other = swap(up_own, "lo")
+
+    def half_spec(block, base):
+        zeros = (0,) * (len(block) - 1)
+        return pl.BlockSpec(block, lambda r: (r + base, *zeros))
+
+    def attend(qkv, base, before):
+        return call(
+            attend_body,
+            rows // 2,
+            [SMEM, SMEM, half_spec((slots, 3 * width), base), *[ANY] * len(before)],
+            [half_spec((slots, width), base), half_spec((1, HEADS, slots), base)],
+            [shape_of((count, width), BF16), shape_of((rows, HEADS, slots), F32)],
+            [pltpu.VMEM((slots, slots), F32)],
+            7,
+            "attend",
+            {3: 0, 4: 1} if before else None,
+        )(later if base else place, row_lengths, qkv, *before)
+
+    attn, lse = attend(qkv, 0, [])
+    up_other, attn, lse = lax.optimization_barrier((up_other, attn, lse))
+    attn, lse = attend(qkv, rows // 2, [attn, lse])
+    up_pieces = [up_own, up_other, swap(up_own, "core"), swap(up_other, "core")]
     if not fits:
         up_pieces = settle(up_pieces, lo, core)
     x_one, h_two, act, slope = call(
@@ -592,18 +752,6 @@
     def parts_shape(quarter):
         return (dims[1], 2, dims[0], dims[2], quarter)
 
-    def grad_call(body, args, quarter, scratch, cost, name):
-        shape = parts_shape(quarter)
-        return call(
-            functools.partial(body, dims),
-            1,
-            [SMEM, *[whole_spec(a.shape) for a in args]],
-            [ANY, ANY],
-            [shape_of(shape, BF16)] * 2,
-            [scratch, pltpu.VMEM((2, *shape), BF16), dma((2,))],
-            cost,
-            name,
-        )(place, *args)
 
     def in_dp_order(value):
         if fits:
@@ -612,9 +760,18 @@
         return value.transpose(2, 0, 1, 3, 4)
 
     turned = pltpu.VMEM((width, count), BF16)
-    down_keep, down_send = grad_call(
-        down_grad_body, [act, *dys], hidden // 4, turned, 4, "down_grad"
-    )
+    n_part = 4 * dims[1]
+    shape = parts_shape(hidden // 4)
+    down_keep, down_send = call(
+        functools.partial(down_grad_body, dims),
+        1,
+        [SMEM, whole_spec(act.shape), *[whole_spec(xs[0].shape)] * 4],
+        [ANY, ANY],
+        [shape_of(shape, BF16)] * 2,
+        [turned, pltpu.VMEM((2, *shape), BF16), dma((n_part,))],
+        5,
+        "down_grad",
+    )(flat, act, *dys)
     down_got = swap(down_send, "core")
     down_far = swap(down_own, "core")
     down_pieces = [down_own, down_far]
@@ -622,116 +779,206 @@
         whole = ordered(down_own, down_far, core, 1).reshape(8, 2, -1, hidden)
         down_pieces = [whole[:, 0], whole[:, 1]]
     n_down = 2 * down_pieces[0].shape[0]
+    shape = parts_shape(hidden // 4 + width // 4)
     outs = call(
-        down_body,
+        functools.partial(down_body, dims),
         rows,
-        [SMEM, narrow, wide, wide, *[slot_spec] * 4, *[ANY] * 6, vec_spec],
-        [*[slot_spec] * 4, narrow, narrow, wide, narrow, vec_spec],
+        [SMEM, narrow, narrow, narrow, wide, wide, *[slot_spec] * 4, *[ANY] * 6, vec_spec],
+        [*[slot_spec] * 4, narrow, narrow, vec_spec, ANY, ANY],
         [
             *[shape_of((rows, part, width), BF16)] * 4,
             shape_of((count, width), F32),
             shape_of((count, width), BF16),
-            shape_of((count, hidden), BF16),
-            shape_of((count, width), BF16),
             shape_of((16, width), F32),
+            shape_of(shape, BF16),
+            shape_of(shape, BF16),
         ],
         [
             pltpu.VMEM((width, width), BF16),
             pltpu.VMEM((width, hidden), BF16),
             pltpu.VMEM((width, hidden), BF16),
+            turned,
+            turned,
+            pltpu.VMEM((count, hidden), BF16),
+            pltpu.VMEM((count, width), BF16),
+            pltpu.VMEM((2, *shape), BF16),
             dma((2 * n_piece,)),
             dma((n_down,)),
+            dma((n_part,)),
         ],
-        18,
+        20,
         "down",
-    )(place, x_one, act, slope, *dys, *up_pieces, *down_pieces, vec_float)
-    results, (dx, dattn, dup, dao, vec_mlp) = outs[:4], outs[4:]
+    )(place, x_one, h_two, attn, act, slope, *dys, *up_pieces, *down_pieces, vec_float)
+    results, (dx, dattn, vec_mlp, up_keep, up_send) = outs[:4], outs[4:]
+    up_got = swap(up_send, "core")
     down_part = in_dp_order(add_pair(down_keep, down_got))
     down_part = down_part.reshape(4, *down_part.shape[2:])
-    down_part = lax.psum_scatter(down_part, ("lo", "y"), scatter_dimension=0)
-    down_mine = lax.psum_scatter(down_part, "hi", scatter_dimension=0)
-
-    up_keep, up_send = grad_call(
-        up_grad_body, [h_two, dup, attn, dao], hidden // 4 + width // 4, turned, 6, "up_grad"
-    )
-    up_got = swap(up_send, "core")
-
-    def scores_back(qkv, half):
-        base = half * (rows // 2)
+    down_plane = lax.psum_scatter(down_part, ("lo", "y"), scatter_dimension=0)
+    down_mine = lax.psum_scatter(down_plane, "hi", scatter_dimension=0)
+
+    def collect(parts):
         return call(
-            scores_back_body,
-            rows // 2,
-            [
-                SMEM,
-                SMEM,
-                pl.BlockSpec((slots, 3 * width), lambda r: (r + base, 0)),
-                pl.BlockSpec((1, HEADS, slots), lambda r: (r + base, 0, 0)),
-                pl.BlockSpec((slots, width), lambda r: (r + base, 0)),
-            ],
-            triple,
-            shape_of((count // 2, 3 * width), BF16),
-            [pltpu.VMEM((slots, slots), F32)],
-            8,
-            "scores_back",
-        )(place.at[4].set(base), row_lengths, qkv, lse, dattn)
-
-    grad_first = scores_back(after(qkv, up_send), 0)
-    up_part = in_dp_order(add_pair(up_keep, up_got))
-    up_part, grad_first = lax.optimization_barrier((up_part, grad_first))
-    up_part = spread_plane(up_part)
-    grad_last = scores_back(after(qkv, grad_first), 1)
-    qkv_keep, qkv_send = grad_call(
-        qkv_grad_body, [h_one, grad_first, grad_last], 3 * width // 4, turned, 4, "qkv_grad"
-    )
-    qkv_got = swap(qkv_send, "core")
-    outs = call(
-        input_body,
-        rows,
-        [
+            collect_body,
+            1,
+            [SMEM, *[whole_spec(parts[0].shape)] * 4],
+            whole_spec((4, *parts[0].shape)),
+            shape_of((4, *parts[0].shape), BF16),
+            [],
+            2,
+            "collect",
+        )(place, *parts).reshape(tokens.shape)
+
+    results = from_seq(results)
+    back_args = [lse, dattn, *xs, dx]
+    weights = [*qkv_pieces, vec_float]
+
+    def back_specs(base):
+        return [
             SMEM,
-            pl.BlockSpec((slots, 3 * width), lambda r: (jnp.minimum(r, rows // 2 - 1), 0)),
-            pl.BlockSpec((slots, 3 * width), lambda r: (jnp.maximum(r - rows // 2, 0), 0)),
-            *[slot_spec] * 4,
-            narrow,
+            SMEM,
+            half_spec((slots, 3 * width), base),
+            half_spec((1, HEADS, slots), base),
+            half_spec((slots, width), base),
+            *[half_spec((1, part, width), base)] * 4,
+            half_spec((slots, width), base),
             *[ANY] * 4,
             vec_spec,
+        ]
+
+    back_shapes = [shape_of((rows, part, width), BF16)] * 4
+    back_scratch = [pltpu.VMEM((width, 3 * width), BF16), pltpu.VMEM((slots, slots), F32)]
+    outs = call(
+        back_first_body,
+        rows // 2,
+        back_specs(0),
+        [*[half_spec((1, part, width), 0)] * 4, triple, vec_spec],
+        [*back_shapes, shape_of((count // 2, 3 * width), BF16), shape_of((16, width), F32)],
+        [*back_scratch, dma((n_piece,))],
+        11,
+        "back_first",
+    )(place, row_lengths, after(qkv, up_send, down_part), *back_args, *weights)
+    input_first, (grad_first, vec_first) = outs[:4], outs[4:]
+
+    def add_call(keep, got, vecs):
+        dims_of = (4, *keep.shape[2:])
+        more = 16 if vecs else 0
+        out = shape_of((dims_of[1], dims_of[2] + more, dims_of[3]), BF16)
+        return call(
+            functools.partial(add_body, bool(vecs)),
+            1,
+            [whole_spec(dims_of)] * 2 + [whole_spec(v.shape) for v in vecs],
+            [whole_spec(out.shape)] * 4,
+            [out] * 4,
+            [],
+            2,
+            "add",
+        )(keep.reshape(dims_of), got.reshape(dims_of), *vecs)
+
+    def plane_sum(parts):
+        moved = [parts[0]]
+        for k in (2, 1, 3):
+            perm = [(j, j ^ k) for j in range(4)]
+            moved.append(lax.ppermute(parts[k], ("lo", "y"), perm))
+        return moved
+
+    def add_moved(moved):
+        value = (moved[0].astype(F32) + moved[1].astype(F32)) + moved[2].astype(F32)
+        return (value + moved[3].astype(F32)).astype(BF16)
+
+    def plane_total(keep, got, extra):
+        part = in_dp_order(add_pair(keep, got))
+        if extra is not None:
+            part = jnp.concatenate([part, extra], axis=3)
+        return total(spread_plane(part))
+
+    qkv_last = qkv
+    output = collect(results)
+    if fits:
+        parts = add_call(after(up_keep, grad_first, *results), up_got, [])
+        parts = lax.optimization_barrier((*parts, grad_first))
+        qkv_last = after(qkv, *parts, down_plane)
+        up_moved = plane_sum(parts[:4])
+    quarter = 3 * width // 4
+    shape = parts_shape(quarter)
+    outs = call(
+        functools.partial(back_last_body, dims),
+        rows // 2,
+        [
+            *back_specs(rows // 2),
+            whole_spec((count, width)),
+            whole_spec((count // 2, 3 * width)),
+            *[ANY] * 4,
         ],
-        [*[slot_spec] * 4, vec_spec],
-        [*[shape_of((rows, part, width), BF16)] * 4, shape_of((16, width), F32)],
-        [pltpu.VMEM((width, 3 * width), BF16), dma((n_piece,))],
-        6,
-        "input_grad",
-    )(place, grad_first, after(grad_last, qkv_send), *xs, dx, *qkv_pieces, vec_float)
-    input_parts, vec_attn = outs[:4], outs[4]
-
-    def send_back(parts):
-        parts = from_seq(parts)
-        pairs = [ordered(parts[0], parts[1], core, 0), ordered(parts[2], parts[3], core, 0)]
-        return ordered(pairs[0], pairs[1], y, 0).reshape(tokens.shape)
-
-    extra_rows = 8
-    quarter = 3 * width // 4
-    vec_total = (vec_attn + vec_mlp)[:vec_rows].reshape(vec_rows, hi_count, 2, vec_cols)
-    vec_total = vec_total.transpose(2, 1, 0, 3).reshape(2, hi_count, -1)
-    vec_total = jnp.pad(
-        vec_total, ((0, 0), (0, 0), (0, extra_rows * quarter - vec_total.shape[-1]))
-    )
-    vec_total = vec_total.reshape(2, 1, hi_count, extra_rows, quarter).astype(BF16)
-    vec_total = jnp.broadcast_to(vec_total, (2, 2, *vec_total.shape[2:]))
-    qkv_part = in_dp_order(add_pair(qkv_keep, qkv_got))
-    qkv_part = jnp.concatenate([qkv_part, vec_total], axis=3)
-    up_part, qkv_part = lax.optimization_barrier((up_part, qkv_part))
-    qkv_part = spread_plane(qkv_part)
-    up_mine = total(lax.all_to_all(total(up_part), "hi", 0, 0))
-    qkv_mine = total(lax.all_to_all(total(qkv_part), "hi", 0, 0))
+        [*[half_spec((1, part, width), rows // 2)] * 4, vec_spec, ANY, ANY],
+        [*back_shapes, shape_of((16, width), F32), shape_of(shape, BF16), shape_of(shape, BF16)],
+        [
+            pltpu.VMEM((count // 2, 3 * width), BF16),
+            *back_scratch,
+            turned,
+            pltpu.VMEM((2, *shape), BF16),
+            dma((n_piece,)),
+            dma((n_part,)),
+        ],
+        13,
+        "back_last",
+        {17 + k: k for k in range(4)},
+    )(later, row_lengths, qkv_last, *back_args, *weights, h_one, grad_first, *input_first)
+    input_parts, (vec_last, qkv_keep, qkv_send) = outs[:4], outs[4:]
+    if fits:
+        qkv_send = after(qkv_send, *up_moved)
+    qkv_got = swap(qkv_send, "core")
+    vecs = [vec_mlp, vec_first, vec_last]
+
+    if fits:
+        parts = add_call(qkv_keep, qkv_got, vecs)
+        qkv_moved = plane_sum(parts)
+        up_mine = total(lax.all_to_all(add_moved(up_moved), "hi", 0, 0))
+        qkv_mine = total(lax.all_to_all(add_moved(qkv_moved), "hi", 0, 0))
+    else:
+        vec_total = (vec_mlp + vec_first + vec_last).reshape(16, hi_count, 2, vec_cols)
+        vec_total = vec_total.transpose(1, 0, 2, 3).reshape(1, 1, hi_count, 16, 2 * vec_cols)
+        vec_total = jnp.pad(vec_total.astype(BF16), ((0, 0),) * 4 + ((0, quarter - 2 * vec_cols),))
+        vec_total = jnp.broadcast_to(vec_total, (2, 2, *vec_total.shape[2:]))
+        up_mine = total(lax.all_to_all(plane_total(up_keep, up_got, None), "hi", 0, 0))
+        qkv_mine = plane_total(qkv_keep, qkv_got, vec_total)
+        qkv_mine = total(lax.all_to_all(qkv_mine, "hi", 0, 0))
     mlp_pieces = to_all(jnp.concatenate([up_mine, down_mine], axis=1))
-    qkv_mine, *_ = lax.optimization_barrier((qkv_mine, *mlp_pieces[:1]))
     attn_pieces = to_all(qkv_mine)
-    output = send_back(results)
-    input_grad = send_back(input_parts)
+    input_grad = collect(from_seq(input_parts))
+
+    dp_count = 2 * hi_count
+    if fits:
+        pieces = [*mlp_pieces, *attn_pieces]
+        piece_specs = [whole_spec(p.shape) for p in pieces]
+        squares_shape = (dp_count, 8, 128)
+        squares = call(
+            square_body,
+            1,
+            [SMEM, *piece_specs],
+            whole_spec(squares_shape),
+            shape_of(squares_shape, F32),
+            [],
+            2,
+            "squares",
+        )(place, *pieces)
+        squares = lax.all_to_all(squares, ("hi", "lo"), 0, 0)
+        states = [attn_w, attn_m, attn_v, mlp_w, mlp_m, mlp_v, vec_w, vec_m, vec_v]
+        state_specs = [whole_spec(v.shape) for v in states]
+        norm, *new = call(
+            adam_body,
+            1,
+            [SMEM, whole_spec(squares_shape), *piece_specs, *state_specs],
+            [whole_spec((1, 1)), *state_specs],
+            [shape_of((1, 1), F32), *[shape_of(v.shape, F32) for v in states]],
+            [],
+            6,
+            "adam",
+        )(place, squares, *pieces, *states)
+        return (output, input_grad, *new, norm.reshape(()))
 
     vec_sum = attn_pieces[0][shard:].astype(F32) + attn_pieces[2][shard:].astype(F32)
-    vec_sum = vec_sum.reshape(-1)[: vec_rows * vec_cols].reshape(vec_rows, vec_cols)
+    vec_sum = jnp.where(lo == 0, vec_sum[:, :vec_cols], vec_sum[:, vec_cols : 2 * vec_cols])
+    vec_sum = vec_sum[:vec_rows]
     up_at = hidden // 4
     out_at = up_at + width // 4
     up_sum = in_columns([p[:, :up_at] for p in mlp_pieces], y, core)
@@ -741,7 +988,6 @@
     attn_sum = jnp.concatenate([qkv_sum, out_sum], axis=1)
     mlp_sum = jnp.stack([up_sum, down_sum])
     square = jnp.sum(attn_sum * attn_sum) + jnp.sum(mlp_sum * mlp_sum) + jnp.sum(vec_sum * vec_sum)
-    dp_count = 2 * hi_count
     squares = lax.all_to_all(jnp.full((dp_count, 8, 128), square), ("hi", "lo"), 0, 0)
     grad_norm = jnp.sqrt(jnp.sum(squares[:, 0, 0]))
     clip_factor = CLIP_NORM / jnp.maximum(grad_norm, CLIP_NORM)

time: 282 us -> 245 us (0.87)
  other arithmetic: 38 us -> 7.56 us
  waiting for transfers between devices: 65.9 us -> 51.3 us
  Pallas kernels: 98.5 us -> 111 us
  between operations: 20 us -> 16.1 us
    pallas_call x8 -> x12, Pallas kernels: 73.4 us -> 85.9 us  [the longest x1 21.4 us: on_device(): call(functools.partial(down_body, dims), rows, [SMEM, narrow, narrow, nar...]
    another operation x18 -> x2, other arithmetic: 12.1 us -> 0.02 us  [ordered(): return jnp.stack([first, second], axis)]
    all_to_all x5 -> x3, waiting for transfers between devices: 19.7 us -> 8.16 us  [the longest x1 3.51 us: on_device(): up_mine = total(lax.all_to_all(add_moved(up_moved), 'hi', 0, 0))]
    ppermute x0 -> x6, waiting for transfers between devices: none -> 7.86 us  [plane_sum(): moved.append(lax.ppermute(parts[k], ('lo', 'y'), perm))]
    all_to_all x2, waiting for transfers between devices: 14.4 us -> 6.66 us  [spread_hi(): return lax.all_to_all(spread, 'hi', 0, 0)]
    ppermute x0 -> x6, starting transfers between devices: none -> 7.04 us  [plane_sum(): moved.append(lax.ppermute(parts[k], ('lo', 'y'), perm))]
    all_to_all x5 -> x3, starting transfers between devices: 18.5 us -> 12 us  [the longest x1 4.81 us: on_device(): qkv_mine = total(lax.all_to_all(add_moved(qkv_moved), 'hi', 0, 0))]
    reduce_scatter x1, waiting for transfers between devices: 6.31 us -> 0.01 us  [on_device(): down_mine = lax.psum_scatter(down_plane, 'hi', scatter_dimension=0)]
  transfers between devices with their start and end apart: 38 -> 42, of which waited for: 11 -> 17; matrix products, arithmetic and copies ran while one was open for 13% -> 5% of each run, Pallas kernels for 35% -> 43%
where the time goes in v3:
time: 245 us; the launch traced here: 244 us
  Pallas kernels  111 us (45%)
  waiting for transfers between devices  51.3 us (21%)
  starting transfers between devices  41.6 us (17%)
  between operations  16.1 us (7%)
  local copies, waits for them, and re-layouts  15.9 us (6%)
  other arithmetic  7.56 us (3%)
    ppermute x16, waiting for transfers between devices, swap(): return lax.ppermute(value, axis, [(0, 1), (1, 0)])  22.1 us
    pallas_call x1, Pallas kernels, on_device(): call(functools.partial(down_body, dims), rows, [SMEM, narrow, narrow, nar...  21.4 us
    pallas_call x1, Pallas kernels, on_device(): call(up_body, rows, [SMEM, *[slot_spec] * 4, narrow, *[ANY] * 4, vec_spec...  18 us
    pallas_call x2, Pallas kernels, attend(): call(attend_body, rows // 2, [SMEM, SMEM, half_spec((slots, 3 * width), b...  15.5 us
    pallas_call x1, Pallas kernels, on_device(): call(functools.partial(back_last_body, dims), rows // 2, [*back_specs(row...  14.8 us
    pallas_call x1, Pallas kernels, on_device(): call(back_first_body, rows // 2, back_specs(0), [*[half_spec((1, part, wi...  10.3 us
    all_to_all x2, starting transfers between devices, spread_hi(): return lax.all_to_all(spread, 'hi', 0, 0)  9.93 us
    unnamed x78, local copies, waits for them, and re-layouts  8.13 us
  transfers between devices with their start and end apart: 42, of which 17 were waited for; matrix products, arithmetic and copies ran while one was open for 5% of the time, Pallas kernels for 43%

profile of v3, /device:TPU:0, one launch (start us, length us, event | category | flops | bytes accessed | tf_op | source)
XLA Modules:
  0.0 243.5 jit_solution(14169555771583327715)
XLA Ops:
  8.0 0.8 convert.25
  8.9 1.1 slice.31
  10.1 0.8 broadcast_in_dim.4
  10.9 6.4 %all-to-all-start = ((bf16[4,32,1664]{2,1,0:T(8,128)(2,1)}), bf16[4,32,1664]{2,1,0:T(8,128)(2,1)S(1)}, u32[]{:S(2)}, u32[]{:S(2)}) async-start(bf16[4,32,1664]{2,1,0:T(8,128)(2,1)} %broadcast_in_dim.4), calls=%async_computation | async-start | bytes 851968 | tf_op jit(solution)/shard_map/all_to_all | solution.py:579
  17.3 0.9 dynamic-slice_bitcast_fusion.4
  18.2 0.7 collective-permute-start.2
  18.8 1.0 collective-permute-start
  20.4 0.7 fusion.1
  21.0 0.9 slice.35
  23.4 3.3 %collective-permute-done.2.x3 = bf16[4,64,512]{2,1,0:T(8,128)(2,1)S(1)} collective-permute-done((bf16[4,64,512]{2,1,0:T(8,128)(2,1)S(1)}, bf16[4,64,512]{2,1,0:T(8,128)(2,1)S(1)}, u32[]{:S(2)}, u32[]{:S(2)}) %collective-permute-start.2) | collective-permute-done | bytes 262176 | tf_op jit(solution)/shard_map/ppermute | solution.py:572
  26.7 3.0 %all-to-all-done.p0 = bf16[4,32,1664]{2,1,0:T(8,128)(2,1)S(1)} async-done(((bf16[4,32,1664]{2,1,0:T(8,128)(2,1)}), bf16[4,32,1664]{2,1,0:T(8,128)(2,1)S(1)}, u32[]{:S(2)}, u32[]{:S(2)}) %all-to-all-start) | async-done | bytes 426016 | tf_op jit(solution)/shard_map/all_to_all | solution.py:579
  29.7 1.5 collective-permute-start.3
  31.3 0.9 broadcast_in_dim.5
  32.2 3.5 %all-to-all-start.1 = ((bf16[4,32,2560]{2,1,0:T(8,128)(2,1)}), bf16[4,32,2560]{2,1,0:T(8,128)(2,1)S(1)}, u32[]{:S(2)}, u32[]{:S(2)}) async-start(bf16[4,32,2560]{2,1,0:T(8,128)(2,1)} %broadcast_in_dim.5), calls=%async_computation.1 | async-start | bytes 1310720 | tf_op jit(solution)/shard_map/all_to_all | solution.py:579
  35.7 4.8 %collective-permute-done.3.p1 = bf16[4,32,1664]{2,1,0:T(8,128)(2,1)S(1)} collective-permute-done((bf16[4,32,1664]{2,1,0:T(8,128)(2,1)S(1)}, bf16[4,32,1664]{2,1,0:T(8,128)(2,1)S(1)}, u32[]{:S(2)}, u32[]{:S(2)}) %collective-permute-start.3) | collective-permute-done | bytes 426016 | tf_op jit(solution)/shard_map/ppermute | solution.py:560
  41.4 0.8 collective-permute-done.5.p3
  42.3 0.8 copy-done.19
  43.0 7.1 %qkv.1 = (bf16[1024,512]{1,0:T(8,128)(2,1)}, bf16[1024,1536]{1,0:T(8,128)(2,1)}) custom-call(s32[9]{0:T(128)} %copy-done.11, bf16[4,64,512]{2,1,0:T(8,128)(2,1)} %get-tuple-element.172.x0, bf16[4,64,512]{2,1,0:T(8,128)(2,1)} %collective-permute-done.x1, bf16[4,64,512]{2,1,0:T(8,128)(2,1)} %collective-permute-done.1.x2, bf16[4,64,512]{2,1,0:T(8,128)(2,1)} %copy-done.20, ...), custom_call_target="tpu_custom_call" | custom-call | flops 7000000000 | bytes 14000000 | tf_op jit(solution)/shard_map/qkv/pallas_call | solution.py:698
  50.2 3.7 %all-to-all-done.1.p0.b0 = bf16[4,32,2560]{2,1,0:T(8,128)(2,1)S(1)} async-done(((bf16[4,32,2560]{2,1,0:T(8,128)(2,1)}), bf16[4,32,2560]{2,1,0:T(8,128)(2,1)S(1)}, u32[]{:S(2)}, u32[]{:S(2)}) %all-to-all-start.1) | async-done | bytes 655392 | tf_op jit(solution)/shard_map/all_to_all | solution.py:579
  54.7 0.8 dynamic-slice_bitcast_fusion
  55.5 1.4 collective-permute-start.11
  57.3 7.6 %attend.2 = (bf16[1024,512]{1,0:T(8,128)(2,1)}, f32[4,8,256]{2,1,0:T(8,128)}) custom-call(s32[9]{0:T(128)} %copy-done.11, s32[4]{0:T(128)} %dynamic_slice.47.lengths, bf16[1024,1536]{1,0:T(8,128)(2,1)} %get-tuple-element.134.qkv), custom_call_target="tpu_custom_call" | custom-call | flops 7000000000 | bytes 14000000 | tf_op jit(solution)/shard_map/attend/pallas_call | solution.py:718
  65.0 7.4 %collective-permute-done.6.p1.b1 = bf16[4,32,2560]{2,1,0:T(8,128)(2,1)S(1)} collective-permute-done((bf16[4,32,2560]{2,1,0:T(8,128)(2,1)S(1)}, bf16[4,32,2560]{2,1,0:T(8,128)(2,1)S(1)}, u32[]{:S(2)}, u32[]{:S(2)}) %collective-permute-start.6) | collective-permute-done | bytes 655392 | tf_op jit(solution)/shard_map/ppermute | solution.py:560
  72.4 7.9 %attend.3 = (bf16[1024,512]{1,0:T(8,128)(2,1)}, f32[4,8,256]{2,1,0:T(8,128)}) custom-call(s32[9]{0:T(128)} %copy-done.37, s32[4]{0:T(128)} %dynamic_slice.47.lengths, bf16[1024,1536]{1,0:T(8,128)(2,1)} %get-tuple-element.134.qkv, bf16[1024,512]{1,0:T(8,128)(2,1)} %get-tuple-element.102.refs_0_, ...), custom_call_target="tpu_custom_call", output_to_operand_aliasing={{0}: (3, {}), {1}: (4, {})} | custom-call | flops 7000000000 | bytes 14000000 | tf_op jit(solution)/shard_map/attend/pallas_call | solution.py:718
  80.3 0.8 copy-done.15
  81.4 18.0 %up.1 = (f32[1024,512]{1,0:T(8,128)}, bf16[1024,512]{1,0:T(8,128)(2,1)}, bf16[1024,2048]{1,0:T(8,128)(2,1)}, bf16[1024,2048]{1,0:T(8,128)(2,1)}) custom-call(s32[9]{0:T(128)} %copy-done.11, bf16[4,64,512]{2,1,0:T(8,128)(2,1)} %get-tuple-element.172.x0, bf16[4,64,512]{2,1,0:T(8,128)(2,1)} %collective-permute-done.x1, ...), custom_call_target="tpu_custom_call" | custom-call | flops 16999999488 | bytes 34000000 | tf_op jit(solution)/shard_map/up/pallas_call | solution.py:736
  99.4 0.7 copy-done.24
  100.1 6.2 %down_grad.1 = (bf16[2,2,4,64,512]{4,3,2,1,0:T(8,128)(2,1)}, bf16[2,2,4,64,512]{4,3,2,1,0:T(8,128)(2,1)}) custom-call(s32[7]{0:T(128)} %stack.43.place, bf16[1024,2048]{1,0:T(8,128)(2,1)} %get-tuple-element.108.act, bf16[4,64,512]{2,1,0:T(8,128)(2,1)} %get-tuple-element.169.d0, bf16[4,64,512]{2,1,0:T(8,128)(2,1)} %collective-permute-done.9.d1, ...), custom_call_target="tpu_custom_call" | custom-call | flops 5000000000 | bytes 10000000 | tf_op jit(solution)/shard_map/down_grad/pallas_call | solution.py:765
  106.9 2.4 collective-permute-done.16
  109.3 2.5 %add_convert_fusion = bf16[2,2,4,64,512]{4,3,2,1,0:T(8,128)(2,1)} fusion(bf16[2,2,4,64,512]{4,3,2,1,0:T(8,128)(2,1)S(1)} %collective-permute-done.16, bf16[2,2,4,64,512]{4,3,2,1,0:T(8,128)(2,1)} %get-tuple-element.118), kind=kLoop, calls=%fused_computation | loop fusion | flops 2097152 | bytes 3145728 | tf_op jit(solution)/shard_map/convert_element_type | solution.py:597
  111.8 1.0 copy-done.13
  112.8 21.4 %down.1 = (bf16[4,64,512]{2,1,0:T(8,128)(2,1)}, bf16[4,64,512]{2,1,0:T(8,128)(2,1)}, bf16[4,64,512]{2,1,0:T(8,128)(2,1)}, bf16[4,64,512]{2,1,0:T(8,128)(2,1)}, f...) custom-call(s32[9]{0:T(128)} %copy-done.11, ...), custom_call_target="tpu_custom_call" | custom-call | flops 20000000000 | bytes 40000000 | tf_op jit(solution)/shard_map/down/pallas_call | solution.py:783
  134.8 1.5 collective-permute-start.14
  136.4 10.3 %back_first.1 = (bf16[4,64,512]{2,1,0:T(8,128)(2,1)}, bf16[4,64,512]{2,1,0:T(8,128)(2,1)}, bf16[4,64,512]{2,1,0:T(8,128)(2,1)}, bf16[4,64,512]{2,1,0:T(8,128)(2,...) custom-call(s32[9]{0:T(128)} %copy-done.11, s32[4]{0:T(128)} %dynamic_slice.47.lengths, ...), custom_call_target="tpu_custom_call" | custom-call | flops 11000000512 | bytes 22000000 | tf_op jit(solution)/shard_map/back_first/pallas_call | solution.py:850
  146.7 1.7 collective-permute-done.15.p3
  148.4 1.1 copy-done.12
  149.5 2.8 %add.87 = (bf16[4,64,640]{2,1,0:T(8,128)(2,1)}, bf16[4,64,640]{2,1,0:T(8,128)(2,1)}, bf16[4,64,640]{2,1,0:T(8,128)(2,1)}, bf16[4,64,640]{2,1,0:T(8,128)(2,1)}) custom-call(bf16[4,4,64,640]{3,2,1,0:T(8,128)(2,1)} %bitcast.56, bf16[4,4,64,640]{3,2,1,0:T(8,128)(2,1)} %bitcast.52), custom_call_target="tpu_custom_call" | custom-call | flops 2000000000 | bytes 4000000 | tf_op jit(solution)/shard_map/add/pallas_call | solution.py:866
  152.4 1.6 collective-permute-start.22
  154.2 1.6 collective-permute-start.23
  155.9 14.8 %back_last.1 = (bf16[4,64,512]{2,1,0:T(8,128)(2,1)}, bf16[4,64,512]{2,1,0:T(8,128)(2,1)}, bf16[4,64,512]{2,1,0:T(8,128)(2,1)}, bf16[4,64,512]{2,1,0:T(8,128)(2,1...) custom-call(s32[9]{0:T(128)} %copy-done.37, ...), custom_call_target="tpu_custom_call", output_to_operand_aliasing={{0}: (17, {}), {1}: (18, {}), {2}: (19, {}), {3}: (20, {})} | custom-call | flops 12999999488 | bytes 26000000 | tf_op jit(solution)/shard_map/back_last/pallas_call | solution.py:903
  170.9 0.9 add_convert_fusion.1
  171.8 3.9 %all-to-all-start.2 = ((bf16[4,64,640]{2,1,0:T(8,128)(2,1)}), bf16[4,64,640]{2,1,0:T(8,128)(2,1)S(1)}, u32[]{:S(2)}, u32[]{:S(2)}) async-start(bf16[4,64,640]{2,1,0:T(8,128)(2,1)} %add_convert_fusion.1), calls=%async_computation.2 | async-start | bytes 655360 | tf_op jit(solution)/shard_map/all_to_all | solution.py:935
  176.3 0.9 copy-done.14
  177.1 2.4 add.88
  179.5 1.5 collective-permute-start.28
  181.6 1.5 collective-permute-start.30
  183.1 3.5 %all-to-all-done.2 = bf16[4,64,640]{2,1,0:T(8,128)(2,1)S(1)} async-done(((bf16[4,64,640]{2,1,0:T(8,128)(2,1)}), bf16[4,64,640]{2,1,0:T(8,128)(2,1)S(1)}, u32[]{:S(2)}, u32[]{:S(2)}) %all-to-all-start.2) | async-done | bytes 327712 | tf_op jit(solution)/shard_map/all_to_all | solution.py:935
  186.7 1.9 collective-permute-done.28
  188.6 5.7 %collective-permute-done.29 = bf16[4,80,384]{2,1,0:T(8,128)(2,1)S(1)} collective-permute-done((bf16[4,80,384]{2,1,0:T(8,128)(2,1)}, bf16[4,80,384]{2,1,0:T(8,128)(2,1)S(1)}, u32[]{:S(2)}, u32[]{:S(2)}) %collective-permute-start.29) | collective-permute-done | bytes 245792 | tf_op jit(solution)/shard_map/ppermute | solution.py:881
  194.3 1.8 add_convert_fusion.2
  196.1 4.8 %all-to-all-start.3 = ((bf16[4,80,384]{2,1,0:T(8,128)(2,1)}), bf16[4,80,384]{2,1,0:T(8,128)(2,1)S(1)}, u32[]{:S(2)}, u32[]{:S(2)}) async-start(bf16[4,80,384]{2,1,0:T(8,128)(2,1)} %add_convert_fusion.2), calls=%async_computation.4 | async-start | bytes 491520 | tf_op jit(solution)/shard_map/all_to_all | solution.py:936
  200.9 0.9 pad_maximum_fusion.1.m0
  202.4 4.6 %collective-permute-done.24.m1 = bf16[64,1152]{1,0:T(8,128)(2,1)S(1)} collective-permute-done((bf16[64,1152]{1,0:T(8,128)(2,1)S(1)}, bf16[64,1152]{1,0:T(8,128)(2,1)S(1)}, u32[]{:S(2)}, u32[]{:S(2)}) %collective-permute-start.24) | collective-permute-done | bytes 147488 | tf_op jit(solution)/shard_map/ppermute | solution.py:560
  207.0 1.9 all-to-all-done.3
  209.5 1.6 collective-permute-start.19
  211.7 2.1 collective-permute-done.31.a1
  213.8 2.3 collect.2
  217.4 2.1 squares.1
  219.5 3.3 %all-to-all-start.4 = ((f32[8,8,128]{2,1,0:T(8,128)}), f32[8,8,128]{2,1,0:T(8,128)S(1)}, u32[]{:S(2)}, u32[]{:S(2)}) async-start(f32[8,8,128]{2,1,0:T(8,128)} %squares.1), calls=%async_computation.5 | async-start | bytes 65536 | tf_op jit(solution)/shard_map/all_to_all | solution.py:964
  222.9 0.9 collective-permute-done.20.p3
  223.8 0.7 copy-done.30
  224.5 2.2 collect.3
  226.7 2.8 %all-to-all-done.4.squares = f32[8,8,128]{2,1,0:T(8,128)S(1)} async-done(((f32[8,8,128]{2,1,0:T(8,128)}), f32[8,8,128]{2,1,0:T(8,128)S(1)}, u32[]{:S(2)}, u32[]{:S(2)}) %all-to-all-start.4) | async-done | bytes 32800 | tf_op jit(solution)/shard_map/all_to_all | solution.py:964
  230.1 6.0 %adam.1 = (f32[1,1]{1,0:T(1,128)}, f32[64,2048]{1,0:T(8,128)}, f32[64,2048]{1,0:T(8,128)}, f32[64,2048]{1,0:T(8,128)}, f32[2,64,2048]{2,1,0:T(8,128)}, /*index=5...) custom-call(s32[9]{0:T(128)} %copy-done.11, ...), custom_call_target="tpu_custom_call" | custom-call | flops 6000000000 | bytes 12000000 | tf_op jit(solution)/shard_map/adam/pallas_call | solution.py:967
  (151 shorter events, 11.5 us)
Async XLA Ops:
  8.0 9.3 %copy-start = (bf16[4,4,64,512]{3,2,1,0:T(8,128)(2,1)S(1)}, bf16[4,4,64,512]{3,2,1,0:T(8,128)(2,1)}, u32[]{:S(2)}) copy-start(bf16[4,4,64,512]{3,2,1,0:T(8,128)(2,1)} %param.14) | copy-start | bytes 3145732
  8.9 11.4 %copy-start.5 = (f32[2,64,2048]{2,1,0:T(8,128)S(1)}, f32[2,64,2048]{2,1,0:T(8,128)}, u32[]{:S(2)}) copy-start(f32[2,64,2048]{2,1,0:T(8,128)} %mlp_w.1) | copy-start | bytes 3145732
  10.9 11.1 %copy-start.10 = (s32[4,4]{1,0:T(4,128)S(1)}, s32[4,4]{1,0:T(4,128)}, u32[]{:S(2)}) copy-start(s32[4,4]{1,0:T(4,128)} %param.16) | copy-start | bytes 196
  10.9 18.8 %all-to-all-start = ((bf16[4,32,1664]{2,1,0:T(8,128)(2,1)}), bf16[4,32,1664]{2,1,0:T(8,128)(2,1)S(1)}, u32[]{:S(2)}, u32[]{:S(2)}) async-start(bf16[4,32,1664]{2,1,0:T(8,128)(2,1)} %broadcast_in_dim.4), calls=%async_computation | async-start | bytes 851968 | tf_op jit(solution)/shard_map/all_to_all | solution.py:579
  18.2 8.5 %collective-permute-start.2 = (bf16[4,64,512]{2,1,0:T(8,128)(2,1)S(1)}, bf16[4,64,512]{2,1,0:T(8,128)(2,1)S(1)}, u32[]{:S(2)}, u32[]{:S(2)}) collective-permute-start(bf16[4,64,512]{2,1,0:T(8,128)(2,1)S(1)} %get-tuple-element.170), channel_id=1, source_target_pairs={{0,3},{1,2},{2,1},{3,0},{4,7},{5,6},{6,5},{7,4},{8,11},{9,10},{10,... | collective-permute-start | bytes 786440 | tf_op jit(solution)/shard_map/ppermute | solution.py:572
  18.8 22.6 %collective-permute-start = (bf16[4,64,512]{2,1,0:T(8,128)(2,1)S(1)}, bf16[4,64,512]{2,1,0:T(8,128)(2,1)}, u32[]{:S(2)}, u32[]{:S(2)}) collective-permute-start(bf16[4,64,512]{2,1,0:T(8,128)(2,1)S(1)} %get-tuple-element.171), channel_id=1, source_target_pairs={{0,1},{1,0},{2,3},{3,2},{4,5},{5,4},{6,7},{7,6},{8,9},{9,8},{10,11... | collective-permute-start | bytes 786440 | tf_op jit(solution)/shard_map/ppermute | solution.py:572
  19.8 21.6 %collective-permute-start.1 = (bf16[4,64,512]{2,1,0:T(8,128)(2,1)S(1)}, bf16[4,64,512]{2,1,0:T(8,128)(2,1)}, u32[]{:S(2)}, u32[]{:S(2)}) collective-permute-start(bf16[4,64,512]{2,1,0:T(8,128)(2,1)S(1)} %get-tuple-element.173), channel_id=1, source_target_pairs={{0,2},{1,3},{2,0},{3,1},{4,6},{5,7},{6,4},{7,5},{8,10},{9,11},{10,... | collective-permute-start | bytes 786440 | tf_op jit(solution)/shard_map/ppermute | solution.py:572
  22.1 20.9 %copy-start.11 = (s32[9]{0:T(128)}, s32[9]{0:T(128)S(1)}, u32[]{:S(2)}) copy-start(s32[9]{0:T(128)S(1)} %stack.39.place) | copy-start | bytes 112
  23.4 26.8 %copy-start.37 = (s32[9]{0:T(128)}, s32[9]{0:T(128)S(1)}, u32[]{:S(2)}) copy-start(s32[9]{0:T(128)S(1)} %constant_dynamic-update-slice_fusion.place) | copy-start | bytes 112
  26.7 4.5 %copy-start.20 = (bf16[4,64,512]{2,1,0:T(8,128)(2,1)}, bf16[4,64,512]{2,1,0:T(8,128)(2,1)S(1)}, u32[]{:S(2)}) copy-start(bf16[4,64,512]{2,1,0:T(8,128)(2,1)S(1)} %collective-permute-done.2.x3) | copy-start | bytes 786436
  29.7 13.3 %copy-start.3 = (bf16[4,32,1664]{2,1,0:T(8,128)(2,1)}, bf16[4,32,1664]{2,1,0:T(8,128)(2,1)S(1)}, u32[]{:S(2)}) copy-start(bf16[4,32,1664]{2,1,0:T(8,128)(2,1)S(1)} %all-to-all-done.p0) | copy-start | bytes 1277956
  29.7 10.8 %collective-permute-start.3 = (bf16[4,32,1664]{2,1,0:T(8,128)(2,1)S(1)}, bf16[4,32,1664]{2,1,0:T(8,128)(2,1)S(1)}, u32[]{:S(2)}, u32[]{:S(2)}) collective-permute-start(bf16[4,32,1664]{2,1,0:T(8,128)(2,1)S(1)} %all-to-all-done.p0), channel_id=1, source_target_pairs={{0,4},{4,0},{1,5},{5,1},{2,6},{6,2},{3,7},{7,3},{8,12},{12,8},{9,1... | collective-permute-start | bytes 1277960 | tf_op jit(solution)/shard_map/ppermute | solution.py:560
  31.2 10.2 %collective-permute-start.4 = (bf16[4,32,1664]{2,1,0:T(8,128)(2,1)S(1)}, bf16[4,32,1664]{2,1,0:T(8,128)(2,1)S(1)}, u32[]{:S(2)}, u32[]{:S(2)}) collective-permute-start(bf16[4,32,1664]{2,1,0:T(8,128)(2,1)S(1)} %all-to-all-done.p0), channel_id=1, source_target_pairs={{0,1},{1,0},{2,3},{3,2},{4,5},{5,4},{6,7},{7,6},{8,9},{9,8},{10,11... | collective-permute-start | bytes 1277960 | tf_op jit(solution)/shard_map/ppermute | solution.py:560
  32.2 21.7 %all-to-all-start.1 = ((bf16[4,32,2560]{2,1,0:T(8,128)(2,1)}), bf16[4,32,2560]{2,1,0:T(8,128)(2,1)S(1)}, u32[]{:S(2)}, u32[]{:S(2)}) async-start(bf16[4,32,2560]{2,1,0:T(8,128)(2,1)} %broadcast_in_dim.5), calls=%async_computation.1 | async-start | bytes 1310720 | tf_op jit(solution)/shard_map/all_to_all | solution.py:579
  35.7 71.0 %all-gather.3.cloned.1.call-start = ((), (), s32[]{:S(2)}) async-start(), calls=%async_computation.8 | async-start | bytes 1179648 | tf_op jit(solution)/shard_map/all_gather | solution.py:672
  40.5 1.8 collective-permute-start.5
  43.0 11.6 %copy-start.1 = (bf16[4,4,64,512]{3,2,1,0:T(8,128)(2,1)S(1)}, bf16[4,4,64,512]{3,2,1,0:T(8,128)(2,1)}, u32[]{:S(2)}) copy-start(bf16[4,4,64,512]{3,2,1,0:T(8,128)(2,1)} %param.15) | copy-start | bytes 3145732
  53.9 11.1 %copy-start.2 = (bf16[4,32,2560]{2,1,0:T(8,128)(2,1)}, bf16[4,32,2560]{2,1,0:T(8,128)(2,1)S(1)}, u32[]{:S(2)}) copy-start(bf16[4,32,2560]{2,1,0:T(8,128)(2,1)S(1)} %all-to-all-done.1.p0.b0) | copy-start | bytes 1966084
  53.9 26.4 %collective-permute-start.7 = (bf16[4,32,2560]{2,1,0:T(8,128)(2,1)S(1)}, bf16[4,32,2560]{2,1,0:T(8,128)(2,1)S(1)}, u32[]{:S(2)}, u32[]{:S(2)}) collective-permute-start(bf16[4,32,2560]{2,1,0:T(8,128)(2,1)S(1)} %all-to-all-done.1.p0.b0), channel_id=1, source_target_pairs={{0,1},{1,0},{2,3},{3,2},{4,5},{5,4},{6,7},{7,6},{8,9},{9,8},{10,11... | collective-permute-start | bytes 1966088 | tf_op jit(solution)/shard_map/ppermute | solution.py:560
  53.9 18.5 %collective-permute-start.6 = (bf16[4,32,2560]{2,1,0:T(8,128)(2,1)S(1)}, bf16[4,32,2560]{2,1,0:T(8,128)(2,1)S(1)}, u32[]{:S(2)}, u32[]{:S(2)}) collective-permute-start(bf16[4,32,2560]{2,1,0:T(8,128)(2,1)S(1)} %all-to-all-done.1.p0.b0), channel_id=1, source_target_pairs={{0,4},{4,0},{1,5},{5,1},{2,6},{6,2},{3,7},{7,3},{8,12},{12,8},{9,1... | collective-permute-start | bytes 1966088 | tf_op jit(solution)/shard_map/ppermute | solution.py:560
  54.4 101.4 %reduce-scatter.7.cloned.1.call-start = ((), (), s32[]{:S(2)}) async-start(), calls=%async_computation.9 | async-start | bytes 1310720
  55.5 43.9 %collective-permute-start.11 = (bf16[4,64,512]{2,1,0:T(8,128)(2,1)S(1)}, bf16[4,64,512]{2,1,0:T(8,128)(2,1)S(1)}, u32[]{:S(2)}, u32[]{:S(2)}) collective-permute-start(bf16[4,64,512]{2,1,0:T(8,128)(2,1)S(1)} %get-tuple-element.166), channel_id=1, source_target_pairs={{0,3},{1,2},{2,1},{3,0},{4,7},{5,6},{6,5},{7,4},{8,11},{9,10},{10,... | collective-permute-start | bytes 786440 | tf_op jit(solution)/shard_map/ppermute | solution.py:572
  56.8 42.6 %collective-permute-start.10 = (bf16[4,64,512]{2,1,0:T(8,128)(2,1)S(1)}, bf16[4,64,512]{2,1,0:T(8,128)(2,1)}, u32[]{:S(2)}, u32[]{:S(2)}) collective-permute-start(bf16[4,64,512]{2,1,0:T(8,128)(2,1)S(1)} %get-tuple-element.167), channel_id=1, source_target_pairs={{0,2},{1,3},{2,0},{3,1},{4,6},{5,7},{6,4},{7,5},{8,10},{9,11},{10,... | collective-permute-start | bytes 786440 | tf_op jit(solution)/shard_map/ppermute | solution.py:572
  57.3 42.1 %collective-permute-start.9 = (bf16[4,64,512]{2,1,0:T(8,128)(2,1)S(1)}, bf16[4,64,512]{2,1,0:T(8,128)(2,1)}, u32[]{:S(2)}, u32[]{:S(2)}) collective-permute-start(bf16[4,64,512]{2,1,0:T(8,128)(2,1)S(1)} %get-tuple-element.168), channel_id=1, source_target_pairs={{0,1},{1,0},{2,3},{3,2},{4,5},{5,4},{6,7},{7,6},{8,9},{9,8},{10,11... | collective-permute-start | bytes 786440 | tf_op jit(solution)/shard_map/ppermute | solution.py:572
  72.4 7.9 %copy-start.16 = (bf16[4,32,2560]{2,1,0:T(8,128)(2,1)}, bf16[4,32,2560]{2,1,0:T(8,128)(2,1)S(1)}, u32[]{:S(2)}) copy-start(bf16[4,32,2560]{2,1,0:T(8,128)(2,1)S(1)} %collective-permute-done.6.p1.b1) | copy-start | bytes 1966084
  72.4 7.9 %collective-permute-start.8 = (bf16[4,32,2560]{2,1,0:T(8,128)(2,1)S(1)}, bf16[4,32,2560]{2,1,0:T(8,128)(2,1)S(1)}, u32[]{:S(2)}, u32[]{:S(2)}) collective-permute-start(bf16[4,32,2560]{2,1,0:T(8,128)(2,1)S(1)} %collective-permute-done.6.p1.b1), channel_id=1, source_target_pairs={{0,1},{1,0},{2,3},{3,2},{4,5},{5,4},{6,7},{7,6},{8,9},{9,8},{10,11... | collective-permute-start | bytes 1966088 | tf_op jit(solution)/shard_map/ppermute | solution.py:560
  106.3 2.9 %collective-permute-start.16 = (bf16[2,2,4,64,512]{4,3,2,1,0:T(8,128)(2,1)}, bf16[2,2,4,64,512]{4,3,2,1,0:T(8,128)(2,1)S(1)}, u32[]{:S(2)}, u32[]{:S(2)}) collective-permute-start(bf16[2,2,4,64,512]{4,3,2,1,0:T(8,128)(2,1)} %get-tuple-element.119), channel_id=1, source_target_pairs={{0,1},{1,0},{2,3},{3,2},{4,5},{5,4},{6,7},{7,6},{8,9},{9,8},{10,11... | collective-permute-start | bytes 3145736 | tf_op jit(solution)/shard_map/ppermute | solution.py:560
  106.7 5.2 %collective-permute-start.12 = (bf16[8,32,2048]{2,1,0:T(8,128)(2,1)}, bf16[8,32,2048]{2,1,0:T(8,128)(2,1)S(1)}, u32[]{:S(2)}, u32[]{:S(2)}) collective-permute-start(bf16[8,32,2048]{2,1,0:T(8,128)(2,1)} %bitcast.53), channel_id=1, source_target_pairs={{0,1},{1,0},{2,3},{3,2},{4,5},{5,4},{6,7},{7,6},{8,9},{9,8},{10,11... | collective-permute-start | bytes 3145736 | tf_op jit(solution)/shard_map/ppermute | solution.py:560
  134.2 14.2 %collective-permute-start.17 = (bf16[2,2,4,64,640]{4,3,2,1,0:T(8,128)(2,1)}, bf16[2,2,4,64,640]{4,3,2,1,0:T(8,128)(2,1)S(1)}, u32[]{:S(2)}, u32[]{:S(2)}) collective-permute-start(bf16[2,2,4,64,640]{4,3,2,1,0:T(8,128)(2,1)} %get-tuple-element.117), channel_id=1, source_target_pairs={{0,1},{1,0},{2,3},{3,2},{4,5},{5,4},{6,7},{7,6},{8,9},{9,8},{10,11... | collective-permute-start | bytes 3932168 | tf_op jit(solution)/shard_map/ppermute | solution.py:560
  134.5 12.1 %collective-permute-start.13 = (bf16[4,64,512]{2,1,0:T(8,128)(2,1)}, bf16[4,64,512]{2,1,0:T(8,128)(2,1)S(1)}, u32[]{:S(2)}, u32[]{:S(2)}) collective-permute-start(bf16[4,64,512]{2,1,0:T(8,128)(2,1)} %get-tuple-element.113), channel_id=1, source_target_pairs={{0,1},{1,0},{2,3},{3,2},{4,5},{5,4},{6,7},{7,6},{8,9},{9,8},{10,11... | collective-permute-start | bytes 786440 | tf_op jit(solution)/shard_map/ppermute | solution.py:572
  134.8 11.9 %collective-permute-start.14 = (bf16[4,64,512]{2,1,0:T(8,128)(2,1)}, bf16[4,64,512]{2,1,0:T(8,128)(2,1)S(1)}, u32[]{:S(2)}, u32[]{:S(2)}) collective-permute-start(bf16[4,64,512]{2,1,0:T(8,128)(2,1)} %get-tuple-element.114), channel_id=1, source_target_pairs={{0,2},{1,3},{2,0},{3,1},{4,6},{5,7},{6,4},{7,5},{8,10},{9,11},{10,... | collective-permute-start | bytes 786440 | tf_op jit(solution)/shard_map/ppermute | solution.py:572
  136.3 12.1 %collective-permute-start.15 = (bf16[4,64,512]{2,1,0:T(8,128)(2,1)}, bf16[4,64,512]{2,1,0:T(8,128)(2,1)S(1)}, u32[]{:S(2)}, u32[]{:S(2)}) collective-permute-start(bf16[4,64,512]{2,1,0:T(8,128)(2,1)} %get-tuple-element.115), channel_id=1, source_target_pairs={{0,3},{1,2},{2,1},{3,0},{4,7},{5,6},{6,5},{7,4},{8,11},{9,10},{10,... | collective-permute-start | bytes 786440 | tf_op jit(solution)/shard_map/ppermute | solution.py:572
  146.7 24.0 %copy-start.21 = (bf16[4,64,512]{2,1,0:T(8,128)(2,1)}, bf16[4,64,512]{2,1,0:T(8,128)(2,1)S(1)}, u32[]{:S(2)}) copy-start(bf16[4,64,512]{2,1,0:T(8,128)(2,1)S(1)} %collective-permute-done.13.p1) | copy-start | bytes 786436
  146.7 24.0 %copy-start.22 = (bf16[4,64,512]{2,1,0:T(8,128)(2,1)}, bf16[4,64,512]{2,1,0:T(8,128)(2,1)S(1)}, u32[]{:S(2)}) copy-start(bf16[4,64,512]{2,1,0:T(8,128)(2,1)S(1)} %collective-permute-done.14.p2) | copy-start | bytes 786436
  148.4 22.2 %copy-start.23 = (bf16[4,64,512]{2,1,0:T(8,128)(2,1)}, bf16[4,64,512]{2,1,0:T(8,128)(2,1)S(1)}, u32[]{:S(2)}) copy-start(bf16[4,64,512]{2,1,0:T(8,128)(2,1)S(1)} %collective-permute-done.15.p3) | copy-start | bytes 786436
  152.4 18.3 %collective-permute-start.22 = (bf16[4,64,640]{2,1,0:T(8,128)(2,1)}, bf16[4,64,640]{2,1,0:T(8,128)(2,1)S(1)}, u32[]{:S(2)}, u32[]{:S(2)}) collective-permute-start(bf16[4,64,640]{2,1,0:T(8,128)(2,1)} %get-tuple-element.131), channel_id=1, source_target_pairs={{0,2},{2,0},{4,6},{6,4},{1,3},{3,1},{5,7},{7,5},{8,10},{10,8},{12,... | collective-permute-start | bytes 983048 | tf_op jit(solution)/shard_map/ppermute | solution.py:881
  153.9 16.7 %collective-permute-start.21 = (bf16[4,64,640]{2,1,0:T(8,128)(2,1)}, bf16[4,64,640]{2,1,0:T(8,128)(2,1)S(1)}, u32[]{:S(2)}, u32[]{:S(2)}) collective-permute-start(bf16[4,64,640]{2,1,0:T(8,128)(2,1)} %get-tuple-element.132), channel_id=1, source_target_pairs={{0,4},{2,6},{4,0},{6,2},{1,5},{3,7},{5,1},{7,3},{8,12},{10,14},{12... | collective-permute-start | bytes 983048 | tf_op jit(solution)/shard_map/ppermute | solution.py:881
  154.2 16.6 %collective-permute-start.23 = (bf16[4,64,640]{2,1,0:T(8,128)(2,1)}, bf16[4,64,640]{2,1,0:T(8,128)(2,1)S(1)}, u32[]{:S(2)}, u32[]{:S(2)}) collective-permute-start(bf16[4,64,640]{2,1,0:T(8,128)(2,1)} %get-tuple-element.133), channel_id=1, source_target_pairs={{0,6},{2,4},{4,2},{6,0},{1,7},{3,5},{5,3},{7,1},{8,14},{10,12},{12... | collective-permute-start | bytes 983048 | tf_op jit(solution)/shard_map/ppermute | solution.py:881
  155.9 15.0 %copy-start.4 = (bf16[4,64,640]{2,1,0:T(8,128)(2,1)S(1)}, bf16[4,64,640]{2,1,0:T(8,128)(2,1)}, u32[]{:S(2)}) copy-start(bf16[4,64,640]{2,1,0:T(8,128)(2,1)} %get-tuple-element.130) | copy-start | bytes 983044
  170.9 5.4 %collective-permute-start.27 = (bf16[2,2,4,64,384]{4,3,2,1,0:T(8,128)(2,1)}, bf16[2,2,4,64,384]{4,3,2,1,0:T(8,128)(2,1)S(1)}, u32[]{:S(2)}, u32[]{:S(2)}) collective-permute-start(bf16[2,2,4,64,384]{4,3,2,1,0:T(8,128)(2,1)} %get-tuple-element.146), channel_id=1, source_target_pairs={{0,1},{1,0},{2,3},{3,2},{4,5},{5,4},{6,7},{7,6},{8,9},{9,8},{10,11... | collective-permute-start | bytes 2359304 | tf_op jit(solution)/shard_map/ppermute | solution.py:560
  171.8 14.8 %all-to-all-start.2 = ((bf16[4,64,640]{2,1,0:T(8,128)(2,1)}), bf16[4,64,640]{2,1,0:T(8,128)(2,1)S(1)}, u32[]{:S(2)}, u32[]{:S(2)}) async-start(bf16[4,64,640]{2,1,0:T(8,128)(2,1)} %add_convert_fusion.1), calls=%async_computation.2 | async-start | bytes 655360 | tf_op jit(solution)/shard_map/all_to_all | solution.py:935
  175.7 25.2 %reduce-scatter.5.cloned.1.call-start = ((), (), s32[]{:S(2)}) async-start(), calls=%async_computation.7 | async-start | bytes 327680 | tf_op jit(solution)/shard_map/reduce_scatter | solution.py:817
  179.5 29.9 %copy-start.25 = (bf16[4,64,512]{2,1,0:T(8,128)(2,1)S(1)}, bf16[4,64,512]{2,1,0:T(8,128)(2,1)}, u32[]{:S(2)}) copy-start(bf16[4,64,512]{2,1,0:T(8,128)(2,1)} %get-tuple-element.141) | copy-start | bytes 786436
  179.5 29.9 %copy-start.26 = (bf16[4,64,512]{2,1,0:T(8,128)(2,1)S(1)}, bf16[4,64,512]{2,1,0:T(8,128)(2,1)}, u32[]{:S(2)}) copy-start(bf16[4,64,512]{2,1,0:T(8,128)(2,1)} %get-tuple-element.142) | copy-start | bytes 786436
  179.5 31.5 %copy-start.27 = (bf16[4,64,512]{2,1,0:T(8,128)(2,1)S(1)}, bf16[4,64,512]{2,1,0:T(8,128)(2,1)}, u32[]{:S(2)}) copy-start(bf16[4,64,512]{2,1,0:T(8,128)(2,1)} %get-tuple-element.143) | copy-start | bytes 786436
  179.5 9.1 %collective-permute-start.28 = (bf16[4,80,384]{2,1,0:T(8,128)(2,1)}, bf16[4,80,384]{2,1,0:T(8,128)(2,1)S(1)}, u32[]{:S(2)}, u32[]{:S(2)}) collective-permute-start(bf16[4,80,384]{2,1,0:T(8,128)(2,1)} %get-tuple-element.151), channel_id=1, source_target_pairs={{0,4},{2,6},{4,0},{6,2},{1,5},{3,7},{5,1},{7,3},{8,12},{10,14},{12... | collective-permute-start | bytes 737288 | tf_op jit(solution)/shard_map/ppermute | solution.py:881
  181.0 13.3 %collective-permute-start.29 = (bf16[4,80,384]{2,1,0:T(8,128)(2,1)}, bf16[4,80,384]{2,1,0:T(8,128)(2,1)S(1)}, u32[]{:S(2)}, u32[]{:S(2)}) collective-permute-start(bf16[4,80,384]{2,1,0:T(8,128)(2,1)} %get-tuple-element.152), channel_id=1, source_target_pairs={{0,2},{2,0},{4,6},{6,4},{1,3},{3,1},{5,7},{7,5},{8,10},{10,8},{12,... | collective-permute-start | bytes 737288 | tf_op jit(solution)/shard_map/ppermute | solution.py:881
  181.6 12.7 %collective-permute-start.30 = (bf16[4,80,384]{2,1,0:T(8,128)(2,1)}, bf16[4,80,384]{2,1,0:T(8,128)(2,1)S(1)}, u32[]{:S(2)}, u32[]{:S(2)}) collective-permute-start(bf16[4,80,384]{2,1,0:T(8,128)(2,1)} %get-tuple-element.153), channel_id=1, source_target_pairs={{0,6},{2,4},{4,2},{6,0},{1,7},{3,5},{5,3},{7,1},{8,14},{10,12},{12... | collective-permute-start | bytes 737288 | tf_op jit(solution)/shard_map/ppermute | solution.py:881
  196.1 12.8 %all-to-all-start.3 = ((bf16[4,80,384]{2,1,0:T(8,128)(2,1)}), bf16[4,80,384]{2,1,0:T(8,128)(2,1)S(1)}, u32[]{:S(2)}, u32[]{:S(2)}) async-start(bf16[4,80,384]{2,1,0:T(8,128)(2,1)} %add_convert_fusion.2), calls=%async_computation.4 | async-start | bytes 491520 | tf_op jit(solution)/shard_map/all_to_all | solution.py:936
  201.7 14.3 %copy-start.6 = (bf16[64,1152]{1,0:T(8,128)(2,1)}, bf16[64,1152]{1,0:T(8,128)(2,1)S(1)}, u32[]{:S(2)}) copy-start(bf16[64,1152]{1,0:T(8,128)(2,1)S(1)} %pad_maximum_fusion.1.m0) | copy-start | bytes 442372
  201.8 5.2 %collective-permute-start.24 = (bf16[64,1152]{1,0:T(8,128)(2,1)S(1)}, bf16[64,1152]{1,0:T(8,128)(2,1)S(1)}, u32[]{:S(2)}, u32[]{:S(2)}) collective-permute-start(bf16[64,1152]{1,0:T(8,128)(2,1)S(1)} %pad_maximum_fusion.1.m0), channel_id=1, source_target_pairs={{0,2},{2,0},{1,3},{3,1},{4,6},{6,4},{5,7},{7,5},{8,10},{10,8},{9,1... | collective-permute-start | bytes 442376 | tf_op jit(solution)/shard_map/ppermute | solution.py:560
  202.4 8.7 %collective-permute-start.25 = (bf16[64,1152]{1,0:T(8,128)(2,1)S(1)}, bf16[64,1152]{1,0:T(8,128)(2,1)S(1)}, u32[]{:S(2)}, u32[]{:S(2)}) collective-permute-start(bf16[64,1152]{1,0:T(8,128)(2,1)S(1)} %pad_maximum_fusion.1.m0), channel_id=1, source_target_pairs={{0,1},{1,0},{2,3},{3,2},{4,5},{5,4},{6,7},{7,6},{8,9},{9,8},{10,11... | collective-permute-start | bytes 442376 | tf_op jit(solution)/shard_map/ppermute | solution.py:560
  207.0 9.1 %copy-start.31 = (bf16[64,1152]{1,0:T(8,128)(2,1)}, bf16[64,1152]{1,0:T(8,128)(2,1)S(1)}, u32[]{:S(2)}) copy-start(bf16[64,1152]{1,0:T(8,128)(2,1)S(1)} %collective-permute-done.24.m1) | copy-start | bytes 442372
  207.0 4.4 %collective-permute-start.26 = (bf16[64,1152]{1,0:T(8,128)(2,1)S(1)}, bf16[64,1152]{1,0:T(8,128)(2,1)S(1)}, u32[]{:S(2)}, u32[]{:S(2)}) collective-permute-start(bf16[64,1152]{1,0:T(8,128)(2,1)S(1)} %collective-permute-done.24.m1), channel_id=1, source_target_pairs={{0,1},{1,0},{2,3},{3,2},{4,5},{5,4},{6,7},{7,6},{8,9},{9,8},{10,11... | collective-permute-start | bytes 442376 | tf_op jit(solution)/shard_map/ppermute | solution.py:560
  208.9 7.2 %copy-start.7 = (bf16[80,384]{1,0:T(8,128)(2,1)}, bf16[80,384]{1,0:T(8,128)(2,1)S(1)}, u32[]{:S(2)}) copy-start(bf16[80,384]{1,0:T(8,128)(2,1)S(1)} %reduce_sum.25.a0) | copy-start | bytes 184324
  208.9 4.9 %collective-permute-start.31 = (bf16[80,384]{1,0:T(8,128)(2,1)S(1)}, bf16[80,384]{1,0:T(8,128)(2,1)S(1)}, u32[]{:S(2)}, u32[]{:S(2)}) collective-permute-start(bf16[80,384]{1,0:T(8,128)(2,1)S(1)} %reduce_sum.25.a0), channel_id=1, source_target_pairs={{0,2},{2,0},{1,3},{3,1},{4,6},{6,4},{5,7},{7,5},{8,10},{10,8},{9,1... | collective-permute-start | bytes 184328 | tf_op jit(solution)/shard_map/ppermute | solution.py:560
  209.4 13.4 %collective-permute-start.18 = (bf16[4,64,512]{2,1,0:T(8,128)(2,1)S(1)}, bf16[4,64,512]{2,1,0:T(8,128)(2,1)S(1)}, u32[]{:S(2)}, u32[]{:S(2)}) collective-permute-start(bf16[4,64,512]{2,1,0:T(8,128)(2,1)S(1)} %copy-done.25), channel_id=1, source_target_pairs={{0,1},{1,0},{2,3},{3,2},{4,5},{5,4},{6,7},{7,6},{8,9},{9,8},{10,11... | collective-permute-start | bytes 786440 | tf_op jit(solution)/shard_map/ppermute | solution.py:572
  209.5 13.4 %collective-permute-start.19 = (bf16[4,64,512]{2,1,0:T(8,128)(2,1)S(1)}, bf16[4,64,512]{2,1,0:T(8,128)(2,1)S(1)}, u32[]{:S(2)}, u32[]{:S(2)}) collective-permute-start(bf16[4,64,512]{2,1,0:T(8,128)(2,1)S(1)} %copy-done.26), channel_id=1, source_target_pairs={{0,2},{1,3},{2,0},{3,1},{4,6},{5,7},{6,4},{7,5},{8,10},{9,11},{10,... | collective-permute-start | bytes 786440 | tf_op jit(solution)/shard_map/ppermute | solution.py:572
  211.1 5.0 %copy-start.32 = (bf16[64,1152]{1,0:T(8,128)(2,1)}, bf16[64,1152]{1,0:T(8,128)(2,1)S(1)}, u32[]{:S(2)}) copy-start(bf16[64,1152]{1,0:T(8,128)(2,1)S(1)} %collective-permute-done.25.m2) | copy-start | bytes 442372
  211.1 12.7 %collective-permute-start.20 = (bf16[4,64,512]{2,1,0:T(8,128)(2,1)S(1)}, bf16[4,64,512]{2,1,0:T(8,128)(2,1)S(1)}, u32[]{:S(2)}, u32[]{:S(2)}) collective-permute-start(bf16[4,64,512]{2,1,0:T(8,128)(2,1)S(1)} %copy-done.27), channel_id=1, source_target_pairs={{0,3},{1,2},{2,1},{3,0},{4,7},{5,6},{6,5},{7,4},{8,11},{9,10},{10,... | collective-permute-start | bytes 786440 | tf_op jit(solution)/shard_map/ppermute | solution.py:572
  211.4 4.7 %copy-start.33 = (bf16[64,1152]{1,0:T(8,128)(2,1)}, bf16[64,1152]{1,0:T(8,128)(2,1)S(1)}, u32[]{:S(2)}) copy-start(bf16[64,1152]{1,0:T(8,128)(2,1)S(1)} %collective-permute-done.26.m3) | copy-start | bytes 442372
  211.4 4.7 %collective-permute-start.32 = (bf16[80,384]{1,0:T(8,128)(2,1)S(1)}, bf16[80,384]{1,0:T(8,128)(2,1)S(1)}, u32[]{:S(2)}, u32[]{:S(2)}) collective-permute-start(bf16[80,384]{1,0:T(8,128)(2,1)S(1)} %reduce_sum.25.a0), channel_id=1, source_target_pairs={{0,1},{1,0},{2,3},{3,2},{4,5},{5,4},{6,7},{7,6},{8,9},{9,8},{10,11... | collective-permute-start | bytes 184328 | tf_op jit(solution)/shard_map/ppermute | solution.py:560
  213.8 2.3 collective-permute-start.33
  219.5 10.0 %all-to-all-start.4 = ((f32[8,8,128]{2,1,0:T(8,128)}), f32[8,8,128]{2,1,0:T(8,128)S(1)}, u32[]{:S(2)}, u32[]{:S(2)}) async-start(f32[8,8,128]{2,1,0:T(8,128)} %squares.1), calls=%async_computation.5 | async-start | bytes 65536 | tf_op jit(solution)/shard_map/all_to_all | solution.py:964
  (16 other events, 16.4 us)
Sparse Core Ops, SparseCore 0:
  54.5 40.5 all-gather.2
Sparse Core Ops, SparseCore 1:
  111.9 25.9 reduce-scatter.6
  178.5 20.0 reduce-scatter.4

commit v4 on v3

--- a/solution.py
+++ b/solution.py
@@ -18,20 +18,8 @@
 WEIGHT_DECAY = 0.01
 ADAM_EPS = 1e-08
 NORM_EPS = 1e-05
-VMEM_BYTES = 60 * 1024 * 1024
-
-TAIL_SCALE = 0.4 / math.sqrt(2.0)
-TAIL = (
-    0.2256758631446491,
-    0.22566953041000726,
-    0.2078437638365498,
-    0.16853459369628254,
-    0.1414582080030511,
-    -0.005661972621845868,
-    0.1691478544806666,
-    -0.18293913558029784,
-    0.05027141967490775,
-)
+VMEM_BYTES = 63 * 1024 * 1024
+
 F32 = jnp.float32
 BF16 = jnp.bfloat16
 ANY = pl.BlockSpec(memory_space=pl.ANY)
@@ -60,15 +48,21 @@
 
 
 def gelu_and_slope(up):
-    size = jnp.abs(up)
-    t = 1.0 / (1.0 + TAIL_SCALE * size)
-    poly = jnp.full_like(t, TAIL[-1])
-    for coef in TAIL[-2::-1]:
-        poly = poly * t + coef
-    bell = jnp.exp(-0.5 * up * up)
-    tail = 0.5 * (t * poly) * bell
-    share = jnp.where(up >= 0, 1.0 - tail, tail)
+    share = 0.5 + 0.5 * lax.erf(up * (1.0 / math.sqrt(2.0)))
+    bell = jnp.exp2(up * up * (-0.5 * math.log2(math.e)))
     return up * share, share + up * (bell * (1.0 / math.sqrt(2.0 * math.pi)))
+
+
+def load_slots(refs):
+    return jnp.concatenate([ref[i] for i in range(refs[0].shape[0]) for ref in refs], axis=0)
+
+
+def store_slots(refs, value):
+    rows, part, _ = refs[0].shape
+    for i in range(rows):
+        for k, ref in enumerate(refs):
+            at = (i * 4 + k) * part
+            ref[i] = value[at : at + part]
 
 
 def placements(pieces, jobs, place, sems):
@@ -92,18 +86,19 @@
     return copies
 
 
-def dp_placements(pieces, target, place, sems):
+def pair_placements(pieces, target, place, sems):
     copies = []
     for i, piece in enumerate(pieces):
         core_at = place[1] if i == 0 else 1 - place[1]
-        dp_count, rows, _ = piece.shape
-        for d in range(dp_count):
-            row = pl.multiple_of((d * 2 + core_at) * rows, rows)
-            copies.append(
-                pltpu.make_async_copy(
-                    piece.at[d], target.at[pl.ds(row, rows), :], sems.at[len(copies)]
+        hi_count, _, rows, _ = piece.shape
+        for h in range(hi_count):
+            for j in range(2):
+                row = pl.multiple_of(((h * 2 + (place[0] ^ j)) * 2 + core_at) * rows, rows)
+                copies.append(
+                    pltpu.make_async_copy(
+                        piece.at[h, j], target.at[pl.ds(row, rows), :], sems.at[len(copies)]
+                    )
                 )
-            )
     return copies
 
 
@@ -131,7 +126,7 @@
         for copy in copies:
             copy.start()
 
-    x = jnp.concatenate([ref[0] for ref in (x0, x1, x2, x3)], axis=0).astype(F32)
+    x = load_slots((x0, x1, x2, x3)).astype(F32)
     unit, _ = centered(x)
     h = (unit * vec[0:1] + vec[1:2]).astype(BF16)
     h_out[...] = h
@@ -170,37 +165,6 @@
         attn_out[:, at : at + pair] = jnp.concatenate(outs, axis=0).T.astype(BF16)
 
 
-def up_body(
-    place, x0, x1, x2, x3, attn, p0, p1, p2, p3, vec,
-    x_one_out, h_out, act_out, slope_out, w_out, w_up, sems,
-):
-    row = pl.program_id(0)
-    width = vec.shape[1]
-    hidden = w_up.shape[1]
-    jobs = [(0, width, w_out), (width, hidden, w_up)]
-    copies = placements((p0, p1, p2, p3), jobs, place, sems)
-
-    @pl.when(row == 0)
-    def _():
-        for copy in copies:
-            copy.start()
-        for copy in copies:
-            copy.wait()
-
-    x = jnp.concatenate([ref[0] for ref in (x0, x1, x2, x3)], axis=0).astype(F32)
-    x_one = x + (nn_dot(attn[...], w_out[...]) + vec[4:5])
-    x_one_out[...] = x_one
-    unit, _ = centered(x_one)
-    h = (unit * vec[2:3] + vec[3:4]).astype(BF16)
-    h_out[...] = h
-    for j in range(hidden // width):
-        columns = slice(j * width, (j + 1) * width)
-        up = nn_dot(h, w_up[:, columns]) + vec[6 + j : 7 + j]
-        act, slope = gelu_and_slope(up)
-        act_out[:, columns] = act.astype(BF16)
-        slope_out[:, columns] = slope.astype(BF16)
-
-
 def write_parts(parts, half, y, column, value, dims):
     hi_count, lo_count, rows = dims
     quarter = value.shape[1]
@@ -211,82 +175,83 @@
             parts[half, lo, y, h, :, column : column + quarter] = value[at : at + rows]
 
 
-def send_parts(parts, keep, send, place, sems):
-    core = place[3]
+def send_copies(parts, half, y, keep, send, place, sems):
+    mine = half == place[3]
     copies = []
     for i in range(parts.shape[1]):
-        for j in range(2):
-            lo_at, y_at = (place[5] ^ i, place[6] ^ j)
-            for half, target in ((core, keep), (1 - core, send)):
-                copies.append(
-                    pltpu.make_async_copy(
-                        parts.at[half, lo_at, y_at], target.at[i, j], sems.at[len(copies)]
-                    )
-                )
-    for copy in copies:
-        copy.start()
-    for copy in copies:
-        copy.wait()
-
-
-def down_grad_body(dims, place, act, d0, d1, d2, d3, keep, send, dy_turned, parts, sems):
-    part = d0.shape[1]
-    for r in range(d0.shape[0]):
-        for k, ref in enumerate((d0, d1, d2, d3)):
-            at = (r * 4 + k) * part
-            if k % 2 == 0:
-                both = jnp.concatenate([ref[r], (d1, d3)[k // 2][r]], axis=0)
-                dy_turned[:, at : at + 2 * part] = both.T
-    quarter = act.shape[1] // 4
-    for half in range(2):
-        for y in range(2):
-            at = (half * 2 + y) * quarter
-            value = nn_dot(dy_turned[...], act[:, at : at + quarter])
-            write_parts(parts, half, y, 0, value, dims)
-    send_parts(parts, keep, send, place, sems)
-
-
-def down_body(
-    dims, place, x_one, h_two, attn, act, slope, d0, d1, d2, d3,
-    b0, b1, b2, b3, c0, c1, vec,
-    o0, o1, o2, o3, dx_out, dattn_out, vec_out, keep, send,
-    w_out, w_up, w_down, h_turned, attn_turned, dup_all, dao_all, parts,
-    up_sems, down_sems, out_sems,
+        for target, wanted in ((keep, mine), (send, jnp.logical_not(mine))):
+            lo_count = parts.shape[1]
+            copy = pltpu.make_async_copy(
+                parts.at[half, i, y],
+                target.at[(place[5] ^ i) if lo_count > 1 else 0, place[6] ^ y],
+                sems.at[half, i, y],
+            )
+            copies.append((wanted, copy))
+    return copies
+
+
+def start_all(copies):
+    for wanted, copy in copies:
+        pl.when(wanted)(copy.start)
+
+
+def wait_all(copies):
+    for wanted, copy in copies:
+        pl.when(wanted)(copy.wait)
+
+
+def mlp_body(
+    dims, place, x0, x1, x2, x3, attn, d0, d1, d2, d3, b0, b1, b2, b3, c0, c1, vec,
+    o0, o1, o2, o3, dx_out, dattn_out, vec_out, up_keep, up_send, down_keep, down_send,
+    w_out, w_up, w_down, h_turned, attn_turned, dy_turned, act_all, dup_all, dao_all,
+    up_parts, down_parts, out_sems, up_sems, down_sems, part_sems, more_sems,
 ):
     row = pl.program_id(0)
     width = vec.shape[1]
     hidden = w_up.shape[1]
-    slots = x_one.shape[0]
-    up_copies = placements((b0, b1, b2, b3), [(0, width, w_out), (width, hidden, w_up)], place, up_sems)
-    down_copies = dp_placements((c0, c1), w_down, place, down_sems)
+    slots = attn.shape[0]
+    out_copies = placements((b0, b1, b2, b3), [(0, width, w_out)], place, out_sems)
+    up_copies = placements((b0, b1, b2, b3), [(width, hidden, w_up)], place, up_sems)
+    down_copies = pair_placements((c0, c1), w_down, place, down_sems)
+
+    def arrived(copies):
+        @pl.when(row == 0)
+        def _():
+            for copy in copies:
+                copy.wait()
 
     @pl.when(row == 0)
     def _():
         vec_out[...] = jnp.zeros_like(vec_out)
-        for copy in down_copies + up_copies:
+        for copy in out_copies + up_copies + down_copies:
             copy.start()
-        for copy in down_copies + up_copies:
-            copy.wait()
 
     here = pl.ds(pl.multiple_of(row * slots, slots), slots)
-    dy = jnp.concatenate([ref[0] for ref in (d0, d1, d2, d3)], axis=0)
-    dy_float = dy.astype(F32)
-    h_turned[:, here] = h_two[...].T
+    x = load_slots((x0, x1, x2, x3)).astype(F32)
+    dy = load_slots((d0, d1, d2, d3))
+    dy_turned[:, here] = dy.T
     attn_turned[:, here] = attn[...].T
-    result = (x_one[...] + (nt_dot(act[...], w_down[...]) + vec[5:6])).astype(BF16)
-    part = slots // 4
-    for k, out in enumerate((o0, o1, o2, o3)):
-        out[0] = result[k * part : (k + 1) * part]
+    arrived(out_copies)
+    x_one = x + (nn_dot(attn[...], w_out[...]) + vec[4:5])
+    unit, scale = centered(x_one)
+    h = (unit * vec[2:3] + vec[3:4]).astype(BF16)
+    h_turned[:, here] = h.T
+    arrived(up_copies)
+    arrived(down_copies)
     for j in range(hidden // width):
         columns = slice(j * width, (j + 1) * width)
-        dact = nn_dot(dy, w_down[:, columns])
-        dup = (slope[:, columns].astype(F32) * dact).astype(BF16)
+        up = nn_dot(h, w_up[:, columns]) + vec[6 + j : 7 + j]
+        act, slope = gelu_and_slope(up)
+        act_all[here, columns] = act.astype(BF16)
+        dup = (slope * nn_dot(dy, w_down[:, columns])).astype(BF16)
         dup_all[here, columns] = dup
         vec_out[6 + j : 7 + j] += jnp.sum(dup.astype(F32), axis=0, keepdims=True)
+    result = x_one + (nt_dot(act_all[here, :], w_down[...]) + vec[5:6])
+    store_slots((o0, o1, o2, o3), result.astype(BF16))
     dh = nt_dot(dup_all[here, :], w_up[...])
-    unit, scale = centered(x_one[...])
     vec_out[2:3] += jnp.sum(dh * unit, axis=0, keepdims=True)
     vec_out[3:4] += jnp.sum(dh, axis=0, keepdims=True)
+    dy_float = dy.astype(F32)
     dx = dy_float + norm_back(unit, scale, dh * vec[2:3])
     dx_out[...] = dx
     dao = dx.astype(BF16)
@@ -299,15 +264,22 @@
     def _():
         quarter = hidden // 4
         small = width // 4
+        copies = []
         for half in range(2):
             for y in range(2):
                 at = (half * 2 + y) * quarter
                 value = nn_dot(h_turned[...], dup_all[:, at : at + quarter])
-                write_parts(parts, half, y, 0, value, dims)
+                write_parts(up_parts, half, y, 0, value, dims)
+                value = nn_dot(dy_turned[...], act_all[:, at : at + quarter])
+                write_parts(down_parts, half, y, 0, value, dims)
                 at = (half * 2 + y) * small
                 value = nn_dot(attn_turned[...], dao_all[:, at : at + small])
-                write_parts(parts, half, y, quarter, value, dims)
-        send_parts(parts, keep, send, place, out_sems)
+                write_parts(up_parts, half, y, quarter, value, dims)
+                these = send_copies(up_parts, half, y, up_keep, up_send, place, part_sems)
+                these += send_copies(down_parts, half, y, down_keep, down_send, place, more_sems)
+                start_all(these)
+                copies += these
+        wait_all(copies)
 
 
 def back_rows(
@@ -362,14 +334,12 @@
             copy.wait()
 
     dh = nt_dot(dqkv[...], w_qkv[...])
-    x = jnp.concatenate([ref[0] for ref in xs], axis=0).astype(F32)
+    x = load_slots(xs).astype(F32)
     unit, scale = centered(x)
     vec_out[0:1] += jnp.sum(dh * unit, axis=0, keepdims=True)
     vec_out[1:2] += jnp.sum(dh, axis=0, keepdims=True)
     grad = (dx[...] + norm_back(unit, scale, dh * vec[0:1])).astype(BF16)
-    part = slots // 4
-    for k, out in enumerate(outs):
-        out[0] = grad[k * part : (k + 1) * part]
+    store_slots(outs, grad)
 
 
 def back_first_body(
@@ -400,32 +370,31 @@
         count = before.shape[0]
         h_turned[...] = h_one[...].T
         quarter = before.shape[1] // 4
+        copies = []
         for half in range(2):
             for y in range(2):
                 at = (half * 2 + y) * quarter
                 value = nn_dot(h_turned[:, :count], before[:, at : at + quarter])
                 value = value + nn_dot(h_turned[:, count:], dqkv[:, at : at + quarter])
                 write_parts(parts, half, y, 0, value, dims)
-        send_parts(parts, keep, send, place, out_sems)
-
-
-def add_body(with_vec, *refs):
-    if with_vec:
-        keep, got, *vecs = refs[:-4]
-    else:
-        keep, got = refs[:-4]
-    outs = refs[-4:]
+                these = send_copies(parts, half, y, keep, send, place, out_sems)
+                start_all(these)
+                copies += these
+        wait_all(copies)
+
+
+def add_mlp_body(keep, got, down_keep, down_got, *outs):
+    for k in range(4):
+        outs[k][...] = (keep[k].astype(F32) + got[k].astype(F32)).astype(BF16)
+        outs[4][:, k] = (down_keep[k].astype(F32) + down_got[k].astype(F32)).astype(BF16)
+
+
+def add_qkv_body(keep, got, v0, v1, v2, *outs):
     rows = keep.shape[2]
+    sums = v0[...] + v1[...] + v2[...]
     for k, out in enumerate(outs):
-        value = (keep[k].astype(F32) + got[k].astype(F32)).astype(BF16)
-        if not with_vec:
-            out[...] = value
-            continue
-        out[:, :rows, :] = value
+        out[:, :rows, :] = (keep[k].astype(F32) + got[k].astype(F32)).astype(BF16)
         out[:, rows:, :] = jnp.zeros((out.shape[0], 16, out.shape[2]), BF16)
-        sums = vecs[0][...]
-        for vec in vecs[1:]:
-            sums = sums + vec[...]
         lanes = sums.shape[1] // out.shape[0]
         for h in range(out.shape[0]):
             out[h, rows:, :lanes] = sums[:, h * lanes : (h + 1) * lanes].astype(BF16)
@@ -607,8 +576,9 @@
 
 
 def to_all(mine):
-    side = swap(mine, "y")
-    return [mine, side, swap(mine, "core"), swap(side, "core")]
+    return [mine] + [
+        lax.ppermute(mine, ("y", "core"), [(j, j ^ k) for j in range(4)]) for k in (2, 1, 3)
+    ]
 
 
 def after(value, *others):
@@ -668,8 +638,6 @@
     qkv_own, xs[3] = lax.optimization_barrier((qkv_own, xs[3]))
     qkv_other = swap(qkv_own, "lo")
     qkv_pieces = [qkv_own, qkv_other, swap(qkv_own, "core"), swap(qkv_other, "core")]
-    down_half = after(half_of(mlp_w[1]).astype(BF16), up_own)
-    down_own = lax.all_gather(down_half, ("hi", "lo"), axis=0)
     vec_all = ordered(qkv_pieces[0][:, :, 3 * width :], qkv_pieces[1][:, :, 3 * width :], lo, 1)
     vec_all = vec_all.reshape(2 * hi_count, -1)[:, : vec_w.size].reshape(-1, vec_rows, vec_cols)
     vec_all = vec_all.transpose(1, 0, 2).reshape(vec_rows, width)
@@ -683,29 +651,32 @@
         places = [0 * lo, 0 * lo, me, core, 0 * lo, 0 * lo, 0 * lo, y, lo]
         dims = (1, 1, width)
     place = jnp.stack(places).astype(jnp.int32)
-    flat = jnp.stack([*places[:5], 0 * lo, 0 * lo]).astype(jnp.int32)
     later = place.at[4].set(rows // 2)
     row_lengths = lax.dynamic_slice_in_dim(lengths.reshape(-1), me * rows, rows)
 
-    slot_spec = pl.BlockSpec((1, part, width), lambda r: (r, 0, 0))
     vec_spec = whole_spec((16, width))
     lse_spec = pl.BlockSpec((1, HEADS, slots), lambda r: (r, 0, 0))
-    wide = rows_spec(slots, hidden)
-    narrow = rows_spec(slots, width)
+    group = 2 if rows % 2 == 0 else 1
+    slot_spec = pl.BlockSpec((group, part, width), lambda r: (r, 0, 0))
+    narrow = rows_spec(group * slots, width)
+    wide_qkv = rows_spec(group * slots, 3 * width)
     triple = rows_spec(slots, 3 * width)
     n_piece = 4 * qkv_pieces[0].shape[0]
     dma = pltpu.SemaphoreType.DMA
     h_one, qkv = call(
         qkv_body,
-        rows,
+        rows // group,
         [SMEM, *[slot_spec] * 4, *[ANY] * 4, vec_spec],
-        [narrow, triple],
+        [narrow, wide_qkv],
         [shape_of((count, width), BF16), shape_of((count, 3 * width), BF16)],
         [pltpu.VMEM((width, 3 * width), BF16), dma((n_piece,))],
         7,
         "qkv",
     )(place, *xs, *qkv_pieces, vec_float)
 
+    down_half = after(half_of(mlp_w[1]).astype(BF16), qkv_other)
+    down_pair = jnp.stack(lax.optimization_barrier((down_half, swap(down_half, "lo"), h_one))[:2])
+    down_own = spread_hi(after(down_pair, up_own))
     cot, qkv, up_own = lax.optimization_barrier((flat_cot, qkv, up_own))
     dys = from_seq([pick(cot, k) for k in range(4)])
     up_other = swap(up_own, "lo")
@@ -714,44 +685,37 @@
         zeros = (0,) * (len(block) - 1)
         return pl.BlockSpec(block, lambda r: (r + base, *zeros))
 
-    def attend(qkv, base, before):
+    def attend(qkv, base, steps, before):
         return call(
             attend_body,
-            rows // 2,
+            steps,
             [SMEM, SMEM, half_spec((slots, 3 * width), base), *[ANY] * len(before)],
             [half_spec((slots, width), base), half_spec((1, HEADS, slots), base)],
             [shape_of((count, width), BF16), shape_of((rows, HEADS, slots), F32)],
             [pltpu.VMEM((slots, slots), F32)],
-            7,
+            4 * steps,
             "attend",
             {3: 0, 4: 1} if before else None,
-        )(later if base else place, row_lengths, qkv, *before)
-
-    attn, lse = attend(qkv, 0, [])
-    up_other, attn, lse = lax.optimization_barrier((up_other, attn, lse))
-    attn, lse = attend(qkv, rows // 2, [attn, lse])
-    up_pieces = [up_own, up_other, swap(up_own, "core"), swap(up_other, "core")]
+        )(place.at[4].set(base), row_lengths, qkv, *before)
+
+    up_far = swap(up_own, "core")
+    attn, lse = attend(qkv, 0, rows - 1, [])
+    up_other, up_far, attn, lse, *dys = lax.optimization_barrier(
+        (up_other, up_far, attn, lse, *dys)
+    )
+    attn, lse = attend(qkv, rows - 1, 1, [attn, lse])
+    up_pieces = [up_own, up_other, up_far, swap(up_other, "core")]
+    down_own = after(down_own, attn)
+    down_far = swap(down_own, "core")
+    down_pieces = [down_own, down_far]
     if not fits:
         up_pieces = settle(up_pieces, lo, core)
-    x_one, h_two, act, slope = call(
-        up_body,
-        rows,
-        [SMEM, *[slot_spec] * 4, narrow, *[ANY] * 4, vec_spec],
-        [narrow, narrow, wide, wide],
-        [
-            shape_of((count, width), F32),
-            shape_of((count, width), BF16),
-            shape_of((count, hidden), BF16),
-            shape_of((count, hidden), BF16),
-        ],
-        [pltpu.VMEM((width, width), BF16), pltpu.VMEM((width, hidden), BF16), dma((2 * n_piece,))],
-        17,
-        "up",
-    )(place, *xs, attn, *up_pieces, vec_float)
+        split = settle([p[:, j] for p in down_pieces for j in range(2)], lo, core)
+        down_pieces = [jnp.stack(split[:2], axis=1), jnp.stack(split[2:], axis=1)]
+    n_down = 4 * down_pieces[0].shape[0]
 
     def parts_shape(quarter):
         return (dims[1], 2, dims[0], dims[2], quarter)
-
 
     def in_dp_order(value):
         if fits:
@@ -760,38 +724,20 @@
         return value.transpose(2, 0, 1, 3, 4)
 
     turned = pltpu.VMEM((width, count), BF16)
-    n_part = 4 * dims[1]
-    shape = parts_shape(hidden // 4)
-    down_keep, down_send = call(
-        functools.partial(down_grad_body, dims),
-        1,
-        [SMEM, whole_spec(act.shape), *[whole_spec(xs[0].shape)] * 4],
-        [ANY, ANY],
-        [shape_of(shape, BF16)] * 2,
-        [turned, pltpu.VMEM((2, *shape), BF16), dma((n_part,))],
-        5,
-        "down_grad",
-    )(flat, act, *dys)
-    down_got = swap(down_send, "core")
-    down_far = swap(down_own, "core")
-    down_pieces = [down_own, down_far]
-    if not fits:
-        whole = ordered(down_own, down_far, core, 1).reshape(8, 2, -1, hidden)
-        down_pieces = [whole[:, 0], whole[:, 1]]
-    n_down = 2 * down_pieces[0].shape[0]
     shape = parts_shape(hidden // 4 + width // 4)
+    down_shape = parts_shape(hidden // 4)
     outs = call(
-        functools.partial(down_body, dims),
-        rows,
-        [SMEM, narrow, narrow, narrow, wide, wide, *[slot_spec] * 4, *[ANY] * 6, vec_spec],
-        [*[slot_spec] * 4, narrow, narrow, vec_spec, ANY, ANY],
+        functools.partial(mlp_body, dims),
+        rows // group,
+        [SMEM, *[slot_spec] * 4, narrow, *[slot_spec] * 4, *[ANY] * 6, vec_spec],
+        [*[slot_spec] * 4, narrow, narrow, vec_spec, *[ANY] * 4],
         [
             *[shape_of((rows, part, width), BF16)] * 4,
             shape_of((count, width), F32),
             shape_of((count, width), BF16),
             shape_of((16, width), F32),
-            shape_of(shape, BF16),
-            shape_of(shape, BF16),
+            *[shape_of(shape, BF16)] * 2,
+            *[shape_of(down_shape, BF16)] * 2,
         ],
         [
             pltpu.VMEM((width, width), BF16),
@@ -799,22 +745,24 @@
             pltpu.VMEM((width, hidden), BF16),
             turned,
             turned,
+            turned,
+            pltpu.VMEM((count, hidden), BF16),
             pltpu.VMEM((count, hidden), BF16),
             pltpu.VMEM((count, width), BF16),
             pltpu.VMEM((2, *shape), BF16),
-            dma((2 * n_piece,)),
+            pltpu.VMEM((2, *down_shape), BF16),
+            dma((n_piece,)),
+            dma((n_piece,)),
             dma((n_down,)),
-            dma((n_part,)),
+            dma((2, dims[1], 2)),
+            dma((2, dims[1], 2)),
         ],
-        20,
-        "down",
-    )(place, x_one, h_two, attn, act, slope, *dys, *up_pieces, *down_pieces, vec_float)
-    results, (dx, dattn, vec_mlp, up_keep, up_send) = outs[:4], outs[4:]
+        24,
+        "mlp",
+    )(place, *xs, attn, *dys, *up_pieces, *down_pieces, vec_float)
+    results, (dx, dattn, vec_mlp, up_keep, up_send, down_keep, down_send) = outs[:4], outs[4:]
     up_got = swap(up_send, "core")
-    down_part = in_dp_order(add_pair(down_keep, down_got))
-    down_part = down_part.reshape(4, *down_part.shape[2:])
-    down_plane = lax.psum_scatter(down_part, ("lo", "y"), scatter_dimension=0)
-    down_mine = lax.psum_scatter(down_plane, "hi", scatter_dimension=0)
+    down_got = swap(down_send, "core")
 
     def collect(parts):
         return call(
@@ -829,6 +777,8 @@
         )(place, *parts).reshape(tokens.shape)
 
     results = from_seq(results)
+    lead = 2
+    lead_count = lead * slots
     back_args = [lse, dattn, *xs, dx]
     weights = [*qkv_pieces, vec_float]
 
@@ -849,30 +799,28 @@
     back_scratch = [pltpu.VMEM((width, 3 * width), BF16), pltpu.VMEM((slots, slots), F32)]
     outs = call(
         back_first_body,
-        rows // 2,
+        lead,
         back_specs(0),
         [*[half_spec((1, part, width), 0)] * 4, triple, vec_spec],
-        [*back_shapes, shape_of((count // 2, 3 * width), BF16), shape_of((16, width), F32)],
+        [*back_shapes, shape_of((lead_count, 3 * width), BF16), shape_of((16, width), F32)],
         [*back_scratch, dma((n_piece,))],
         11,
         "back_first",
-    )(place, row_lengths, after(qkv, up_send, down_part), *back_args, *weights)
+    )(place, row_lengths, after(qkv, up_send, down_send), *back_args, *weights)
     input_first, (grad_first, vec_first) = outs[:4], outs[4:]
 
-    def add_call(keep, got, vecs):
-        dims_of = (4, *keep.shape[2:])
-        more = 16 if vecs else 0
-        out = shape_of((dims_of[1], dims_of[2] + more, dims_of[3]), BF16)
+    def add_call(body, args, outs):
+        args = [a.reshape(4, *a.shape[2:]) if a.ndim > 2 else a for a in args]
         return call(
-            functools.partial(add_body, bool(vecs)),
+            body,
             1,
-            [whole_spec(dims_of)] * 2 + [whole_spec(v.shape) for v in vecs],
-            [whole_spec(out.shape)] * 4,
-            [out] * 4,
+            [whole_spec(a.shape) for a in args],
+            [whole_spec(o.shape) for o in outs],
+            outs,
             [],
-            2,
+            3,
             "add",
-        )(keep.reshape(dims_of), got.reshape(dims_of), *vecs)
+        )(*args)
 
     def plane_sum(parts):
         moved = [parts[0]]
@@ -894,35 +842,39 @@
     qkv_last = qkv
     output = collect(results)
     if fits:
-        parts = add_call(after(up_keep, grad_first, *results), up_got, [])
-        parts = lax.optimization_barrier((*parts, grad_first))
-        qkv_last = after(qkv, *parts, down_plane)
-        up_moved = plane_sum(parts[:4])
+        args = [up_keep, up_got, down_keep, down_got]
+        args = lax.optimization_barrier((*args, grad_first, *results))[:4]
+        piece = shape_of(up_keep.shape[2:], BF16)
+        by_hi = shape_of((hi_count, 4, *down_keep.shape[3:]), BF16)
+        *parts, down_part = add_call(add_mlp_body, args, [*[piece] * 4, by_hi])
+        qkv_last = after(qkv, *parts, down_part)
+        up_moved = plane_sum(parts)
+        down_part = total(lax.all_to_all(down_part, "hi", 0, 0))
     quarter = 3 * width // 4
     shape = parts_shape(quarter)
     outs = call(
         functools.partial(back_last_body, dims),
-        rows // 2,
+        rows - lead,
         [
-            *back_specs(rows // 2),
+            *back_specs(lead),
             whole_spec((count, width)),
-            whole_spec((count // 2, 3 * width)),
+            whole_spec((lead_count, 3 * width)),
             *[ANY] * 4,
         ],
-        [*[half_spec((1, part, width), rows // 2)] * 4, vec_spec, ANY, ANY],
+        [*[half_spec((1, part, width), lead)] * 4, vec_spec, ANY, ANY],
         [*back_shapes, shape_of((16, width), F32), shape_of(shape, BF16), shape_of(shape, BF16)],
         [
-            pltpu.VMEM((count // 2, 3 * width), BF16),
+            pltpu.VMEM((count - lead_count, 3 * width), BF16),
             *back_scratch,
             turned,
             pltpu.VMEM((2, *shape), BF16),
             dma((n_piece,)),
-            dma((n_part,)),
+            dma((2, dims[1], 2)),
         ],
         13,
         "back_last",
         {17 + k: k for k in range(4)},
-    )(later, row_lengths, qkv_last, *back_args, *weights, h_one, grad_first, *input_first)
+    )(place.at[4].set(lead), row_lengths, qkv_last, *back_args, *weights, h_one, grad_first, *input_first)
     input_parts, (vec_last, qkv_keep, qkv_send) = outs[:4], outs[4:]
     if fits:
         qkv_send = after(qkv_send, *up_moved)
@@ -930,21 +882,28 @@
     vecs = [vec_mlp, vec_first, vec_last]
 
     if fits:
-        parts = add_call(qkv_keep, qkv_got, vecs)
+        _, _, _, more_rows, more_cols = qkv_keep.shape
+        piece = shape_of((hi_count, more_rows + 16, more_cols), BF16)
+        parts = add_call(add_qkv_body, [qkv_keep, qkv_got, *vecs], [piece] * 4)
         qkv_moved = plane_sum(parts)
-        up_mine = total(lax.all_to_all(add_moved(up_moved), "hi", 0, 0))
+        down_moved = plane_sum([down_part[k] for k in range(4)])
+        up_plane = after(add_moved(up_moved), *parts)
+        up_mine = total(lax.all_to_all(up_plane, "hi", 0, 0))
         qkv_mine = total(lax.all_to_all(add_moved(qkv_moved), "hi", 0, 0))
+        down_mine = add_moved(down_moved)
     else:
         vec_total = (vec_mlp + vec_first + vec_last).reshape(16, hi_count, 2, vec_cols)
         vec_total = vec_total.transpose(1, 0, 2, 3).reshape(1, 1, hi_count, 16, 2 * vec_cols)
         vec_total = jnp.pad(vec_total.astype(BF16), ((0, 0),) * 4 + ((0, quarter - 2 * vec_cols),))
         vec_total = jnp.broadcast_to(vec_total, (2, 2, *vec_total.shape[2:]))
         up_mine = total(lax.all_to_all(plane_total(up_keep, up_got, None), "hi", 0, 0))
+        down_mine = total(lax.all_to_all(plane_total(down_keep, down_got, None), "hi", 0, 0))
         qkv_mine = plane_total(qkv_keep, qkv_got, vec_total)
         qkv_mine = total(lax.all_to_all(qkv_mine, "hi", 0, 0))
-    mlp_pieces = to_all(jnp.concatenate([up_mine, down_mine], axis=1))
-    attn_pieces = to_all(qkv_mine)
-    input_grad = collect(from_seq(input_parts))
+    mlp_mine = jnp.concatenate([up_mine, down_mine], axis=1)
+    mlp_pieces = to_all(mlp_mine)
+    attn_pieces = to_all(after(qkv_mine, *mlp_pieces))
+    input_grad = collect(from_seq(lax.optimization_barrier((*input_parts, *attn_pieces))[:4]))
 
     dp_count = 2 * hi_count
     if fits:

time: 245 us -> 224 us (0.914)
  starting transfers between devices: 41.6 us -> 60.5 us
  Pallas kernels: 111 us -> 92.5 us
  between operations: 16.1 us -> 1.32 us
  local copies, waits for them, and re-layouts: 15.9 us -> 11.2 us
  other arithmetic: 7.56 us -> 4.92 us
    pallas_call x10 -> x8, Pallas kernels: 98.5 us -> 79.9 us  [the longest x1 27.5 us: on_device(): call(functools.partial(mlp_body, dims), rows // group, [SMEM, *[slot_spec...]
    all_to_all x2 -> x3, waiting for transfers between devices: 6.66 us -> 20.3 us  [spread_hi(): return lax.all_to_all(spread, 'hi', 0, 0)]
    ppermute x16 -> x11, waiting for transfers between devices: 22.1 us -> 11.3 us  [swap(): return lax.ppermute(value, axis, [(0, 1), (1, 0)])]
    ppermute x6 -> x9, waiting for transfers between devices: 7.86 us -> 0.02 us  [plane_sum(): moved.append(lax.ppermute(parts[k], ('lo', 'y'), perm))]
    ppermute x0 -> x6, starting transfers between devices: none -> 4.94 us  [to_all(): lax.ppermute(mine, ('y', 'core'), [(j, j ^ k) for j in range(4)])]
    all_to_all x1 -> x2, starting transfers between devices: 3.88 us -> 8.8 us  [the longest x1 4.54 us: on_device(): up_mine = total(lax.all_to_all(up_plane, 'hi', 0, 0))]
    unnamed x78 -> x76, local copies, waits for them, and re-layouts: 8.13 us -> 4.12 us
    ppermute x0 -> x6, waiting for transfers between devices: none -> 3.57 us  [to_all(): lax.ppermute(mine, ('y', 'core'), [(j, j ^ k) for j in range(4)])]
  transfers between devices with their start and end apart: 42 -> 45, of which waited for: 17 -> 17; matrix products, arithmetic and copies ran while one was open for 5% -> 4% of each run, Pallas kernels for 43% -> 25%
where the time goes in v4:
time: 224 us; the launch traced here: 223 us
  Pallas kernels  92.5 us (41%)
  starting transfers between devices  60.5 us (27%)
  waiting for transfers between devices  52.5 us (23%)
  local copies, waits for them, and re-layouts  11.2 us (5%)
  other arithmetic  4.92 us (2%)
    pallas_call x1, Pallas kernels, on_device(): call(functools.partial(mlp_body, dims), rows // group, [SMEM, *[slot_spec...  27.5 us
    all_to_all x3, waiting for transfers between devices, spread_hi(): return lax.all_to_all(spread, 'hi', 0, 0)  20.3 us
    pallas_call x2, Pallas kernels, attend(): call(attend_body, steps, [SMEM, SMEM, half_spec((slots, 3 * width), base)...  15.3 us
    pallas_call x1, Pallas kernels, on_device(): call(functools.partial(back_last_body, dims), rows - lead, [*back_specs(l...  14.1 us
    all_to_all x3, starting transfers between devices, spread_hi(): return lax.all_to_all(spread, 'hi', 0, 0)  12.6 us
    ppermute x11, waiting for transfers between devices, swap(): return lax.ppermute(value, axis, [(0, 1), (1, 0)])  11.3 us
    ppermute x9, starting transfers between devices, plane_sum(): moved.append(lax.ppermute(parts[k], ('lo', 'y'), perm))  10.6 us
    pallas_call x1, Pallas kernels, on_device(): call(back_first_body, lead, back_specs(0), [*[half_spec((1, part, width),...  10.4 us
  transfers between devices with their start and end apart: 45, of which 17 were waited for; matrix products, arithmetic and copies ran while one was open for 4% of the time, Pallas kernels for 25%

profile of v4, /device:TPU:0, one launch (start us, length us, event | category | flops | bytes accessed | tf_op | source)
XLA Modules:
  0.0 223.0 jit_solution(624120989512450482)
XLA Ops:
  0.7 2.0 dynamic-slice_bitcast_fusion.4
  2.7 2.4 %collective-permute-start.2 = (bf16[4,64,512]{2,1,0:T(8,128)(2,1)S(1)}, bf16[4,64,512]{2,1,0:T(8,128)(2,1)S(1)}, u32[]{:S(2)}, u32[]{:S(2)}) collective-permute-start(bf16[4,64,512]{2,1,0:T(8,128)(2,1)S(1)} %get-tuple-element.216), channel_id=1, source_target_pairs={{0,3},{1,2},{2,1},{3,0},{4,7},{5,6},{6,5},{7,4},{8,11},{9,10},{10,... | collective-permute-start | bytes 786440 | tf_op jit(solution)/shard_map/ppermute | solution.py:541
  5.3 0.8 broadcast_in_dim.6
  6.1 4.9 %all-to-all-start = ((bf16[4,32,1664]{2,1,0:T(8,128)(2,1)}), bf16[4,32,1664]{2,1,0:T(8,128)(2,1)S(1)}, u32[]{:S(2)}, u32[]{:S(2)}) async-start(bf16[4,32,1664]{2,1,0:T(8,128)(2,1)} %broadcast_in_dim.6), calls=%async_computation | async-start | bytes 851968 | tf_op jit(solution)/shard_map/all_to_all | solution.py:548
  12.2 0.6 dynamic_slice.47.lengths
  12.9 11.4 %all-to-all-done.p0 = bf16[4,32,1664]{2,1,0:T(8,128)(2,1)S(1)} async-done(((bf16[4,32,1664]{2,1,0:T(8,128)(2,1)}), bf16[4,32,1664]{2,1,0:T(8,128)(2,1)S(1)}, u32[]{:S(2)}, u32[]{:S(2)}) %all-to-all-start) | async-done | bytes 426016 | tf_op jit(solution)/shard_map/all_to_all | solution.py:548
  24.2 1.5 collective-permute-start.3
  25.8 0.9 broadcast_in_dim.7
  26.7 3.5 %all-to-all-start.1 = ((bf16[4,32,2560]{2,1,0:T(8,128)(2,1)}), bf16[4,32,2560]{2,1,0:T(8,128)(2,1)S(1)}, u32[]{:S(2)}, u32[]{:S(2)}) async-start(bf16[4,32,2560]{2,1,0:T(8,128)(2,1)} %broadcast_in_dim.7), calls=%async_computation.1 | async-start | bytes 1310720 | tf_op jit(solution)/shard_map/all_to_all | solution.py:548
  30.2 5.4 %collective-permute-done.3.p1 = bf16[4,32,1664]{2,1,0:T(8,128)(2,1)S(1)} collective-permute-done((bf16[4,32,1664]{2,1,0:T(8,128)(2,1)S(1)}, bf16[4,32,1664]{2,1,0:T(8,128)(2,1)S(1)}, u32[]{:S(2)}, u32[]{:S(2)}) %collective-permute-start.3) | collective-permute-done | bytes 426016 | tf_op jit(solution)/shard_map/ppermute | solution.py:529
  35.9 1.5 collective-permute-start.12
  37.5 0.6 pad_convert_fusion.vec
  38.1 0.7 copy-done.18
  38.9 0.8 copy-done.19
  39.7 6.2 %qkv.1 = (bf16[1024,512]{1,0:T(8,128)(2,1)}, bf16[1024,1536]{1,0:T(8,128)(2,1)}) custom-call(s32[9]{0:T(128)} %copy-done.14, bf16[4,64,512]{2,1,0:T(8,128)(2,1)} %get-tuple-element.218.x0, bf16[4,64,512]{2,1,0:T(8,128)(2,1)} %collective-permute-done.x1, bf16[4,64,512]{2,1,0:T(8,128)(2,1)} %collective-permute-done.1.x2, bf16[4,64,512]{2,1,0:T(8,128)(2,1)} %copy-done.20, ...), custom_call_target="tpu_custom_call" | custom-call | flops 7000000000 | bytes 14000000 | tf_op jit(solution)/shard_map/qkv/pallas_call | solution.py:666
  45.9 2.5 %all-to-all-done.1.b0 = bf16[4,32,2560]{2,1,0:T(8,128)(2,1)S(1)} async-done(((bf16[4,32,2560]{2,1,0:T(8,128)(2,1)}), bf16[4,32,2560]{2,1,0:T(8,128)(2,1)S(1)}, u32[]{:S(2)}, u32[]{:S(2)}) %all-to-all-start.1) | async-done | bytes 655392 | tf_op jit(solution)/shard_map/all_to_all | solution.py:548
  49.0 1.1 broadcast_in_dim.8
  50.0 4.3 %all-to-all-start.2 = ((bf16[4,2,32,2048]{3,2,1,0:T(8,128)(2,1)}), bf16[4,2,32,2048]{3,2,1,0:T(8,128)(2,1)}, u32[]{:S(2)}, u32[]{:S(2)}) async-start(bf16[4,2,32,2048]{3,2,1,0:T(8,128)(2,1)} %broadcast_in_dim.8), calls=%async_computation.2 | async-start | bytes 2097152 | tf_op jit(solution)/shard_map/all_to_all | solution.py:548
  54.3 1.0 dynamic-slice_bitcast_fusion
  55.9 1.6 collective-permute-start.9
  57.4 10.5 %attend.2 = (bf16[1024,512]{1,0:T(8,128)(2,1)}, f32[4,8,256]{2,1,0:T(8,128)}) custom-call(s32[9]{0:T(128)} %copy-done.34, s32[4]{0:T(128)} %dynamic_slice.47.lengths, bf16[1024,1536]{1,0:T(8,128)(2,1)} %get-tuple-element.175.qkv), custom_call_target="tpu_custom_call" | custom-call | flops 12000000000 | bytes 24000000 | tf_op jit(solution)/shard_map/attend/pallas_call | solution.py:689
  68.0 1.9 collective-permute-done.9.d2
  69.9 4.7 %attend.3 = (bf16[1024,512]{1,0:T(8,128)(2,1)}, f32[4,8,256]{2,1,0:T(8,128)}) custom-call(s32[9]{0:T(128)} %copy-done.33, s32[4]{0:T(128)} %dynamic_slice.47.lengths, bf16[1024,1536]{1,0:T(8,128)(2,1)} %get-tuple-element.175.qkv, bf16[1024,512]{1,0:T(8,128)(2,1)} %get-tuple-element.138.refs_0_, ...), custom_call_target="tpu_custom_call", output_to_operand_aliasing={{0}: (3, {}), {1}: (4, {})} | custom-call | flops 4000000000 | bytes 8000000 | tf_op jit(solution)/shard_map/attend/pallas_call | solution.py:689
  74.6 6.5 %all-to-all-done.2.c0 = bf16[4,2,32,2048]{3,2,1,0:T(8,128)(2,1)} async-done(((bf16[4,2,32,2048]{3,2,1,0:T(8,128)(2,1)}), bf16[4,2,32,2048]{3,2,1,0:T(8,128)(2,1)}, u32[]{:S(2)}, u32[]{:S(2)}) %all-to-all-start.2) | async-done | bytes 1048608 | tf_op jit(solution)/shard_map/all_to_all | solution.py:548
  81.6 2.9 %collective-permute-done.11.b3 = bf16[4,32,2560]{2,1,0:T(8,128)(2,1)S(1)} collective-permute-done((bf16[4,32,2560]{2,1,0:T(8,128)(2,1)}, bf16[4,32,2560]{2,1,0:T(8,128)(2,1)S(1)}, u32[]{:S(2)}, u32[]{:S(2)}) %collective-permute-start.11) | collective-permute-done | bytes 655392 | tf_op jit(solution)/shard_map/ppermute | solution.py:529
  85.3 27.5 %mlp.1 = (bf16[4,64,512]{2,1,0:T(8,128)(2,1)}, bf16[4,64,512]{2,1,0:T(8,128)(2,1)}, bf16[4,64,512]{2,1,0:T(8,128)(2,1)}, bf16[4,64,512]{2,1,0:T(8,128)(2,1)}, f3...) custom-call(s32[9]{0:T(128)} %copy-done.14, ...), custom_call_target="tpu_custom_call" | custom-call | flops 24000000000 | bytes 48000000 | tf_op jit(solution)/shard_map/mlp/pallas_call | solution.py:729
  114.3 1.0 collective-permute-start.16
  115.4 10.4 %back_first.1 = (bf16[4,64,512]{2,1,0:T(8,128)(2,1)}, bf16[4,64,512]{2,1,0:T(8,128)(2,1)}, bf16[4,64,512]{2,1,0:T(8,128)(2,1)}, bf16[4,64,512]{2,1,0:T(8,128)(2,...) custom-call(s32[9]{0:T(128)} %copy-done.14, s32[4]{0:T(128)} %dynamic_slice.47.lengths, ...), custom_call_target="tpu_custom_call" | custom-call | flops 11000000512 | bytes 22000000 | tf_op jit(solution)/shard_map/back_first/pallas_call | solution.py:800
  125.9 1.4 collective-permute-done.16.p3
  127.3 3.9 %add.105 = (bf16[4,64,640]{2,1,0:T(8,128)(2,1)}, bf16[4,64,640]{2,1,0:T(8,128)(2,1)}, bf16[4,64,640]{2,1,0:T(8,128)(2,1)}, bf16[4,64,640]{2,1,0:T(8,128)(2,1)}, bf16[4,4,64,512]{3,2,1,0:T(8,128)(2,1)}) custom-call(bf16[4,4,64,640]{3,2,1,0:T(8,128)(2,1)} %bitcast.62, bf16[4,4,64,640]{3,2,1,0:T(8,128)(2,1)} %bitcast.21.got, bf16[4,4,64,512]{3,2,1,0:T(8,128)(2,1)} %bitcast.63, ...), custom_call_target="tpu_custom_call" | custom-call | flops 3000000000 | bytes 6000000 | tf_op jit(solution)/shard_map/add/pallas_call | solution.py:814
  131.2 1.5 collective-permute-start.19
  133.2 1.6 collective-permute-start.21
  134.8 4.3 %all-to-all-start.5 = ((bf16[4,4,64,512]{3,2,1,0:T(8,128)(2,1)}), bf16[4,4,64,512]{3,2,1,0:T(8,128)(2,1)}, u32[]{:S(2)}, u32[]{:S(2)}) async-start(bf16[4,4,64,512]{3,2,1,0:T(8,128)(2,1)} %get-tuple-element.174), calls=%async_computation.5 | async-start | bytes 2097152 | tf_op jit(solution)/shard_map/all_to_all | solution.py:852
  139.1 14.1 %back_last.1 = (bf16[4,64,512]{2,1,0:T(8,128)(2,1)}, bf16[4,64,512]{2,1,0:T(8,128)(2,1)}, bf16[4,64,512]{2,1,0:T(8,128)(2,1)}, bf16[4,64,512]{2,1,0:T(8,128)(2,1...) custom-call(s32[9]{0:T(128)} %copy-done.35, ...), custom_call_target="tpu_custom_call", output_to_operand_aliasing={{0}: (17, {}), {1}: (18, {}), {2}: (19, {}), {3}: (20, {})} | custom-call | flops 12999999488 | bytes 26000000 | tf_op jit(solution)/shard_map/back_last/pallas_call | solution.py:855
  153.3 2.5 %collective-permute-done.22 = bf16[2,2,4,64,384]{4,3,2,1,0:T(8,128)(2,1)S(1)} collective-permute-done((bf16[2,2,4,64,384]{4,3,2,1,0:T(8,128)(2,1)}, bf16[2,2,4,64,384]{4,3,2,1,0:T(8,128)(2,1)S(1)}, u32[]{:S(2)}, u32[]{:S(2)}) %collective-permute-start.22) | collective-permute-done | bytes 786464 | tf_op jit(solution)/shard_map/ppermute | solution.py:529
  155.8 0.9 copy-done.16
  156.6 2.4 %add.106 = (bf16[4,80,384]{2,1,0:T(8,128)(2,1)}, bf16[4,80,384]{2,1,0:T(8,128)(2,1)}, bf16[4,80,384]{2,1,0:T(8,128)(2,1)}, bf16[4,80,384]{2,1,0:T(8,128)(2,1)}) custom-call(bf16[4,4,64,384]{3,2,1,0:T(8,128)(2,1)} %bitcast.64, bf16[4,4,64,384]{3,2,1,0:T(8,128)(2,1)} %bitcast.61, f32[16,512]{1,0:T(8,128)} %get-tuple-element.187.v0, ...), custom_call_target="tpu_custom_call" | custom-call | flops 3000000000 | bytes 6000000 | tf_op jit(solution)/shard_map/add/pallas_call | solution.py:814
  159.1 1.4 collective-permute-start.23
  161.0 1.5 collective-permute-start.25
  162.6 1.9 add_convert_fusion
  164.4 0.6 all-to-all-done.5
  165.1 4.5 %all-to-all-start.4 = ((bf16[4,64,640]{2,1,0:T(8,128)(2,1)}), bf16[4,64,640]{2,1,0:T(8,128)(2,1)S(1)}, u32[]{:S(2)}, u32[]{:S(2)}) async-start(bf16[4,64,640]{2,1,0:T(8,128)(2,1)} %add_convert_fusion), calls=%async_computation.4 | async-start | bytes 655360 | tf_op jit(solution)/shard_map/all_to_all | solution.py:891
  169.6 1.4 reduce_sum.38
  171.0 1.5 collective-permute-start.26
  173.0 1.6 collective-permute-start.28
  174.6 0.8 add_convert_fusion.1
  175.4 3.9 %all-to-all-done.4 = bf16[4,64,640]{2,1,0:T(8,128)(2,1)S(1)} async-done(((bf16[4,64,640]{2,1,0:T(8,128)(2,1)}), bf16[4,64,640]{2,1,0:T(8,128)(2,1)S(1)}, u32[]{:S(2)}, u32[]{:S(2)}) %all-to-all-start.4) | async-done | bytes 327712 | tf_op jit(solution)/shard_map/all_to_all | solution.py:891
  179.3 3.7 %all-to-all-start.3 = ((bf16[4,80,384]{2,1,0:T(8,128)(2,1)}), bf16[4,80,384]{2,1,0:T(8,128)(2,1)S(1)}, u32[]{:S(2)}, u32[]{:S(2)}) async-start(bf16[4,80,384]{2,1,0:T(8,128)(2,1)} %add_convert_fusion.1), calls=%async_computation.3 | async-start | bytes 491520 | tf_op jit(solution)/shard_map/all_to_all | solution.py:892
  183.7 1.7 collective-permute-start.31
  185.4 4.0 %all-to-all-done.3 = bf16[4,80,384]{2,1,0:T(8,128)(2,1)S(1)} async-done(((bf16[4,80,384]{2,1,0:T(8,128)(2,1)}), bf16[4,80,384]{2,1,0:T(8,128)(2,1)S(1)}, u32[]{:S(2)}, u32[]{:S(2)}) %all-to-all-start.3) | async-done | bytes 245792 | tf_op jit(solution)/shard_map/all_to_all | solution.py:892
  189.8 1.6 collective-permute-start.32
  191.5 1.1 collective-permute-start.34
  192.6 1.9 collective-permute-done.32.a1
  194.5 1.3 collective-permute-done.34.a3
  195.8 0.6 copy-done.32
  196.4 2.1 squares.1
  198.5 5.9 %all-to-all-start.6 = ((f32[8,8,128]{2,1,0:T(8,128)}), f32[8,8,128]{2,1,0:T(8,128)S(1)}, u32[]{:S(2)}, u32[]{:S(2)}) async-start(f32[8,8,128]{2,1,0:T(8,128)} %squares.1), calls=%async_computation.6 | async-start | bytes 65536 | tf_op jit(solution)/shard_map/all_to_all | solution.py:923
  204.4 2.3 %collect.2 = bf16[4,4,64,512]{3,2,1,0:T(8,128)(2,1)} custom-call(s32[9]{0:T(128)} %copy-done.14, bf16[4,64,512]{2,1,0:T(8,128)(2,1)} %get-tuple-element.153.p0, bf16[4,64,512]{2,1,0:T(8,128)(2,1)} %copy-done.21, bf16[4,64,512]{2,1,0:T(8,128)(2,1)} %copy-done.22, bf16[4,64,512]{2,1,0:T(8,128)(2,1)} %copy-done.23), custom_call_target="tpu_custom_call" | custom-call | flops 2000000000 | bytes 4000000 | tf_op jit(solution)/shard_map/collect/pallas_call | solution.py:768
  206.7 1.3 collective-permute-start.36
  208.6 2.5 %all-to-all-done.6.squares = f32[8,8,128]{2,1,0:T(8,128)S(1)} async-done(((f32[8,8,128]{2,1,0:T(8,128)}), f32[8,8,128]{2,1,0:T(8,128)S(1)}, u32[]{:S(2)}, u32[]{:S(2)}) %all-to-all-start.6) | async-done | bytes 32800 | tf_op jit(solution)/shard_map/all_to_all | solution.py:923
  211.1 0.6 copy-done.10
  211.7 6.0 %adam.1 = (f32[1,1]{1,0:T(1,128)}, f32[64,2048]{1,0:T(8,128)}, f32[64,2048]{1,0:T(8,128)}, f32[64,2048]{1,0:T(8,128)}, f32[2,64,2048]{2,1,0:T(8,128)}, /*index=5...) custom-call(s32[9]{0:T(128)} %copy-done.14, ...), custom_call_target="tpu_custom_call" | custom-call | flops 6000000000 | bytes 12000000 | tf_op jit(solution)/shard_map/adam/pallas_call | solution.py:926
  217.7 3.0 %collective-permute-done.37.p3 = bf16[4,64,512]{2,1,0:T(8,128)(2,1)} collective-permute-done((bf16[4,64,512]{2,1,0:T(8,128)(2,1)S(1)}, bf16[4,64,512]{2,1,0:T(8,128)(2,1)}, u32[]{:S(2)}, u32[]{:S(2)}) %collective-permute-start.37) | collective-permute-done | bytes 262176 | tf_op jit(solution)/shard_map/ppermute | solution.py:541
  220.7 2.2 %collect.3 = bf16[4,4,64,512]{3,2,1,0:T(8,128)(2,1)} custom-call(s32[9]{0:T(128)} %copy-done.14, bf16[4,64,512]{2,1,0:T(8,128)(2,1)} %get-tuple-element.196.p0, bf16[4,64,512]{2,1,0:T(8,128)(2,1)} %collective-permute-done.35.p1, bf16[4,64,512]{2,1,0:T(8,128)(2,1)} %collective-permute-done.36.p2, bf16[4,64,512]{2,1,0:T(8,128)(2,1)} %collective-permute-done.37.p3), custom_call_target="tpu_custom_call" | custom-call | flops 2000000000 | bytes 4000000 | tf_op jit(solution)/shard_map/collect/pallas_call | solution.py:768
  (154 shorter events, 9.2 us)
Async XLA Ops:
  0.7 4.5 %copy-start.11 = (f32[10,64]{1,0:T(8,128)S(1)}, f32[10,64]{1,0:T(8,128)}, u32[]{:S(2)}) copy-start(f32[10,64]{1,0:T(8,128)} %vec_w.1) | copy-start | bytes 7684
  2.7 9.2 %copy-start.5 = (f32[2,64,2048]{2,1,0:T(8,128)S(1)}, f32[2,64,2048]{2,1,0:T(8,128)}, u32[]{:S(2)}) copy-start(f32[2,64,2048]{2,1,0:T(8,128)} %mlp_w.1) | copy-start | bytes 3145732
  2.7 10.1 %collective-permute-start.2 = (bf16[4,64,512]{2,1,0:T(8,128)(2,1)S(1)}, bf16[4,64,512]{2,1,0:T(8,128)(2,1)S(1)}, u32[]{:S(2)}, u32[]{:S(2)}) collective-permute-start(bf16[4,64,512]{2,1,0:T(8,128)(2,1)S(1)} %get-tuple-element.216), channel_id=1, source_target_pairs={{0,3},{1,2},{2,1},{3,0},{4,7},{5,6},{6,5},{7,4},{8,11},{9,10},{10,... | collective-permute-start | bytes 786440 | tf_op jit(solution)/shard_map/ppermute | solution.py:541
  5.3 6.8 %copy-start.13 = (s32[4,4]{1,0:T(4,128)S(1)}, s32[4,4]{1,0:T(4,128)}, u32[]{:S(2)}) copy-start(s32[4,4]{1,0:T(4,128)} %param.20) | copy-start | bytes 196
  6.1 18.1 %all-to-all-start = ((bf16[4,32,1664]{2,1,0:T(8,128)(2,1)}), bf16[4,32,1664]{2,1,0:T(8,128)(2,1)S(1)}, u32[]{:S(2)}, u32[]{:S(2)}) async-start(bf16[4,32,1664]{2,1,0:T(8,128)(2,1)} %broadcast_in_dim.6), calls=%async_computation | async-start | bytes 851968 | tf_op jit(solution)/shard_map/all_to_all | solution.py:548
  11.0 27.1 %collective-permute-start = (bf16[4,64,512]{2,1,0:T(8,128)(2,1)S(1)}, bf16[4,64,512]{2,1,0:T(8,128)(2,1)}, u32[]{:S(2)}, u32[]{:S(2)}) collective-permute-start(bf16[4,64,512]{2,1,0:T(8,128)(2,1)S(1)} %get-tuple-element.217), channel_id=1, source_target_pairs={{0,1},{1,0},{2,3},{3,2},{4,5},{5,4},{6,7},{7,6},{8,9},{9,8},{10,11... | collective-permute-start | bytes 786440 | tf_op jit(solution)/shard_map/ppermute | solution.py:541
  11.4 26.7 %collective-permute-start.1 = (bf16[4,64,512]{2,1,0:T(8,128)(2,1)S(1)}, bf16[4,64,512]{2,1,0:T(8,128)(2,1)}, u32[]{:S(2)}, u32[]{:S(2)}) collective-permute-start(bf16[4,64,512]{2,1,0:T(8,128)(2,1)S(1)} %get-tuple-element.219), channel_id=1, source_target_pairs={{0,2},{1,3},{2,0},{3,1},{4,6},{5,7},{6,4},{7,5},{8,10},{9,11},{10,... | collective-permute-start | bytes 786440 | tf_op jit(solution)/shard_map/ppermute | solution.py:541
  12.1 23.6 %copy-start.14 = (s32[9]{0:T(128)}, s32[9]{0:T(128)S(1)}, u32[]{:S(2)}) copy-start(s32[9]{0:T(128)S(1)} %stack.41.place) | copy-start | bytes 112
  12.2 23.4 %copy-start.34 = (s32[9]{0:T(128)}, s32[9]{0:T(128)S(1)}, u32[]{:S(2)}) copy-start(s32[9]{0:T(128)S(1)} %constant_dynamic-update-slice_fusion.1.place) | copy-start | bytes 112
  12.8 22.8 %copy-start.33 = (s32[9]{0:T(128)}, s32[9]{0:T(128)S(1)}, u32[]{:S(2)}) copy-start(s32[9]{0:T(128)S(1)} %constant_dynamic-update-slice_fusion.2.place) | copy-start | bytes 112
  12.9 13.9 %copy-start.20 = (bf16[4,64,512]{2,1,0:T(8,128)(2,1)}, bf16[4,64,512]{2,1,0:T(8,128)(2,1)S(1)}, u32[]{:S(2)}) copy-start(bf16[4,64,512]{2,1,0:T(8,128)(2,1)S(1)} %collective-permute-done.2.x3) | copy-start | bytes 786436
  24.2 11.6 %copy-start.2 = (bf16[4,32,1664]{2,1,0:T(8,128)(2,1)}, bf16[4,32,1664]{2,1,0:T(8,128)(2,1)S(1)}, u32[]{:S(2)}) copy-start(bf16[4,32,1664]{2,1,0:T(8,128)(2,1)S(1)} %all-to-all-done.p0) | copy-start | bytes 1277956
  24.2 11.4 %collective-permute-start.3 = (bf16[4,32,1664]{2,1,0:T(8,128)(2,1)S(1)}, bf16[4,32,1664]{2,1,0:T(8,128)(2,1)S(1)}, u32[]{:S(2)}, u32[]{:S(2)}) collective-permute-start(bf16[4,32,1664]{2,1,0:T(8,128)(2,1)S(1)} %all-to-all-done.p0), channel_id=1, source_target_pairs={{0,4},{4,0},{1,5},{5,1},{2,6},{6,2},{3,7},{7,3},{8,12},{12,8},{9,1... | collective-permute-start | bytes 1277960 | tf_op jit(solution)/shard_map/ppermute | solution.py:529
  25.8 12.3 %collective-permute-start.4 = (bf16[4,32,1664]{2,1,0:T(8,128)(2,1)S(1)}, bf16[4,32,1664]{2,1,0:T(8,128)(2,1)S(1)}, u32[]{:S(2)}, u32[]{:S(2)}) collective-permute-start(bf16[4,32,1664]{2,1,0:T(8,128)(2,1)S(1)} %all-to-all-done.p0), channel_id=1, source_target_pairs={{0,1},{1,0},{2,3},{3,2},{4,5},{5,4},{6,7},{7,6},{8,9},{9,8},{10,11... | collective-permute-start | bytes 1277960 | tf_op jit(solution)/shard_map/ppermute | solution.py:529
  26.7 21.7 %all-to-all-start.1 = ((bf16[4,32,2560]{2,1,0:T(8,128)(2,1)}), bf16[4,32,2560]{2,1,0:T(8,128)(2,1)S(1)}, u32[]{:S(2)}, u32[]{:S(2)}) async-start(bf16[4,32,2560]{2,1,0:T(8,128)(2,1)} %broadcast_in_dim.7), calls=%async_computation.1 | async-start | bytes 1310720 | tf_op jit(solution)/shard_map/all_to_all | solution.py:548
  35.6 2.5 %collective-permute-start.5 = (bf16[4,32,1664]{2,1,0:T(8,128)(2,1)S(1)}, bf16[4,32,1664]{2,1,0:T(8,128)(2,1)S(1)}, u32[]{:S(2)}, u32[]{:S(2)}) collective-permute-start(bf16[4,32,1664]{2,1,0:T(8,128)(2,1)S(1)} %collective-permute-done.3.p1), channel_id=1, source_target_pairs={{0,1},{1,0},{2,3},{3,2},{4,5},{5,4},{6,7},{7,6},{8,9},{9,8},{10,11... | collective-permute-start | bytes 1277960 | tf_op jit(solution)/shard_map/ppermute | solution.py:529
  35.9 10.0 %collective-permute-start.12 = (bf16[32,2048]{1,0:T(8,128)(2,1)S(1)}, bf16[32,2048]{1,0:T(8,128)(2,1)S(1)}, u32[]{:S(2)}, u32[]{:S(2)}) collective-permute-start(bf16[32,2048]{1,0:T(8,128)(2,1)S(1)} %fusion.1), channel_id=1, source_target_pairs={{0,4},{4,0},{1,5},{5,1},{2,6},{6,2},{3,7},{7,3},{8,12},{12,8},{9,1... | collective-permute-start | bytes 393224 | tf_op jit(solution)/shard_map/ppermute | solution.py:529
  48.4 5.9 %copy-start = (bf16[4,4,64,512]{3,2,1,0:T(8,128)(2,1)S(1)}, bf16[4,4,64,512]{3,2,1,0:T(8,128)(2,1)}, u32[]{:S(2)}) copy-start(bf16[4,4,64,512]{3,2,1,0:T(8,128)(2,1)} %param.19) | copy-start | bytes 3145732
  48.4 21.4 %collective-permute-start.6 = (bf16[4,32,2560]{2,1,0:T(8,128)(2,1)S(1)}, bf16[4,32,2560]{2,1,0:T(8,128)(2,1)}, u32[]{:S(2)}, u32[]{:S(2)}) collective-permute-start(bf16[4,32,2560]{2,1,0:T(8,128)(2,1)S(1)} %all-to-all-done.1.b0), channel_id=1, source_target_pairs={{0,4},{4,0},{1,5},{5,1},{2,6},{6,2},{3,7},{7,3},{8,12},{12,8},{9,1... | collective-permute-start | bytes 1966088 | tf_op jit(solution)/shard_map/ppermute | solution.py:529
  48.9 20.9 %collective-permute-start.7 = (bf16[4,32,2560]{2,1,0:T(8,128)(2,1)S(1)}, bf16[4,32,2560]{2,1,0:T(8,128)(2,1)}, u32[]{:S(2)}, u32[]{:S(2)}) collective-permute-start(bf16[4,32,2560]{2,1,0:T(8,128)(2,1)S(1)} %all-to-all-done.1.b0), channel_id=1, source_target_pairs={{0,1},{1,0},{2,3},{3,2},{4,5},{5,4},{6,7},{7,6},{8,9},{9,8},{10,11... | collective-permute-start | bytes 1966088 | tf_op jit(solution)/shard_map/ppermute | solution.py:529
  50.0 31.0 %all-to-all-start.2 = ((bf16[4,2,32,2048]{3,2,1,0:T(8,128)(2,1)}), bf16[4,2,32,2048]{3,2,1,0:T(8,128)(2,1)}, u32[]{:S(2)}, u32[]{:S(2)}) async-start(bf16[4,2,32,2048]{3,2,1,0:T(8,128)(2,1)} %broadcast_in_dim.8), calls=%async_computation.2 | async-start | bytes 2097152 | tf_op jit(solution)/shard_map/all_to_all | solution.py:548
  55.3 12.7 %collective-permute-start.10 = (bf16[4,64,512]{2,1,0:T(8,128)(2,1)}, bf16[4,64,512]{2,1,0:T(8,128)(2,1)}, u32[]{:S(2)}, u32[]{:S(2)}) collective-permute-start(bf16[4,64,512]{2,1,0:T(8,128)(2,1)} %get-tuple-element.212), channel_id=1, source_target_pairs={{0,3},{1,2},{2,1},{3,0},{4,7},{5,6},{6,5},{7,4},{8,11},{9,10},{10,... | collective-permute-start | bytes 786440 | tf_op jit(solution)/shard_map/ppermute | solution.py:541
  55.9 12.1 %collective-permute-start.8 = (bf16[4,64,512]{2,1,0:T(8,128)(2,1)}, bf16[4,64,512]{2,1,0:T(8,128)(2,1)}, u32[]{:S(2)}, u32[]{:S(2)}) collective-permute-start(bf16[4,64,512]{2,1,0:T(8,128)(2,1)} %get-tuple-element.214), channel_id=1, source_target_pairs={{0,1},{1,0},{2,3},{3,2},{4,5},{5,4},{6,7},{7,6},{8,9},{9,8},{10,11... | collective-permute-start | bytes 786440 | tf_op jit(solution)/shard_map/ppermute | solution.py:541
  55.9 14.0 %collective-permute-start.9 = (bf16[4,64,512]{2,1,0:T(8,128)(2,1)}, bf16[4,64,512]{2,1,0:T(8,128)(2,1)}, u32[]{:S(2)}, u32[]{:S(2)}) collective-permute-start(bf16[4,64,512]{2,1,0:T(8,128)(2,1)} %get-tuple-element.213), channel_id=1, source_target_pairs={{0,2},{1,3},{2,0},{3,1},{4,6},{5,7},{6,4},{7,5},{8,10},{9,11},{10,... | collective-permute-start | bytes 786440 | tf_op jit(solution)/shard_map/ppermute | solution.py:541
  81.0 32.4 %copy-start.15 = (s32[9]{0:T(128)S(1)}, s32[9]{0:T(128)}, u32[]{:S(2)}) copy-start(s32[9]{0:T(128)} %copy-done.14) | copy-start | bytes 112
  81.0 3.9 %collective-permute-start.13 = (bf16[4,2,32,2048]{3,2,1,0:T(8,128)(2,1)}, bf16[4,2,32,2048]{3,2,1,0:T(8,128)(2,1)}, u32[]{:S(2)}, u32[]{:S(2)}) collective-permute-start(bf16[4,2,32,2048]{3,2,1,0:T(8,128)(2,1)} %all-to-all-done.2.c0), channel_id=1, source_target_pairs={{0,1},{1,0},{2,3},{3,2},{4,5},{5,4},{6,7},{7,6},{8,9},{9,8},{10,11... | collective-permute-start | bytes 3145736 | tf_op jit(solution)/shard_map/ppermute | solution.py:529
  81.1 3.4 %collective-permute-start.11 = (bf16[4,32,2560]{2,1,0:T(8,128)(2,1)}, bf16[4,32,2560]{2,1,0:T(8,128)(2,1)S(1)}, u32[]{:S(2)}, u32[]{:S(2)}) collective-permute-start(bf16[4,32,2560]{2,1,0:T(8,128)(2,1)} %collective-permute-done.6.b1), channel_id=1, source_target_pairs={{0,1},{1,0},{2,3},{3,2},{4,5},{5,4},{6,7},{7,6},{8,9},{9,8},{10,11... | collective-permute-start | bytes 1966088 | tf_op jit(solution)/shard_map/ppermute | solution.py:529
  112.9 14.4 %collective-permute-start.17 = (bf16[2,2,4,64,640]{4,3,2,1,0:T(8,128)(2,1)}, bf16[2,2,4,64,640]{4,3,2,1,0:T(8,128)(2,1)}, u32[]{:S(2)}, u32[]{:S(2)}) collective-permute-start(bf16[2,2,4,64,640]{4,3,2,1,0:T(8,128)(2,1)} %get-tuple-element.158), channel_id=1, source_target_pairs={{0,1},{1,0},{2,3},{3,2},{4,5},{5,4},{6,7},{7,6},{8,9},{9,8},{10,11... | collective-permute-start | bytes 3932168 | tf_op jit(solution)/shard_map/ppermute | solution.py:529
  113.3 14.0 %collective-permute-start.18 = (bf16[2,2,4,64,512]{4,3,2,1,0:T(8,128)(2,1)}, bf16[2,2,4,64,512]{4,3,2,1,0:T(8,128)(2,1)}, u32[]{:S(2)}, u32[]{:S(2)}) collective-permute-start(bf16[2,2,4,64,512]{4,3,2,1,0:T(8,128)(2,1)} %get-tuple-element.160), channel_id=1, source_target_pairs={{0,1},{1,0},{2,3},{3,2},{4,5},{5,4},{6,7},{7,6},{8,9},{9,8},{10,11... | collective-permute-start | bytes 3145736 | tf_op jit(solution)/shard_map/ppermute | solution.py:529
  113.5 12.4 %collective-permute-start.14 = (bf16[4,64,512]{2,1,0:T(8,128)(2,1)}, bf16[4,64,512]{2,1,0:T(8,128)(2,1)S(1)}, u32[]{:S(2)}, u32[]{:S(2)}) collective-permute-start(bf16[4,64,512]{2,1,0:T(8,128)(2,1)} %get-tuple-element.154), channel_id=1, source_target_pairs={{0,1},{1,0},{2,3},{3,2},{4,5},{5,4},{6,7},{7,6},{8,9},{9,8},{10,11... | collective-permute-start | bytes 786440 | tf_op jit(solution)/shard_map/ppermute | solution.py:541
  113.9 12.0 %collective-permute-start.15 = (bf16[4,64,512]{2,1,0:T(8,128)(2,1)}, bf16[4,64,512]{2,1,0:T(8,128)(2,1)S(1)}, u32[]{:S(2)}, u32[]{:S(2)}) collective-permute-start(bf16[4,64,512]{2,1,0:T(8,128)(2,1)} %get-tuple-element.155), channel_id=1, source_target_pairs={{0,2},{1,3},{2,0},{3,1},{4,6},{5,7},{6,4},{7,5},{8,10},{9,11},{10,... | collective-permute-start | bytes 786440 | tf_op jit(solution)/shard_map/ppermute | solution.py:541
  114.3 12.9 %collective-permute-start.16 = (bf16[4,64,512]{2,1,0:T(8,128)(2,1)}, bf16[4,64,512]{2,1,0:T(8,128)(2,1)S(1)}, u32[]{:S(2)}, u32[]{:S(2)}) collective-permute-start(bf16[4,64,512]{2,1,0:T(8,128)(2,1)} %get-tuple-element.156), channel_id=1, source_target_pairs={{0,3},{1,2},{2,1},{3,0},{4,7},{5,6},{6,5},{7,4},{8,11},{9,10},{10,... | collective-permute-start | bytes 786440 | tf_op jit(solution)/shard_map/ppermute | solution.py:541
  125.8 5.4 %copy-start.21 = (bf16[4,64,512]{2,1,0:T(8,128)(2,1)}, bf16[4,64,512]{2,1,0:T(8,128)(2,1)S(1)}, u32[]{:S(2)}) copy-start(bf16[4,64,512]{2,1,0:T(8,128)(2,1)S(1)} %collective-permute-done.14.p1) | copy-start | bytes 786436
  125.9 5.4 %copy-start.22 = (bf16[4,64,512]{2,1,0:T(8,128)(2,1)}, bf16[4,64,512]{2,1,0:T(8,128)(2,1)S(1)}, u32[]{:S(2)}) copy-start(bf16[4,64,512]{2,1,0:T(8,128)(2,1)S(1)} %collective-permute-done.15.p2) | copy-start | bytes 786436
  131.2 21.9 %collective-permute-start.19 = (bf16[4,64,640]{2,1,0:T(8,128)(2,1)}, bf16[4,64,640]{2,1,0:T(8,128)(2,1)S(1)}, u32[]{:S(2)}, u32[]{:S(2)}) collective-permute-start(bf16[4,64,640]{2,1,0:T(8,128)(2,1)} %get-tuple-element.172), channel_id=1, source_target_pairs={{0,4},{2,6},{4,0},{6,2},{1,5},{3,7},{5,1},{7,3},{8,12},{10,14},{12... | collective-permute-start | bytes 983048 | tf_op jit(solution)/shard_map/ppermute | solution.py:829
  132.7 20.5 %collective-permute-start.20 = (bf16[4,64,640]{2,1,0:T(8,128)(2,1)}, bf16[4,64,640]{2,1,0:T(8,128)(2,1)S(1)}, u32[]{:S(2)}, u32[]{:S(2)}) collective-permute-start(bf16[4,64,640]{2,1,0:T(8,128)(2,1)} %get-tuple-element.171), channel_id=1, source_target_pairs={{0,2},{2,0},{4,6},{6,4},{1,3},{3,1},{5,7},{7,5},{8,10},{10,8},{12,... | collective-permute-start | bytes 983048 | tf_op jit(solution)/shard_map/ppermute | solution.py:829
  133.2 19.9 %collective-permute-start.21 = (bf16[4,64,640]{2,1,0:T(8,128)(2,1)}, bf16[4,64,640]{2,1,0:T(8,128)(2,1)S(1)}, u32[]{:S(2)}, u32[]{:S(2)}) collective-permute-start(bf16[4,64,640]{2,1,0:T(8,128)(2,1)} %get-tuple-element.173), channel_id=1, source_target_pairs={{0,6},{2,4},{4,2},{6,0},{1,7},{3,5},{5,3},{7,1},{8,14},{10,12},{12... | collective-permute-start | bytes 983048 | tf_op jit(solution)/shard_map/ppermute | solution.py:829
  134.8 30.3 %all-to-all-start.5 = ((bf16[4,4,64,512]{3,2,1,0:T(8,128)(2,1)}), bf16[4,4,64,512]{3,2,1,0:T(8,128)(2,1)}, u32[]{:S(2)}, u32[]{:S(2)}) async-start(bf16[4,4,64,512]{3,2,1,0:T(8,128)(2,1)} %get-tuple-element.174), calls=%async_computation.5 | async-start | bytes 2097152 | tf_op jit(solution)/shard_map/all_to_all | solution.py:852
  153.2 2.6 %collective-permute-start.22 = (bf16[2,2,4,64,384]{4,3,2,1,0:T(8,128)(2,1)}, bf16[2,2,4,64,384]{4,3,2,1,0:T(8,128)(2,1)S(1)}, u32[]{:S(2)}, u32[]{:S(2)}) collective-permute-start(bf16[2,2,4,64,384]{4,3,2,1,0:T(8,128)(2,1)} %get-tuple-element.186), channel_id=1, source_target_pairs={{0,1},{1,0},{2,3},{3,2},{4,5},{5,4},{6,7},{7,6},{8,9},{9,8},{10,11... | collective-permute-start | bytes 2359304 | tf_op jit(solution)/shard_map/ppermute | solution.py:529
  156.6 5.9 %copy-start.3 = (bf16[4,64,640]{2,1,0:T(8,128)(2,1)S(1)}, bf16[4,64,640]{2,1,0:T(8,128)(2,1)}, u32[]{:S(2)}) copy-start(bf16[4,64,640]{2,1,0:T(8,128)(2,1)} %get-tuple-element.170) | copy-start | bytes 983044
  159.1 14.0 %collective-permute-start.23 = (bf16[4,80,384]{2,1,0:T(8,128)(2,1)}, bf16[4,80,384]{2,1,0:T(8,128)(2,1)S(1)}, u32[]{:S(2)}, u32[]{:S(2)}) collective-permute-start(bf16[4,80,384]{2,1,0:T(8,128)(2,1)} %get-tuple-element.191), channel_id=1, source_target_pairs={{0,4},{2,6},{4,0},{6,2},{1,5},{3,7},{5,1},{7,3},{8,12},{10,14},{12... | collective-permute-start | bytes 737288 | tf_op jit(solution)/shard_map/ppermute | solution.py:829
  160.5 14.1 %collective-permute-start.24 = (bf16[4,80,384]{2,1,0:T(8,128)(2,1)}, bf16[4,80,384]{2,1,0:T(8,128)(2,1)S(1)}, u32[]{:S(2)}, u32[]{:S(2)}) collective-permute-start(bf16[4,80,384]{2,1,0:T(8,128)(2,1)} %get-tuple-element.192), channel_id=1, source_target_pairs={{0,2},{2,0},{4,6},{6,4},{1,3},{3,1},{5,7},{7,5},{8,10},{10,8},{12,... | collective-permute-start | bytes 737288 | tf_op jit(solution)/shard_map/ppermute | solution.py:829
  161.0 13.6 %collective-permute-start.25 = (bf16[4,80,384]{2,1,0:T(8,128)(2,1)}, bf16[4,80,384]{2,1,0:T(8,128)(2,1)S(1)}, u32[]{:S(2)}, u32[]{:S(2)}) collective-permute-start(bf16[4,80,384]{2,1,0:T(8,128)(2,1)} %get-tuple-element.193), channel_id=1, source_target_pairs={{0,6},{2,4},{4,2},{6,0},{1,7},{3,5},{5,3},{7,1},{8,14},{10,12},{12... | collective-permute-start | bytes 737288 | tf_op jit(solution)/shard_map/ppermute | solution.py:829
  164.4 10.2 %copy-start.6 = (bf16[4,80,384]{2,1,0:T(8,128)(2,1)S(1)}, bf16[4,80,384]{2,1,0:T(8,128)(2,1)}, u32[]{:S(2)}) copy-start(bf16[4,80,384]{2,1,0:T(8,128)(2,1)} %get-tuple-element.190) | copy-start | bytes 737284
  165.1 14.3 %all-to-all-start.4 = ((bf16[4,64,640]{2,1,0:T(8,128)(2,1)}), bf16[4,64,640]{2,1,0:T(8,128)(2,1)S(1)}, u32[]{:S(2)}, u32[]{:S(2)}) async-start(bf16[4,64,640]{2,1,0:T(8,128)(2,1)} %add_convert_fusion), calls=%async_computation.4 | async-start | bytes 655360 | tf_op jit(solution)/shard_map/all_to_all | solution.py:891
  171.0 12.0 %collective-permute-start.26 = (bf16[64,512]{1,0:T(8,128)(2,1)S(1)}, bf16[64,512]{1,0:T(8,128)(2,1)S(1)}, u32[]{:S(2)}, u32[]{:S(2)}) collective-permute-start(bf16[64,512]{1,0:T(8,128)(2,1)S(1)} %get-tuple-element.222), channel_id=1, source_target_pairs={{0,4},{2,6},{4,0},{6,2},{1,5},{3,7},{5,1},{7,3},{8,12},{10,14},{12... | collective-permute-start | bytes 196616 | tf_op jit(solution)/shard_map/ppermute | solution.py:829
  172.5 10.5 %collective-permute-start.27 = (bf16[64,512]{1,0:T(8,128)(2,1)S(1)}, bf16[64,512]{1,0:T(8,128)(2,1)S(1)}, u32[]{:S(2)}, u32[]{:S(2)}) collective-permute-start(bf16[64,512]{1,0:T(8,128)(2,1)S(1)} %get-tuple-element.224), channel_id=1, source_target_pairs={{0,2},{2,0},{4,6},{6,4},{1,3},{3,1},{5,7},{7,5},{8,10},{10,8},{12,... | collective-permute-start | bytes 196616 | tf_op jit(solution)/shard_map/ppermute | solution.py:829
  173.0 10.0 %collective-permute-start.28 = (bf16[64,512]{1,0:T(8,128)(2,1)S(1)}, bf16[64,512]{1,0:T(8,128)(2,1)S(1)}, u32[]{:S(2)}, u32[]{:S(2)}) collective-permute-start(bf16[64,512]{1,0:T(8,128)(2,1)S(1)} %get-tuple-element.223), channel_id=1, source_target_pairs={{0,6},{2,4},{4,2},{6,0},{1,7},{3,5},{5,3},{7,1},{8,14},{10,12},{12... | collective-permute-start | bytes 196616 | tf_op jit(solution)/shard_map/ppermute | solution.py:829
  179.3 10.0 %all-to-all-start.3 = ((bf16[4,80,384]{2,1,0:T(8,128)(2,1)}), bf16[4,80,384]{2,1,0:T(8,128)(2,1)S(1)}, u32[]{:S(2)}, u32[]{:S(2)}) async-start(bf16[4,80,384]{2,1,0:T(8,128)(2,1)} %add_convert_fusion.1), calls=%async_computation.3 | async-start | bytes 491520 | tf_op jit(solution)/shard_map/all_to_all | solution.py:892
  183.2 12.6 %copy-start.7 = (bf16[64,1152]{1,0:T(8,128)(2,1)}, bf16[64,1152]{1,0:T(8,128)(2,1)S(1)}, u32[]{:S(2)}) copy-start(bf16[64,1152]{1,0:T(8,128)(2,1)S(1)} %pad_maximum_fusion.2.m0) | copy-start | bytes 442372
  183.2 6.6 %collective-permute-start.29 = (bf16[64,1152]{1,0:T(8,128)(2,1)S(1)}, bf16[64,1152]{1,0:T(8,128)(2,1)S(1)}, u32[]{:S(2)}, u32[]{:S(2)}) collective-permute-start(bf16[64,1152]{1,0:T(8,128)(2,1)S(1)} %pad_maximum_fusion.2.m0), channel_id=1, source_target_pairs={{0,2},{1,3},{2,0},{3,1},{4,6},{5,7},{6,4},{7,5},{8,10},{9,11},{10,... | collective-permute-start | bytes 442376 | tf_op jit(solution)/shard_map/ppermute | solution.py:580
  183.7 6.2 %collective-permute-start.30 = (bf16[64,1152]{1,0:T(8,128)(2,1)S(1)}, bf16[64,1152]{1,0:T(8,128)(2,1)S(1)}, u32[]{:S(2)}, u32[]{:S(2)}) collective-permute-start(bf16[64,1152]{1,0:T(8,128)(2,1)S(1)} %pad_maximum_fusion.2.m0), channel_id=1, source_target_pairs={{0,1},{1,0},{2,3},{3,2},{4,5},{5,4},{6,7},{7,6},{8,9},{9,8},{10,11... | collective-permute-start | bytes 442376 | tf_op jit(solution)/shard_map/ppermute | solution.py:580
  183.7 6.2 %collective-permute-start.31 = (bf16[64,1152]{1,0:T(8,128)(2,1)S(1)}, bf16[64,1152]{1,0:T(8,128)(2,1)S(1)}, u32[]{:S(2)}, u32[]{:S(2)}) collective-permute-start(bf16[64,1152]{1,0:T(8,128)(2,1)S(1)} %pad_maximum_fusion.2.m0), channel_id=1, source_target_pairs={{0,3},{1,2},{2,1},{3,0},{4,7},{5,6},{6,5},{7,4},{8,11},{9,10},{10,... | collective-permute-start | bytes 442376 | tf_op jit(solution)/shard_map/ppermute | solution.py:580
  189.4 6.3 %copy-start.9 = (bf16[80,384]{1,0:T(8,128)(2,1)}, bf16[80,384]{1,0:T(8,128)(2,1)S(1)}, u32[]{:S(2)}) copy-start(bf16[80,384]{1,0:T(8,128)(2,1)S(1)} %reduce_sum.36.a0) | copy-start | bytes 184324
  189.8 5.9 %copy-start.27 = (bf16[64,1152]{1,0:T(8,128)(2,1)}, bf16[64,1152]{1,0:T(8,128)(2,1)S(1)}, u32[]{:S(2)}) copy-start(bf16[64,1152]{1,0:T(8,128)(2,1)S(1)} %collective-permute-done.29.m1) | copy-start | bytes 442372
  189.8 5.9 %copy-start.28 = (bf16[64,1152]{1,0:T(8,128)(2,1)}, bf16[64,1152]{1,0:T(8,128)(2,1)S(1)}, u32[]{:S(2)}) copy-start(bf16[64,1152]{1,0:T(8,128)(2,1)S(1)} %collective-permute-done.30.m2) | copy-start | bytes 442372
  189.8 5.9 %copy-start.29 = (bf16[64,1152]{1,0:T(8,128)(2,1)}, bf16[64,1152]{1,0:T(8,128)(2,1)S(1)}, u32[]{:S(2)}) copy-start(bf16[64,1152]{1,0:T(8,128)(2,1)S(1)} %collective-permute-done.31.m3) | copy-start | bytes 442372
  189.8 4.6 %collective-permute-start.32 = (bf16[80,384]{1,0:T(8,128)(2,1)S(1)}, bf16[80,384]{1,0:T(8,128)(2,1)S(1)}, u32[]{:S(2)}, u32[]{:S(2)}) collective-permute-start(bf16[80,384]{1,0:T(8,128)(2,1)S(1)} %reduce_sum.36.a0), channel_id=1, source_target_pairs={{0,2},{1,3},{2,0},{3,1},{4,6},{5,7},{6,4},{7,5},{8,10},{9,11},{10,... | collective-permute-start | bytes 184328 | tf_op jit(solution)/shard_map/ppermute | solution.py:580
  191.4 3.0 %collective-permute-start.33 = (bf16[80,384]{1,0:T(8,128)(2,1)S(1)}, bf16[80,384]{1,0:T(8,128)(2,1)S(1)}, u32[]{:S(2)}, u32[]{:S(2)}) collective-permute-start(bf16[80,384]{1,0:T(8,128)(2,1)S(1)} %reduce_sum.36.a0), channel_id=1, source_target_pairs={{0,1},{1,0},{2,3},{3,2},{4,5},{5,4},{6,7},{7,6},{8,9},{9,8},{10,11... | collective-permute-start | bytes 184328 | tf_op jit(solution)/shard_map/ppermute | solution.py:580
  191.5 4.2 %collective-permute-start.34 = (bf16[80,384]{1,0:T(8,128)(2,1)S(1)}, bf16[80,384]{1,0:T(8,128)(2,1)S(1)}, u32[]{:S(2)}, u32[]{:S(2)}) collective-permute-start(bf16[80,384]{1,0:T(8,128)(2,1)S(1)} %reduce_sum.36.a0), channel_id=1, source_target_pairs={{0,3},{1,2},{2,1},{3,0},{4,7},{5,6},{6,5},{7,4},{8,11},{9,10},{10,... | collective-permute-start | bytes 184328 | tf_op jit(solution)/shard_map/ppermute | solution.py:580
  198.5 12.6 %all-to-all-start.6 = ((f32[8,8,128]{2,1,0:T(8,128)}), f32[8,8,128]{2,1,0:T(8,128)S(1)}, u32[]{:S(2)}, u32[]{:S(2)}) async-start(f32[8,8,128]{2,1,0:T(8,128)} %squares.1), calls=%async_computation.6 | async-start | bytes 65536 | tf_op jit(solution)/shard_map/all_to_all | solution.py:923
  206.7 10.9 %collective-permute-start.35 = (bf16[4,64,512]{2,1,0:T(8,128)(2,1)S(1)}, bf16[4,64,512]{2,1,0:T(8,128)(2,1)}, u32[]{:S(2)}, u32[]{:S(2)}) collective-permute-start(bf16[4,64,512]{2,1,0:T(8,128)(2,1)S(1)} %copy-done.24), channel_id=1, source_target_pairs={{0,1},{1,0},{2,3},{3,2},{4,5},{5,4},{6,7},{7,6},{8,9},{9,8},{10,11... | collective-permute-start | bytes 786440 | tf_op jit(solution)/shard_map/ppermute | solution.py:541
  206.7 10.9 %collective-permute-start.36 = (bf16[4,64,512]{2,1,0:T(8,128)(2,1)S(1)}, bf16[4,64,512]{2,1,0:T(8,128)(2,1)}, u32[]{:S(2)}, u32[]{:S(2)}) collective-permute-start(bf16[4,64,512]{2,1,0:T(8,128)(2,1)S(1)} %copy-done.25), channel_id=1, source_target_pairs={{0,2},{1,3},{2,0},{3,1},{4,6},{5,7},{6,4},{7,5},{8,10},{9,11},{10,... | collective-permute-start | bytes 786440 | tf_op jit(solution)/shard_map/ppermute | solution.py:541
  208.0 12.7 %collective-permute-start.37 = (bf16[4,64,512]{2,1,0:T(8,128)(2,1)S(1)}, bf16[4,64,512]{2,1,0:T(8,128)(2,1)}, u32[]{:S(2)}, u32[]{:S(2)}) collective-permute-start(bf16[4,64,512]{2,1,0:T(8,128)(2,1)S(1)} %copy-done.26), channel_id=1, source_target_pairs={{0,3},{1,2},{2,1},{3,0},{4,7},{5,6},{6,5},{7,4},{8,11},{9,10},{10,... | collective-permute-start | bytes 786440 | tf_op jit(solution)/shard_map/ppermute | solution.py:541
  (17 other events, 31.5 us)

commit v5 on v4

--- a/solution.py
+++ b/solution.py
@@ -75,11 +75,11 @@
         hi_count, rows, _ = piece.shape
         for h in range(hi_count):
             row = pl.multiple_of(((h * 2 + lo_at) * 2 + core_at) * rows, rows)
-            for column, width, target in jobs:
+            for column, width, target, at in jobs:
                 copies.append(
                     pltpu.make_async_copy(
                         piece.at[h, :, pl.ds(column, width)],
-                        target.at[pl.ds(row, rows), :],
+                        target.at[pl.ds(row, rows), pl.ds(at, width)],
                         sems.at[len(copies)],
                     )
                 )
@@ -96,7 +96,9 @@
                 row = pl.multiple_of(((h * 2 + (place[0] ^ j)) * 2 + core_at) * rows, rows)
                 copies.append(
                     pltpu.make_async_copy(
-                        piece.at[h, j], target.at[pl.ds(row, rows), :], sems.at[len(copies)]
+                        piece.at[h, j],
+                        target.at[pl.ds(row, rows), pl.ds(0, piece.shape[-1])],
+                        sems.at[len(copies)],
                     )
                 )
     return copies
@@ -119,7 +121,7 @@
 def qkv_body(place, x0, x1, x2, x3, p0, p1, p2, p3, vec, h_out, qkv_out, w_qkv, sems):
     row = pl.program_id(0)
     width = vec.shape[1]
-    copies = placements((p0, p1, p2, p3), [(0, 3 * width, w_qkv)], place, sems)
+    copies = placements((p0, p1, p2, p3), [(0, 3 * width, w_qkv, 0)], place, sems)
 
     @pl.when(row == 0)
     def _():
@@ -210,8 +212,10 @@
     width = vec.shape[1]
     hidden = w_up.shape[1]
     slots = attn.shape[0]
-    out_copies = placements((b0, b1, b2, b3), [(0, width, w_out)], place, out_sems)
-    up_copies = placements((b0, b1, b2, b3), [(width, hidden, w_up)], place, up_sems)
+    out_copies = placements((b0, b1, b2, b3), [(0, width, w_out, 0)], place, out_sems)
+    split = c0.shape[-1]
+    jobs = [(width, hidden, w_up, 0), (width + hidden, hidden - split, w_down, split)]
+    up_copies = placements((b0, b1, b2, b3), jobs, place, up_sems)
     down_copies = pair_placements((c0, c1), w_down, place, down_sems)
 
     def arrived(copies):
@@ -283,18 +287,18 @@
 
 
 def back_rows(
-    place, lengths, qkv, lse, dattn, xs, dx, pieces, vec, outs, dqkv, vec_out, w_qkv, bias, sems
+    place, lengths, qkv, lse, dattn, xs, dx, pieces, vec, sums, outs, dqkv, vec_out, w_qkv, bias, sems
 ):
     step = pl.program_id(0)
     width = vec.shape[1]
     slots = qkv.shape[0]
     pair = 2 * (width // HEADS)
     score_scale = 1.0 / math.sqrt(width // HEADS)
-    copies = placements(pieces, [(0, 3 * width, w_qkv)], place, sems)
+    copies = placements(pieces, [(0, 3 * width, w_qkv, 0)], place, sems)
 
     @pl.when(step == 0)
     def _():
-        vec_out[...] = jnp.zeros_like(vec_out)
+        vec_out[...] = sums[...]
         for copy in copies:
             copy.start()
 
@@ -343,25 +347,25 @@
 
 
 def back_first_body(
-    place, lengths, qkv, lse, dattn, x0, x1, x2, x3, dx, p0, p1, p2, p3, vec,
+    place, lengths, qkv, lse, dattn, x0, x1, x2, x3, dx, p0, p1, p2, p3, vec, sums,
     o0, o1, o2, o3, dqkv_out, vec_out, w_qkv, bias, sems,
 ):
     back_rows(
-        place, lengths, qkv, lse, dattn, (x0, x1, x2, x3), dx, (p0, p1, p2, p3), vec,
+        place, lengths, qkv, lse, dattn, (x0, x1, x2, x3), dx, (p0, p1, p2, p3), vec, sums,
         (o0, o1, o2, o3), dqkv_out, vec_out, w_qkv, bias, sems,
     )
 
 
 def back_last_body(
-    dims, place, lengths, qkv, lse, dattn, x0, x1, x2, x3, dx, p0, p1, p2, p3, vec, h_one, before,
-    u0, u1, u2, u3,
+    dims, place, lengths, qkv, lse, dattn, x0, x1, x2, x3, dx, p0, p1, p2, p3, vec, sums,
+    h_one, before,
     o0, o1, o2, o3, vec_out, keep, send, dqkv, w_qkv, bias, h_turned, parts, sems, out_sems,
 ):
     step = pl.program_id(0)
     slots = qkv.shape[0]
     here = pl.ds(pl.multiple_of(step * slots, slots), slots)
     back_rows(
-        place, lengths, qkv, lse, dattn, (x0, x1, x2, x3), dx, (p0, p1, p2, p3), vec,
+        place, lengths, qkv, lse, dattn, (x0, x1, x2, x3), dx, (p0, p1, p2, p3), vec, sums,
         (o0, o1, o2, o3), dqkv.at[here], vec_out, w_qkv, bias, sems,
     )
 
@@ -389,9 +393,9 @@
         outs[4][:, k] = (down_keep[k].astype(F32) + down_got[k].astype(F32)).astype(BF16)
 
 
-def add_qkv_body(keep, got, v0, v1, v2, *outs):
+def add_qkv_body(keep, got, vec, *outs):
     rows = keep.shape[2]
-    sums = v0[...] + v1[...] + v2[...]
+    sums = vec[...]
     for k, out in enumerate(outs):
         out[:, :rows, :] = (keep[k].astype(F32) + got[k].astype(F32)).astype(BF16)
         out[:, rows:, :] = jnp.zeros((out.shape[0], 16, out.shape[2]), BF16)
@@ -400,9 +404,14 @@
             out[h, rows:, :lanes] = sums[:, h * lanes : (h + 1) * lanes].astype(BF16)
 
 
-def collect_body(place, p0, p1, p2, p3, out):
-    for k, piece in enumerate((p0, p1, p2, p3)):
-        out[place[2] ^ k] = piece[...]
+def collect_body(place, *refs):
+    out = refs[-1]
+    at = 0
+    for i in range(0, len(refs) - 1, 4):
+        count = refs[i].shape[0]
+        for k in range(4):
+            out[place[2] ^ k, at : at + count] = refs[i + k][...]
+        at += count
 
 
 def in_order(values, place):
@@ -423,17 +432,27 @@
     return jnp.where(lane == place[8], both, 0.0)
 
 
-def square_body(place, m0, m1, m2, m3, a0, a1, a2, a3, out):
-    shard = m0.shape[0]
+def square_mlp_body(place, m0, m1, m2, m3, out):
     values = []
-    for mlp, attn in ((m0, a0), (m1, a1), (m2, a2), (m3, a3)):
-        big = mlp[...].astype(F32)
-        small = attn[:shard].astype(F32)
-        values.append(jnp.sum(big * big) + jnp.sum(small * small))
+    for mlp in (m0, m1, m2, m3):
+        value = mlp[...].astype(F32)
+        values.append(jnp.sum(value * value))
+    first, second, third, fourth = in_order(values, place)
+    out[...] = jnp.full(out.shape, (first + second) + (third + fourth), F32)
+
+
+def square_body(place, before, a0, a1, a2, a3, out):
+    shard = a0.shape[0] - 16
+    values = []
+    for attn in (a0, a1, a2, a3):
+        value = attn[:shard].astype(F32)
+        values.append(jnp.sum(value * value))
     vec = vec_sums(a0, a2, place, shard)
     first, second, third, fourth = in_order(values, place)
     value = ((first + second) + (third + fourth)) + jnp.sum(vec * vec)
-    out[...] = jnp.full(out.shape, value, F32)
+    total_value = before[...] + value
+    for d in range(out.shape[0]):
+        out[d] = total_value
 
 
 def adam_parts(weight, moment, second, grad, decay, rate):
@@ -633,7 +652,10 @@
     ride = jnp.pad(vec_w.reshape(-1), (0, half_rows * lanes - vec_w.size)).reshape(half_rows, lanes)
     first_half = jnp.concatenate([half_of(attn_w[:, : 3 * width]), ride], axis=1).astype(BF16)
     qkv_own = spread_hi(first_half)
-    up_half = jnp.concatenate([half_of(attn_w[:, 3 * width :]), half_of(mlp_w[0])], axis=1)
+    split = 3 * hidden // 4
+    up_half = jnp.concatenate(
+        [half_of(attn_w[:, 3 * width :]), half_of(mlp_w[0]), half_of(mlp_w[1, :, split:])], axis=1
+    )
     up_own = spread_hi(after(up_half.astype(BF16), qkv_own))
     qkv_own, xs[3] = lax.optimization_barrier((qkv_own, xs[3]))
     qkv_other = swap(qkv_own, "lo")
@@ -674,11 +696,12 @@
         "qkv",
     )(place, *xs, *qkv_pieces, vec_float)
 
-    down_half = after(half_of(mlp_w[1]).astype(BF16), qkv_other)
+    down_half = after(half_of(mlp_w[1, :, :split]).astype(BF16), qkv_other)
     down_pair = jnp.stack(lax.optimization_barrier((down_half, swap(down_half, "lo"), h_one))[:2])
     down_own = spread_hi(after(down_pair, up_own))
-    cot, qkv, up_own = lax.optimization_barrier((flat_cot, qkv, up_own))
+    cot = after(flat_cot, qkv_other)
     dys = from_seq([pick(cot, k) for k in range(4)])
+    qkv, up_own = lax.optimization_barrier((qkv, up_own))
     up_other = swap(up_own, "lo")
 
     def half_spec(block, base):
@@ -752,7 +775,7 @@
             pltpu.VMEM((2, *shape), BF16),
             pltpu.VMEM((2, *down_shape), BF16),
             dma((n_piece,)),
-            dma((n_piece,)),
+            dma((2 * n_piece,)),
             dma((n_down,)),
             dma((2, dims[1], 2)),
             dma((2, dims[1], 2)),
@@ -765,12 +788,13 @@
     down_got = swap(down_send, "core")
 
     def collect(parts):
+        out = (4, rows, part, width)
         return call(
             collect_body,
             1,
-            [SMEM, *[whole_spec(parts[0].shape)] * 4],
-            whole_spec((4, *parts[0].shape)),
-            shape_of((4, *parts[0].shape), BF16),
+            [SMEM, *[whole_spec(p.shape) for p in parts]],
+            whole_spec(out),
+            shape_of(out, BF16),
             [],
             2,
             "collect",
@@ -793,20 +817,22 @@
             half_spec((slots, width), base),
             *[ANY] * 4,
             vec_spec,
+            vec_spec,
         ]
 
-    back_shapes = [shape_of((rows, part, width), BF16)] * 4
+    first_shapes = [shape_of((lead, part, width), BF16)] * 4
+    last_shapes = [shape_of((rows - lead, part, width), BF16)] * 4
     back_scratch = [pltpu.VMEM((width, 3 * width), BF16), pltpu.VMEM((slots, slots), F32)]
     outs = call(
         back_first_body,
         lead,
         back_specs(0),
         [*[half_spec((1, part, width), 0)] * 4, triple, vec_spec],
-        [*back_shapes, shape_of((lead_count, 3 * width), BF16), shape_of((16, width), F32)],
+        [*first_shapes, shape_of((lead_count, 3 * width), BF16), shape_of((16, width), F32)],
         [*back_scratch, dma((n_piece,))],
         11,
         "back_first",
-    )(place, row_lengths, after(qkv, up_send, down_send), *back_args, *weights)
+    )(place, row_lengths, after(qkv, up_send, down_send), *back_args, *weights, vec_mlp)
     input_first, (grad_first, vec_first) = outs[:4], outs[4:]
 
     def add_call(body, args, outs):
@@ -839,6 +865,7 @@
             part = jnp.concatenate([part, extra], axis=3)
         return total(spread_plane(part))
 
+    input_first = from_seq(input_first)
     qkv_last = qkv
     output = collect(results)
     if fits:
@@ -859,10 +886,9 @@
             *back_specs(lead),
             whole_spec((count, width)),
             whole_spec((lead_count, 3 * width)),
-            *[ANY] * 4,
         ],
-        [*[half_spec((1, part, width), lead)] * 4, vec_spec, ANY, ANY],
-        [*back_shapes, shape_of((16, width), F32), shape_of(shape, BF16), shape_of(shape, BF16)],
+        [*[half_spec((1, part, width), 0)] * 4, vec_spec, ANY, ANY],
+        [*last_shapes, shape_of((16, width), F32), shape_of(shape, BF16), shape_of(shape, BF16)],
         [
             pltpu.VMEM((count - lead_count, 3 * width), BF16),
             *back_scratch,
@@ -873,26 +899,25 @@
         ],
         13,
         "back_last",
-        {17 + k: k for k in range(4)},
-    )(place.at[4].set(lead), row_lengths, qkv_last, *back_args, *weights, h_one, grad_first, *input_first)
-    input_parts, (vec_last, qkv_keep, qkv_send) = outs[:4], outs[4:]
+    )(place.at[4].set(lead), row_lengths, qkv_last, *back_args, *weights, vec_first, h_one, grad_first)
+    input_last, (vec_last, qkv_keep, qkv_send) = outs[:4], outs[4:]
     if fits:
-        qkv_send = after(qkv_send, *up_moved)
+        qkv_send = after(qkv_send, *up_moved, *input_first)
     qkv_got = swap(qkv_send, "core")
-    vecs = [vec_mlp, vec_first, vec_last]
 
     if fits:
         _, _, _, more_rows, more_cols = qkv_keep.shape
         piece = shape_of((hi_count, more_rows + 16, more_cols), BF16)
-        parts = add_call(add_qkv_body, [qkv_keep, qkv_got, *vecs], [piece] * 4)
+        parts = add_call(add_qkv_body, [qkv_keep, qkv_got, vec_last], [piece] * 4)
         qkv_moved = plane_sum(parts)
         down_moved = plane_sum([down_part[k] for k in range(4)])
         up_plane = after(add_moved(up_moved), *parts)
         up_mine = total(lax.all_to_all(up_plane, "hi", 0, 0))
-        qkv_mine = total(lax.all_to_all(add_moved(qkv_moved), "hi", 0, 0))
         down_mine = add_moved(down_moved)
+        qkv_plane = after(add_moved(qkv_moved), up_mine, down_mine)
+        qkv_mine = total(lax.all_to_all(qkv_plane, "hi", 0, 0))
     else:
-        vec_total = (vec_mlp + vec_first + vec_last).reshape(16, hi_count, 2, vec_cols)
+        vec_total = vec_last.reshape(16, hi_count, 2, vec_cols)
         vec_total = vec_total.transpose(1, 0, 2, 3).reshape(1, 1, hi_count, 16, 2 * vec_cols)
         vec_total = jnp.pad(vec_total.astype(BF16), ((0, 0),) * 4 + ((0, quarter - 2 * vec_cols),))
         vec_total = jnp.broadcast_to(vec_total, (2, 2, *vec_total.shape[2:]))
@@ -903,23 +928,34 @@
     mlp_mine = jnp.concatenate([up_mine, down_mine], axis=1)
     mlp_pieces = to_all(mlp_mine)
     attn_pieces = to_all(after(qkv_mine, *mlp_pieces))
-    input_grad = collect(from_seq(lax.optimization_barrier((*input_parts, *attn_pieces))[:4]))
+    input_last = from_seq(lax.optimization_barrier((*input_last, *attn_pieces))[:4])
+    input_grad = collect([*input_first, *input_last])
 
     dp_count = 2 * hi_count
     if fits:
         pieces = [*mlp_pieces, *attn_pieces]
         piece_specs = [whole_spec(p.shape) for p in pieces]
         squares_shape = (dp_count, 8, 128)
+        mlp_square = call(
+            square_mlp_body,
+            1,
+            [SMEM, *piece_specs[:4]],
+            whole_spec((8, 128)),
+            shape_of((8, 128), F32),
+            [],
+            2,
+            "mlp_squares",
+        )(place, *mlp_pieces)
         squares = call(
             square_body,
             1,
-            [SMEM, *piece_specs],
+            [SMEM, whole_spec((8, 128)), *piece_specs[4:]],
             whole_spec(squares_shape),
             shape_of(squares_shape, F32),
             [],
-            2,
+            1,
             "squares",
-        )(place, *pieces)
+        )(place, mlp_square, *attn_pieces)
         squares = lax.all_to_all(squares, ("hi", "lo"), 0, 0)
         states = [attn_w, attn_m, attn_v, mlp_w, mlp_m, mlp_v, vec_w, vec_m, vec_v]
         state_specs = [whole_spec(v.shape) for v in states]

time: 224 us -> 218 us (0.973)
  waiting for transfers between devices: 52.5 us -> 36.2 us
  local copies, waits for them, and re-layouts: 11.2 us -> 15.9 us
    all_to_all x3, waiting for transfers between devices: 20.3 us -> 9.25 us  [spread_hi(): return lax.all_to_all(spread, 'hi', 0, 0)]
    ppermute x12 -> x15, waiting for transfers between devices: 6.33 us -> 0.04 us  [from_seq(): lax.ppermute(pieces[k], ('y', 'core'), [(j, j ^ k) for j in range(4)])]
    slice x1 -> x3, local copies, waits for them, and re-layouts: 0.06 us -> 3.01 us  [the longest x1 1.07 us: on_device(): mlp_w[0]]
    ppermute x12 -> x15, starting transfers between devices: 9.23 us -> 11.3 us  [from_seq(): lax.ppermute(pieces[k], ('y', 'core'), [(j, j ^ k) for j in range(4)])]
    pallas_call x3 -> x4, Pallas kernels: 6.67 us -> 8.35 us  [the longest x2 4.62 us: collect(): call(collect_body, 1, [SMEM, *[whole_spec(p.shape) for p in parts]], whol...]
  transfers between devices with their start and end apart: 45 -> 48, of which waited for: 17 -> 14; matrix products, arithmetic and copies ran while one was open for 4% -> 7% of each run, Pallas kernels for 25% -> 29%
where the time goes in v5:
time: 218 us; the launch traced here: 217 us
  Pallas kernels  94.4 us (43%)
  starting transfers between devices  62.7 us (29%)
  waiting for transfers between devices  36.2 us (17%)
  local copies, waits for them, and re-layouts  15.9 us (7%)
  other arithmetic  6.39 us (3%)
    pallas_call x1, Pallas kernels, on_device(): call(functools.partial(mlp_body, dims), rows // group, [SMEM, *[slot_spec...  27.8 us
    pallas_call x2, Pallas kernels, attend(): call(attend_body, steps, [SMEM, SMEM, half_spec((slots, 3 * width), base)...  15.3 us
    pallas_call x1, Pallas kernels, on_device(): call(functools.partial(back_last_body, dims), rows - lead, [*back_specs(l...  14.1 us
    all_to_all x3, starting transfers between devices, spread_hi(): return lax.all_to_all(spread, 'hi', 0, 0)  14 us
    ppermute x11, waiting for transfers between devices, swap(): return lax.ppermute(value, axis, [(0, 1), (1, 0)])  12.9 us
    ppermute x15, starting transfers between devices, from_seq(): lax.ppermute(pieces[k], ('y', 'core'), [(j, j ^ k) for j in range(4)])  11.3 us
    ppermute x9, starting transfers between devices, plane_sum(): moved.append(lax.ppermute(parts[k], ('lo', 'y'), perm))  10.6 us
    pallas_call x1, Pallas kernels, on_device(): call(back_first_body, lead, back_specs(0), [*[half_spec((1, part, width),...  10.4 us
  transfers between devices with their start and end apart: 48, of which 14 were waited for; matrix products, arithmetic and copies ran while one was open for 7% of the time, Pallas kernels for 29%

profile of v5, /device:TPU:0, one launch (start us, length us, event | category | flops | bytes accessed | tf_op | source)
XLA Modules:
  0.0 216.8 jit_solution(15607972925765798346)
XLA Ops:
  0.7 1.1 slice.64
  2.6 0.8 broadcast_in_dim.6
  3.4 6.3 %all-to-all-start = ((bf16[4,32,1664]{2,1,0:T(8,128)(2,1)}), bf16[4,32,1664]{2,1,0:T(8,128)(2,1)S(1)}, u32[]{:S(2)}, u32[]{:S(2)}) async-start(bf16[4,32,1664]{2,1,0:T(8,128)(2,1)} %broadcast_in_dim.6), calls=%async_computation | async-start | bytes 851968 | tf_op jit(solution)/shard_map/all_to_all | solution.py:567
  9.7 0.8 dynamic-slice_bitcast_fusion.4
  11.2 1.0 collective-permute-start
  12.7 0.9 slice.68
  13.6 1.0 slice.71
  14.7 1.1 slice.69
  15.7 0.9 slice.70
  18.0 1.2 constant_dynamic-update-slice_fusion.2.place
  19.2 2.9 %all-to-all-done.p0 = bf16[4,32,1664]{2,1,0:T(8,128)(2,1)S(1)} async-done(((bf16[4,32,1664]{2,1,0:T(8,128)(2,1)}), bf16[4,32,1664]{2,1,0:T(8,128)(2,1)S(1)}, u32[]{:S(2)}, u32[]{:S(2)}) %all-to-all-start) | async-done | bytes 426016 | tf_op jit(solution)/shard_map/all_to_all | solution.py:567
  22.1 1.5 collective-permute-start.3
  23.7 1.0 broadcast_in_dim.7
  24.7 3.5 %all-to-all-start.1 = ((bf16[4,32,3072]{2,1,0:T(8,128)(2,1)}), bf16[4,32,3072]{2,1,0:T(8,128)(2,1)S(1)}, u32[]{:S(2)}, u32[]{:S(2)}) async-start(bf16[4,32,3072]{2,1,0:T(8,128)(2,1)} %broadcast_in_dim.7), calls=%async_computation.1 | async-start | bytes 1572864 | tf_op jit(solution)/shard_map/all_to_all | solution.py:567
  28.2 4.8 %collective-permute-done.3.p1 = bf16[4,32,1664]{2,1,0:T(8,128)(2,1)} collective-permute-done((bf16[4,32,1664]{2,1,0:T(8,128)(2,1)S(1)}, bf16[4,32,1664]{2,1,0:T(8,128)(2,1)}, u32[]{:S(2)}, u32[]{:S(2)}) %collective-permute-start.3) | collective-permute-done | bytes 426016 | tf_op jit(solution)/shard_map/ppermute | solution.py:548
  33.0 0.8 select_bitcast_fusion.1
  34.0 1.5 collective-permute-start.12
  36.2 1.0 dynamic-slice_bitcast_fusion
  37.2 1.4 collective-permute-start.10
  39.3 6.3 %qkv.1 = (bf16[1024,512]{1,0:T(8,128)(2,1)}, bf16[1024,1536]{1,0:T(8,128)(2,1)}) custom-call(s32[9]{0:T(128)} %copy-done.11, bf16[4,64,512]{2,1,0:T(8,128)(2,1)} %get-tuple-element.218.x0, bf16[4,64,512]{2,1,0:T(8,128)(2,1)} %collective-permute-done.x1, bf16[4,64,512]{2,1,0:T(8,128)(2,1)} %collective-permute-done.1.x2, bf16[4,64,512]{2,1,0:T(8,128)(2,1)} %copy-done.15, ...), custom_call_target="tpu_custom_call" | custom-call | flops 7000000000 | bytes 14000000 | tf_op jit(solution)/shard_map/qkv/pallas_call | solution.py:688
  45.6 3.5 %all-to-all-done.1.b0 = bf16[4,32,3072]{2,1,0:T(8,128)(2,1)S(1)} async-done(((bf16[4,32,3072]{2,1,0:T(8,128)(2,1)}), bf16[4,32,3072]{2,1,0:T(8,128)(2,1)S(1)}, u32[]{:S(2)}, u32[]{:S(2)}) %all-to-all-start.1) | async-done | bytes 786464 | tf_op jit(solution)/shard_map/all_to_all | solution.py:567
  49.7 0.9 broadcast_in_dim.8
  50.7 4.2 %all-to-all-start.2 = ((bf16[4,2,32,1536]{3,2,1,0:T(8,128)(2,1)}), bf16[4,2,32,1536]{3,2,1,0:T(8,128)(2,1)}, u32[]{:S(2)}, u32[]{:S(2)}) async-start(bf16[4,2,32,1536]{3,2,1,0:T(8,128)(2,1)} %broadcast_in_dim.8), calls=%async_computation.2 | async-start | bytes 1572864 | tf_op jit(solution)/shard_map/all_to_all | solution.py:567
  54.9 10.5 %attend.2 = (bf16[1024,512]{1,0:T(8,128)(2,1)}, f32[4,8,256]{2,1,0:T(8,128)}) custom-call(s32[9]{0:T(128)} %copy-done.31, s32[4]{0:T(128)} %dynamic_slice.52.lengths, bf16[1024,1536]{1,0:T(8,128)(2,1)} %get-tuple-element.181.qkv), custom_call_target="tpu_custom_call" | custom-call | flops 12000000000 | bytes 24000000 | tf_op jit(solution)/shard_map/attend/pallas_call | solution.py:712
  65.4 3.0 %collective-permute-done.6.b1 = bf16[4,32,3072]{2,1,0:T(8,128)(2,1)} collective-permute-done((bf16[4,32,3072]{2,1,0:T(8,128)(2,1)S(1)}, bf16[4,32,3072]{2,1,0:T(8,128)(2,1)}, u32[]{:S(2)}, u32[]{:S(2)}) %collective-permute-start.6) | collective-permute-done | bytes 786464 | tf_op jit(solution)/shard_map/ppermute | solution.py:548
  68.4 4.7 %attend.3 = (bf16[1024,512]{1,0:T(8,128)(2,1)}, f32[4,8,256]{2,1,0:T(8,128)}) custom-call(s32[9]{0:T(128)} %constant_dynamic-update-slice_fusion.2.place, s32[4]{0:T(128)} %dynamic_slice.52.lengths, bf16[1024,1536]{1,0:T(8,128)(2,1)} %get-tuple-element.181.qkv, ...), custom_call_target="tpu_custom_call", output_to_operand_aliasing={{0}: (3, {}), {1}: (4, {})} | custom-call | flops 4000000000 | bytes 8000000 | tf_op jit(solution)/shard_map/attend/pallas_call | solution.py:712
  73.2 2.8 %all-to-all-done.2.c0 = bf16[4,2,32,1536]{3,2,1,0:T(8,128)(2,1)} async-done(((bf16[4,2,32,1536]{3,2,1,0:T(8,128)(2,1)}), bf16[4,2,32,1536]{3,2,1,0:T(8,128)(2,1)}, u32[]{:S(2)}, u32[]{:S(2)}) %all-to-all-start.2) | async-done | bytes 786464 | tf_op jit(solution)/shard_map/all_to_all | solution.py:567
  76.0 2.6 %collective-permute-done.13.c1 = bf16[4,2,32,1536]{3,2,1,0:T(8,128)(2,1)} collective-permute-done((bf16[4,2,32,1536]{3,2,1,0:T(8,128)(2,1)}, bf16[4,2,32,1536]{3,2,1,0:T(8,128)(2,1)}, u32[]{:S(2)}, u32[]{:S(2)}) %collective-permute-start.13) | collective-permute-done | bytes 786464 | tf_op jit(solution)/shard_map/ppermute | solution.py:548
  78.6 27.8 %mlp.1 = (bf16[4,64,512]{2,1,0:T(8,128)(2,1)}, bf16[4,64,512]{2,1,0:T(8,128)(2,1)}, bf16[4,64,512]{2,1,0:T(8,128)(2,1)}, bf16[4,64,512]{2,1,0:T(8,128)(2,1)}, f3...) custom-call(s32[9]{0:T(128)} %copy-done.11, ...), custom_call_target="tpu_custom_call" | custom-call | flops 24000000000 | bytes 48000000 | tf_op jit(solution)/shard_map/mlp/pallas_call | solution.py:752
  107.2 1.5 collective-permute-start.15
  108.9 10.4 %back_first.1 = (bf16[2,64,512]{2,1,0:T(8,128)(2,1)}, bf16[2,64,512]{2,1,0:T(8,128)(2,1)}, bf16[2,64,512]{2,1,0:T(8,128)(2,1)}, bf16[2,64,512]{2,1,0:T(8,128)(2,...) custom-call(s32[9]{0:T(128)} %copy-done.11, s32[4]{0:T(128)} %dynamic_slice.52.lengths, ...), custom_call_target="tpu_custom_call" | custom-call | flops 11000000512 | bytes 22000000 | tf_op jit(solution)/shard_map/back_first/pallas_call | solution.py:826
  119.9 1.5 collective-permute-start.18
  121.4 1.2 collective-permute-start.19
  122.6 3.8 %add.106 = (bf16[4,64,640]{2,1,0:T(8,128)(2,1)}, bf16[4,64,640]{2,1,0:T(8,128)(2,1)}, bf16[4,64,640]{2,1,0:T(8,128)(2,1)}, bf16[4,64,640]{2,1,0:T(8,128)(2,1)}, bf16[4,4,64,512]{3,2,1,0:T(8,128)(2,1)}) custom-call(bf16[4,4,64,640]{3,2,1,0:T(8,128)(2,1)} %bitcast.64, bf16[4,4,64,640]{3,2,1,0:T(8,128)(2,1)} %bitcast.22.got, bf16[4,4,64,512]{3,2,1,0:T(8,128)(2,1)} %bitcast.65, ...), custom_call_target="tpu_custom_call" | custom-call | flops 3000000000 | bytes 6000000 | tf_op jit(solution)/shard_map/add/pallas_call | solution.py:840
  126.4 4.3 %all-to-all-start.4 = ((bf16[4,4,64,512]{3,2,1,0:T(8,128)(2,1)}), bf16[4,4,64,512]{3,2,1,0:T(8,128)(2,1)}, u32[]{:S(2)}, u32[]{:S(2)}) async-start(bf16[4,4,64,512]{3,2,1,0:T(8,128)(2,1)} %get-tuple-element.180), calls=%async_computation.4 | async-start | bytes 2097152 | tf_op jit(solution)/shard_map/all_to_all | solution.py:879
  130.7 1.6 collective-permute-start.22
  132.8 1.5 collective-permute-start.24
  134.3 14.1 %back_last.1 = (bf16[2,64,512]{2,1,0:T(8,128)(2,1)}, bf16[2,64,512]{2,1,0:T(8,128)(2,1)}, bf16[2,64,512]{2,1,0:T(8,128)(2,1)}, bf16[2,64,512]{2,1,0:T(8,128)(2,1...) custom-call(s32[9]{0:T(128)} %copy-done.32, ...), custom_call_target="tpu_custom_call" | custom-call | flops 12999999488 | bytes 26000000 | tf_op jit(solution)/shard_map/back_last/pallas_call | solution.py:882
  149.0 2.5 %collective-permute-done.25 = bf16[2,2,4,64,384]{4,3,2,1,0:T(8,128)(2,1)S(1)} collective-permute-done((bf16[2,2,4,64,384]{4,3,2,1,0:T(8,128)(2,1)}, bf16[2,2,4,64,384]{4,3,2,1,0:T(8,128)(2,1)S(1)}, u32[]{:S(2)}, u32[]{:S(2)}) %collective-permute-start.25) | collective-permute-done | bytes 786464 | tf_op jit(solution)/shard_map/ppermute | solution.py:548
  151.5 0.9 copy-done.14
  152.3 2.4 %add.107 = (bf16[4,80,384]{2,1,0:T(8,128)(2,1)}, bf16[4,80,384]{2,1,0:T(8,128)(2,1)}, bf16[4,80,384]{2,1,0:T(8,128)(2,1)}, bf16[4,80,384]{2,1,0:T(8,128)(2,1)}) custom-call(bf16[4,4,64,384]{3,2,1,0:T(8,128)(2,1)} %bitcast.66, bf16[4,4,64,384]{3,2,1,0:T(8,128)(2,1)} %bitcast.63, f32[16,512]{1,0:T(8,128)} %get-tuple-element.190.vec), custom_call_target="tpu_custom_call" | custom-call | flops 3000000000 | bytes 6000000 | tf_op jit(solution)/shard_map/add/pallas_call | solution.py:840
  154.8 1.1 collective-permute-start.26
  156.5 1.8 collective-permute-start.28
  158.2 1.9 add_convert_fusion
  160.1 4.8 %all-to-all-start.3 = ((bf16[4,64,640]{2,1,0:T(8,128)(2,1)}), bf16[4,64,640]{2,1,0:T(8,128)(2,1)S(1)}, u32[]{:S(2)}, u32[]{:S(2)}) async-start(bf16[4,64,640]{2,1,0:T(8,128)(2,1)} %add_convert_fusion), calls=%async_computation.3 | async-start | bytes 655360 | tf_op jit(solution)/shard_map/all_to_all | solution.py:915
  164.9 1.4 reduce_sum.37
  166.4 1.4 collective-permute-start.29
  168.3 1.6 collective-permute-start.31
  170.0 0.8 add_convert_fusion.1
  170.8 3.9 %all-to-all-done.3 = bf16[4,64,640]{2,1,0:T(8,128)(2,1)S(1)} async-done(((bf16[4,64,640]{2,1,0:T(8,128)(2,1)}), bf16[4,64,640]{2,1,0:T(8,128)(2,1)S(1)}, u32[]{:S(2)}, u32[]{:S(2)}) %all-to-all-start.3) | async-done | bytes 327712 | tf_op jit(solution)/shard_map/all_to_all | solution.py:915
  174.8 3.8 %all-to-all-start.5 = ((bf16[4,80,384]{2,1,0:T(8,128)(2,1)}), bf16[4,80,384]{2,1,0:T(8,128)(2,1)S(1)}, u32[]{:S(2)}, u32[]{:S(2)}) async-start(bf16[4,80,384]{2,1,0:T(8,128)(2,1)} %add_convert_fusion.1), calls=%async_computation.5 | async-start | bytes 491520 | tf_op jit(solution)/shard_map/all_to_all | solution.py:918
  178.6 1.6 collective-permute-start.32
  180.8 4.4 %all-to-all-done.5 = bf16[4,80,384]{2,1,0:T(8,128)(2,1)S(1)} async-done(((bf16[4,80,384]{2,1,0:T(8,128)(2,1)}), bf16[4,80,384]{2,1,0:T(8,128)(2,1)S(1)}, u32[]{:S(2)}, u32[]{:S(2)}) %all-to-all-start.5) | async-done | bytes 245792 | tf_op jit(solution)/shard_map/all_to_all | solution.py:918
  185.3 1.0 collective-permute-done.34.m3
  187.0 1.0 collective-permute-start.36
  188.5 2.0 mlp_squares.1.before
  190.7 1.4 collective-permute-done.37.a3
  192.8 1.7 squares.1
  194.5 5.4 %all-to-all-start.6 = ((f32[8,8,128]{2,1,0:T(8,128)}), f32[8,8,128]{2,1,0:T(8,128)S(1)}, u32[]{:S(2)}, u32[]{:S(2)}) async-start(f32[8,8,128]{2,1,0:T(8,128)} %squares.1), calls=%async_computation.6 | async-start | bytes 65536 | tf_op jit(solution)/shard_map/all_to_all | solution.py:959
  199.9 2.3 %collect.2 = bf16[4,4,64,512]{3,2,1,0:T(8,128)(2,1)} custom-call(s32[9]{0:T(128)} %copy-done.11, bf16[4,64,512]{2,1,0:T(8,128)(2,1)} %get-tuple-element.154.refs_0_, bf16[4,64,512]{2,1,0:T(8,128)(2,1)} %copy-done.16, bf16[4,64,512]{2,1,0:T(8,128)(2,1)} %copy-done.17, bf16[4,64,512]{2,1,0:T(8,128)(2,1)} %copy-done.18), custom_call_target="tpu_custom_call" | custom-call | flops 2000000000 | bytes 4000000 | tf_op jit(solution)/shard_map/collect/pallas_call | solution.py:792
  202.2 1.2 collective-permute-start.39
  204.1 2.5 %all-to-all-done.6.squares = f32[8,8,128]{2,1,0:T(8,128)S(1)} async-done(((f32[8,8,128]{2,1,0:T(8,128)}), f32[8,8,128]{2,1,0:T(8,128)S(1)}, u32[]{:S(2)}, u32[]{:S(2)}) %all-to-all-start.6) | async-done | bytes 32800 | tf_op jit(solution)/shard_map/all_to_all | solution.py:959
  207.2 6.0 %adam.1 = (f32[1,1]{1,0:T(1,128)}, f32[64,2048]{1,0:T(8,128)}, f32[64,2048]{1,0:T(8,128)}, f32[64,2048]{1,0:T(8,128)}, f32[2,64,2048]{2,1,0:T(8,128)}, /*index=5...) custom-call(s32[9]{0:T(128)} %copy-done.11, ...), custom_call_target="tpu_custom_call" | custom-call | flops 6000000000 | bytes 12000000 | tf_op jit(solution)/shard_map/adam/pallas_call | solution.py:962
  214.5 2.3 %collect.3 = bf16[4,4,64,512]{3,2,1,0:T(8,128)(2,1)} custom-call(s32[9]{0:T(128)} %copy-done.11, bf16[2,64,512]{2,1,0:T(8,128)(2,1)} %get-tuple-element.165.refs_0_, bf16[2,64,512]{2,1,0:T(8,128)(2,1)} %collective-permute-done.17.refs_1_, bf16[2,64,512]{2,1,0:T(8,128)(2,1)} %collective-permute-done.18.refs_2_, ...), custom_call_target="tpu_custom_call" | custom-call | flops 2000000000 | bytes 4000000 | tf_op jit(solution)/shard_map/collect/pallas_call | solution.py:792
  (158 shorter events, 14.8 us)
Async XLA Ops:
  0.6 9.1 %copy-start = (bf16[4,4,64,512]{3,2,1,0:T(8,128)(2,1)S(1)}, bf16[4,4,64,512]{3,2,1,0:T(8,128)(2,1)}, u32[]{:S(2)}) copy-start(bf16[4,4,64,512]{3,2,1,0:T(8,128)(2,1)} %param.18) | copy-start | bytes 3145732
  3.4 18.7 %all-to-all-start = ((bf16[4,32,1664]{2,1,0:T(8,128)(2,1)}), bf16[4,32,1664]{2,1,0:T(8,128)(2,1)S(1)}, u32[]{:S(2)}, u32[]{:S(2)}) async-start(bf16[4,32,1664]{2,1,0:T(8,128)(2,1)} %broadcast_in_dim.6), calls=%async_computation | async-start | bytes 851968 | tf_op jit(solution)/shard_map/all_to_all | solution.py:567
  9.7 7.6 %copy-start.10 = (s32[4,4]{1,0:T(4,128)S(1)}, s32[4,4]{1,0:T(4,128)}, u32[]{:S(2)}) copy-start(s32[4,4]{1,0:T(4,128)} %param.20) | copy-start | bytes 196
  10.5 8.6 %collective-permute-start.2 = (bf16[4,64,512]{2,1,0:T(8,128)(2,1)S(1)}, bf16[4,64,512]{2,1,0:T(8,128)(2,1)S(1)}, u32[]{:S(2)}, u32[]{:S(2)}) collective-permute-start(bf16[4,64,512]{2,1,0:T(8,128)(2,1)S(1)} %get-tuple-element.216), channel_id=1, source_target_pairs={{0,3},{1,2},{2,1},{3,0},{4,7},{5,6},{6,5},{7,4},{8,11},{9,10},{10,... | collective-permute-start | bytes 786440 | tf_op jit(solution)/shard_map/ppermute | solution.py:560
  11.2 26.0 %collective-permute-start = (bf16[4,64,512]{2,1,0:T(8,128)(2,1)S(1)}, bf16[4,64,512]{2,1,0:T(8,128)(2,1)}, u32[]{:S(2)}, u32[]{:S(2)}) collective-permute-start(bf16[4,64,512]{2,1,0:T(8,128)(2,1)S(1)} %get-tuple-element.217), channel_id=1, source_target_pairs={{0,1},{1,0},{2,3},{3,2},{4,5},{5,4},{6,7},{7,6},{8,9},{9,8},{10,11... | collective-permute-start | bytes 786440 | tf_op jit(solution)/shard_map/ppermute | solution.py:560
  12.2 26.4 %collective-permute-start.1 = (bf16[4,64,512]{2,1,0:T(8,128)(2,1)S(1)}, bf16[4,64,512]{2,1,0:T(8,128)(2,1)}, u32[]{:S(2)}, u32[]{:S(2)}) collective-permute-start(bf16[4,64,512]{2,1,0:T(8,128)(2,1)S(1)} %get-tuple-element.219), channel_id=1, source_target_pairs={{0,2},{1,3},{2,0},{3,1},{4,6},{5,7},{6,4},{7,5},{8,10},{9,11},{10,... | collective-permute-start | bytes 786440 | tf_op jit(solution)/shard_map/ppermute | solution.py:560
  16.7 7.9 %copy-start.11 = (s32[9]{0:T(128)}, s32[9]{0:T(128)S(1)}, u32[]{:S(2)}) copy-start(s32[9]{0:T(128)S(1)} %stack.41.place) | copy-start | bytes 112
  19.2 4.4 %copy-start.15 = (bf16[4,64,512]{2,1,0:T(8,128)(2,1)}, bf16[4,64,512]{2,1,0:T(8,128)(2,1)S(1)}, u32[]{:S(2)}) copy-start(bf16[4,64,512]{2,1,0:T(8,128)(2,1)S(1)} %collective-permute-done.2.x3) | copy-start | bytes 786436
  22.1 11.7 %copy-start.3 = (bf16[4,32,1664]{2,1,0:T(8,128)(2,1)}, bf16[4,32,1664]{2,1,0:T(8,128)(2,1)S(1)}, u32[]{:S(2)}) copy-start(bf16[4,32,1664]{2,1,0:T(8,128)(2,1)S(1)} %all-to-all-done.p0) | copy-start | bytes 1277956
  22.1 10.9 %collective-permute-start.3 = (bf16[4,32,1664]{2,1,0:T(8,128)(2,1)S(1)}, bf16[4,32,1664]{2,1,0:T(8,128)(2,1)}, u32[]{:S(2)}, u32[]{:S(2)}) collective-permute-start(bf16[4,32,1664]{2,1,0:T(8,128)(2,1)S(1)} %all-to-all-done.p0), channel_id=1, source_target_pairs={{0,4},{4,0},{1,5},{5,1},{2,6},{6,2},{3,7},{7,3},{8,12},{12,8},{9,1... | collective-permute-start | bytes 1277960 | tf_op jit(solution)/shard_map/ppermute | solution.py:548
  23.6 12.6 %copy-start.1 = (bf16[4,4,64,512]{3,2,1,0:T(8,128)(2,1)S(1)}, bf16[4,4,64,512]{3,2,1,0:T(8,128)(2,1)}, u32[]{:S(2)}) copy-start(bf16[4,4,64,512]{3,2,1,0:T(8,128)(2,1)} %param.19) | copy-start | bytes 3145732
  23.6 15.2 %collective-permute-start.4 = (bf16[4,32,1664]{2,1,0:T(8,128)(2,1)S(1)}, bf16[4,32,1664]{2,1,0:T(8,128)(2,1)}, u32[]{:S(2)}, u32[]{:S(2)}) collective-permute-start(bf16[4,32,1664]{2,1,0:T(8,128)(2,1)S(1)} %all-to-all-done.p0), channel_id=1, source_target_pairs={{0,1},{1,0},{2,3},{3,2},{4,5},{5,4},{6,7},{7,6},{8,9},{9,8},{10,11... | collective-permute-start | bytes 1277960 | tf_op jit(solution)/shard_map/ppermute | solution.py:548
  24.7 24.5 %all-to-all-start.1 = ((bf16[4,32,3072]{2,1,0:T(8,128)(2,1)}), bf16[4,32,3072]{2,1,0:T(8,128)(2,1)S(1)}, u32[]{:S(2)}, u32[]{:S(2)}) async-start(bf16[4,32,3072]{2,1,0:T(8,128)(2,1)} %broadcast_in_dim.7), calls=%async_computation.1 | async-start | bytes 1572864 | tf_op jit(solution)/shard_map/all_to_all | solution.py:567
  33.0 6.4 %collective-permute-start.5 = (bf16[4,32,1664]{2,1,0:T(8,128)(2,1)}, bf16[4,32,1664]{2,1,0:T(8,128)(2,1)}, u32[]{:S(2)}, u32[]{:S(2)}) collective-permute-start(bf16[4,32,1664]{2,1,0:T(8,128)(2,1)} %collective-permute-done.3.p1), channel_id=1, source_target_pairs={{0,1},{1,0},{2,3},{3,2},{4,5},{5,4},{6,7},{7,6},{8,9},{9,8},{10,11... | collective-permute-start | bytes 1277960 | tf_op jit(solution)/shard_map/ppermute | solution.py:548
  34.0 11.6 %collective-permute-start.12 = (bf16[32,1536]{1,0:T(8,128)(2,1)S(1)}, bf16[32,1536]{1,0:T(8,128)(2,1)S(1)}, u32[]{:S(2)}, u32[]{:S(2)}) collective-permute-start(bf16[32,1536]{1,0:T(8,128)(2,1)S(1)} %fusion.4), channel_id=1, source_target_pairs={{0,4},{4,0},{1,5},{5,1},{2,6},{6,2},{3,7},{7,3},{8,12},{12,8},{9,1... | collective-permute-start | bytes 294920 | tf_op jit(solution)/shard_map/ppermute | solution.py:548
  37.2 28.2 %collective-permute-start.10 = (bf16[4,64,512]{2,1,0:T(8,128)(2,1)}, bf16[4,64,512]{2,1,0:T(8,128)(2,1)}, u32[]{:S(2)}, u32[]{:S(2)}) collective-permute-start(bf16[4,64,512]{2,1,0:T(8,128)(2,1)} %get-tuple-element.212), channel_id=1, source_target_pairs={{0,3},{1,2},{2,1},{3,0},{4,7},{5,6},{6,5},{7,4},{8,11},{9,10},{10,... | collective-permute-start | bytes 786440 | tf_op jit(solution)/shard_map/ppermute | solution.py:560
  38.5 26.9 %collective-permute-start.8 = (bf16[4,64,512]{2,1,0:T(8,128)(2,1)}, bf16[4,64,512]{2,1,0:T(8,128)(2,1)}, u32[]{:S(2)}, u32[]{:S(2)}) collective-permute-start(bf16[4,64,512]{2,1,0:T(8,128)(2,1)} %get-tuple-element.214), channel_id=1, source_target_pairs={{0,1},{1,0},{2,3},{3,2},{4,5},{5,4},{6,7},{7,6},{8,9},{9,8},{10,11... | collective-permute-start | bytes 786440 | tf_op jit(solution)/shard_map/ppermute | solution.py:560
  38.8 26.6 %collective-permute-start.9 = (bf16[4,64,512]{2,1,0:T(8,128)(2,1)}, bf16[4,64,512]{2,1,0:T(8,128)(2,1)}, u32[]{:S(2)}, u32[]{:S(2)}) collective-permute-start(bf16[4,64,512]{2,1,0:T(8,128)(2,1)} %get-tuple-element.213), channel_id=1, source_target_pairs={{0,2},{1,3},{2,0},{3,1},{4,6},{5,7},{6,4},{7,5},{8,10},{9,11},{10,... | collective-permute-start | bytes 786440 | tf_op jit(solution)/shard_map/ppermute | solution.py:560
  49.2 16.2 %copy-start.2 = (bf16[4,32,3072]{2,1,0:T(8,128)(2,1)}, bf16[4,32,3072]{2,1,0:T(8,128)(2,1)S(1)}, u32[]{:S(2)}) copy-start(bf16[4,32,3072]{2,1,0:T(8,128)(2,1)S(1)} %all-to-all-done.1.b0) | copy-start | bytes 2359300
  49.2 19.3 %collective-permute-start.6 = (bf16[4,32,3072]{2,1,0:T(8,128)(2,1)S(1)}, bf16[4,32,3072]{2,1,0:T(8,128)(2,1)}, u32[]{:S(2)}, u32[]{:S(2)}) collective-permute-start(bf16[4,32,3072]{2,1,0:T(8,128)(2,1)S(1)} %all-to-all-done.1.b0), channel_id=1, source_target_pairs={{0,4},{4,0},{1,5},{5,1},{2,6},{6,2},{3,7},{7,3},{8,12},{12,8},{9,1... | collective-permute-start | bytes 2359304 | tf_op jit(solution)/shard_map/ppermute | solution.py:548
  49.7 18.7 %collective-permute-start.7 = (bf16[4,32,3072]{2,1,0:T(8,128)(2,1)S(1)}, bf16[4,32,3072]{2,1,0:T(8,128)(2,1)}, u32[]{:S(2)}, u32[]{:S(2)}) collective-permute-start(bf16[4,32,3072]{2,1,0:T(8,128)(2,1)S(1)} %all-to-all-done.1.b0), channel_id=1, source_target_pairs={{0,1},{1,0},{2,3},{3,2},{4,5},{5,4},{6,7},{7,6},{8,9},{9,8},{10,11... | collective-permute-start | bytes 2359304 | tf_op jit(solution)/shard_map/ppermute | solution.py:548
  50.7 25.3 %all-to-all-start.2 = ((bf16[4,2,32,1536]{3,2,1,0:T(8,128)(2,1)}), bf16[4,2,32,1536]{3,2,1,0:T(8,128)(2,1)}, u32[]{:S(2)}, u32[]{:S(2)}) async-start(bf16[4,2,32,1536]{3,2,1,0:T(8,128)(2,1)} %broadcast_in_dim.8), calls=%async_computation.2 | async-start | bytes 1572864 | tf_op jit(solution)/shard_map/all_to_all | solution.py:567
  68.4 7.5 %collective-permute-start.11 = (bf16[4,32,3072]{2,1,0:T(8,128)(2,1)}, bf16[4,32,3072]{2,1,0:T(8,128)(2,1)S(1)}, u32[]{:S(2)}, u32[]{:S(2)}) collective-permute-start(bf16[4,32,3072]{2,1,0:T(8,128)(2,1)} %collective-permute-done.6.b1), channel_id=1, source_target_pairs={{0,1},{1,0},{2,3},{3,2},{4,5},{5,4},{6,7},{7,6},{8,9},{9,8},{10,11... | collective-permute-start | bytes 2359304 | tf_op jit(solution)/shard_map/ppermute | solution.py:548
  76.0 31.0 %copy-start.12 = (s32[9]{0:T(128)S(1)}, s32[9]{0:T(128)}, u32[]{:S(2)}) copy-start(s32[9]{0:T(128)} %copy-done.11) | copy-start | bytes 112
  76.0 2.6 %collective-permute-start.13 = (bf16[4,2,32,1536]{3,2,1,0:T(8,128)(2,1)}, bf16[4,2,32,1536]{3,2,1,0:T(8,128)(2,1)}, u32[]{:S(2)}, u32[]{:S(2)}) collective-permute-start(bf16[4,2,32,1536]{3,2,1,0:T(8,128)(2,1)} %all-to-all-done.2.c0), channel_id=1, source_target_pairs={{0,1},{1,0},{2,3},{3,2},{4,5},{5,4},{6,7},{7,6},{8,9},{9,8},{10,11... | collective-permute-start | bytes 2359304 | tf_op jit(solution)/shard_map/ppermute | solution.py:548
  106.4 16.2 %collective-permute-start.20 = (bf16[2,2,4,64,640]{4,3,2,1,0:T(8,128)(2,1)}, bf16[2,2,4,64,640]{4,3,2,1,0:T(8,128)(2,1)}, u32[]{:S(2)}, u32[]{:S(2)}) collective-permute-start(bf16[2,2,4,64,640]{4,3,2,1,0:T(8,128)(2,1)} %get-tuple-element.158), channel_id=1, source_target_pairs={{0,1},{1,0},{2,3},{3,2},{4,5},{5,4},{6,7},{7,6},{8,9},{9,8},{10,11... | collective-permute-start | bytes 3932168 | tf_op jit(solution)/shard_map/ppermute | solution.py:548
  106.6 16.0 %collective-permute-start.21 = (bf16[2,2,4,64,512]{4,3,2,1,0:T(8,128)(2,1)}, bf16[2,2,4,64,512]{4,3,2,1,0:T(8,128)(2,1)}, u32[]{:S(2)}, u32[]{:S(2)}) collective-permute-start(bf16[2,2,4,64,512]{4,3,2,1,0:T(8,128)(2,1)} %get-tuple-element.159), channel_id=1, source_target_pairs={{0,1},{1,0},{2,3},{3,2},{4,5},{5,4},{6,7},{7,6},{8,9},{9,8},{10,11... | collective-permute-start | bytes 3145736 | tf_op jit(solution)/shard_map/ppermute | solution.py:548
  107.0 12.3 %collective-permute-start.14 = (bf16[4,64,512]{2,1,0:T(8,128)(2,1)}, bf16[4,64,512]{2,1,0:T(8,128)(2,1)S(1)}, u32[]{:S(2)}, u32[]{:S(2)}) collective-permute-start(bf16[4,64,512]{2,1,0:T(8,128)(2,1)} %get-tuple-element.155), channel_id=1, source_target_pairs={{0,1},{1,0},{2,3},{3,2},{4,5},{5,4},{6,7},{7,6},{8,9},{9,8},{10,11... | collective-permute-start | bytes 786440 | tf_op jit(solution)/shard_map/ppermute | solution.py:560
  107.2 12.7 %collective-permute-start.15 = (bf16[4,64,512]{2,1,0:T(8,128)(2,1)}, bf16[4,64,512]{2,1,0:T(8,128)(2,1)S(1)}, u32[]{:S(2)}, u32[]{:S(2)}) collective-permute-start(bf16[4,64,512]{2,1,0:T(8,128)(2,1)} %get-tuple-element.156), channel_id=1, source_target_pairs={{0,2},{1,3},{2,0},{3,1},{4,6},{5,7},{6,4},{7,5},{8,10},{9,11},{10,... | collective-permute-start | bytes 786440 | tf_op jit(solution)/shard_map/ppermute | solution.py:560
  108.8 12.7 %collective-permute-start.16 = (bf16[4,64,512]{2,1,0:T(8,128)(2,1)}, bf16[4,64,512]{2,1,0:T(8,128)(2,1)S(1)}, u32[]{:S(2)}, u32[]{:S(2)}) collective-permute-start(bf16[4,64,512]{2,1,0:T(8,128)(2,1)} %get-tuple-element.157), channel_id=1, source_target_pairs={{0,3},{1,2},{2,1},{3,0},{4,7},{5,6},{6,5},{7,4},{8,11},{9,10},{10,... | collective-permute-start | bytes 786440 | tf_op jit(solution)/shard_map/ppermute | solution.py:560
  119.4 7.1 %copy-start.16 = (bf16[4,64,512]{2,1,0:T(8,128)(2,1)}, bf16[4,64,512]{2,1,0:T(8,128)(2,1)S(1)}, u32[]{:S(2)}) copy-start(bf16[4,64,512]{2,1,0:T(8,128)(2,1)S(1)} %collective-permute-done.14.refs_1_) | copy-start | bytes 786436
  119.4 13.4 %collective-permute-start.17 = (bf16[2,64,512]{2,1,0:T(8,128)(2,1)}, bf16[2,64,512]{2,1,0:T(8,128)(2,1)}, u32[]{:S(2)}, u32[]{:S(2)}) collective-permute-start(bf16[2,64,512]{2,1,0:T(8,128)(2,1)} %get-tuple-element.166), channel_id=1, source_target_pairs={{0,1},{1,0},{2,3},{3,2},{4,5},{5,4},{6,7},{7,6},{8,9},{9,8},{10,11... | collective-permute-start | bytes 393224 | tf_op jit(solution)/shard_map/ppermute | solution.py:560
  119.9 6.5 %copy-start.17 = (bf16[4,64,512]{2,1,0:T(8,128)(2,1)}, bf16[4,64,512]{2,1,0:T(8,128)(2,1)S(1)}, u32[]{:S(2)}) copy-start(bf16[4,64,512]{2,1,0:T(8,128)(2,1)S(1)} %collective-permute-done.15.refs_2_) | copy-start | bytes 786436
  119.9 28.5 %collective-permute-start.18 = (bf16[2,64,512]{2,1,0:T(8,128)(2,1)}, bf16[2,64,512]{2,1,0:T(8,128)(2,1)}, u32[]{:S(2)}, u32[]{:S(2)}) collective-permute-start(bf16[2,64,512]{2,1,0:T(8,128)(2,1)} %get-tuple-element.167), channel_id=1, source_target_pairs={{0,2},{1,3},{2,0},{3,1},{4,6},{5,7},{6,4},{7,5},{8,10},{9,11},{10,... | collective-permute-start | bytes 393224 | tf_op jit(solution)/shard_map/ppermute | solution.py:560
  121.4 5.0 %copy-start.18 = (bf16[4,64,512]{2,1,0:T(8,128)(2,1)}, bf16[4,64,512]{2,1,0:T(8,128)(2,1)S(1)}, u32[]{:S(2)}) copy-start(bf16[4,64,512]{2,1,0:T(8,128)(2,1)S(1)} %collective-permute-done.16.refs_3_) | copy-start | bytes 786436
  121.4 27.0 %collective-permute-start.19 = (bf16[2,64,512]{2,1,0:T(8,128)(2,1)}, bf16[2,64,512]{2,1,0:T(8,128)(2,1)}, u32[]{:S(2)}, u32[]{:S(2)}) collective-permute-start(bf16[2,64,512]{2,1,0:T(8,128)(2,1)} %get-tuple-element.168), channel_id=1, source_target_pairs={{0,3},{1,2},{2,1},{3,0},{4,7},{5,6},{6,5},{7,4},{8,11},{9,10},{10,... | collective-permute-start | bytes 393224 | tf_op jit(solution)/shard_map/ppermute | solution.py:560
  126.4 33.7 %all-to-all-start.4 = ((bf16[4,4,64,512]{3,2,1,0:T(8,128)(2,1)}), bf16[4,4,64,512]{3,2,1,0:T(8,128)(2,1)}, u32[]{:S(2)}, u32[]{:S(2)}) async-start(bf16[4,4,64,512]{3,2,1,0:T(8,128)(2,1)} %get-tuple-element.180), calls=%async_computation.4 | async-start | bytes 2097152 | tf_op jit(solution)/shard_map/all_to_all | solution.py:879
  130.7 17.7 %collective-permute-start.22 = (bf16[4,64,640]{2,1,0:T(8,128)(2,1)}, bf16[4,64,640]{2,1,0:T(8,128)(2,1)S(1)}, u32[]{:S(2)}, u32[]{:S(2)}) collective-permute-start(bf16[4,64,640]{2,1,0:T(8,128)(2,1)} %get-tuple-element.178), channel_id=1, source_target_pairs={{0,4},{2,6},{4,0},{6,2},{1,5},{3,7},{5,1},{7,3},{8,12},{10,14},{12... | collective-permute-start | bytes 983048 | tf_op jit(solution)/shard_map/ppermute | solution.py:855
  132.3 16.6 %collective-permute-start.23 = (bf16[4,64,640]{2,1,0:T(8,128)(2,1)}, bf16[4,64,640]{2,1,0:T(8,128)(2,1)S(1)}, u32[]{:S(2)}, u32[]{:S(2)}) collective-permute-start(bf16[4,64,640]{2,1,0:T(8,128)(2,1)} %get-tuple-element.177), channel_id=1, source_target_pairs={{0,2},{2,0},{4,6},{6,4},{1,3},{3,1},{5,7},{7,5},{8,10},{10,8},{12,... | collective-permute-start | bytes 983048 | tf_op jit(solution)/shard_map/ppermute | solution.py:855
  132.8 16.2 %collective-permute-start.24 = (bf16[4,64,640]{2,1,0:T(8,128)(2,1)}, bf16[4,64,640]{2,1,0:T(8,128)(2,1)S(1)}, u32[]{:S(2)}, u32[]{:S(2)}) collective-permute-start(bf16[4,64,640]{2,1,0:T(8,128)(2,1)} %get-tuple-element.179), channel_id=1, source_target_pairs={{0,6},{2,4},{4,2},{6,0},{1,7},{3,5},{5,3},{7,1},{8,14},{10,12},{12... | collective-permute-start | bytes 983048 | tf_op jit(solution)/shard_map/ppermute | solution.py:855
  149.0 2.5 %collective-permute-start.25 = (bf16[2,2,4,64,384]{4,3,2,1,0:T(8,128)(2,1)}, bf16[2,2,4,64,384]{4,3,2,1,0:T(8,128)(2,1)S(1)}, u32[]{:S(2)}, u32[]{:S(2)}) collective-permute-start(bf16[2,2,4,64,384]{4,3,2,1,0:T(8,128)(2,1)} %get-tuple-element.189), channel_id=1, source_target_pairs={{0,1},{1,0},{2,3},{3,2},{4,5},{5,4},{6,7},{7,6},{8,9},{9,8},{10,11... | collective-permute-start | bytes 2359304 | tf_op jit(solution)/shard_map/ppermute | solution.py:548
  152.3 5.9 %copy-start.4 = (bf16[4,64,640]{2,1,0:T(8,128)(2,1)S(1)}, bf16[4,64,640]{2,1,0:T(8,128)(2,1)}, u32[]{:S(2)}) copy-start(bf16[4,64,640]{2,1,0:T(8,128)(2,1)} %get-tuple-element.176) | copy-start | bytes 983044
  154.8 13.5 %collective-permute-start.26 = (bf16[4,80,384]{2,1,0:T(8,128)(2,1)}, bf16[4,80,384]{2,1,0:T(8,128)(2,1)S(1)}, u32[]{:S(2)}, u32[]{:S(2)}) collective-permute-start(bf16[4,80,384]{2,1,0:T(8,128)(2,1)} %get-tuple-element.192), channel_id=1, source_target_pairs={{0,4},{2,6},{4,0},{6,2},{1,5},{3,7},{5,1},{7,3},{8,12},{10,14},{12... | collective-permute-start | bytes 737288 | tf_op jit(solution)/shard_map/ppermute | solution.py:855
  155.8 14.1 %collective-permute-start.27 = (bf16[4,80,384]{2,1,0:T(8,128)(2,1)}, bf16[4,80,384]{2,1,0:T(8,128)(2,1)S(1)}, u32[]{:S(2)}, u32[]{:S(2)}) collective-permute-start(bf16[4,80,384]{2,1,0:T(8,128)(2,1)} %get-tuple-element.193), channel_id=1, source_target_pairs={{0,2},{2,0},{4,6},{6,4},{1,3},{3,1},{5,7},{7,5},{8,10},{10,8},{12,... | collective-permute-start | bytes 737288 | tf_op jit(solution)/shard_map/ppermute | solution.py:855
  156.5 13.5 %collective-permute-start.28 = (bf16[4,80,384]{2,1,0:T(8,128)(2,1)}, bf16[4,80,384]{2,1,0:T(8,128)(2,1)S(1)}, u32[]{:S(2)}, u32[]{:S(2)}) collective-permute-start(bf16[4,80,384]{2,1,0:T(8,128)(2,1)} %get-tuple-element.194), channel_id=1, source_target_pairs={{0,6},{2,4},{4,2},{6,0},{1,7},{3,5},{5,3},{7,1},{8,14},{10,12},{12... | collective-permute-start | bytes 737288 | tf_op jit(solution)/shard_map/ppermute | solution.py:855
  160.1 9.8 %copy-start.6 = (bf16[4,80,384]{2,1,0:T(8,128)(2,1)S(1)}, bf16[4,80,384]{2,1,0:T(8,128)(2,1)}, u32[]{:S(2)}) copy-start(bf16[4,80,384]{2,1,0:T(8,128)(2,1)} %get-tuple-element.191) | copy-start | bytes 737284
  160.1 14.6 %all-to-all-start.3 = ((bf16[4,64,640]{2,1,0:T(8,128)(2,1)}), bf16[4,64,640]{2,1,0:T(8,128)(2,1)S(1)}, u32[]{:S(2)}, u32[]{:S(2)}) async-start(bf16[4,64,640]{2,1,0:T(8,128)(2,1)} %add_convert_fusion), calls=%async_computation.3 | async-start | bytes 655360 | tf_op jit(solution)/shard_map/all_to_all | solution.py:915
  166.4 8.4 %collective-permute-start.29 = (bf16[64,512]{1,0:T(8,128)(2,1)S(1)}, bf16[64,512]{1,0:T(8,128)(2,1)S(1)}, u32[]{:S(2)}, u32[]{:S(2)}) collective-permute-start(bf16[64,512]{1,0:T(8,128)(2,1)S(1)} %get-tuple-element.222), channel_id=1, source_target_pairs={{0,4},{2,6},{4,0},{6,2},{1,5},{3,7},{5,1},{7,3},{8,12},{10,14},{12... | collective-permute-start | bytes 196616 | tf_op jit(solution)/shard_map/ppermute | solution.py:855
  167.8 6.9 %collective-permute-start.30 = (bf16[64,512]{1,0:T(8,128)(2,1)S(1)}, bf16[64,512]{1,0:T(8,128)(2,1)S(1)}, u32[]{:S(2)}, u32[]{:S(2)}) collective-permute-start(bf16[64,512]{1,0:T(8,128)(2,1)S(1)} %get-tuple-element.224), channel_id=1, source_target_pairs={{0,2},{2,0},{4,6},{6,4},{1,3},{3,1},{5,7},{7,5},{8,10},{10,8},{12,... | collective-permute-start | bytes 196616 | tf_op jit(solution)/shard_map/ppermute | solution.py:855
  168.3 6.5 %collective-permute-start.31 = (bf16[64,512]{1,0:T(8,128)(2,1)S(1)}, bf16[64,512]{1,0:T(8,128)(2,1)S(1)}, u32[]{:S(2)}, u32[]{:S(2)}) collective-permute-start(bf16[64,512]{1,0:T(8,128)(2,1)S(1)} %get-tuple-element.223), channel_id=1, source_target_pairs={{0,6},{2,4},{4,2},{6,0},{1,7},{3,5},{5,3},{7,1},{8,14},{10,12},{12... | collective-permute-start | bytes 196616 | tf_op jit(solution)/shard_map/ppermute | solution.py:855
  174.8 10.4 %all-to-all-start.5 = ((bf16[4,80,384]{2,1,0:T(8,128)(2,1)}), bf16[4,80,384]{2,1,0:T(8,128)(2,1)S(1)}, u32[]{:S(2)}, u32[]{:S(2)}) async-start(bf16[4,80,384]{2,1,0:T(8,128)(2,1)} %add_convert_fusion.1), calls=%async_computation.5 | async-start | bytes 491520 | tf_op jit(solution)/shard_map/all_to_all | solution.py:918
  178.6 9.9 %copy-start.7 = (bf16[64,1152]{1,0:T(8,128)(2,1)}, bf16[64,1152]{1,0:T(8,128)(2,1)S(1)}, u32[]{:S(2)}) copy-start(bf16[64,1152]{1,0:T(8,128)(2,1)S(1)} %pad_maximum_fusion.2.m0) | copy-start | bytes 442372
  178.6 6.7 %collective-permute-start.32 = (bf16[64,1152]{1,0:T(8,128)(2,1)S(1)}, bf16[64,1152]{1,0:T(8,128)(2,1)S(1)}, u32[]{:S(2)}, u32[]{:S(2)}) collective-permute-start(bf16[64,1152]{1,0:T(8,128)(2,1)S(1)} %pad_maximum_fusion.2.m0), channel_id=1, source_target_pairs={{0,2},{1,3},{2,0},{3,1},{4,6},{5,7},{6,4},{7,5},{8,10},{9,11},{10,... | collective-permute-start | bytes 442376 | tf_op jit(solution)/shard_map/ppermute | solution.py:599
  180.2 5.1 %collective-permute-start.33 = (bf16[64,1152]{1,0:T(8,128)(2,1)S(1)}, bf16[64,1152]{1,0:T(8,128)(2,1)S(1)}, u32[]{:S(2)}, u32[]{:S(2)}) collective-permute-start(bf16[64,1152]{1,0:T(8,128)(2,1)S(1)} %pad_maximum_fusion.2.m0), channel_id=1, source_target_pairs={{0,1},{1,0},{2,3},{3,2},{4,5},{5,4},{6,7},{7,6},{8,9},{9,8},{10,11... | collective-permute-start | bytes 442376 | tf_op jit(solution)/shard_map/ppermute | solution.py:599
  180.2 6.1 %collective-permute-start.34 = (bf16[64,1152]{1,0:T(8,128)(2,1)S(1)}, bf16[64,1152]{1,0:T(8,128)(2,1)S(1)}, u32[]{:S(2)}, u32[]{:S(2)}) collective-permute-start(bf16[64,1152]{1,0:T(8,128)(2,1)S(1)} %pad_maximum_fusion.2.m0), channel_id=1, source_target_pairs={{0,3},{1,2},{2,1},{3,0},{4,7},{5,6},{6,5},{7,4},{8,11},{9,10},{10,... | collective-permute-start | bytes 442376 | tf_op jit(solution)/shard_map/ppermute | solution.py:599
  185.3 5.3 %copy-start.8 = (bf16[80,384]{1,0:T(8,128)(2,1)}, bf16[80,384]{1,0:T(8,128)(2,1)S(1)}, u32[]{:S(2)}) copy-start(bf16[80,384]{1,0:T(8,128)(2,1)S(1)} %reduce_sum.38.a0) | copy-start | bytes 184324
  186.4 4.3 %collective-permute-start.35 = (bf16[80,384]{1,0:T(8,128)(2,1)S(1)}, bf16[80,384]{1,0:T(8,128)(2,1)S(1)}, u32[]{:S(2)}, u32[]{:S(2)}) collective-permute-start(bf16[80,384]{1,0:T(8,128)(2,1)S(1)} %reduce_sum.38.a0), channel_id=1, source_target_pairs={{0,2},{1,3},{2,0},{3,1},{4,6},{5,7},{6,4},{7,5},{8,10},{9,11},{10,... | collective-permute-start | bytes 184328 | tf_op jit(solution)/shard_map/ppermute | solution.py:599
  187.0 3.8 %collective-permute-start.36 = (bf16[80,384]{1,0:T(8,128)(2,1)S(1)}, bf16[80,384]{1,0:T(8,128)(2,1)S(1)}, u32[]{:S(2)}, u32[]{:S(2)}) collective-permute-start(bf16[80,384]{1,0:T(8,128)(2,1)S(1)} %reduce_sum.38.a0), channel_id=1, source_target_pairs={{0,1},{1,0},{2,3},{3,2},{4,5},{5,4},{6,7},{7,6},{8,9},{9,8},{10,11... | collective-permute-start | bytes 184328 | tf_op jit(solution)/shard_map/ppermute | solution.py:599
  188.0 4.1 %collective-permute-start.37 = (bf16[80,384]{1,0:T(8,128)(2,1)S(1)}, bf16[80,384]{1,0:T(8,128)(2,1)S(1)}, u32[]{:S(2)}, u32[]{:S(2)}) collective-permute-start(bf16[80,384]{1,0:T(8,128)(2,1)S(1)} %reduce_sum.38.a0), channel_id=1, source_target_pairs={{0,3},{1,2},{2,1},{3,0},{4,7},{5,6},{6,5},{7,4},{8,11},{9,10},{10,... | collective-permute-start | bytes 184328 | tf_op jit(solution)/shard_map/ppermute | solution.py:599
  194.5 12.1 %all-to-all-start.6 = ((f32[8,8,128]{2,1,0:T(8,128)}), f32[8,8,128]{2,1,0:T(8,128)S(1)}, u32[]{:S(2)}, u32[]{:S(2)}) async-start(f32[8,8,128]{2,1,0:T(8,128)} %squares.1), calls=%async_computation.6 | async-start | bytes 65536 | tf_op jit(solution)/shard_map/all_to_all | solution.py:959
  199.9 3.5 %copy-start.22 = (bf16[2,64,512]{2,1,0:T(8,128)(2,1)S(1)}, bf16[2,64,512]{2,1,0:T(8,128)(2,1)}, u32[]{:S(2)}) copy-start(bf16[2,64,512]{2,1,0:T(8,128)(2,1)} %get-tuple-element.201) | copy-start | bytes 393220
  202.2 10.9 %collective-permute-start.38 = (bf16[2,64,512]{2,1,0:T(8,128)(2,1)S(1)}, bf16[2,64,512]{2,1,0:T(8,128)(2,1)S(1)}, u32[]{:S(2)}, u32[]{:S(2)}) collective-permute-start(bf16[2,64,512]{2,1,0:T(8,128)(2,1)S(1)} %copy-done.24), channel_id=1, source_target_pairs={{0,1},{1,0},{2,3},{3,2},{4,5},{5,4},{6,7},{7,6},{8,9},{9,8},{10,11... | collective-permute-start | bytes 393224 | tf_op jit(solution)/shard_map/ppermute | solution.py:560
  202.2 11.0 %collective-permute-start.39 = (bf16[2,64,512]{2,1,0:T(8,128)(2,1)S(1)}, bf16[2,64,512]{2,1,0:T(8,128)(2,1)S(1)}, u32[]{:S(2)}, u32[]{:S(2)}) collective-permute-start(bf16[2,64,512]{2,1,0:T(8,128)(2,1)S(1)} %copy-done.23), channel_id=1, source_target_pairs={{0,2},{1,3},{2,0},{3,1},{4,6},{5,7},{6,4},{7,5},{8,10},{9,11},{10,... | collective-permute-start | bytes 393224 | tf_op jit(solution)/shard_map/ppermute | solution.py:560
  203.4 9.8 %collective-permute-start.40 = (bf16[2,64,512]{2,1,0:T(8,128)(2,1)S(1)}, bf16[2,64,512]{2,1,0:T(8,128)(2,1)S(1)}, u32[]{:S(2)}, u32[]{:S(2)}) collective-permute-start(bf16[2,64,512]{2,1,0:T(8,128)(2,1)S(1)} %copy-done.22), channel_id=1, source_target_pairs={{0,3},{1,2},{2,1},{3,0},{4,7},{5,6},{6,5},{7,4},{8,11},{9,10},{10,... | collective-permute-start | bytes 393224 | tf_op jit(solution)/shard_map/ppermute | solution.py:560
  (17 other events, 27.5 us)

commit v6 on v5

--- a/solution.py
+++ b/solution.py
@@ -18,7 +18,7 @@
 WEIGHT_DECAY = 0.01
 ADAM_EPS = 1e-08
 NORM_EPS = 1e-05
-VMEM_BYTES = 63 * 1024 * 1024
+VMEM_BYTES = 65408 * 1024
 
 F32 = jnp.float32
 BF16 = jnp.bfloat16
@@ -148,23 +148,31 @@
     row = pl.program_id(0) + place[4]
     width = attn_out.shape[1]
     pair = 2 * (width // HEADS)
+    half = pair // 2
     fill_bias(place, lengths, row, bias)
     masks = head_masks(pair)
+
+    def score(h):
+        at = (h // 2) * pair
+        return nt_dot(qkv[:, width + at : width + at + pair], qkv[:, at : at + pair] * masks[h % 2])
+
+    def soft(h, scores):
+        scores = scores + bias[...]
+        top = jnp.max(scores, axis=0, keepdims=True)
+        grown = jnp.exp(scores - top)
+        total = jnp.sum(grown, axis=0, keepdims=True)
+        lse_out[0, h : h + 1, :] = top + jnp.log(total)
+        return (grown * (1.0 / total)).astype(BF16)
+
+    def value(h, turned, probs):
+        return nn_dot(turned[(h % 2) * half : (h % 2 + 1) * half], probs)
+
+    turned = [qkv[:, 2 * width + p * pair : 2 * width + (p + 1) * pair].T for p in range(HEADS // 2)]
+    scores = [score(h) for h in range(HEADS)]
+    probs = [soft(h, scores[h]) for h in range(HEADS)]
+    outs = [value(h, turned[h // 2], probs[h]) for h in range(HEADS)]
     for p in range(HEADS // 2):
-        at = p * pair
-        qp = qkv[:, at : at + pair]
-        kp = qkv[:, width + at : width + at + pair]
-        v_turned = qkv[:, 2 * width + at : 2 * width + at + pair].T
-        outs = []
-        for i in range(2):
-            scores = nt_dot(kp, qp * masks[i]) + bias[...]
-            top = jnp.max(scores, axis=0, keepdims=True)
-            grown = jnp.exp(scores - top)
-            total = jnp.sum(grown, axis=0, keepdims=True)
-            lse_out[0, 2 * p + i : 2 * p + i + 1, :] = top + jnp.log(total)
-            probs = (grown * (1.0 / total)).astype(BF16)
-            outs.append(nn_dot(v_turned[i * (pair // 2) : (i + 1) * (pair // 2)], probs))
-        attn_out[:, at : at + pair] = jnp.concatenate(outs, axis=0).T.astype(BF16)
+        attn_out[:, p * pair : (p + 1) * pair] = jnp.concatenate(outs[2 * p : 2 * p + 2], axis=0).T.astype(BF16)
 
 
 def write_parts(parts, half, y, column, value, dims):
@@ -304,33 +312,34 @@
 
     fill_bias(place, lengths, step + place[4], bias)
     masks = head_masks(pair)
-    for p in range(HEADS // 2):
-        at = p * pair
-        qp = qkv[:, at : at + pair]
-        kp = qkv[:, width + at : width + at + pair]
-        vp = qkv[:, 2 * width + at : 2 * width + at + pair]
-        gp = dattn[:, at : at + pair]
-        k_turned = kp.T
-        probs_list, ds_list, dq_list, q_list, g_list = [], [], [], [], []
-        for i in range(2):
-            qh = qp * masks[i]
-            gh = gp * masks[i]
-            scores = nt_dot(kp, qh) + bias[...]
-            probs = jnp.exp(scores - lse[0, 2 * p + i : 2 * p + i + 1, :])
-            dprobs = nt_dot(vp, gh)
-            inner = jnp.sum(probs * dprobs, axis=0, keepdims=True)
-            ds = (probs * (dprobs - inner)).astype(BF16)
-            dq_list.append(nn_dot(k_turned[i * (pair // 2) : (i + 1) * (pair // 2)], ds))
-            probs_list.append(probs.astype(BF16))
-            ds_list.append(ds)
-            q_list.append(qh)
-            g_list.append(gh)
-        dq = jnp.concatenate(dq_list, axis=0).T * score_scale
-        dk = nn_dot(jnp.concatenate(ds_list, axis=1), jnp.concatenate(q_list, axis=0))
-        dv = nn_dot(jnp.concatenate(probs_list, axis=1), jnp.concatenate(g_list, axis=0))
-        dqkv[:, at : at + pair] = dq.astype(BF16)
-        dqkv[:, width + at : width + at + pair] = dk.astype(BF16)
-        dqkv[:, 2 * width + at : 2 * width + at + pair] = dv.astype(BF16)
+    half = pair // 2
+    pairs = range(HEADS // 2)
+
+    def part(base, p):
+        return qkv[:, base + p * pair : base + (p + 1) * pair]
+
+    grads = [dattn[:, p * pair : (p + 1) * pair] for p in pairs]
+    qs = [part(0, h // 2) * masks[h % 2] for h in range(HEADS)]
+    gs = [grads[h // 2] * masks[h % 2] for h in range(HEADS)]
+    k_turned = [part(width, p).T for p in pairs]
+    scores = [nt_dot(part(width, h // 2), qs[h]) for h in range(HEADS)]
+    dprobs = [nt_dot(part(2 * width, h // 2), gs[h]) for h in range(HEADS)]
+    probs_low, ds = [], []
+    for h in range(HEADS):
+        probs = jnp.exp(scores[h] + bias[...] - lse[0, h : h + 1, :])
+        inner = jnp.sum(probs * dprobs[h], axis=0, keepdims=True)
+        ds.append((probs * (dprobs[h] - inner)).astype(BF16))
+        probs_low.append(probs.astype(BF16))
+    dqs = [nn_dot(k_turned[h // 2][(h % 2) * half : (h % 2 + 1) * half], ds[h]) for h in range(HEADS)]
+    for p in pairs:
+        two = slice(2 * p, 2 * p + 2)
+        queries, given = jnp.concatenate(qs[two], axis=0), jnp.concatenate(gs[two], axis=0)
+        dk = nn_dot(jnp.concatenate(ds[two], axis=1), queries)
+        dv = nn_dot(jnp.concatenate(probs_low[two], axis=1), given)
+        dq = jnp.concatenate(dqs[two], axis=0).T * score_scale
+        dqkv[:, p * pair : (p + 1) * pair] = dq.astype(BF16)
+        dqkv[:, width + p * pair : width + (p + 1) * pair] = dk.astype(BF16)
+        dqkv[:, 2 * width + p * pair : 2 * width + (p + 1) * pair] = dv.astype(BF16)
 
     @pl.when(step == 0)
     def _():
@@ -905,6 +914,7 @@
         qkv_send = after(qkv_send, *up_moved, *input_first)
     qkv_got = swap(qkv_send, "core")
 
+    input_last = from_seq(input_last)
     if fits:
         _, _, _, more_rows, more_cols = qkv_keep.shape
         piece = shape_of((hi_count, more_rows + 16, more_cols), BF16)
@@ -914,7 +924,8 @@
         up_plane = after(add_moved(up_moved), *parts)
         up_mine = total(lax.all_to_all(up_plane, "hi", 0, 0))
         down_mine = add_moved(down_moved)
-        qkv_plane = after(add_moved(qkv_moved), up_mine, down_mine)
+        qkv_moved = lax.optimization_barrier((*qkv_moved, *input_last))[:4]
+        qkv_plane = after(add_moved(qkv_moved), up_mine)
         qkv_mine = total(lax.all_to_all(qkv_plane, "hi", 0, 0))
     else:
         vec_total = vec_last.reshape(16, hi_count, 2, vec_cols)
@@ -928,7 +939,6 @@
     mlp_mine = jnp.concatenate([up_mine, down_mine], axis=1)
     mlp_pieces = to_all(mlp_mine)
     attn_pieces = to_all(after(qkv_mine, *mlp_pieces))
-    input_last = from_seq(lax.optimization_barrier((*input_last, *attn_pieces))[:4])
     input_grad = collect([*input_first, *input_last])
 
     dp_count = 2 * hi_count

time: 218 us -> 214 us (0.982)
  Pallas kernels: 94.4 us -> 83.1 us
  waiting for transfers between devices: 36.2 us -> 45 us
  local copies, waits for them, and re-layouts: 15.9 us -> 10 us
  starting transfers between devices: 62.7 us -> 65.4 us
    pallas_call x2, Pallas kernels: 15.3 us -> 8.28 us  [attend(): call(attend_body, steps, [SMEM, SMEM, half_spec((slots, 3 * width), base)...]
    ppermute x15, waiting for transfers between devices: 0.04 us -> 5.9 us  [from_seq(): lax.ppermute(pieces[k], ('y', 'core'), [(j, j ^ k) for j in range(4)])]
    all_to_all x1, waiting for transfers between devices: 3.91 us -> 0.01 us  [on_device(): up_mine = total(lax.all_to_all(up_plane, 'hi', 0, 0))]
    ppermute x9, waiting for transfers between devices: 0.55 us -> 3.93 us  [plane_sum(): moved.append(lax.ppermute(parts[k], ('lo', 'y'), perm))]
    ppermute x11, waiting for transfers between devices: 12.9 us -> 15.8 us  [swap(): return lax.ppermute(value, axis, [(0, 1), (1, 0)])]
    all_to_all x1, waiting for transfers between devices: 4.41 us -> 1.64 us  [on_device(): qkv_mine = total(lax.all_to_all(qkv_plane, 'hi', 0, 0))]
    unnamed x70 -> x38, local copies, waits for them, and re-layouts: 4.07 us -> 1.65 us
  transfers between devices with their start and end apart: 48 -> 48, of which waited for: 14 -> 15; matrix products, arithmetic and copies ran while one was open for 7% -> 7% of each run, Pallas kernels for 29% -> 22%
where the time goes in v6:
time: 214 us; the launch traced here: 213 us
  Pallas kernels  83.1 us (39%)
  starting transfers between devices  65.4 us (31%)
  waiting for transfers between devices  45 us (21%)
  local copies, waits for them, and re-layouts  10 us (5%)
  other arithmetic  8.45 us (4%)
    pallas_call x1, Pallas kernels, on_device(): call(functools.partial(mlp_body, dims), rows // group, [SMEM, *[slot_spec...  27.8 us
    ppermute x11, waiting for transfers between devices, swap(): return lax.ppermute(value, axis, [(0, 1), (1, 0)])  15.8 us
    all_to_all x3, starting transfers between devices, spread_hi(): return lax.all_to_all(spread, 'hi', 0, 0)  14.8 us
    ppermute x15, starting transfers between devices, from_seq(): lax.ppermute(pieces[k], ('y', 'core'), [(j, j ^ k) for j in range(4)])  12.1 us
    pallas_call x1, Pallas kernels, on_device(): call(functools.partial(back_last_body, dims), rows - lead, [*back_specs(l...  12 us
    all_to_all x3, waiting for transfers between devices, spread_hi(): return lax.all_to_all(spread, 'hi', 0, 0)  10.6 us
    ppermute x9, starting transfers between devices, plane_sum(): moved.append(lax.ppermute(parts[k], ('lo', 'y'), perm))  10.6 us
    pallas_call x1, Pallas kernels, on_device(): call(back_first_body, lead, back_specs(0), [*[half_spec((1, part, width),...  8.33 us
  transfers between devices with their start and end apart: 48, of which 15 were waited for; matrix products, arithmetic and copies ran while one was open for 7% of the time, Pallas kernels for 22%

profile of v6, /device:TPU:0, one launch (start us, length us, event | category | flops | bytes accessed | tf_op | source)
XLA Modules:
  0.0 213.3 jit_solution(3077176953781898309)
XLA Ops:
  0.7 1.1 slice.64
  1.8 0.7 convert.31
  2.6 0.8 broadcast_in_dim.6
  3.4 6.4 %all-to-all-start = ((bf16[4,32,1664]{2,1,0:T(8,128)(2,1)}), bf16[4,32,1664]{2,1,0:T(8,128)(2,1)S(1)}, u32[]{:S(2)}, u32[]{:S(2)}) async-start(bf16[4,32,1664]{2,1,0:T(8,128)(2,1)} %broadcast_in_dim.6), calls=%async_computation | async-start | bytes 851968 | tf_op jit(solution)/shard_map/all_to_all | solution.py:576
  9.8 0.8 dynamic-slice_bitcast_fusion.4
  11.3 1.0 collective-permute-start
  12.8 0.9 slice.68
  15.3 3.9 %collective-permute-done.2.x3 = bf16[4,64,512]{2,1,0:T(8,128)(2,1)S(1)} collective-permute-done((bf16[4,64,512]{2,1,0:T(8,128)(2,1)S(1)}, bf16[4,64,512]{2,1,0:T(8,128)(2,1)S(1)}, u32[]{:S(2)}, u32[]{:S(2)}) %collective-permute-start.2) | collective-permute-done | bytes 262176 | tf_op jit(solution)/shard_map/ppermute | solution.py:569
  19.2 3.0 %all-to-all-done.p0 = bf16[4,32,1664]{2,1,0:T(8,128)(2,1)S(1)} async-done(((bf16[4,32,1664]{2,1,0:T(8,128)(2,1)}), bf16[4,32,1664]{2,1,0:T(8,128)(2,1)S(1)}, u32[]{:S(2)}, u32[]{:S(2)}) %all-to-all-start) | async-done | bytes 426016 | tf_op jit(solution)/shard_map/all_to_all | solution.py:576
  22.2 1.5 collective-permute-start.3
  23.8 1.0 broadcast_in_dim.7
  24.8 4.2 %all-to-all-start.1 = ((bf16[4,32,3072]{2,1,0:T(8,128)(2,1)}), bf16[4,32,3072]{2,1,0:T(8,128)(2,1)}, u32[]{:S(2)}, u32[]{:S(2)}) async-start(bf16[4,32,3072]{2,1,0:T(8,128)(2,1)} %broadcast_in_dim.7), calls=%async_computation.1 | async-start | bytes 1572864 | tf_op jit(solution)/shard_map/all_to_all | solution.py:576
  29.0 4.0 %collective-permute-done.3.p1 = bf16[4,32,1664]{2,1,0:T(8,128)(2,1)S(1)} collective-permute-done((bf16[4,32,1664]{2,1,0:T(8,128)(2,1)S(1)}, bf16[4,32,1664]{2,1,0:T(8,128)(2,1)S(1)}, u32[]{:S(2)}, u32[]{:S(2)}) %collective-permute-start.3) | collective-permute-done | bytes 426016 | tf_op jit(solution)/shard_map/ppermute | solution.py:557
  33.3 1.5 collective-permute-start.12
  35.5 1.0 dynamic-slice_bitcast_fusion
  36.5 1.4 collective-permute-start.10
  38.9 0.8 copy-done.12
  39.6 6.2 %qkv.1 = (bf16[1024,512]{1,0:T(8,128)(2,1)}, bf16[1024,1536]{1,0:T(8,128)(2,1)}) custom-call(s32[9]{0:T(128)} %copy-done.9, bf16[4,64,512]{2,1,0:T(8,128)(2,1)} %get-tuple-element.218.x0, bf16[4,64,512]{2,1,0:T(8,128)(2,1)} %collective-permute-done.x1, bf16[4,64,512]{2,1,0:T(8,128)(2,1)} %collective-permute-done.1.x2, bf16[4,64,512]{2,1,0:T(8,128)(2,1)} %copy-done.13, ...), custom_call_target="tpu_custom_call" | custom-call | flops 7000000000 | bytes 14000000 | tf_op jit(solution)/shard_map/qkv/pallas_call | solution.py:697
  45.9 1.0 pad_maximum_fusion.1
  46.9 3.3 %all-to-all-done.1.b0 = bf16[4,32,3072]{2,1,0:T(8,128)(2,1)} async-done(((bf16[4,32,3072]{2,1,0:T(8,128)(2,1)}), bf16[4,32,3072]{2,1,0:T(8,128)(2,1)}, u32[]{:S(2)}, u32[]{:S(2)}) %all-to-all-start.1) | async-done | bytes 786464 | tf_op jit(solution)/shard_map/all_to_all | solution.py:576
  50.6 0.9 broadcast_in_dim.8
  51.6 4.2 %all-to-all-start.2 = ((bf16[4,2,32,1536]{3,2,1,0:T(8,128)(2,1)}), bf16[4,2,32,1536]{3,2,1,0:T(8,128)(2,1)}, u32[]{:S(2)}, u32[]{:S(2)}) async-start(bf16[4,2,32,1536]{3,2,1,0:T(8,128)(2,1)} %broadcast_in_dim.8), calls=%async_computation.2 | async-start | bytes 1572864 | tf_op jit(solution)/shard_map/all_to_all | solution.py:576
  55.8 5.3 %attend.2 = (bf16[1024,512]{1,0:T(8,128)(2,1)}, f32[4,8,256]{2,1,0:T(8,128)}) custom-call(s32[9]{0:T(128)} %copy-done.15, s32[4]{0:T(128)} %dynamic_slice.52.lengths, bf16[1024,1536]{1,0:T(8,128)(2,1)} %get-tuple-element.181.qkv), custom_call_target="tpu_custom_call" | custom-call | flops 12000000000 | bytes 24000000 | tf_op jit(solution)/shard_map/attend/pallas_call | solution.py:721
  61.1 8.4 %collective-permute-done.6.b1 = bf16[4,32,3072]{2,1,0:T(8,128)(2,1)} collective-permute-done((bf16[4,32,3072]{2,1,0:T(8,128)(2,1)}, bf16[4,32,3072]{2,1,0:T(8,128)(2,1)}, u32[]{:S(2)}, u32[]{:S(2)}) %collective-permute-start.6) | collective-permute-done | bytes 786464 | tf_op jit(solution)/shard_map/ppermute | solution.py:557
  69.6 3.0 %attend.3 = (bf16[1024,512]{1,0:T(8,128)(2,1)}, f32[4,8,256]{2,1,0:T(8,128)}) custom-call(s32[9]{0:T(128)} %copy-done.14, s32[4]{0:T(128)} %dynamic_slice.52.lengths, bf16[1024,1536]{1,0:T(8,128)(2,1)} %get-tuple-element.181.qkv, bf16[1024,512]{1,0:T(8,128)(2,1)} %get-tuple-element.139.refs_0_, ...), custom_call_target="tpu_custom_call", output_to_operand_aliasing={{0}: (3, {}), {1}: (4, {})} | custom-call | flops 4000000000 | bytes 8000000 | tf_op jit(solution)/shard_map/attend/pallas_call | solution.py:721
  72.5 4.4 %all-to-all-done.2.c0 = bf16[4,2,32,1536]{3,2,1,0:T(8,128)(2,1)} async-done(((bf16[4,2,32,1536]{3,2,1,0:T(8,128)(2,1)}), bf16[4,2,32,1536]{3,2,1,0:T(8,128)(2,1)}, u32[]{:S(2)}, u32[]{:S(2)}) %all-to-all-start.2) | async-done | bytes 786464 | tf_op jit(solution)/shard_map/all_to_all | solution.py:576
  76.9 2.6 %collective-permute-done.13.c1 = bf16[4,2,32,1536]{3,2,1,0:T(8,128)(2,1)} collective-permute-done((bf16[4,2,32,1536]{3,2,1,0:T(8,128)(2,1)}, bf16[4,2,32,1536]{3,2,1,0:T(8,128)(2,1)}, u32[]{:S(2)}, u32[]{:S(2)}) %collective-permute-start.13) | collective-permute-done | bytes 786464 | tf_op jit(solution)/shard_map/ppermute | solution.py:557
  79.5 27.8 %mlp.1 = (bf16[4,64,512]{2,1,0:T(8,128)(2,1)}, bf16[4,64,512]{2,1,0:T(8,128)(2,1)}, bf16[4,64,512]{2,1,0:T(8,128)(2,1)}, bf16[4,64,512]{2,1,0:T(8,128)(2,1)}, f3...) custom-call(s32[9]{0:T(128)} %copy-done.9, ...), custom_call_target="tpu_custom_call" | custom-call | flops 24000000000 | bytes 48000000 | tf_op jit(solution)/shard_map/mlp/pallas_call | solution.py:761
  108.1 1.5 collective-permute-start.15
  109.9 8.3 %back_first.1 = (bf16[2,64,512]{2,1,0:T(8,128)(2,1)}, bf16[2,64,512]{2,1,0:T(8,128)(2,1)}, bf16[2,64,512]{2,1,0:T(8,128)(2,1)}, bf16[2,64,512]{2,1,0:T(8,128)(2,...) custom-call(s32[9]{0:T(128)} %copy-done.9, s32[4]{0:T(128)} %dynamic_slice.52.lengths, ...), custom_call_target="tpu_custom_call" | custom-call | flops 11000000512 | bytes 22000000 | tf_op jit(solution)/shard_map/back_first/pallas_call | solution.py:835
  118.7 1.5 collective-permute-start.18
  120.2 2.0 collective-permute-done.16.refs_3_
  122.2 1.9 collective-permute-start.19
  124.2 3.8 %add.106 = (bf16[4,64,640]{2,1,0:T(8,128)(2,1)}, bf16[4,64,640]{2,1,0:T(8,128)(2,1)}, bf16[4,64,640]{2,1,0:T(8,128)(2,1)}, bf16[4,64,640]{2,1,0:T(8,128)(2,1)}, bf16[4,4,64,512]{3,2,1,0:T(8,128)(2,1)}) custom-call(bf16[4,4,64,640]{3,2,1,0:T(8,128)(2,1)} %bitcast.61, bf16[4,4,64,640]{3,2,1,0:T(8,128)(2,1)} %bitcast.22.got, bf16[4,4,64,512]{3,2,1,0:T(8,128)(2,1)} %bitcast.62, ...), custom_call_target="tpu_custom_call" | custom-call | flops 3000000000 | bytes 6000000 | tf_op jit(solution)/shard_map/add/pallas_call | solution.py:849
  128.0 1.5 collective-permute-start.25
  130.0 4.3 %all-to-all-start.4 = ((bf16[4,4,64,512]{3,2,1,0:T(8,128)(2,1)}), bf16[4,4,64,512]{3,2,1,0:T(8,128)(2,1)}, u32[]{:S(2)}, u32[]{:S(2)}) async-start(bf16[4,4,64,512]{3,2,1,0:T(8,128)(2,1)} %get-tuple-element.180), calls=%async_computation.4 | async-start | bytes 2097152 | tf_op jit(solution)/shard_map/all_to_all | solution.py:888
  134.3 1.5 collective-permute-start.27
  135.8 12.0 %back_last.1 = (bf16[2,64,512]{2,1,0:T(8,128)(2,1)}, bf16[2,64,512]{2,1,0:T(8,128)(2,1)}, bf16[2,64,512]{2,1,0:T(8,128)(2,1)}, bf16[2,64,512]{2,1,0:T(8,128)(2,1...) custom-call(s32[9]{0:T(128)} %copy-done.16, ...), custom_call_target="tpu_custom_call" | custom-call | flops 12999999488 | bytes 26000000 | tf_op jit(solution)/shard_map/back_last/pallas_call | solution.py:891
  149.0 0.9 collective-permute-start.24
  150.6 2.4 %add.107 = (bf16[4,80,384]{2,1,0:T(8,128)(2,1)}, bf16[4,80,384]{2,1,0:T(8,128)(2,1)}, bf16[4,80,384]{2,1,0:T(8,128)(2,1)}, bf16[4,80,384]{2,1,0:T(8,128)(2,1)}) custom-call(bf16[4,4,64,384]{3,2,1,0:T(8,128)(2,1)} %bitcast.63, bf16[4,4,64,384]{3,2,1,0:T(8,128)(2,1)} %bitcast.26.got, f32[16,512]{1,0:T(8,128)} %get-tuple-element.190.vec), custom_call_target="tpu_custom_call" | custom-call | flops 3000000000 | bytes 6000000 | tf_op jit(solution)/shard_map/add/pallas_call | solution.py:849
  153.0 1.5 collective-permute-start.35
  155.0 1.5 collective-permute-start.37
  156.5 2.2 %add_convert_fusion = bf16[4,64,640]{2,1,0:T(8,128)(2,1)} fusion(bf16[4,64,640]{2,1,0:T(8,128)(2,1)} %collective-permute-done.27, bf16[4,64,640]{2,1,0:T(8,128)(2,1)} %collective-permute-done.26, bf16[4,64,640]{2,1,0:T(8,128)(2,1)} %collective-permute-done.25, bf16[4,64,640]{2,1,0:T(8,128)(2,1)} %get-tuple-element.176), kind=kLoop, calls=%fused_computation | loop fusion | flops 1310720 | bytes 1638400 | tf_op jit(solution)/shard_map/convert_element_type | solution.py:869
  158.6 1.2 all-to-all-done.4
  159.8 3.9 %all-to-all-start.3 = ((bf16[4,64,640]{2,1,0:T(8,128)(2,1)}), bf16[4,64,640]{2,1,0:T(8,128)(2,1)S(1)}, u32[]{:S(2)}, u32[]{:S(2)}) async-start(bf16[4,64,640]{2,1,0:T(8,128)(2,1)} %add_convert_fusion), calls=%async_computation.3 | async-start | bytes 655360 | tf_op jit(solution)/shard_map/all_to_all | solution.py:925
  163.7 3.9 %collective-permute-done.36 = bf16[4,80,384]{2,1,0:T(8,128)(2,1)S(1)} collective-permute-done((bf16[4,80,384]{2,1,0:T(8,128)(2,1)}, bf16[4,80,384]{2,1,0:T(8,128)(2,1)S(1)}, u32[]{:S(2)}, u32[]{:S(2)}) %collective-permute-start.36) | collective-permute-done | bytes 245792 | tf_op jit(solution)/shard_map/ppermute | solution.py:864
  167.7 1.4 reduce_sum.37
  169.1 1.4 collective-permute-start.29
  171.0 1.6 collective-permute-start.31
  172.7 0.8 add_convert_fusion.1
  173.5 5.0 %all-to-all-start.5 = ((bf16[4,80,384]{2,1,0:T(8,128)(2,1)}), bf16[4,80,384]{2,1,0:T(8,128)(2,1)}, u32[]{:S(2)}, u32[]{:S(2)}) async-start(bf16[4,80,384]{2,1,0:T(8,128)(2,1)} %add_convert_fusion.1), calls=%async_computation.5 | async-start | bytes 491520 | tf_op jit(solution)/shard_map/all_to_all | solution.py:929
  179.8 1.6 collective-permute-start.34
  181.4 2.2 %collect.2 = bf16[4,4,64,512]{3,2,1,0:T(8,128)(2,1)} custom-call(s32[9]{0:T(128)} %copy-done.9, bf16[4,64,512]{2,1,0:T(8,128)(2,1)} %get-tuple-element.154.refs_0_, bf16[4,64,512]{2,1,0:T(8,128)(2,1)} %collective-permute-done.14.refs_1_, bf16[4,64,512]{2,1,0:T(8,128)(2,1)} %collective-permute-done.15.refs_2_, bf16[4,64,512]{2,1,0:T(8,128)(2,1)} %collective-permute-done.16.refs_3_), custom_call_target="tpu_custom_call" | custom-call | flops 2000000000 | bytes 4000000 | tf_op jit(solution)/shard_map/collect/pallas_call | solution.py:801
  183.6 1.6 all-to-all-done.5
  185.3 1.0 reduce_sum.38.a0
  186.3 1.4 collective-permute-start.38
  187.9 1.1 collective-permute-start.40
  189.0 2.0 mlp_squares.1.before
  191.1 1.4 collective-permute-done.40.a3
  192.5 1.7 squares.1
  194.2 5.6 %all-to-all-start.6 = ((f32[8,8,128]{2,1,0:T(8,128)}), f32[8,8,128]{2,1,0:T(8,128)S(1)}, u32[]{:S(2)}, u32[]{:S(2)}) async-start(f32[8,8,128]{2,1,0:T(8,128)} %squares.1), calls=%async_computation.6 | async-start | bytes 65536 | tf_op jit(solution)/shard_map/all_to_all | solution.py:969
  199.8 2.3 %collect.3 = bf16[4,4,64,512]{3,2,1,0:T(8,128)(2,1)} custom-call(s32[9]{0:T(128)} %copy-done.9, bf16[2,64,512]{2,1,0:T(8,128)(2,1)} %get-tuple-element.165.refs_0_, bf16[2,64,512]{2,1,0:T(8,128)(2,1)} %collective-permute-done.17.refs_1_, bf16[2,64,512]{2,1,0:T(8,128)(2,1)} %collective-permute-done.18.refs_2_, ...), custom_call_target="tpu_custom_call" | custom-call | flops 2000000000 | bytes 4000000 | tf_op jit(solution)/shard_map/collect/pallas_call | solution.py:801
  202.2 4.4 %all-to-all-done.6.squares = f32[8,8,128]{2,1,0:T(8,128)S(1)} async-done(((f32[8,8,128]{2,1,0:T(8,128)}), f32[8,8,128]{2,1,0:T(8,128)S(1)}, u32[]{:S(2)}, u32[]{:S(2)}) %all-to-all-start.6) | async-done | bytes 32800 | tf_op jit(solution)/shard_map/all_to_all | solution.py:969
  207.1 6.0 %adam.1 = (f32[1,1]{1,0:T(1,128)}, f32[64,2048]{1,0:T(8,128)}, f32[64,2048]{1,0:T(8,128)}, f32[64,2048]{1,0:T(8,128)}, f32[2,64,2048]{2,1,0:T(8,128)}, /*index=5...) custom-call(s32[9]{0:T(128)} %copy-done.9, ...), custom_call_target="tpu_custom_call" | custom-call | flops 6000000000 | bytes 12000000 | tf_op jit(solution)/shard_map/adam/pallas_call | solution.py:972
  (126 shorter events, 12.4 us)
Async XLA Ops:
  0.6 9.2 %copy-start = (bf16[4,4,64,512]{3,2,1,0:T(8,128)(2,1)S(1)}, bf16[4,4,64,512]{3,2,1,0:T(8,128)(2,1)}, u32[]{:S(2)}) copy-start(bf16[4,4,64,512]{3,2,1,0:T(8,128)(2,1)} %param.18) | copy-start | bytes 3145732
  3.4 10.3 %copy-start.3 = (f32[2,64,2048]{2,1,0:T(8,128)S(1)}, f32[2,64,2048]{2,1,0:T(8,128)}, u32[]{:S(2)}) copy-start(f32[2,64,2048]{2,1,0:T(8,128)} %mlp_w.1) | copy-start | bytes 3145732
  3.4 18.8 %all-to-all-start = ((bf16[4,32,1664]{2,1,0:T(8,128)(2,1)}), bf16[4,32,1664]{2,1,0:T(8,128)(2,1)S(1)}, u32[]{:S(2)}, u32[]{:S(2)}) async-start(bf16[4,32,1664]{2,1,0:T(8,128)(2,1)} %broadcast_in_dim.6), calls=%async_computation | async-start | bytes 851968 | tf_op jit(solution)/shard_map/all_to_all | solution.py:576
  9.8 4.7 %copy-start.8 = (s32[4,4]{1,0:T(4,128)S(1)}, s32[4,4]{1,0:T(4,128)}, u32[]{:S(2)}) copy-start(s32[4,4]{1,0:T(4,128)} %param.20) | copy-start | bytes 196
  10.7 8.5 %collective-permute-start.2 = (bf16[4,64,512]{2,1,0:T(8,128)(2,1)S(1)}, bf16[4,64,512]{2,1,0:T(8,128)(2,1)S(1)}, u32[]{:S(2)}, u32[]{:S(2)}) collective-permute-start(bf16[4,64,512]{2,1,0:T(8,128)(2,1)S(1)} %get-tuple-element.216), channel_id=1, source_target_pairs={{0,3},{1,2},{2,1},{3,0},{4,7},{5,6},{6,5},{7,4},{8,11},{9,10},{10,... | collective-permute-start | bytes 786440 | tf_op jit(solution)/shard_map/ppermute | solution.py:569
  11.3 25.1 %collective-permute-start = (bf16[4,64,512]{2,1,0:T(8,128)(2,1)S(1)}, bf16[4,64,512]{2,1,0:T(8,128)(2,1)}, u32[]{:S(2)}, u32[]{:S(2)}) collective-permute-start(bf16[4,64,512]{2,1,0:T(8,128)(2,1)S(1)} %get-tuple-element.217), channel_id=1, source_target_pairs={{0,1},{1,0},{2,3},{3,2},{4,5},{5,4},{6,7},{7,6},{8,9},{9,8},{10,11... | collective-permute-start | bytes 786440 | tf_op jit(solution)/shard_map/ppermute | solution.py:569
  12.3 25.5 %collective-permute-start.1 = (bf16[4,64,512]{2,1,0:T(8,128)(2,1)S(1)}, bf16[4,64,512]{2,1,0:T(8,128)(2,1)}, u32[]{:S(2)}, u32[]{:S(2)}) collective-permute-start(bf16[4,64,512]{2,1,0:T(8,128)(2,1)S(1)} %get-tuple-element.219), channel_id=1, source_target_pairs={{0,2},{1,3},{2,0},{3,1},{4,6},{5,7},{6,4},{7,5},{8,10},{9,11},{10,... | collective-permute-start | bytes 786440 | tf_op jit(solution)/shard_map/ppermute | solution.py:569
  14.6 10.2 %copy-start.9 = (s32[9]{0:T(128)}, s32[9]{0:T(128)S(1)}, u32[]{:S(2)}) copy-start(s32[9]{0:T(128)S(1)} %stack.41.place) | copy-start | bytes 112
  14.7 10.1 %copy-start.15 = (s32[9]{0:T(128)}, s32[9]{0:T(128)S(1)}, u32[]{:S(2)}) copy-start(s32[9]{0:T(128)S(1)} %constant_dynamic-update-slice_fusion.1.place) | copy-start | bytes 112
  15.3 9.5 %copy-start.14 = (s32[9]{0:T(128)}, s32[9]{0:T(128)S(1)}, u32[]{:S(2)}) copy-start(s32[9]{0:T(128)S(1)} %constant_dynamic-update-slice_fusion.2.place) | copy-start | bytes 112
  19.2 4.5 %copy-start.13 = (bf16[4,64,512]{2,1,0:T(8,128)(2,1)}, bf16[4,64,512]{2,1,0:T(8,128)(2,1)S(1)}, u32[]{:S(2)}) copy-start(bf16[4,64,512]{2,1,0:T(8,128)(2,1)S(1)} %collective-permute-done.2.x3) | copy-start | bytes 786436
  22.2 10.8 %copy-start.2 = (bf16[4,32,1664]{2,1,0:T(8,128)(2,1)}, bf16[4,32,1664]{2,1,0:T(8,128)(2,1)S(1)}, u32[]{:S(2)}) copy-start(bf16[4,32,1664]{2,1,0:T(8,128)(2,1)S(1)} %all-to-all-done.p0) | copy-start | bytes 1277956
  22.2 10.8 %collective-permute-start.3 = (bf16[4,32,1664]{2,1,0:T(8,128)(2,1)S(1)}, bf16[4,32,1664]{2,1,0:T(8,128)(2,1)S(1)}, u32[]{:S(2)}, u32[]{:S(2)}) collective-permute-start(bf16[4,32,1664]{2,1,0:T(8,128)(2,1)S(1)} %all-to-all-done.p0), channel_id=1, source_target_pairs={{0,4},{4,0},{1,5},{5,1},{2,6},{6,2},{3,7},{7,3},{8,12},{12,8},{9,1... | collective-permute-start | bytes 1277960 | tf_op jit(solution)/shard_map/ppermute | solution.py:557
  23.7 11.7 %copy-start.1 = (bf16[4,4,64,512]{3,2,1,0:T(8,128)(2,1)S(1)}, bf16[4,4,64,512]{3,2,1,0:T(8,128)(2,1)}, u32[]{:S(2)}) copy-start(bf16[4,4,64,512]{3,2,1,0:T(8,128)(2,1)} %param.19) | copy-start | bytes 3145732
  23.7 14.4 %collective-permute-start.4 = (bf16[4,32,1664]{2,1,0:T(8,128)(2,1)S(1)}, bf16[4,32,1664]{2,1,0:T(8,128)(2,1)S(1)}, u32[]{:S(2)}, u32[]{:S(2)}) collective-permute-start(bf16[4,32,1664]{2,1,0:T(8,128)(2,1)S(1)} %all-to-all-done.p0), channel_id=1, source_target_pairs={{0,1},{1,0},{2,3},{3,2},{4,5},{5,4},{6,7},{7,6},{8,9},{9,8},{10,11... | collective-permute-start | bytes 1277960 | tf_op jit(solution)/shard_map/ppermute | solution.py:557
  24.8 25.3 %all-to-all-start.1 = ((bf16[4,32,3072]{2,1,0:T(8,128)(2,1)}), bf16[4,32,3072]{2,1,0:T(8,128)(2,1)}, u32[]{:S(2)}, u32[]{:S(2)}) async-start(bf16[4,32,3072]{2,1,0:T(8,128)(2,1)} %broadcast_in_dim.7), calls=%async_computation.1 | async-start | bytes 1572864 | tf_op jit(solution)/shard_map/all_to_all | solution.py:576
  33.0 5.1 %copy-start.7 = (bf16[4,32,1664]{2,1,0:T(8,128)(2,1)}, bf16[4,32,1664]{2,1,0:T(8,128)(2,1)S(1)}, u32[]{:S(2)}) copy-start(bf16[4,32,1664]{2,1,0:T(8,128)(2,1)S(1)} %collective-permute-done.3.p1) | copy-start | bytes 1277956
  33.0 5.7 %collective-permute-start.5 = (bf16[4,32,1664]{2,1,0:T(8,128)(2,1)S(1)}, bf16[4,32,1664]{2,1,0:T(8,128)(2,1)S(1)}, u32[]{:S(2)}, u32[]{:S(2)}) collective-permute-start(bf16[4,32,1664]{2,1,0:T(8,128)(2,1)S(1)} %collective-permute-done.3.p1), channel_id=1, source_target_pairs={{0,1},{1,0},{2,3},{3,2},{4,5},{5,4},{6,7},{7,6},{8,9},{9,8},{10,11... | collective-permute-start | bytes 1277960 | tf_op jit(solution)/shard_map/ppermute | solution.py:557
  33.3 12.6 %collective-permute-start.12 = (bf16[32,1536]{1,0:T(8,128)(2,1)}, bf16[32,1536]{1,0:T(8,128)(2,1)}, u32[]{:S(2)}, u32[]{:S(2)}) collective-permute-start(bf16[32,1536]{1,0:T(8,128)(2,1)} %fusion.4), channel_id=1, source_target_pairs={{0,4},{4,0},{1,5},{5,1},{2,6},{6,2},{3,7},{7,3},{8,12},{12,8},{9,1... | collective-permute-start | bytes 294920 | tf_op jit(solution)/shard_map/ppermute | solution.py:557
  36.5 24.7 %collective-permute-start.10 = (bf16[4,64,512]{2,1,0:T(8,128)(2,1)}, bf16[4,64,512]{2,1,0:T(8,128)(2,1)}, u32[]{:S(2)}, u32[]{:S(2)}) collective-permute-start(bf16[4,64,512]{2,1,0:T(8,128)(2,1)} %get-tuple-element.212), channel_id=1, source_target_pairs={{0,3},{1,2},{2,1},{3,0},{4,7},{5,6},{6,5},{7,4},{8,11},{9,10},{10,... | collective-permute-start | bytes 786440 | tf_op jit(solution)/shard_map/ppermute | solution.py:569
  37.8 23.3 %collective-permute-start.8 = (bf16[4,64,512]{2,1,0:T(8,128)(2,1)}, bf16[4,64,512]{2,1,0:T(8,128)(2,1)}, u32[]{:S(2)}, u32[]{:S(2)}) collective-permute-start(bf16[4,64,512]{2,1,0:T(8,128)(2,1)} %get-tuple-element.214), channel_id=1, source_target_pairs={{0,1},{1,0},{2,3},{3,2},{4,5},{5,4},{6,7},{7,6},{8,9},{9,8},{10,11... | collective-permute-start | bytes 786440 | tf_op jit(solution)/shard_map/ppermute | solution.py:569
  38.1 0.8 copy-start.11
  38.1 23.0 %collective-permute-start.9 = (bf16[4,64,512]{2,1,0:T(8,128)(2,1)}, bf16[4,64,512]{2,1,0:T(8,128)(2,1)}, u32[]{:S(2)}, u32[]{:S(2)}) collective-permute-start(bf16[4,64,512]{2,1,0:T(8,128)(2,1)} %get-tuple-element.213), channel_id=1, source_target_pairs={{0,2},{1,3},{2,0},{3,1},{4,6},{5,7},{6,4},{7,5},{8,10},{9,11},{10,... | collective-permute-start | bytes 786440 | tf_op jit(solution)/shard_map/ppermute | solution.py:569
  38.9 0.8 copy-start.12
  50.1 19.5 %collective-permute-start.6 = (bf16[4,32,3072]{2,1,0:T(8,128)(2,1)}, bf16[4,32,3072]{2,1,0:T(8,128)(2,1)}, u32[]{:S(2)}, u32[]{:S(2)}) collective-permute-start(bf16[4,32,3072]{2,1,0:T(8,128)(2,1)} %all-to-all-done.1.b0), channel_id=1, source_target_pairs={{0,4},{4,0},{1,5},{5,1},{2,6},{6,2},{3,7},{7,3},{8,12},{12,8},{9,1... | collective-permute-start | bytes 2359304 | tf_op jit(solution)/shard_map/ppermute | solution.py:557
  50.6 18.9 %collective-permute-start.7 = (bf16[4,32,3072]{2,1,0:T(8,128)(2,1)}, bf16[4,32,3072]{2,1,0:T(8,128)(2,1)}, u32[]{:S(2)}, u32[]{:S(2)}) collective-permute-start(bf16[4,32,3072]{2,1,0:T(8,128)(2,1)} %all-to-all-done.1.b0), channel_id=1, source_target_pairs={{0,1},{1,0},{2,3},{3,2},{4,5},{5,4},{6,7},{7,6},{8,9},{9,8},{10,11... | collective-permute-start | bytes 2359304 | tf_op jit(solution)/shard_map/ppermute | solution.py:557
  51.6 25.3 %all-to-all-start.2 = ((bf16[4,2,32,1536]{3,2,1,0:T(8,128)(2,1)}), bf16[4,2,32,1536]{3,2,1,0:T(8,128)(2,1)}, u32[]{:S(2)}, u32[]{:S(2)}) async-start(bf16[4,2,32,1536]{3,2,1,0:T(8,128)(2,1)} %broadcast_in_dim.8), calls=%async_computation.2 | async-start | bytes 1572864 | tf_op jit(solution)/shard_map/all_to_all | solution.py:576
  69.6 7.3 %collective-permute-start.11 = (bf16[4,32,3072]{2,1,0:T(8,128)(2,1)}, bf16[4,32,3072]{2,1,0:T(8,128)(2,1)}, u32[]{:S(2)}, u32[]{:S(2)}) collective-permute-start(bf16[4,32,3072]{2,1,0:T(8,128)(2,1)} %collective-permute-done.6.b1), channel_id=1, source_target_pairs={{0,1},{1,0},{2,3},{3,2},{4,5},{5,4},{6,7},{7,6},{8,9},{9,8},{10,11... | collective-permute-start | bytes 2359304 | tf_op jit(solution)/shard_map/ppermute | solution.py:557
  76.9 31.0 %copy-start.10 = (s32[9]{0:T(128)S(1)}, s32[9]{0:T(128)}, u32[]{:S(2)}) copy-start(s32[9]{0:T(128)} %copy-done.9) | copy-start | bytes 112
  76.9 2.6 %collective-permute-start.13 = (bf16[4,2,32,1536]{3,2,1,0:T(8,128)(2,1)}, bf16[4,2,32,1536]{3,2,1,0:T(8,128)(2,1)}, u32[]{:S(2)}, u32[]{:S(2)}) collective-permute-start(bf16[4,2,32,1536]{3,2,1,0:T(8,128)(2,1)} %all-to-all-done.2.c0), channel_id=1, source_target_pairs={{0,1},{1,0},{2,3},{3,2},{4,5},{5,4},{6,7},{7,6},{8,9},{9,8},{10,11... | collective-permute-start | bytes 2359304 | tf_op jit(solution)/shard_map/ppermute | solution.py:557
  107.3 16.8 %collective-permute-start.20 = (bf16[2,2,4,64,640]{4,3,2,1,0:T(8,128)(2,1)}, bf16[2,2,4,64,640]{4,3,2,1,0:T(8,128)(2,1)}, u32[]{:S(2)}, u32[]{:S(2)}) collective-permute-start(bf16[2,2,4,64,640]{4,3,2,1,0:T(8,128)(2,1)} %get-tuple-element.158), channel_id=1, source_target_pairs={{0,1},{1,0},{2,3},{3,2},{4,5},{5,4},{6,7},{7,6},{8,9},{9,8},{10,11... | collective-permute-start | bytes 3932168 | tf_op jit(solution)/shard_map/ppermute | solution.py:557
  107.5 16.6 %collective-permute-start.21 = (bf16[2,2,4,64,512]{4,3,2,1,0:T(8,128)(2,1)}, bf16[2,2,4,64,512]{4,3,2,1,0:T(8,128)(2,1)}, u32[]{:S(2)}, u32[]{:S(2)}) collective-permute-start(bf16[2,2,4,64,512]{4,3,2,1,0:T(8,128)(2,1)} %get-tuple-element.159), channel_id=1, source_target_pairs={{0,1},{1,0},{2,3},{3,2},{4,5},{5,4},{6,7},{7,6},{8,9},{9,8},{10,11... | collective-permute-start | bytes 3145736 | tf_op jit(solution)/shard_map/ppermute | solution.py:557
  107.9 10.3 %copy-start.16 = (s32[9]{0:T(128)}, s32[9]{0:T(128)S(1)}, u32[]{:S(2)}) copy-start(s32[9]{0:T(128)S(1)} %constant_dynamic-update-slice_fusion.place) | copy-start | bytes 112
  107.9 10.3 %collective-permute-start.14 = (bf16[4,64,512]{2,1,0:T(8,128)(2,1)}, bf16[4,64,512]{2,1,0:T(8,128)(2,1)}, u32[]{:S(2)}, u32[]{:S(2)}) collective-permute-start(bf16[4,64,512]{2,1,0:T(8,128)(2,1)} %get-tuple-element.155), channel_id=1, source_target_pairs={{0,1},{1,0},{2,3},{3,2},{4,5},{5,4},{6,7},{7,6},{8,9},{9,8},{10,11... | collective-permute-start | bytes 786440 | tf_op jit(solution)/shard_map/ppermute | solution.py:569
  108.1 10.6 %collective-permute-start.15 = (bf16[4,64,512]{2,1,0:T(8,128)(2,1)}, bf16[4,64,512]{2,1,0:T(8,128)(2,1)}, u32[]{:S(2)}, u32[]{:S(2)}) collective-permute-start(bf16[4,64,512]{2,1,0:T(8,128)(2,1)} %get-tuple-element.156), channel_id=1, source_target_pairs={{0,2},{1,3},{2,0},{3,1},{4,6},{5,7},{6,4},{7,5},{8,10},{9,11},{10,... | collective-permute-start | bytes 786440 | tf_op jit(solution)/shard_map/ppermute | solution.py:569
  109.7 12.6 %collective-permute-start.16 = (bf16[4,64,512]{2,1,0:T(8,128)(2,1)}, bf16[4,64,512]{2,1,0:T(8,128)(2,1)}, u32[]{:S(2)}, u32[]{:S(2)}) collective-permute-start(bf16[4,64,512]{2,1,0:T(8,128)(2,1)} %get-tuple-element.157), channel_id=1, source_target_pairs={{0,3},{1,2},{2,1},{3,0},{4,7},{5,6},{6,5},{7,4},{8,11},{9,10},{10,... | collective-permute-start | bytes 786440 | tf_op jit(solution)/shard_map/ppermute | solution.py:569
  118.2 16.1 %collective-permute-start.17 = (bf16[2,64,512]{2,1,0:T(8,128)(2,1)}, bf16[2,64,512]{2,1,0:T(8,128)(2,1)}, u32[]{:S(2)}, u32[]{:S(2)}) collective-permute-start(bf16[2,64,512]{2,1,0:T(8,128)(2,1)} %get-tuple-element.166), channel_id=1, source_target_pairs={{0,1},{1,0},{2,3},{3,2},{4,5},{5,4},{6,7},{7,6},{8,9},{9,8},{10,11... | collective-permute-start | bytes 393224 | tf_op jit(solution)/shard_map/ppermute | solution.py:569
  118.7 29.1 %collective-permute-start.18 = (bf16[2,64,512]{2,1,0:T(8,128)(2,1)}, bf16[2,64,512]{2,1,0:T(8,128)(2,1)}, u32[]{:S(2)}, u32[]{:S(2)}) collective-permute-start(bf16[2,64,512]{2,1,0:T(8,128)(2,1)} %get-tuple-element.167), channel_id=1, source_target_pairs={{0,2},{1,3},{2,0},{3,1},{4,6},{5,7},{6,4},{7,5},{8,10},{9,11},{10,... | collective-permute-start | bytes 393224 | tf_op jit(solution)/shard_map/ppermute | solution.py:569
  122.2 25.6 %collective-permute-start.19 = (bf16[2,64,512]{2,1,0:T(8,128)(2,1)}, bf16[2,64,512]{2,1,0:T(8,128)(2,1)}, u32[]{:S(2)}, u32[]{:S(2)}) collective-permute-start(bf16[2,64,512]{2,1,0:T(8,128)(2,1)} %get-tuple-element.168), channel_id=1, source_target_pairs={{0,3},{1,2},{2,1},{3,0},{4,7},{5,6},{6,5},{7,4},{8,11},{9,10},{10,... | collective-permute-start | bytes 393224 | tf_op jit(solution)/shard_map/ppermute | solution.py:569
  128.0 19.9 %collective-permute-start.25 = (bf16[4,64,640]{2,1,0:T(8,128)(2,1)}, bf16[4,64,640]{2,1,0:T(8,128)(2,1)}, u32[]{:S(2)}, u32[]{:S(2)}) collective-permute-start(bf16[4,64,640]{2,1,0:T(8,128)(2,1)} %get-tuple-element.178), channel_id=1, source_target_pairs={{0,4},{2,6},{4,0},{6,2},{1,5},{3,7},{5,1},{7,3},{8,12},{10,14},{12... | collective-permute-start | bytes 983048 | tf_op jit(solution)/shard_map/ppermute | solution.py:864
  129.5 18.4 %collective-permute-start.26 = (bf16[4,64,640]{2,1,0:T(8,128)(2,1)}, bf16[4,64,640]{2,1,0:T(8,128)(2,1)}, u32[]{:S(2)}, u32[]{:S(2)}) collective-permute-start(bf16[4,64,640]{2,1,0:T(8,128)(2,1)} %get-tuple-element.177), channel_id=1, source_target_pairs={{0,2},{2,0},{4,6},{6,4},{1,3},{3,1},{5,7},{7,5},{8,10},{10,8},{12,... | collective-permute-start | bytes 983048 | tf_op jit(solution)/shard_map/ppermute | solution.py:864
  130.0 29.8 %all-to-all-start.4 = ((bf16[4,4,64,512]{3,2,1,0:T(8,128)(2,1)}), bf16[4,4,64,512]{3,2,1,0:T(8,128)(2,1)}, u32[]{:S(2)}, u32[]{:S(2)}) async-start(bf16[4,4,64,512]{3,2,1,0:T(8,128)(2,1)} %get-tuple-element.180), calls=%async_computation.4 | async-start | bytes 2097152 | tf_op jit(solution)/shard_map/all_to_all | solution.py:888
  134.3 13.6 %collective-permute-start.27 = (bf16[4,64,640]{2,1,0:T(8,128)(2,1)}, bf16[4,64,640]{2,1,0:T(8,128)(2,1)}, u32[]{:S(2)}, u32[]{:S(2)}) collective-permute-start(bf16[4,64,640]{2,1,0:T(8,128)(2,1)} %get-tuple-element.179), channel_id=1, source_target_pairs={{0,6},{2,4},{4,2},{6,0},{1,7},{3,5},{5,3},{7,1},{8,14},{10,12},{12... | collective-permute-start | bytes 983048 | tf_op jit(solution)/shard_map/ppermute | solution.py:864
  147.9 2.7 %collective-permute-start.28 = (bf16[2,2,4,64,384]{4,3,2,1,0:T(8,128)(2,1)}, bf16[2,2,4,64,384]{4,3,2,1,0:T(8,128)(2,1)}, u32[]{:S(2)}, u32[]{:S(2)}) collective-permute-start(bf16[2,2,4,64,384]{4,3,2,1,0:T(8,128)(2,1)} %get-tuple-element.189), channel_id=1, source_target_pairs={{0,1},{1,0},{2,3},{3,2},{4,5},{5,4},{6,7},{7,6},{8,9},{9,8},{10,11... | collective-permute-start | bytes 2359304 | tf_op jit(solution)/shard_map/ppermute | solution.py:557
  148.0 7.0 %collective-permute-start.22 = (bf16[2,64,512]{2,1,0:T(8,128)(2,1)}, bf16[2,64,512]{2,1,0:T(8,128)(2,1)}, u32[]{:S(2)}, u32[]{:S(2)}) collective-permute-start(bf16[2,64,512]{2,1,0:T(8,128)(2,1)} %get-tuple-element.184), channel_id=1, source_target_pairs={{0,1},{1,0},{2,3},{3,2},{4,5},{5,4},{6,7},{7,6},{8,9},{9,8},{10,11... | collective-permute-start | bytes 393224 | tf_op jit(solution)/shard_map/ppermute | solution.py:569
  148.5 15.3 %collective-permute-start.23 = (bf16[2,64,512]{2,1,0:T(8,128)(2,1)}, bf16[2,64,512]{2,1,0:T(8,128)(2,1)}, u32[]{:S(2)}, u32[]{:S(2)}) collective-permute-start(bf16[2,64,512]{2,1,0:T(8,128)(2,1)} %get-tuple-element.185), channel_id=1, source_target_pairs={{0,2},{1,3},{2,0},{3,1},{4,6},{5,7},{6,4},{7,5},{8,10},{9,11},{10,... | collective-permute-start | bytes 393224 | tf_op jit(solution)/shard_map/ppermute | solution.py:569
  149.0 14.8 %collective-permute-start.24 = (bf16[2,64,512]{2,1,0:T(8,128)(2,1)}, bf16[2,64,512]{2,1,0:T(8,128)(2,1)}, u32[]{:S(2)}, u32[]{:S(2)}) collective-permute-start(bf16[2,64,512]{2,1,0:T(8,128)(2,1)} %get-tuple-element.186), channel_id=1, source_target_pairs={{0,3},{1,2},{2,1},{3,0},{4,7},{5,6},{6,5},{7,4},{8,11},{9,10},{10,... | collective-permute-start | bytes 393224 | tf_op jit(solution)/shard_map/ppermute | solution.py:569
  153.0 10.8 %collective-permute-start.35 = (bf16[4,80,384]{2,1,0:T(8,128)(2,1)}, bf16[4,80,384]{2,1,0:T(8,128)(2,1)S(1)}, u32[]{:S(2)}, u32[]{:S(2)}) collective-permute-start(bf16[4,80,384]{2,1,0:T(8,128)(2,1)} %get-tuple-element.193), channel_id=1, source_target_pairs={{0,4},{2,6},{4,0},{6,2},{1,5},{3,7},{5,1},{7,3},{8,12},{10,14},{12... | collective-permute-start | bytes 737288 | tf_op jit(solution)/shard_map/ppermute | solution.py:864
  154.5 13.2 %collective-permute-start.36 = (bf16[4,80,384]{2,1,0:T(8,128)(2,1)}, bf16[4,80,384]{2,1,0:T(8,128)(2,1)S(1)}, u32[]{:S(2)}, u32[]{:S(2)}) collective-permute-start(bf16[4,80,384]{2,1,0:T(8,128)(2,1)} %get-tuple-element.192), channel_id=1, source_target_pairs={{0,2},{2,0},{4,6},{6,4},{1,3},{3,1},{5,7},{7,5},{8,10},{10,8},{12,... | collective-permute-start | bytes 737288 | tf_op jit(solution)/shard_map/ppermute | solution.py:864
  155.0 12.7 %collective-permute-start.37 = (bf16[4,80,384]{2,1,0:T(8,128)(2,1)}, bf16[4,80,384]{2,1,0:T(8,128)(2,1)S(1)}, u32[]{:S(2)}, u32[]{:S(2)}) collective-permute-start(bf16[4,80,384]{2,1,0:T(8,128)(2,1)} %get-tuple-element.194), channel_id=1, source_target_pairs={{0,6},{2,4},{4,2},{6,0},{1,7},{3,5},{5,3},{7,1},{8,14},{10,12},{12... | collective-permute-start | bytes 737288 | tf_op jit(solution)/shard_map/ppermute | solution.py:864
  158.6 14.0 %copy-start.4 = (bf16[4,80,384]{2,1,0:T(8,128)(2,1)S(1)}, bf16[4,80,384]{2,1,0:T(8,128)(2,1)}, u32[]{:S(2)}) copy-start(bf16[4,80,384]{2,1,0:T(8,128)(2,1)} %get-tuple-element.196) | copy-start | bytes 737284
  159.8 13.6 %all-to-all-start.3 = ((bf16[4,64,640]{2,1,0:T(8,128)(2,1)}), bf16[4,64,640]{2,1,0:T(8,128)(2,1)S(1)}, u32[]{:S(2)}, u32[]{:S(2)}) async-start(bf16[4,64,640]{2,1,0:T(8,128)(2,1)} %add_convert_fusion), calls=%async_computation.3 | async-start | bytes 655360 | tf_op jit(solution)/shard_map/all_to_all | solution.py:925
  169.1 9.4 %collective-permute-start.29 = (bf16[64,512]{1,0:T(8,128)(2,1)S(1)}, bf16[64,512]{1,0:T(8,128)(2,1)S(1)}, u32[]{:S(2)}, u32[]{:S(2)}) collective-permute-start(bf16[64,512]{1,0:T(8,128)(2,1)S(1)} %get-tuple-element.222), channel_id=1, source_target_pairs={{0,4},{2,6},{4,0},{6,2},{1,5},{3,7},{5,1},{7,3},{8,12},{10,14},{12... | collective-permute-start | bytes 196616 | tf_op jit(solution)/shard_map/ppermute | solution.py:864
  170.5 8.0 %collective-permute-start.30 = (bf16[64,512]{1,0:T(8,128)(2,1)S(1)}, bf16[64,512]{1,0:T(8,128)(2,1)S(1)}, u32[]{:S(2)}, u32[]{:S(2)}) collective-permute-start(bf16[64,512]{1,0:T(8,128)(2,1)S(1)} %get-tuple-element.224), channel_id=1, source_target_pairs={{0,2},{2,0},{4,6},{6,4},{1,3},{3,1},{5,7},{7,5},{8,10},{10,8},{12,... | collective-permute-start | bytes 196616 | tf_op jit(solution)/shard_map/ppermute | solution.py:864
  171.0 7.5 %collective-permute-start.31 = (bf16[64,512]{1,0:T(8,128)(2,1)S(1)}, bf16[64,512]{1,0:T(8,128)(2,1)S(1)}, u32[]{:S(2)}, u32[]{:S(2)}) collective-permute-start(bf16[64,512]{1,0:T(8,128)(2,1)S(1)} %get-tuple-element.223), channel_id=1, source_target_pairs={{0,6},{2,4},{4,2},{6,0},{1,7},{3,5},{5,3},{7,1},{8,14},{10,12},{12... | collective-permute-start | bytes 196616 | tf_op jit(solution)/shard_map/ppermute | solution.py:864
  173.5 11.7 %all-to-all-start.5 = ((bf16[4,80,384]{2,1,0:T(8,128)(2,1)}), bf16[4,80,384]{2,1,0:T(8,128)(2,1)}, u32[]{:S(2)}, u32[]{:S(2)}) async-start(bf16[4,80,384]{2,1,0:T(8,128)(2,1)} %add_convert_fusion.1), calls=%async_computation.5 | async-start | bytes 491520 | tf_op jit(solution)/shard_map/all_to_all | solution.py:929
  179.3 7.0 %collective-permute-start.32 = (bf16[64,1152]{1,0:T(8,128)(2,1)}, bf16[64,1152]{1,0:T(8,128)(2,1)}, u32[]{:S(2)}, u32[]{:S(2)}) collective-permute-start(bf16[64,1152]{1,0:T(8,128)(2,1)} %pad_maximum_fusion.2.m0), channel_id=1, source_target_pairs={{0,2},{1,3},{2,0},{3,1},{4,6},{5,7},{6,4},{7,5},{8,10},{9,11},{10,... | collective-permute-start | bytes 442376 | tf_op jit(solution)/shard_map/ppermute | solution.py:608
  179.8 6.5 %collective-permute-start.33 = (bf16[64,1152]{1,0:T(8,128)(2,1)}, bf16[64,1152]{1,0:T(8,128)(2,1)}, u32[]{:S(2)}, u32[]{:S(2)}) collective-permute-start(bf16[64,1152]{1,0:T(8,128)(2,1)} %pad_maximum_fusion.2.m0), channel_id=1, source_target_pairs={{0,1},{1,0},{2,3},{3,2},{4,5},{5,4},{6,7},{7,6},{8,9},{9,8},{10,11... | collective-permute-start | bytes 442376 | tf_op jit(solution)/shard_map/ppermute | solution.py:608
  179.8 6.5 %collective-permute-start.34 = (bf16[64,1152]{1,0:T(8,128)(2,1)}, bf16[64,1152]{1,0:T(8,128)(2,1)}, u32[]{:S(2)}, u32[]{:S(2)}) collective-permute-start(bf16[64,1152]{1,0:T(8,128)(2,1)} %pad_maximum_fusion.2.m0), channel_id=1, source_target_pairs={{0,3},{1,2},{2,1},{3,0},{4,7},{5,6},{6,5},{7,4},{8,11},{9,10},{10,... | collective-permute-start | bytes 442376 | tf_op jit(solution)/shard_map/ppermute | solution.py:608
  186.3 4.7 %copy-start.5 = (bf16[80,384]{1,0:T(8,128)(2,1)}, bf16[80,384]{1,0:T(8,128)(2,1)S(1)}, u32[]{:S(2)}) copy-start(bf16[80,384]{1,0:T(8,128)(2,1)S(1)} %reduce_sum.38.a0) | copy-start | bytes 184324
  186.3 4.7 %collective-permute-start.38 = (bf16[80,384]{1,0:T(8,128)(2,1)S(1)}, bf16[80,384]{1,0:T(8,128)(2,1)}, u32[]{:S(2)}, u32[]{:S(2)}) collective-permute-start(bf16[80,384]{1,0:T(8,128)(2,1)S(1)} %reduce_sum.38.a0), channel_id=1, source_target_pairs={{0,2},{1,3},{2,0},{3,1},{4,6},{5,7},{6,4},{7,5},{8,10},{9,11},{10,... | collective-permute-start | bytes 184328 | tf_op jit(solution)/shard_map/ppermute | solution.py:608
  187.7 3.3 %collective-permute-start.39 = (bf16[80,384]{1,0:T(8,128)(2,1)S(1)}, bf16[80,384]{1,0:T(8,128)(2,1)}, u32[]{:S(2)}, u32[]{:S(2)}) collective-permute-start(bf16[80,384]{1,0:T(8,128)(2,1)S(1)} %reduce_sum.38.a0), channel_id=1, source_target_pairs={{0,1},{1,0},{2,3},{3,2},{4,5},{5,4},{6,7},{7,6},{8,9},{9,8},{10,11... | collective-permute-start | bytes 184328 | tf_op jit(solution)/shard_map/ppermute | solution.py:608
  187.9 4.5 %collective-permute-start.40 = (bf16[80,384]{1,0:T(8,128)(2,1)S(1)}, bf16[80,384]{1,0:T(8,128)(2,1)}, u32[]{:S(2)}, u32[]{:S(2)}) collective-permute-start(bf16[80,384]{1,0:T(8,128)(2,1)S(1)} %reduce_sum.38.a0), channel_id=1, source_target_pairs={{0,3},{1,2},{2,1},{3,0},{4,7},{5,6},{6,5},{7,4},{8,11},{9,10},{10,... | collective-permute-start | bytes 184328 | tf_op jit(solution)/shard_map/ppermute | solution.py:608
  194.2 12.3 %all-to-all-start.6 = ((f32[8,8,128]{2,1,0:T(8,128)}), f32[8,8,128]{2,1,0:T(8,128)S(1)}, u32[]{:S(2)}, u32[]{:S(2)}) async-start(f32[8,8,128]{2,1,0:T(8,128)} %squares.1), calls=%async_computation.6 | async-start | bytes 65536 | tf_op jit(solution)/shard_map/all_to_all | solution.py:969
  (1 other events, 0.6 us)

commit v7 on v6

--- a/solution.py
+++ b/solution.py
@@ -18,8 +18,9 @@
 WEIGHT_DECAY = 0.01
 ADAM_EPS = 1e-08
 NORM_EPS = 1e-05
-VMEM_BYTES = 65408 * 1024
-
+
+LIMITS = {"squares": 4, "mlp_squares": 4, "collect": 6, "attend": 8}
+LIMIT = 63
 F32 = jnp.float32
 BF16 = jnp.bfloat16
 ANY = pl.BlockSpec(memory_space=pl.ANY)
@@ -544,10 +545,11 @@
         scratch_shapes=scratch,
         input_output_aliases=aliases or {},
         compiler_params=pltpu.CompilerParams(
-            vmem_limit_bytes=VMEM_BYTES, dimension_semantics=("arbitrary",)
+            vmem_limit_bytes=LIMITS.get(name, LIMIT) * 2**20,
+            dimension_semantics=("arbitrary",),
         ),
         cost_estimate=pl.CostEstimate(
-            flops=int(cost * 1e9), bytes_accessed=int(cost * 2e6), transcendentals=0
+            flops=int(cost * 5e8), bytes_accessed=int(cost * 1e6), transcendentals=0
         ),
         name=name,
     )
@@ -879,7 +881,7 @@
     output = collect(results)
     if fits:
         args = [up_keep, up_got, down_keep, down_got]
-        args = lax.optimization_barrier((*args, grad_first, *results))[:4]
+        args = lax.optimization_barrier((*args, grad_first, *results[:3]))[:4]
         piece = shape_of(up_keep.shape[2:], BF16)
         by_hi = shape_of((hi_count, 4, *down_keep.shape[3:]), BF16)
         *parts, down_part = add_call(add_mlp_body, args, [*[piece] * 4, by_hi])

time: 214 us -> 207 us (0.967)
  Pallas kernels: 83.1 us -> 77.9 us
  local copies, waits for them, and re-layouts: 10 us -> 14.4 us
  waiting for transfers between devices: 45 us -> 42.4 us
  other arithmetic: 8.45 us -> 5.91 us
    ppermute x11, waiting for transfers between devices: 15.8 us -> 10.5 us  [swap(): return lax.ppermute(value, axis, [(0, 1), (1, 0)])]
    unnamed x38 -> x86, local copies, waits for them, and re-layouts: 1.65 us -> 6.78 us
    ppermute x15, waiting for transfers between devices: 5.9 us -> 11 us  [from_seq(): lax.ppermute(pieces[k], ('y', 'core'), [(j, j ^ k) for j in range(4)])]
    all_to_all x3, waiting for transfers between devices: 10.6 us -> 6.71 us  [spread_hi(): return lax.all_to_all(spread, 'hi', 0, 0)]
    pallas_call x2, Pallas kernels: 8.28 us -> 5.59 us  [attend(): call(attend_body, steps, [SMEM, SMEM, half_spec((slots, 3 * width), base)...]
    ppermute x15, starting transfers between devices: 12.1 us -> 9.87 us  [from_seq(): lax.ppermute(pieces[k], ('y', 'core'), [(j, j ^ k) for j in range(4)])]
  transfers between devices with their start and end apart: 48 -> 48, of which waited for: 15 -> 16; matrix products, arithmetic and copies ran while one was open for 7% -> 5% of each run, Pallas kernels for 22% -> 21%
where the time goes in v7:
time: 207 us; the launch traced here: 206 us
  Pallas kernels  77.9 us (38%)
  starting transfers between devices  63.4 us (31%)
  waiting for transfers between devices  42.4 us (20%)
  local copies, waits for them, and re-layouts  14.4 us (7%)
  other arithmetic  5.91 us (3%)
    pallas_call x1, Pallas kernels, on_device(): call(functools.partial(mlp_body, dims), rows // group, [SMEM, *[slot_spec...  27.8 us
    all_to_all x3, starting transfers between devices, spread_hi(): return lax.all_to_all(spread, 'hi', 0, 0)  13.4 us
    pallas_call x1, Pallas kernels, on_device(): call(functools.partial(back_last_body, dims), rows - lead, [*back_specs(l...  12 us
    ppermute x15, waiting for transfers between devices, from_seq(): lax.ppermute(pieces[k], ('y', 'core'), [(j, j ^ k) for j in range(4)])  11 us
    ppermute x9, starting transfers between devices, plane_sum(): moved.append(lax.ppermute(parts[k], ('lo', 'y'), perm))  10.6 us
    ppermute x11, waiting for transfers between devices, swap(): return lax.ppermute(value, axis, [(0, 1), (1, 0)])  10.5 us
    ppermute x15, starting transfers between devices, from_seq(): lax.ppermute(pieces[k], ('y', 'core'), [(j, j ^ k) for j in range(4)])  9.87 us
    pallas_call x1, Pallas kernels, on_device(): call(back_first_body, lead, back_specs(0), [*[half_spec((1, part, width),...  8.34 us
  transfers between devices with their start and end apart: 48, of which 16 were waited for; matrix products, arithmetic and copies ran while one was open for 5% of the time, Pallas kernels for 21%

profile of v7, /device:TPU:0, one launch (start us, length us, event | category | flops | bytes accessed | tf_op | source)
XLA Modules:
  0.0 205.7 jit_solution(16584324009344579574)
XLA Ops:
  0.7 1.1 slice.64
  2.6 0.8 broadcast_in_dim.6
  3.4 6.4 %all-to-all-start = ((bf16[4,32,1664]{2,1,0:T(8,128)(2,1)}), bf16[4,32,1664]{2,1,0:T(8,128)(2,1)S(1)}, u32[]{:S(2)}, u32[]{:S(2)}) async-start(bf16[4,32,1664]{2,1,0:T(8,128)(2,1)} %broadcast_in_dim.6), calls=%async_computation | async-start | bytes 851968 | tf_op jit(solution)/shard_map/all_to_all | solution.py:578
  9.8 0.8 dynamic-slice_bitcast_fusion.4
  11.3 1.0 collective-permute-start
  12.8 0.9 slice.68
  14.5 4.7 %collective-permute-done.2.x3 = bf16[4,64,512]{2,1,0:T(8,128)(2,1)S(1)} collective-permute-done((bf16[4,64,512]{2,1,0:T(8,128)(2,1)S(1)}, bf16[4,64,512]{2,1,0:T(8,128)(2,1)S(1)}, u32[]{:S(2)}, u32[]{:S(2)}) %collective-permute-start.2) | collective-permute-done | bytes 262176 | tf_op jit(solution)/shard_map/ppermute | solution.py:571
  19.9 2.3 %all-to-all-done.p0 = bf16[4,32,1664]{2,1,0:T(8,128)(2,1)S(1)} async-done(((bf16[4,32,1664]{2,1,0:T(8,128)(2,1)}), bf16[4,32,1664]{2,1,0:T(8,128)(2,1)S(1)}, u32[]{:S(2)}, u32[]{:S(2)}) %all-to-all-start) | async-done | bytes 426016 | tf_op jit(solution)/shard_map/all_to_all | solution.py:578
  22.2 1.5 collective-permute-start.3
  23.7 1.0 broadcast_in_dim.7
  24.7 3.5 %all-to-all-start.1 = ((bf16[4,32,3072]{2,1,0:T(8,128)(2,1)}), bf16[4,32,3072]{2,1,0:T(8,128)(2,1)S(1)}, u32[]{:S(2)}, u32[]{:S(2)}) async-start(bf16[4,32,3072]{2,1,0:T(8,128)(2,1)} %broadcast_in_dim.7), calls=%async_computation.1 | async-start | bytes 1572864 | tf_op jit(solution)/shard_map/all_to_all | solution.py:578
  28.3 4.7 %collective-permute-done.3.p1 = bf16[4,32,1664]{2,1,0:T(8,128)(2,1)S(1)} collective-permute-done((bf16[4,32,1664]{2,1,0:T(8,128)(2,1)S(1)}, bf16[4,32,1664]{2,1,0:T(8,128)(2,1)S(1)}, u32[]{:S(2)}, u32[]{:S(2)}) %collective-permute-start.3) | collective-permute-done | bytes 426016 | tf_op jit(solution)/shard_map/ppermute | solution.py:559
  33.3 1.5 collective-permute-start.12
  35.5 0.7 copy-done.34
  36.2 0.8 copy-done.35
  37.0 6.2 %qkv.1 = (bf16[1024,512]{1,0:T(8,128)(2,1)}, bf16[1024,1536]{1,0:T(8,128)(2,1)}) custom-call(s32[9]{0:T(128)} %stack.41.place, bf16[4,64,512]{2,1,0:T(8,128)(2,1)} %get-tuple-element.218.x0, bf16[4,64,512]{2,1,0:T(8,128)(2,1)} %collective-permute-done.x1, bf16[4,64,512]{2,1,0:T(8,128)(2,1)} %collective-permute-done.1.x2, bf16[4,64,512]{2,1,0:T(8,128)(2,1)} %copy-done.36, ...), custom_call_target="tpu_custom_call" | custom-call | flops 3500000000 | bytes 7000000 | tf_op jit(solution)/shard_map/qkv/pallas_call | solution.py:699
  43.3 4.4 %all-to-all-done.1.b0 = bf16[4,32,3072]{2,1,0:T(8,128)(2,1)S(1)} async-done(((bf16[4,32,3072]{2,1,0:T(8,128)(2,1)}), bf16[4,32,3072]{2,1,0:T(8,128)(2,1)S(1)}, u32[]{:S(2)}, u32[]{:S(2)}) %all-to-all-start.1) | async-done | bytes 786464 | tf_op jit(solution)/shard_map/all_to_all | solution.py:578
  47.7 1.0 broadcast_in_dim.8
  48.7 3.5 %all-to-all-start.2 = ((bf16[4,2,32,1536]{3,2,1,0:T(8,128)(2,1)}), bf16[4,2,32,1536]{3,2,1,0:T(8,128)(2,1)S(1)}, u32[]{:S(2)}, u32[]{:S(2)}) async-start(bf16[4,2,32,1536]{3,2,1,0:T(8,128)(2,1)} %broadcast_in_dim.8), calls=%async_computation.2 | async-start | bytes 1572864 | tf_op jit(solution)/shard_map/all_to_all | solution.py:578
  53.1 0.8 dynamic-slice_bitcast_fusion
  53.9 1.4 collective-permute-start.10
  55.3 0.7 collective-permute-start.9
  56.0 1.9 copy-done.18
  57.9 3.9 %attend.2 = (bf16[1024,512]{1,0:T(8,128)(2,1)S(1)}, f32[4,8,256]{2,1,0:T(8,128)S(1)}) custom-call(s32[9]{0:T(128)S(1)} %constant_dynamic-update-slice_fusion.1.place, s32[4]{0:T(128)S(1)} %dynamic_slice.52.lengths, bf16[1024,1536]{1,0:T(8,128)(2,1)S(1)} %copy-done.18), custom_call_target="tpu_custom_call" | custom-call | flops 6000000000 | bytes 12000000 | tf_op jit(solution)/shard_map/attend/pallas_call | solution.py:723
  61.9 6.2 %collective-permute-done.9.d2 = bf16[4,64,512]{2,1,0:T(8,128)(2,1)S(1)} collective-permute-done((bf16[4,64,512]{2,1,0:T(8,128)(2,1)S(1)}, bf16[4,64,512]{2,1,0:T(8,128)(2,1)S(1)}, u32[]{:S(2)}, u32[]{:S(2)}) %collective-permute-start.9) | collective-permute-done | bytes 262176 | tf_op jit(solution)/shard_map/ppermute | solution.py:571
  68.1 2.8 %collective-permute-done.6.b1 = bf16[4,32,3072]{2,1,0:T(8,128)(2,1)} collective-permute-done((bf16[4,32,3072]{2,1,0:T(8,128)(2,1)S(1)}, bf16[4,32,3072]{2,1,0:T(8,128)(2,1)}, u32[]{:S(2)}, u32[]{:S(2)}) %collective-permute-start.6) | collective-permute-done | bytes 786464 | tf_op jit(solution)/shard_map/ppermute | solution.py:559
  70.9 1.7 attend.3
  72.6 1.0 copy-done.19
  73.6 0.9 copy-done.27
  75.0 2.0 collective-permute-done.13.c1
  77.0 27.8 %mlp.1 = (bf16[4,64,512]{2,1,0:T(8,128)(2,1)}, bf16[4,64,512]{2,1,0:T(8,128)(2,1)}, bf16[4,64,512]{2,1,0:T(8,128)(2,1)}, bf16[4,64,512]{2,1,0:T(8,128)(2,1)}, f3...) custom-call(s32[9]{0:T(128)} %stack.41.place, ...), custom_call_target="tpu_custom_call" | custom-call | flops 12000000000 | bytes 24000000 | tf_op jit(solution)/shard_map/mlp/pallas_call | solution.py:763
  105.9 1.3 collective-permute-start.15
  107.2 8.3 %back_first.1 = (bf16[2,64,512]{2,1,0:T(8,128)(2,1)}, bf16[2,64,512]{2,1,0:T(8,128)(2,1)}, bf16[2,64,512]{2,1,0:T(8,128)(2,1)}, bf16[2,64,512]{2,1,0:T(8,128)(2,...) custom-call(s32[9]{0:T(128)} %stack.41.place, s32[4]{0:T(128)} %copy-done.17, ...), custom_call_target="tpu_custom_call" | custom-call | flops 5500000256 | bytes 11000000 | tf_op jit(solution)/shard_map/back_first/pallas_call | solution.py:837
  115.6 0.8 collective-permute-start.18
  116.4 1.1 collective-permute-start.19
  117.5 3.8 %add.106 = (bf16[4,64,640]{2,1,0:T(8,128)(2,1)}, bf16[4,64,640]{2,1,0:T(8,128)(2,1)}, bf16[4,64,640]{2,1,0:T(8,128)(2,1)}, bf16[4,64,640]{2,1,0:T(8,128)(2,1)}, bf16[4,4,64,512]{3,2,1,0:T(8,128)(2,1)}) custom-call(bf16[4,4,64,640]{3,2,1,0:T(8,128)(2,1)} %bitcast.63, bf16[4,4,64,640]{3,2,1,0:T(8,128)(2,1)} %bitcast.22.got, bf16[4,4,64,512]{3,2,1,0:T(8,128)(2,1)} %bitcast.64, ...), custom_call_target="tpu_custom_call" | custom-call | flops 1500000000 | bytes 3000000 | tf_op jit(solution)/shard_map/add/pallas_call | solution.py:851
  122.6 4.7 %all-to-all-start.4 = ((bf16[4,4,64,512]{3,2,1,0:T(8,128)(2,1)}), bf16[4,4,64,512]{3,2,1,0:T(8,128)(2,1)}, u32[]{:S(2)}, u32[]{:S(2)}) async-start(bf16[4,4,64,512]{3,2,1,0:T(8,128)(2,1)} %get-tuple-element.180), calls=%async_computation.4 | async-start | bytes 2097152 | tf_op jit(solution)/shard_map/all_to_all | solution.py:890
  127.3 2.3 %collective-permute-start.27 = (bf16[4,64,640]{2,1,0:T(8,128)(2,1)}, bf16[4,64,640]{2,1,0:T(8,128)(2,1)}, u32[]{:S(2)}, u32[]{:S(2)}) collective-permute-start(bf16[4,64,640]{2,1,0:T(8,128)(2,1)} %get-tuple-element.179), channel_id=1, source_target_pairs={{0,6},{2,4},{4,2},{6,0},{1,7},{3,5},{5,3},{7,1},{8,14},{10,12},{12... | collective-permute-start | bytes 983048 | tf_op jit(solution)/shard_map/ppermute | solution.py:866
  129.6 12.0 %back_last.1 = (bf16[2,64,512]{2,1,0:T(8,128)(2,1)}, bf16[2,64,512]{2,1,0:T(8,128)(2,1)}, bf16[2,64,512]{2,1,0:T(8,128)(2,1)}, bf16[2,64,512]{2,1,0:T(8,128)(2,1...) custom-call(s32[9]{0:T(128)} %copy-done.40, s32[4]{0:T(128)} %copy-done.17, ...), custom_call_target="tpu_custom_call" | custom-call | flops 6499999744 | bytes 13000000 | tf_op jit(solution)/shard_map/back_last/pallas_call | solution.py:893
  142.2 0.7 collective-permute-start.23
  143.7 0.9 collective-permute-done.28
  144.5 2.4 %add.107 = (bf16[4,80,384]{2,1,0:T(8,128)(2,1)}, bf16[4,80,384]{2,1,0:T(8,128)(2,1)}, bf16[4,80,384]{2,1,0:T(8,128)(2,1)}, bf16[4,80,384]{2,1,0:T(8,128)(2,1)}) custom-call(bf16[4,4,64,384]{3,2,1,0:T(8,128)(2,1)} %bitcast.65, bf16[4,4,64,384]{3,2,1,0:T(8,128)(2,1)} %bitcast.26.got, f32[16,512]{1,0:T(8,128)} %get-tuple-element.190.vec), custom_call_target="tpu_custom_call" | custom-call | flops 1500000000 | bytes 3000000 | tf_op jit(solution)/shard_map/add/pallas_call | solution.py:851
  148.2 2.2 %collective-permute-start.37 = (bf16[4,80,384]{2,1,0:T(8,128)(2,1)}, bf16[4,80,384]{2,1,0:T(8,128)(2,1)S(1)}, u32[]{:S(2)}, u32[]{:S(2)}) collective-permute-start(bf16[4,80,384]{2,1,0:T(8,128)(2,1)} %get-tuple-element.194), channel_id=1, source_target_pairs={{0,6},{2,4},{4,2},{6,0},{1,7},{3,5},{5,3},{7,1},{8,14},{10,12},{12... | collective-permute-start | bytes 737288 | tf_op jit(solution)/shard_map/ppermute | solution.py:866
  150.4 2.2 %add_convert_fusion = bf16[4,64,640]{2,1,0:T(8,128)(2,1)} fusion(bf16[4,64,640]{2,1,0:T(8,128)(2,1)} %collective-permute-done.27, bf16[4,64,640]{2,1,0:T(8,128)(2,1)} %collective-permute-done.26, bf16[4,64,640]{2,1,0:T(8,128)(2,1)} %collective-permute-done.25, bf16[4,64,640]{2,1,0:T(8,128)(2,1)} %get-tuple-element.176), kind=kLoop, calls=%fused_computation | loop fusion | flops 1310720 | bytes 1638400 | tf_op jit(solution)/shard_map/convert_element_type | solution.py:871
  153.1 4.7 %all-to-all-start.3 = ((bf16[4,64,640]{2,1,0:T(8,128)(2,1)}), bf16[4,64,640]{2,1,0:T(8,128)(2,1)S(1)}, u32[]{:S(2)}, u32[]{:S(2)}) async-start(bf16[4,64,640]{2,1,0:T(8,128)(2,1)} %add_convert_fusion), calls=%async_computation.3 | async-start | bytes 655360 | tf_op jit(solution)/shard_map/all_to_all | solution.py:927
  157.8 3.8 %collective-permute-done.36 = bf16[4,80,384]{2,1,0:T(8,128)(2,1)S(1)} collective-permute-done((bf16[4,80,384]{2,1,0:T(8,128)(2,1)}, bf16[4,80,384]{2,1,0:T(8,128)(2,1)S(1)}, u32[]{:S(2)}, u32[]{:S(2)}) %collective-permute-start.36) | collective-permute-done | bytes 245792 | tf_op jit(solution)/shard_map/ppermute | solution.py:866
  161.5 1.4 reduce_sum.37
  163.0 1.3 collective-permute-start.29
  164.6 2.0 collective-permute-start.31
  166.6 0.8 add_convert_fusion.1
  167.5 4.9 %all-to-all-start.5 = ((bf16[4,80,384]{2,1,0:T(8,128)(2,1)}), bf16[4,80,384]{2,1,0:T(8,128)(2,1)S(1)}, u32[]{:S(2)}, u32[]{:S(2)}) async-start(bf16[4,80,384]{2,1,0:T(8,128)(2,1)} %add_convert_fusion.1), calls=%async_computation.5 | async-start | bytes 491520 | tf_op jit(solution)/shard_map/all_to_all | solution.py:931
  173.1 1.6 collective-permute-start.34
  174.7 1.6 collect.2
  176.3 2.9 %all-to-all-done.5 = bf16[4,80,384]{2,1,0:T(8,128)(2,1)S(1)} async-done(((bf16[4,80,384]{2,1,0:T(8,128)(2,1)}), bf16[4,80,384]{2,1,0:T(8,128)(2,1)S(1)}, u32[]{:S(2)}, u32[]{:S(2)}) %all-to-all-start.5) | async-done | bytes 245792 | tf_op jit(solution)/shard_map/all_to_all | solution.py:931
  179.3 1.4 collective-permute-start.38
  181.0 1.1 collective-permute-start.40
  182.0 0.8 mlp_squares.1.before
  182.9 1.0 collective-permute-done.38.a1
  183.9 1.4 collective-permute-done.40.a3
  185.4 1.3 squares.1
  186.7 5.5 %all-to-all-start.6 = ((f32[8,8,128]{2,1,0:T(8,128)}), f32[8,8,128]{2,1,0:T(8,128)S(1)}, u32[]{:S(2)}, u32[]{:S(2)}) async-start(f32[8,8,128]{2,1,0:T(8,128)} %squares.1), calls=%async_computation.6 | async-start | bytes 65536 | tf_op jit(solution)/shard_map/all_to_all | solution.py:971
  192.3 2.1 %collect.3 = bf16[4,4,64,512]{3,2,1,0:T(8,128)(2,1)} custom-call(s32[9]{0:T(128)S(1)} %copy-done.4, bf16[2,64,512]{2,1,0:T(8,128)(2,1)S(1)} %copy-done.21, bf16[2,64,512]{2,1,0:T(8,128)(2,1)S(1)} %copy-done.9, bf16[2,64,512]{2,1,0:T(8,128)(2,1)S(1)} %copy-done.11, bf16[2,64,512]{2,1,0:T(8,128)(2,1)} %collective-permute-done.19.refs_3_, ...), custom_call_target="tpu_custom_call" | custom-call | flops 1000000000 | bytes 2000000 | tf_op jit(solution)/shard_map/collect/pallas_call | solution.py:803
  194.3 4.5 %all-to-all-done.6.squares = f32[8,8,128]{2,1,0:T(8,128)S(1)} async-done(((f32[8,8,128]{2,1,0:T(8,128)}), f32[8,8,128]{2,1,0:T(8,128)S(1)}, u32[]{:S(2)}, u32[]{:S(2)}) %all-to-all-start.6) | async-done | bytes 32800 | tf_op jit(solution)/shard_map/all_to_all | solution.py:971
  199.5 6.0 %adam.1 = (f32[1,1]{1,0:T(1,128)}, f32[64,2048]{1,0:T(8,128)}, f32[64,2048]{1,0:T(8,128)}, f32[64,2048]{1,0:T(8,128)}, f32[2,64,2048]{2,1,0:T(8,128)}, /*index=5...) custom-call(s32[9]{0:T(128)} %stack.41.place, ...), custom_call_target="tpu_custom_call" | custom-call | flops 3000000000 | bytes 6000000 | tf_op jit(solution)/shard_map/adam/pallas_call | solution.py:974
  (174 shorter events, 13.4 us)
Async XLA Ops:
  3.4 10.3 %copy-start.29 = (f32[2,64,2048]{2,1,0:T(8,128)S(1)}, f32[2,64,2048]{2,1,0:T(8,128)}, u32[]{:S(2)}) copy-start(f32[2,64,2048]{2,1,0:T(8,128)} %mlp_w.1) | copy-start | bytes 3145732
  3.4 18.8 %all-to-all-start = ((bf16[4,32,1664]{2,1,0:T(8,128)(2,1)}), bf16[4,32,1664]{2,1,0:T(8,128)(2,1)S(1)}, u32[]{:S(2)}, u32[]{:S(2)}) async-start(bf16[4,32,1664]{2,1,0:T(8,128)(2,1)} %broadcast_in_dim.6), calls=%async_computation | async-start | bytes 851968 | tf_op jit(solution)/shard_map/all_to_all | solution.py:578
  10.7 8.5 %collective-permute-start.2 = (bf16[4,64,512]{2,1,0:T(8,128)(2,1)S(1)}, bf16[4,64,512]{2,1,0:T(8,128)(2,1)S(1)}, u32[]{:S(2)}, u32[]{:S(2)}) collective-permute-start(bf16[4,64,512]{2,1,0:T(8,128)(2,1)S(1)} %get-tuple-element.216), channel_id=1, source_target_pairs={{0,3},{1,2},{2,1},{3,0},{4,7},{5,6},{6,5},{7,4},{8,11},{9,10},{10,... | collective-permute-start | bytes 786440 | tf_op jit(solution)/shard_map/ppermute | solution.py:571
  11.3 24.1 %collective-permute-start = (bf16[4,64,512]{2,1,0:T(8,128)(2,1)S(1)}, bf16[4,64,512]{2,1,0:T(8,128)(2,1)}, u32[]{:S(2)}, u32[]{:S(2)}) collective-permute-start(bf16[4,64,512]{2,1,0:T(8,128)(2,1)S(1)} %get-tuple-element.217), channel_id=1, source_target_pairs={{0,1},{1,0},{2,3},{3,2},{4,5},{5,4},{6,7},{7,6},{8,9},{9,8},{10,11... | collective-permute-start | bytes 786440 | tf_op jit(solution)/shard_map/ppermute | solution.py:571
  12.3 23.2 %collective-permute-start.1 = (bf16[4,64,512]{2,1,0:T(8,128)(2,1)S(1)}, bf16[4,64,512]{2,1,0:T(8,128)(2,1)}, u32[]{:S(2)}, u32[]{:S(2)}) collective-permute-start(bf16[4,64,512]{2,1,0:T(8,128)(2,1)S(1)} %get-tuple-element.219), channel_id=1, source_target_pairs={{0,2},{1,3},{2,0},{3,1},{4,6},{5,7},{6,4},{7,5},{8,10},{9,11},{10,... | collective-permute-start | bytes 786440 | tf_op jit(solution)/shard_map/ppermute | solution.py:571
  22.2 10.8 %copy-start.28 = (bf16[4,32,1664]{2,1,0:T(8,128)(2,1)}, bf16[4,32,1664]{2,1,0:T(8,128)(2,1)S(1)}, u32[]{:S(2)}) copy-start(bf16[4,32,1664]{2,1,0:T(8,128)(2,1)S(1)} %all-to-all-done.p0) | copy-start | bytes 1277956
  22.2 10.8 %collective-permute-start.3 = (bf16[4,32,1664]{2,1,0:T(8,128)(2,1)S(1)}, bf16[4,32,1664]{2,1,0:T(8,128)(2,1)S(1)}, u32[]{:S(2)}, u32[]{:S(2)}) collective-permute-start(bf16[4,32,1664]{2,1,0:T(8,128)(2,1)S(1)} %all-to-all-done.p0), channel_id=1, source_target_pairs={{0,4},{4,0},{1,5},{5,1},{2,6},{6,2},{3,7},{7,3},{8,12},{12,8},{9,1... | collective-permute-start | bytes 1277960 | tf_op jit(solution)/shard_map/ppermute | solution.py:559
  24.7 23.0 %all-to-all-start.1 = ((bf16[4,32,3072]{2,1,0:T(8,128)(2,1)}), bf16[4,32,3072]{2,1,0:T(8,128)(2,1)S(1)}, u32[]{:S(2)}, u32[]{:S(2)}) async-start(bf16[4,32,3072]{2,1,0:T(8,128)(2,1)} %broadcast_in_dim.7), calls=%async_computation.1 | async-start | bytes 1572864 | tf_op jit(solution)/shard_map/all_to_all | solution.py:578
  28.2 7.3 %collective-permute-start.4 = (bf16[4,32,1664]{2,1,0:T(8,128)(2,1)S(1)}, bf16[4,32,1664]{2,1,0:T(8,128)(2,1)S(1)}, u32[]{:S(2)}, u32[]{:S(2)}) collective-permute-start(bf16[4,32,1664]{2,1,0:T(8,128)(2,1)S(1)} %all-to-all-done.p0), channel_id=1, source_target_pairs={{0,1},{1,0},{2,3},{3,2},{4,5},{5,4},{6,7},{7,6},{8,9},{9,8},{10,11... | collective-permute-start | bytes 1277960 | tf_op jit(solution)/shard_map/ppermute | solution.py:559
  33.0 2.5 %collective-permute-start.5 = (bf16[4,32,1664]{2,1,0:T(8,128)(2,1)S(1)}, bf16[4,32,1664]{2,1,0:T(8,128)(2,1)S(1)}, u32[]{:S(2)}, u32[]{:S(2)}) collective-permute-start(bf16[4,32,1664]{2,1,0:T(8,128)(2,1)S(1)} %collective-permute-done.3.p1), channel_id=1, source_target_pairs={{0,1},{1,0},{2,3},{3,2},{4,5},{5,4},{6,7},{7,6},{8,9},{9,8},{10,11... | collective-permute-start | bytes 1277960 | tf_op jit(solution)/shard_map/ppermute | solution.py:559
  33.3 10.0 %collective-permute-start.12 = (bf16[32,1536]{1,0:T(8,128)(2,1)S(1)}, bf16[32,1536]{1,0:T(8,128)(2,1)S(1)}, u32[]{:S(2)}, u32[]{:S(2)}) collective-permute-start(bf16[32,1536]{1,0:T(8,128)(2,1)S(1)} %fusion.4), channel_id=1, source_target_pairs={{0,4},{4,0},{1,5},{5,1},{2,6},{6,2},{3,7},{7,3},{8,12},{12,8},{9,1... | collective-permute-start | bytes 294920 | tf_op jit(solution)/shard_map/ppermute | solution.py:559
  43.2 9.6 %copy-start.2 = (s32[9]{0:T(128)S(1)}, s32[9]{0:T(128)}, u32[]{:S(2)}) copy-start(s32[9]{0:T(128)} %stack.41.place) | copy-start | bytes 112
  43.2 9.6 %copy-start.33 = (s32[4,4]{1,0:T(4,128)S(1)}, s32[4,4]{1,0:T(4,128)}, u32[]{:S(2)}) copy-start(s32[4,4]{1,0:T(4,128)} %param.20) | copy-start | bytes 196
  43.3 9.8 %copy-start.25 = (bf16[4,4,64,512]{3,2,1,0:T(8,128)(2,1)S(1)}, bf16[4,4,64,512]{3,2,1,0:T(8,128)(2,1)}, u32[]{:S(2)}) copy-start(bf16[4,4,64,512]{3,2,1,0:T(8,128)(2,1)} %param.19) | copy-start | bytes 3145732
  48.7 24.9 %all-to-all-start.2 = ((bf16[4,2,32,1536]{3,2,1,0:T(8,128)(2,1)}), bf16[4,2,32,1536]{3,2,1,0:T(8,128)(2,1)S(1)}, u32[]{:S(2)}, u32[]{:S(2)}) async-start(bf16[4,2,32,1536]{3,2,1,0:T(8,128)(2,1)} %broadcast_in_dim.8), calls=%async_computation.2 | async-start | bytes 1572864 | tf_op jit(solution)/shard_map/all_to_all | solution.py:578
  52.2 18.7 %collective-permute-start.6 = (bf16[4,32,3072]{2,1,0:T(8,128)(2,1)S(1)}, bf16[4,32,3072]{2,1,0:T(8,128)(2,1)}, u32[]{:S(2)}, u32[]{:S(2)}) collective-permute-start(bf16[4,32,3072]{2,1,0:T(8,128)(2,1)S(1)} %all-to-all-done.1.b0), channel_id=1, source_target_pairs={{0,4},{4,0},{1,5},{5,1},{2,6},{6,2},{3,7},{7,3},{8,12},{12,8},{9,1... | collective-permute-start | bytes 2359304 | tf_op jit(solution)/shard_map/ppermute | solution.py:559
  52.8 18.1 %collective-permute-start.7 = (bf16[4,32,3072]{2,1,0:T(8,128)(2,1)S(1)}, bf16[4,32,3072]{2,1,0:T(8,128)(2,1)}, u32[]{:S(2)}, u32[]{:S(2)}) collective-permute-start(bf16[4,32,3072]{2,1,0:T(8,128)(2,1)S(1)} %all-to-all-done.1.b0), channel_id=1, source_target_pairs={{0,1},{1,0},{2,3},{3,2},{4,5},{5,4},{6,7},{7,6},{8,9},{9,8},{10,11... | collective-permute-start | bytes 2359304 | tf_op jit(solution)/shard_map/ppermute | solution.py:559
  53.0 17.9 %copy-start.17 = (s32[4]{0:T(128)}, s32[4]{0:T(128)S(1)}, u32[]{:S(2)}) copy-start(s32[4]{0:T(128)S(1)} %dynamic_slice.52.lengths) | copy-start | bytes 52
  53.9 8.0 %collective-permute-start.10 = (bf16[4,64,512]{2,1,0:T(8,128)(2,1)S(1)}, bf16[4,64,512]{2,1,0:T(8,128)(2,1)S(1)}, u32[]{:S(2)}, u32[]{:S(2)}) collective-permute-start(bf16[4,64,512]{2,1,0:T(8,128)(2,1)S(1)} %get-tuple-element.212), channel_id=1, source_target_pairs={{0,3},{1,2},{2,1},{3,0},{4,7},{5,6},{6,5},{7,4},{8,11},{9,10},{10,... | collective-permute-start | bytes 786440 | tf_op jit(solution)/shard_map/ppermute | solution.py:571
  55.2 6.7 %collective-permute-start.8 = (bf16[4,64,512]{2,1,0:T(8,128)(2,1)S(1)}, bf16[4,64,512]{2,1,0:T(8,128)(2,1)S(1)}, u32[]{:S(2)}, u32[]{:S(2)}) collective-permute-start(bf16[4,64,512]{2,1,0:T(8,128)(2,1)S(1)} %get-tuple-element.214), channel_id=1, source_target_pairs={{0,1},{1,0},{2,3},{3,2},{4,5},{5,4},{6,7},{7,6},{8,9},{9,8},{10,11... | collective-permute-start | bytes 786440 | tf_op jit(solution)/shard_map/ppermute | solution.py:571
  55.3 12.8 %collective-permute-start.9 = (bf16[4,64,512]{2,1,0:T(8,128)(2,1)S(1)}, bf16[4,64,512]{2,1,0:T(8,128)(2,1)S(1)}, u32[]{:S(2)}, u32[]{:S(2)}) collective-permute-start(bf16[4,64,512]{2,1,0:T(8,128)(2,1)S(1)} %get-tuple-element.213), channel_id=1, source_target_pairs={{0,2},{1,3},{2,0},{3,1},{4,6},{5,7},{6,4},{7,5},{8,10},{9,11},{10,... | collective-permute-start | bytes 786440 | tf_op jit(solution)/shard_map/ppermute | solution.py:571
  70.9 4.1 %collective-permute-start.11 = (bf16[4,32,3072]{2,1,0:T(8,128)(2,1)}, bf16[4,32,3072]{2,1,0:T(8,128)(2,1)}, u32[]{:S(2)}, u32[]{:S(2)}) collective-permute-start(bf16[4,32,3072]{2,1,0:T(8,128)(2,1)} %collective-permute-done.6.b1), channel_id=1, source_target_pairs={{0,1},{1,0},{2,3},{3,2},{4,5},{5,4},{6,7},{7,6},{8,9},{9,8},{10,11... | collective-permute-start | bytes 2359304 | tf_op jit(solution)/shard_map/ppermute | solution.py:559
  73.6 31.2 %copy-start.23 = (f32[4,8,256]{2,1,0:T(8,128)}, f32[4,8,256]{2,1,0:T(8,128)S(1)}, u32[]{:S(2)}) copy-start(f32[4,8,256]{2,1,0:T(8,128)S(1)} %get-tuple-element.161.lse) | copy-start | bytes 98308
  74.5 30.9 %copy-start.3 = (s32[9]{0:T(128)S(1)}, s32[9]{0:T(128)}, u32[]{:S(2)}) copy-start(s32[9]{0:T(128)} %stack.41.place) | copy-start | bytes 112
  74.5 2.5 %collective-permute-start.13 = (bf16[4,2,32,1536]{3,2,1,0:T(8,128)(2,1)S(1)}, bf16[4,2,32,1536]{3,2,1,0:T(8,128)(2,1)}, u32[]{:S(2)}, u32[]{:S(2)}) collective-permute-start(bf16[4,2,32,1536]{3,2,1,0:T(8,128)(2,1)S(1)} %all-to-all-done.2.c0), channel_id=1, source_target_pairs={{0,1},{1,0},{2,3},{3,2},{4,5},{5,4},{6,7},{7,6},{8,9},{9,8},{10,11... | collective-permute-start | bytes 2359304 | tf_op jit(solution)/shard_map/ppermute | solution.py:559
  104.8 12.6 %collective-permute-start.20 = (bf16[2,2,4,64,640]{4,3,2,1,0:T(8,128)(2,1)}, bf16[2,2,4,64,640]{4,3,2,1,0:T(8,128)(2,1)}, u32[]{:S(2)}, u32[]{:S(2)}) collective-permute-start(bf16[2,2,4,64,640]{4,3,2,1,0:T(8,128)(2,1)} %get-tuple-element.158), channel_id=1, source_target_pairs={{0,1},{1,0},{2,3},{3,2},{4,5},{5,4},{6,7},{7,6},{8,9},{9,8},{10,11... | collective-permute-start | bytes 3932168 | tf_op jit(solution)/shard_map/ppermute | solution.py:559
  105.3 12.2 %collective-permute-start.21 = (bf16[2,2,4,64,512]{4,3,2,1,0:T(8,128)(2,1)}, bf16[2,2,4,64,512]{4,3,2,1,0:T(8,128)(2,1)}, u32[]{:S(2)}, u32[]{:S(2)}) collective-permute-start(bf16[2,2,4,64,512]{4,3,2,1,0:T(8,128)(2,1)} %get-tuple-element.159), channel_id=1, source_target_pairs={{0,1},{1,0},{2,3},{3,2},{4,5},{5,4},{6,7},{7,6},{8,9},{9,8},{10,11... | collective-permute-start | bytes 3145736 | tf_op jit(solution)/shard_map/ppermute | solution.py:559
  105.4 10.1 %copy-start.40 = (s32[9]{0:T(128)}, s32[9]{0:T(128)S(1)}, u32[]{:S(2)}) copy-start(s32[9]{0:T(128)S(1)} %constant_dynamic-update-slice_fusion.place) | copy-start | bytes 112
  105.4 10.2 %collective-permute-start.14 = (bf16[4,64,512]{2,1,0:T(8,128)(2,1)}, bf16[4,64,512]{2,1,0:T(8,128)(2,1)S(1)}, u32[]{:S(2)}, u32[]{:S(2)}) collective-permute-start(bf16[4,64,512]{2,1,0:T(8,128)(2,1)} %get-tuple-element.155), channel_id=1, source_target_pairs={{0,1},{1,0},{2,3},{3,2},{4,5},{5,4},{6,7},{7,6},{8,9},{9,8},{10,11... | collective-permute-start | bytes 786440 | tf_op jit(solution)/shard_map/ppermute | solution.py:571
  105.9 10.5 %collective-permute-start.15 = (bf16[4,64,512]{2,1,0:T(8,128)(2,1)}, bf16[4,64,512]{2,1,0:T(8,128)(2,1)S(1)}, u32[]{:S(2)}, u32[]{:S(2)}) collective-permute-start(bf16[4,64,512]{2,1,0:T(8,128)(2,1)} %get-tuple-element.156), channel_id=1, source_target_pairs={{0,2},{1,3},{2,0},{3,1},{4,6},{5,7},{6,4},{7,5},{8,10},{9,11},{10,... | collective-permute-start | bytes 786440 | tf_op jit(solution)/shard_map/ppermute | solution.py:571
  115.5 11.8 %collective-permute-start.17 = (bf16[2,64,512]{2,1,0:T(8,128)(2,1)}, bf16[2,64,512]{2,1,0:T(8,128)(2,1)S(1)}, u32[]{:S(2)}, u32[]{:S(2)}) collective-permute-start(bf16[2,64,512]{2,1,0:T(8,128)(2,1)} %get-tuple-element.166), channel_id=1, source_target_pairs={{0,1},{1,0},{2,3},{3,2},{4,5},{5,4},{6,7},{7,6},{8,9},{9,8},{10,11... | collective-permute-start | bytes 393224 | tf_op jit(solution)/shard_map/ppermute | solution.py:571
  115.6 26.0 %collective-permute-start.18 = (bf16[2,64,512]{2,1,0:T(8,128)(2,1)}, bf16[2,64,512]{2,1,0:T(8,128)(2,1)S(1)}, u32[]{:S(2)}, u32[]{:S(2)}) collective-permute-start(bf16[2,64,512]{2,1,0:T(8,128)(2,1)} %get-tuple-element.167), channel_id=1, source_target_pairs={{0,2},{1,3},{2,0},{3,1},{4,6},{5,7},{6,4},{7,5},{8,10},{9,11},{10,... | collective-permute-start | bytes 393224 | tf_op jit(solution)/shard_map/ppermute | solution.py:571
  116.4 25.2 %collective-permute-start.19 = (bf16[2,64,512]{2,1,0:T(8,128)(2,1)}, bf16[2,64,512]{2,1,0:T(8,128)(2,1)}, u32[]{:S(2)}, u32[]{:S(2)}) collective-permute-start(bf16[2,64,512]{2,1,0:T(8,128)(2,1)} %get-tuple-element.168), channel_id=1, source_target_pairs={{0,3},{1,2},{2,1},{3,0},{4,7},{5,6},{6,5},{7,4},{8,11},{9,10},{10,... | collective-permute-start | bytes 393224 | tf_op jit(solution)/shard_map/ppermute | solution.py:571
  121.3 20.3 %collective-permute-start.25 = (bf16[4,64,640]{2,1,0:T(8,128)(2,1)}, bf16[4,64,640]{2,1,0:T(8,128)(2,1)}, u32[]{:S(2)}, u32[]{:S(2)}) collective-permute-start(bf16[4,64,640]{2,1,0:T(8,128)(2,1)} %get-tuple-element.178), channel_id=1, source_target_pairs={{0,4},{2,6},{4,0},{6,2},{1,5},{3,7},{5,1},{7,3},{8,12},{10,14},{12... | collective-permute-start | bytes 983048 | tf_op jit(solution)/shard_map/ppermute | solution.py:866
  121.8 19.8 %collective-permute-start.26 = (bf16[4,64,640]{2,1,0:T(8,128)(2,1)}, bf16[4,64,640]{2,1,0:T(8,128)(2,1)}, u32[]{:S(2)}, u32[]{:S(2)}) collective-permute-start(bf16[4,64,640]{2,1,0:T(8,128)(2,1)} %get-tuple-element.177), channel_id=1, source_target_pairs={{0,2},{2,0},{4,6},{6,4},{1,3},{3,1},{5,7},{7,5},{8,10},{10,8},{12,... | collective-permute-start | bytes 983048 | tf_op jit(solution)/shard_map/ppermute | solution.py:866
  122.6 30.5 %all-to-all-start.4 = ((bf16[4,4,64,512]{3,2,1,0:T(8,128)(2,1)}), bf16[4,4,64,512]{3,2,1,0:T(8,128)(2,1)}, u32[]{:S(2)}, u32[]{:S(2)}) async-start(bf16[4,4,64,512]{3,2,1,0:T(8,128)(2,1)} %get-tuple-element.180), calls=%async_computation.4 | async-start | bytes 2097152 | tf_op jit(solution)/shard_map/all_to_all | solution.py:890
  127.3 14.3 %copy-start.8 = (bf16[2,64,512]{2,1,0:T(8,128)(2,1)}, bf16[2,64,512]{2,1,0:T(8,128)(2,1)S(1)}, u32[]{:S(2)}) copy-start(bf16[2,64,512]{2,1,0:T(8,128)(2,1)S(1)} %collective-permute-done.17.refs_1_) | copy-start | bytes 393220
  127.3 14.4 %collective-permute-start.27 = (bf16[4,64,640]{2,1,0:T(8,128)(2,1)}, bf16[4,64,640]{2,1,0:T(8,128)(2,1)}, u32[]{:S(2)}, u32[]{:S(2)}) collective-permute-start(bf16[4,64,640]{2,1,0:T(8,128)(2,1)} %get-tuple-element.179), channel_id=1, source_target_pairs={{0,6},{2,4},{4,2},{6,0},{1,7},{3,5},{5,3},{7,1},{8,14},{10,12},{12... | collective-permute-start | bytes 983048 | tf_op jit(solution)/shard_map/ppermute | solution.py:866
  141.7 2.9 %collective-permute-start.28 = (bf16[2,2,4,64,384]{4,3,2,1,0:T(8,128)(2,1)}, bf16[2,2,4,64,384]{4,3,2,1,0:T(8,128)(2,1)}, u32[]{:S(2)}, u32[]{:S(2)}) collective-permute-start(bf16[2,2,4,64,384]{4,3,2,1,0:T(8,128)(2,1)} %get-tuple-element.189), channel_id=1, source_target_pairs={{0,1},{1,0},{2,3},{3,2},{4,5},{5,4},{6,7},{7,6},{8,9},{9,8},{10,11... | collective-permute-start | bytes 2359304 | tf_op jit(solution)/shard_map/ppermute | solution.py:559
  141.7 6.4 %collective-permute-start.22 = (bf16[2,64,512]{2,1,0:T(8,128)(2,1)}, bf16[2,64,512]{2,1,0:T(8,128)(2,1)S(1)}, u32[]{:S(2)}, u32[]{:S(2)}) collective-permute-start(bf16[2,64,512]{2,1,0:T(8,128)(2,1)} %get-tuple-element.184), channel_id=1, source_target_pairs={{0,1},{1,0},{2,3},{3,2},{4,5},{5,4},{6,7},{7,6},{8,9},{9,8},{10,11... | collective-permute-start | bytes 393224 | tf_op jit(solution)/shard_map/ppermute | solution.py:571
  142.2 15.5 %collective-permute-start.23 = (bf16[2,64,512]{2,1,0:T(8,128)(2,1)}, bf16[2,64,512]{2,1,0:T(8,128)(2,1)}, u32[]{:S(2)}, u32[]{:S(2)}) collective-permute-start(bf16[2,64,512]{2,1,0:T(8,128)(2,1)} %get-tuple-element.185), channel_id=1, source_target_pairs={{0,2},{1,3},{2,0},{3,1},{4,6},{5,7},{6,4},{7,5},{8,10},{9,11},{10,... | collective-permute-start | bytes 393224 | tf_op jit(solution)/shard_map/ppermute | solution.py:571
  143.0 14.8 %collective-permute-start.24 = (bf16[2,64,512]{2,1,0:T(8,128)(2,1)}, bf16[2,64,512]{2,1,0:T(8,128)(2,1)}, u32[]{:S(2)}, u32[]{:S(2)}) collective-permute-start(bf16[2,64,512]{2,1,0:T(8,128)(2,1)} %get-tuple-element.186), channel_id=1, source_target_pairs={{0,3},{1,2},{2,1},{3,0},{4,7},{5,6},{6,5},{7,4},{8,11},{9,10},{10,... | collective-permute-start | bytes 393224 | tf_op jit(solution)/shard_map/ppermute | solution.py:571
  146.9 10.8 %collective-permute-start.35 = (bf16[4,80,384]{2,1,0:T(8,128)(2,1)}, bf16[4,80,384]{2,1,0:T(8,128)(2,1)S(1)}, u32[]{:S(2)}, u32[]{:S(2)}) collective-permute-start(bf16[4,80,384]{2,1,0:T(8,128)(2,1)} %get-tuple-element.193), channel_id=1, source_target_pairs={{0,4},{2,6},{4,0},{6,2},{1,5},{3,7},{5,1},{7,3},{8,12},{10,14},{12... | collective-permute-start | bytes 737288 | tf_op jit(solution)/shard_map/ppermute | solution.py:866
  147.5 14.1 %collective-permute-start.36 = (bf16[4,80,384]{2,1,0:T(8,128)(2,1)}, bf16[4,80,384]{2,1,0:T(8,128)(2,1)S(1)}, u32[]{:S(2)}, u32[]{:S(2)}) collective-permute-start(bf16[4,80,384]{2,1,0:T(8,128)(2,1)} %get-tuple-element.192), channel_id=1, source_target_pairs={{0,2},{2,0},{4,6},{6,4},{1,3},{3,1},{5,7},{7,5},{8,10},{10,8},{12,... | collective-permute-start | bytes 737288 | tf_op jit(solution)/shard_map/ppermute | solution.py:866
  148.2 14.8 %copy-start.12 = (bf16[2,64,512]{2,1,0:T(8,128)(2,1)}, bf16[2,64,512]{2,1,0:T(8,128)(2,1)S(1)}, u32[]{:S(2)}) copy-start(bf16[2,64,512]{2,1,0:T(8,128)(2,1)S(1)} %collective-permute-done.22.refs_5_) | copy-start | bytes 393220
  148.2 13.4 %collective-permute-start.37 = (bf16[4,80,384]{2,1,0:T(8,128)(2,1)}, bf16[4,80,384]{2,1,0:T(8,128)(2,1)S(1)}, u32[]{:S(2)}, u32[]{:S(2)}) collective-permute-start(bf16[4,80,384]{2,1,0:T(8,128)(2,1)} %get-tuple-element.194), channel_id=1, source_target_pairs={{0,6},{2,4},{4,2},{6,0},{1,7},{3,5},{5,3},{7,1},{8,14},{10,12},{12... | collective-permute-start | bytes 737288 | tf_op jit(solution)/shard_map/ppermute | solution.py:866
  152.6 14.0 %copy-start.30 = (bf16[4,80,384]{2,1,0:T(8,128)(2,1)S(1)}, bf16[4,80,384]{2,1,0:T(8,128)(2,1)}, u32[]{:S(2)}) copy-start(bf16[4,80,384]{2,1,0:T(8,128)(2,1)} %get-tuple-element.196) | copy-start | bytes 737284
  153.1 14.4 %all-to-all-start.3 = ((bf16[4,64,640]{2,1,0:T(8,128)(2,1)}), bf16[4,64,640]{2,1,0:T(8,128)(2,1)S(1)}, u32[]{:S(2)}, u32[]{:S(2)}) async-start(bf16[4,64,640]{2,1,0:T(8,128)(2,1)} %add_convert_fusion), calls=%async_computation.3 | async-start | bytes 655360 | tf_op jit(solution)/shard_map/all_to_all | solution.py:927
  157.7 17.0 %collective-permute-start.16 = (bf16[4,64,512]{2,1,0:T(8,128)(2,1)}, bf16[4,64,512]{2,1,0:T(8,128)(2,1)S(1)}, u32[]{:S(2)}, u32[]{:S(2)}) collective-permute-start(bf16[4,64,512]{2,1,0:T(8,128)(2,1)} %get-tuple-element.157), channel_id=1, source_target_pairs={{0,3},{1,2},{2,1},{3,0},{4,7},{5,6},{6,5},{7,4},{8,11},{9,10},{10,... | collective-permute-start | bytes 786440 | tf_op jit(solution)/shard_map/ppermute | solution.py:571
  163.0 11.8 %copy-start.4 = (s32[9]{0:T(128)S(1)}, s32[9]{0:T(128)}, u32[]{:S(2)}) copy-start(s32[9]{0:T(128)} %stack.41.place) | copy-start | bytes 112
  163.0 11.8 %copy-start.20 = (bf16[4,64,512]{2,1,0:T(8,128)(2,1)S(1)}, bf16[4,64,512]{2,1,0:T(8,128)(2,1)}, u32[]{:S(2)}) copy-start(bf16[4,64,512]{2,1,0:T(8,128)(2,1)} %get-tuple-element.154.refs_0_) | copy-start | bytes 786436
  163.0 9.4 %collective-permute-start.29 = (bf16[64,512]{1,0:T(8,128)(2,1)S(1)}, bf16[64,512]{1,0:T(8,128)(2,1)S(1)}, u32[]{:S(2)}, u32[]{:S(2)}) collective-permute-start(bf16[64,512]{1,0:T(8,128)(2,1)S(1)} %get-tuple-element.222), channel_id=1, source_target_pairs={{0,4},{2,6},{4,0},{6,2},{1,5},{3,7},{5,1},{7,3},{8,12},{10,14},{12... | collective-permute-start | bytes 196616 | tf_op jit(solution)/shard_map/ppermute | solution.py:866
  164.3 8.2 %collective-permute-start.30 = (bf16[64,512]{1,0:T(8,128)(2,1)S(1)}, bf16[64,512]{1,0:T(8,128)(2,1)S(1)}, u32[]{:S(2)}, u32[]{:S(2)}) collective-permute-start(bf16[64,512]{1,0:T(8,128)(2,1)S(1)} %get-tuple-element.224), channel_id=1, source_target_pairs={{0,2},{2,0},{4,6},{6,4},{1,3},{3,1},{5,7},{7,5},{8,10},{10,8},{12,... | collective-permute-start | bytes 196616 | tf_op jit(solution)/shard_map/ppermute | solution.py:866
  164.6 7.8 %collective-permute-start.31 = (bf16[64,512]{1,0:T(8,128)(2,1)S(1)}, bf16[64,512]{1,0:T(8,128)(2,1)S(1)}, u32[]{:S(2)}, u32[]{:S(2)}) collective-permute-start(bf16[64,512]{1,0:T(8,128)(2,1)S(1)} %get-tuple-element.223), channel_id=1, source_target_pairs={{0,6},{2,4},{4,2},{6,0},{1,7},{3,5},{5,3},{7,1},{8,14},{10,12},{12... | collective-permute-start | bytes 196616 | tf_op jit(solution)/shard_map/ppermute | solution.py:866
  167.5 11.7 %all-to-all-start.5 = ((bf16[4,80,384]{2,1,0:T(8,128)(2,1)}), bf16[4,80,384]{2,1,0:T(8,128)(2,1)S(1)}, u32[]{:S(2)}, u32[]{:S(2)}) async-start(bf16[4,80,384]{2,1,0:T(8,128)(2,1)} %add_convert_fusion.1), calls=%async_computation.5 | async-start | bytes 491520 | tf_op jit(solution)/shard_map/all_to_all | solution.py:931
  172.5 6.7 %collective-permute-start.32 = (bf16[64,1152]{1,0:T(8,128)(2,1)S(1)}, bf16[64,1152]{1,0:T(8,128)(2,1)S(1)}, u32[]{:S(2)}, u32[]{:S(2)}) collective-permute-start(bf16[64,1152]{1,0:T(8,128)(2,1)S(1)} %pad_maximum_fusion.2.m0), channel_id=1, source_target_pairs={{0,2},{1,3},{2,0},{3,1},{4,6},{5,7},{6,4},{7,5},{8,10},{9,11},{10,... | collective-permute-start | bytes 442376 | tf_op jit(solution)/shard_map/ppermute | solution.py:610
  173.1 6.2 %collective-permute-start.33 = (bf16[64,1152]{1,0:T(8,128)(2,1)S(1)}, bf16[64,1152]{1,0:T(8,128)(2,1)S(1)}, u32[]{:S(2)}, u32[]{:S(2)}) collective-permute-start(bf16[64,1152]{1,0:T(8,128)(2,1)S(1)} %pad_maximum_fusion.2.m0), channel_id=1, source_target_pairs={{0,1},{1,0},{2,3},{3,2},{4,5},{5,4},{6,7},{7,6},{8,9},{9,8},{10,11... | collective-permute-start | bytes 442376 | tf_op jit(solution)/shard_map/ppermute | solution.py:610
  173.1 6.2 %collective-permute-start.34 = (bf16[64,1152]{1,0:T(8,128)(2,1)S(1)}, bf16[64,1152]{1,0:T(8,128)(2,1)S(1)}, u32[]{:S(2)}, u32[]{:S(2)}) collective-permute-start(bf16[64,1152]{1,0:T(8,128)(2,1)S(1)} %pad_maximum_fusion.2.m0), channel_id=1, source_target_pairs={{0,3},{1,2},{2,1},{3,0},{4,7},{5,6},{6,5},{7,4},{8,11},{9,10},{10,... | collective-permute-start | bytes 442376 | tf_op jit(solution)/shard_map/ppermute | solution.py:610
  179.3 4.6 %collective-permute-start.38 = (bf16[80,384]{1,0:T(8,128)(2,1)S(1)}, bf16[80,384]{1,0:T(8,128)(2,1)S(1)}, u32[]{:S(2)}, u32[]{:S(2)}) collective-permute-start(bf16[80,384]{1,0:T(8,128)(2,1)S(1)} %reduce_sum.38.a0), channel_id=1, source_target_pairs={{0,2},{1,3},{2,0},{3,1},{4,6},{5,7},{6,4},{7,5},{8,10},{9,11},{10,... | collective-permute-start | bytes 184328 | tf_op jit(solution)/shard_map/ppermute | solution.py:610
  180.8 3.2 %collective-permute-start.39 = (bf16[80,384]{1,0:T(8,128)(2,1)S(1)}, bf16[80,384]{1,0:T(8,128)(2,1)S(1)}, u32[]{:S(2)}, u32[]{:S(2)}) collective-permute-start(bf16[80,384]{1,0:T(8,128)(2,1)S(1)} %reduce_sum.38.a0), channel_id=1, source_target_pairs={{0,1},{1,0},{2,3},{3,2},{4,5},{5,4},{6,7},{7,6},{8,9},{9,8},{10,11... | collective-permute-start | bytes 184328 | tf_op jit(solution)/shard_map/ppermute | solution.py:610
  181.0 4.4 %collective-permute-start.40 = (bf16[80,384]{1,0:T(8,128)(2,1)S(1)}, bf16[80,384]{1,0:T(8,128)(2,1)S(1)}, u32[]{:S(2)}, u32[]{:S(2)}) collective-permute-start(bf16[80,384]{1,0:T(8,128)(2,1)S(1)} %reduce_sum.38.a0), channel_id=1, source_target_pairs={{0,3},{1,2},{2,1},{3,0},{4,7},{5,6},{6,5},{7,4},{8,11},{9,10},{10,... | collective-permute-start | bytes 184328 | tf_op jit(solution)/shard_map/ppermute | solution.py:610
  183.9 10.4 %copy-start.14 = (bf16[80,384]{1,0:T(8,128)(2,1)}, bf16[80,384]{1,0:T(8,128)(2,1)S(1)}, u32[]{:S(2)}) copy-start(bf16[80,384]{1,0:T(8,128)(2,1)S(1)} %collective-permute-done.38.a1) | copy-start | bytes 184324
  183.9 10.4 %copy-start.15 = (bf16[80,384]{1,0:T(8,128)(2,1)}, bf16[80,384]{1,0:T(8,128)(2,1)S(1)}, u32[]{:S(2)}) copy-start(bf16[80,384]{1,0:T(8,128)(2,1)S(1)} %collective-permute-done.39.a2) | copy-start | bytes 184324
  186.7 12.2 %all-to-all-start.6 = ((f32[8,8,128]{2,1,0:T(8,128)}), f32[8,8,128]{2,1,0:T(8,128)S(1)}, u32[]{:S(2)}, u32[]{:S(2)}) async-start(f32[8,8,128]{2,1,0:T(8,128)} %squares.1), calls=%async_computation.6 | async-start | bytes 65536 | tf_op jit(solution)/shard_map/all_to_all | solution.py:971
  (25 other events, 132.6 us)

commit v8 on v7

--- a/solution.py
+++ b/solution.py
@@ -251,17 +251,20 @@
     h_turned[:, here] = h.T
     arrived(up_copies)
     arrived(down_copies)
-    for j in range(hidden // width):
-        columns = slice(j * width, (j + 1) * width)
-        up = nn_dot(h, w_up[:, columns]) + vec[6 + j : 7 + j]
-        act, slope = gelu_and_slope(up)
-        act_all[here, columns] = act.astype(BF16)
-        dup = (slope * nn_dot(dy, w_down[:, columns])).astype(BF16)
-        dup_all[here, columns] = dup
+    spans = [slice(j * width, (j + 1) * width) for j in range(hidden // width)]
+    result = x_one + vec[5:6]
+    dh = None
+    for j, span in enumerate(spans):
+        act, slope = gelu_and_slope(nn_dot(h, w_up[:, span]) + vec[6 + j : 7 + j])
+        act = act.astype(BF16)
+        act_all[here, span] = act
+        dup = (slope * nn_dot(dy, w_down[:, span])).astype(BF16)
+        dup_all[here, span] = dup
         vec_out[6 + j : 7 + j] += jnp.sum(dup.astype(F32), axis=0, keepdims=True)
-    result = x_one + (nt_dot(act_all[here, :], w_down[...]) + vec[5:6])
+        result = result + nt_dot(act, w_down[:, span])
+        part = nt_dot(dup, w_up[:, span])
+        dh = part if dh is None else dh + part
     store_slots((o0, o1, o2, o3), result.astype(BF16))
-    dh = nt_dot(dup_all[here, :], w_up[...])
     vec_out[2:3] += jnp.sum(dh * unit, axis=0, keepdims=True)
     vec_out[3:4] += jnp.sum(dh, axis=0, keepdims=True)
     dy_float = dy.astype(F32)
@@ -734,8 +737,8 @@
 
     up_far = swap(up_own, "core")
     attn, lse = attend(qkv, 0, rows - 1, [])
-    up_other, up_far, attn, lse, *dys = lax.optimization_barrier(
-        (up_other, up_far, attn, lse, *dys)
+    up_other, attn, lse, *dys = lax.optimization_barrier(
+        (up_other, attn, lse, *dys)
     )
     attn, lse = attend(qkv, rows - 1, 1, [attn, lse])
     up_pieces = [up_own, up_other, up_far, swap(up_other, "core")]
@@ -939,7 +942,8 @@
         qkv_mine = plane_total(qkv_keep, qkv_got, vec_total)
         qkv_mine = total(lax.all_to_all(qkv_mine, "hi", 0, 0))
     mlp_mine = jnp.concatenate([up_mine, down_mine], axis=1)
-    mlp_pieces = to_all(mlp_mine)
+    mlp_side = swap(mlp_mine, "y")
+    mlp_pieces = [mlp_mine, mlp_side, swap(mlp_mine, "core"), swap(mlp_side, "core")]
     attn_pieces = to_all(after(qkv_mine, *mlp_pieces))
     input_grad = collect([*input_first, *input_last])
 

time: 207 us -> 205 us (level)
    ppermute x11 -> x14, waiting for transfers between devices: 10.5 us -> 15 us  [swap(): return lax.ppermute(value, axis, [(0, 1), (1, 0)])]
    all_to_all x1, waiting for transfers between devices: 2.88 us -> 0.01 us  [on_device(): qkv_mine = total(lax.all_to_all(qkv_plane, 'hi', 0, 0))]
    ppermute x6 -> x3, starting transfers between devices: 4.92 us -> 2.21 us  [to_all(): lax.ppermute(mine, ('y', 'core'), [(j, j ^ k) for j in range(4)])]
    ppermute x11 -> x14, starting transfers between devices: 4.83 us -> 5.78 us  [swap(): return lax.ppermute(value, axis, [(0, 1), (1, 0)])]
where the time goes in v8:
time: 205 us; the launch traced here: 204 us
  Pallas kernels  77.6 us (38%)
  starting transfers between devices  61.6 us (30%)
  waiting for transfers between devices  43.6 us (21%)
  local copies, waits for them, and re-layouts  13.8 us (7%)
  other arithmetic  5.91 us (3%)
    pallas_call x1, Pallas kernels, on_device(): call(functools.partial(mlp_body, dims), rows // group, [SMEM, *[slot_spec...  27.4 us
    ppermute x14, waiting for transfers between devices, swap(): return lax.ppermute(value, axis, [(0, 1), (1, 0)])  15 us
    all_to_all x3, starting transfers between devices, spread_hi(): return lax.all_to_all(spread, 'hi', 0, 0)  13.4 us
    pallas_call x1, Pallas kernels, on_device(): call(functools.partial(back_last_body, dims), rows - lead, [*back_specs(l...  12 us
    ppermute x15, waiting for transfers between devices, from_seq(): lax.ppermute(pieces[k], ('y', 'core'), [(j, j ^ k) for j in range(4)])  10.7 us
    ppermute x9, starting transfers between devices, plane_sum(): moved.append(lax.ppermute(parts[k], ('lo', 'y'), perm))  10.6 us
    ppermute x15, starting transfers between devices, from_seq(): lax.ppermute(pieces[k], ('y', 'core'), [(j, j ^ k) for j in range(4)])  9.59 us
    pallas_call x1, Pallas kernels, on_device(): call(back_first_body, lead, back_specs(0), [*[half_spec((1, part, width),...  8.34 us
  transfers between devices with their start and end apart: 48, of which 16 were waited for; matrix products, arithmetic and copies ran while one was open for 5% of the time, Pallas kernels for 21%

profile of v8, /device:TPU:0, one launch (start us, length us, event | category | flops | bytes accessed | tf_op | source)
XLA Modules:
  0.0 204.1 jit_solution(7964794286403210189)
XLA Ops:
  0.7 1.1 slice.64
  2.6 0.8 broadcast_in_dim.6
  3.4 6.4 %all-to-all-start = ((bf16[4,32,1664]{2,1,0:T(8,128)(2,1)}), bf16[4,32,1664]{2,1,0:T(8,128)(2,1)S(1)}, u32[]{:S(2)}, u32[]{:S(2)}) async-start(bf16[4,32,1664]{2,1,0:T(8,128)(2,1)} %broadcast_in_dim.6), calls=%async_computation | async-start | bytes 851968 | tf_op jit(solution)/shard_map/all_to_all | solution.py:581
  9.8 0.8 dynamic-slice_bitcast_fusion.4
  11.3 1.0 collective-permute-start
  12.8 0.9 slice.68
  14.5 4.7 %collective-permute-done.2.x3 = bf16[4,64,512]{2,1,0:T(8,128)(2,1)S(1)} collective-permute-done((bf16[4,64,512]{2,1,0:T(8,128)(2,1)S(1)}, bf16[4,64,512]{2,1,0:T(8,128)(2,1)S(1)}, u32[]{:S(2)}, u32[]{:S(2)}) %collective-permute-start.2) | collective-permute-done | bytes 262176 | tf_op jit(solution)/shard_map/ppermute | solution.py:574
  19.2 0.7 copy-done.36
  19.9 2.3 %all-to-all-done.p0 = bf16[4,32,1664]{2,1,0:T(8,128)(2,1)S(1)} async-done(((bf16[4,32,1664]{2,1,0:T(8,128)(2,1)}), bf16[4,32,1664]{2,1,0:T(8,128)(2,1)S(1)}, u32[]{:S(2)}, u32[]{:S(2)}) %all-to-all-start) | async-done | bytes 426016 | tf_op jit(solution)/shard_map/all_to_all | solution.py:581
  22.2 1.5 collective-permute-start.3
  23.7 1.0 broadcast_in_dim.7
  24.7 3.5 %all-to-all-start.1 = ((bf16[4,32,3072]{2,1,0:T(8,128)(2,1)}), bf16[4,32,3072]{2,1,0:T(8,128)(2,1)S(1)}, u32[]{:S(2)}, u32[]{:S(2)}) async-start(bf16[4,32,3072]{2,1,0:T(8,128)(2,1)} %broadcast_in_dim.7), calls=%async_computation.1 | async-start | bytes 1572864 | tf_op jit(solution)/shard_map/all_to_all | solution.py:581
  28.3 4.7 %collective-permute-done.3.p1 = bf16[4,32,1664]{2,1,0:T(8,128)(2,1)S(1)} collective-permute-done((bf16[4,32,1664]{2,1,0:T(8,128)(2,1)S(1)}, bf16[4,32,1664]{2,1,0:T(8,128)(2,1)S(1)}, u32[]{:S(2)}, u32[]{:S(2)}) %collective-permute-start.3) | collective-permute-done | bytes 426016 | tf_op jit(solution)/shard_map/ppermute | solution.py:562
  33.3 1.5 collective-permute-start.12
  35.5 0.7 copy-done.34
  36.2 0.8 copy-done.35
  37.0 6.2 %qkv.1 = (bf16[1024,512]{1,0:T(8,128)(2,1)}, bf16[1024,1536]{1,0:T(8,128)(2,1)}) custom-call(s32[9]{0:T(128)} %stack.41.place, bf16[4,64,512]{2,1,0:T(8,128)(2,1)} %get-tuple-element.216.x0, bf16[4,64,512]{2,1,0:T(8,128)(2,1)} %collective-permute-done.x1, bf16[4,64,512]{2,1,0:T(8,128)(2,1)} %collective-permute-done.1.x2, bf16[4,64,512]{2,1,0:T(8,128)(2,1)} %copy-done.36, ...), custom_call_target="tpu_custom_call" | custom-call | flops 3500000000 | bytes 7000000 | tf_op jit(solution)/shard_map/qkv/pallas_call | solution.py:702
  43.3 4.4 %all-to-all-done.1.b0 = bf16[4,32,3072]{2,1,0:T(8,128)(2,1)S(1)} async-done(((bf16[4,32,3072]{2,1,0:T(8,128)(2,1)}), bf16[4,32,3072]{2,1,0:T(8,128)(2,1)S(1)}, u32[]{:S(2)}, u32[]{:S(2)}) %all-to-all-start.1) | async-done | bytes 786464 | tf_op jit(solution)/shard_map/all_to_all | solution.py:581
  47.7 1.0 broadcast_in_dim.8
  48.7 3.5 %all-to-all-start.2 = ((bf16[4,2,32,1536]{3,2,1,0:T(8,128)(2,1)}), bf16[4,2,32,1536]{3,2,1,0:T(8,128)(2,1)S(1)}, u32[]{:S(2)}, u32[]{:S(2)}) async-start(bf16[4,2,32,1536]{3,2,1,0:T(8,128)(2,1)} %broadcast_in_dim.8), calls=%async_computation.2 | async-start | bytes 1572864 | tf_op jit(solution)/shard_map/all_to_all | solution.py:581
  53.0 0.8 dynamic-slice_bitcast_fusion
  53.8 1.3 collective-permute-start.8
  56.0 1.9 copy-done.18
  57.9 3.9 %attend.2 = (bf16[1024,512]{1,0:T(8,128)(2,1)S(1)}, f32[4,8,256]{2,1,0:T(8,128)S(1)}) custom-call(s32[9]{0:T(128)S(1)} %constant_dynamic-update-slice_fusion.1.place, s32[4]{0:T(128)S(1)} %dynamic_slice.52.lengths, bf16[1024,1536]{1,0:T(8,128)(2,1)S(1)} %copy-done.18), custom_call_target="tpu_custom_call" | custom-call | flops 6000000000 | bytes 12000000 | tf_op jit(solution)/shard_map/attend/pallas_call | solution.py:726
  61.8 1.1 collective-permute-done.8.d2
  62.9 4.8 %collective-permute-done.9.d3 = bf16[4,64,512]{2,1,0:T(8,128)(2,1)S(1)} collective-permute-done((bf16[4,64,512]{2,1,0:T(8,128)(2,1)S(1)}, bf16[4,64,512]{2,1,0:T(8,128)(2,1)S(1)}, u32[]{:S(2)}, u32[]{:S(2)}) %collective-permute-start.9) | collective-permute-done | bytes 262176 | tf_op jit(solution)/shard_map/ppermute | solution.py:574
  67.8 3.1 %collective-permute-done.6.b1 = bf16[4,32,3072]{2,1,0:T(8,128)(2,1)} collective-permute-done((bf16[4,32,3072]{2,1,0:T(8,128)(2,1)S(1)}, bf16[4,32,3072]{2,1,0:T(8,128)(2,1)}, u32[]{:S(2)}, u32[]{:S(2)}) %collective-permute-start.6) | collective-permute-done | bytes 786464 | tf_op jit(solution)/shard_map/ppermute | solution.py:562
  70.9 1.6 attend.3
  72.6 1.0 copy-done.19
  74.5 1.7 collective-permute-done.13.c1
  76.2 27.4 %mlp.1 = (bf16[4,64,512]{2,1,0:T(8,128)(2,1)}, bf16[4,64,512]{2,1,0:T(8,128)(2,1)}, bf16[4,64,512]{2,1,0:T(8,128)(2,1)}, bf16[4,64,512]{2,1,0:T(8,128)(2,1)}, f3...) custom-call(s32[9]{0:T(128)} %stack.41.place, ...), custom_call_target="tpu_custom_call" | custom-call | flops 12000000000 | bytes 24000000 | tf_op jit(solution)/shard_map/mlp/pallas_call | solution.py:766
  104.6 1.3 collective-permute-start.15
  105.9 8.3 %back_first.1 = (bf16[2,64,512]{2,1,0:T(8,128)(2,1)}, bf16[2,64,512]{2,1,0:T(8,128)(2,1)}, bf16[2,64,512]{2,1,0:T(8,128)(2,1)}, bf16[2,64,512]{2,1,0:T(8,128)(2,...) custom-call(s32[9]{0:T(128)} %stack.41.place, s32[4]{0:T(128)} %copy-done.17, ...), custom_call_target="tpu_custom_call" | custom-call | flops 5500000256 | bytes 11000000 | tf_op jit(solution)/shard_map/back_first/pallas_call | solution.py:840
  114.4 0.8 collective-permute-start.18
  115.2 1.1 collective-permute-start.19
  116.2 3.8 %add.106 = (bf16[4,64,640]{2,1,0:T(8,128)(2,1)}, bf16[4,64,640]{2,1,0:T(8,128)(2,1)}, bf16[4,64,640]{2,1,0:T(8,128)(2,1)}, bf16[4,64,640]{2,1,0:T(8,128)(2,1)}, bf16[4,4,64,512]{3,2,1,0:T(8,128)(2,1)}) custom-call(bf16[4,4,64,640]{3,2,1,0:T(8,128)(2,1)} %bitcast.63, bf16[4,4,64,640]{3,2,1,0:T(8,128)(2,1)} %bitcast.22.got, bf16[4,4,64,512]{3,2,1,0:T(8,128)(2,1)} %bitcast.64, ...), custom_call_target="tpu_custom_call" | custom-call | flops 1500000000 | bytes 3000000 | tf_op jit(solution)/shard_map/add/pallas_call | solution.py:854
  120.6 0.7 collective-permute-start.26
  121.3 4.7 %all-to-all-start.4 = ((bf16[4,4,64,512]{3,2,1,0:T(8,128)(2,1)}), bf16[4,4,64,512]{3,2,1,0:T(8,128)(2,1)}, u32[]{:S(2)}, u32[]{:S(2)}) async-start(bf16[4,4,64,512]{3,2,1,0:T(8,128)(2,1)} %get-tuple-element.178), calls=%async_computation.4 | async-start | bytes 2097152 | tf_op jit(solution)/shard_map/all_to_all | solution.py:893
  126.1 2.3 %collective-permute-start.27 = (bf16[4,64,640]{2,1,0:T(8,128)(2,1)}, bf16[4,64,640]{2,1,0:T(8,128)(2,1)}, u32[]{:S(2)}, u32[]{:S(2)}) collective-permute-start(bf16[4,64,640]{2,1,0:T(8,128)(2,1)} %get-tuple-element.177), channel_id=1, source_target_pairs={{0,6},{2,4},{4,2},{6,0},{1,7},{3,5},{5,3},{7,1},{8,14},{10,12},{12... | collective-permute-start | bytes 983048 | tf_op jit(solution)/shard_map/ppermute | solution.py:869
  128.3 12.0 %back_last.1 = (bf16[2,64,512]{2,1,0:T(8,128)(2,1)}, bf16[2,64,512]{2,1,0:T(8,128)(2,1)}, bf16[2,64,512]{2,1,0:T(8,128)(2,1)}, bf16[2,64,512]{2,1,0:T(8,128)(2,1...) custom-call(s32[9]{0:T(128)} %copy-done.40, s32[4]{0:T(128)} %copy-done.17, ...), custom_call_target="tpu_custom_call" | custom-call | flops 6499999744 | bytes 13000000 | tf_op jit(solution)/shard_map/back_last/pallas_call | solution.py:896
  141.0 0.7 collective-permute-start.23
  141.7 0.7 collective-permute-start.24
  142.4 0.9 collective-permute-done.28
  143.3 2.4 %add.107 = (bf16[4,80,384]{2,1,0:T(8,128)(2,1)}, bf16[4,80,384]{2,1,0:T(8,128)(2,1)}, bf16[4,80,384]{2,1,0:T(8,128)(2,1)}, bf16[4,80,384]{2,1,0:T(8,128)(2,1)}) custom-call(bf16[4,4,64,384]{3,2,1,0:T(8,128)(2,1)} %bitcast.65, bf16[4,4,64,384]{3,2,1,0:T(8,128)(2,1)} %bitcast.26.got, f32[16,512]{1,0:T(8,128)} %get-tuple-element.188.vec), custom_call_target="tpu_custom_call" | custom-call | flops 1500000000 | bytes 3000000 | tf_op jit(solution)/shard_map/add/pallas_call | solution.py:854
  146.2 0.7 collective-permute-start.36
  147.0 2.2 %collective-permute-start.37 = (bf16[4,80,384]{2,1,0:T(8,128)(2,1)}, bf16[4,80,384]{2,1,0:T(8,128)(2,1)S(1)}, u32[]{:S(2)}, u32[]{:S(2)}) collective-permute-start(bf16[4,80,384]{2,1,0:T(8,128)(2,1)} %get-tuple-element.192), channel_id=1, source_target_pairs={{0,6},{2,4},{4,2},{6,0},{1,7},{3,5},{5,3},{7,1},{8,14},{10,12},{12... | collective-permute-start | bytes 737288 | tf_op jit(solution)/shard_map/ppermute | solution.py:869
  149.2 2.2 %add_convert_fusion = bf16[4,64,640]{2,1,0:T(8,128)(2,1)} fusion(bf16[4,64,640]{2,1,0:T(8,128)(2,1)} %collective-permute-done.27, bf16[4,64,640]{2,1,0:T(8,128)(2,1)} %collective-permute-done.26, bf16[4,64,640]{2,1,0:T(8,128)(2,1)} %collective-permute-done.25, bf16[4,64,640]{2,1,0:T(8,128)(2,1)} %get-tuple-element.174), kind=kLoop, calls=%fused_computation | loop fusion | flops 1310720 | bytes 1638400 | tf_op jit(solution)/shard_map/convert_element_type | solution.py:874
  151.8 4.7 %all-to-all-start.3 = ((bf16[4,64,640]{2,1,0:T(8,128)(2,1)}), bf16[4,64,640]{2,1,0:T(8,128)(2,1)S(1)}, u32[]{:S(2)}, u32[]{:S(2)}) async-start(bf16[4,64,640]{2,1,0:T(8,128)(2,1)} %add_convert_fusion), calls=%async_computation.3 | async-start | bytes 655360 | tf_op jit(solution)/shard_map/all_to_all | solution.py:930
  156.5 3.8 %collective-permute-done.36 = bf16[4,80,384]{2,1,0:T(8,128)(2,1)S(1)} collective-permute-done((bf16[4,80,384]{2,1,0:T(8,128)(2,1)}, bf16[4,80,384]{2,1,0:T(8,128)(2,1)S(1)}, u32[]{:S(2)}, u32[]{:S(2)}) %collective-permute-start.36) | collective-permute-done | bytes 245792 | tf_op jit(solution)/shard_map/ppermute | solution.py:869
  160.3 1.4 reduce_sum.37
  161.8 1.3 collective-permute-start.29
  163.4 2.0 collective-permute-start.31
  165.3 0.8 add_convert_fusion.1
  166.3 4.9 %all-to-all-start.5 = ((bf16[4,80,384]{2,1,0:T(8,128)(2,1)}), bf16[4,80,384]{2,1,0:T(8,128)(2,1)S(1)}, u32[]{:S(2)}, u32[]{:S(2)}) async-start(bf16[4,80,384]{2,1,0:T(8,128)(2,1)} %add_convert_fusion.1), calls=%async_computation.5 | async-start | bytes 491520 | tf_op jit(solution)/shard_map/all_to_all | solution.py:934
  171.9 4.6 %collective-permute-done.32.m1 = bf16[64,1152]{1,0:T(8,128)(2,1)S(1)} collective-permute-done((bf16[64,1152]{1,0:T(8,128)(2,1)S(1)}, bf16[64,1152]{1,0:T(8,128)(2,1)S(1)}, u32[]{:S(2)}, u32[]{:S(2)}) %collective-permute-start.32) | collective-permute-done | bytes 147488 | tf_op jit(solution)/shard_map/ppermute | solution.py:562
  176.5 1.6 collect.2
  179.0 1.4 collective-permute-start.40
  180.4 0.8 mlp_squares.1.before
  181.3 1.8 collective-permute-done.38.a1
  183.6 1.3 squares.1
  184.9 5.7 %all-to-all-start.6 = ((f32[8,8,128]{2,1,0:T(8,128)}), f32[8,8,128]{2,1,0:T(8,128)S(1)}, u32[]{:S(2)}, u32[]{:S(2)}) async-start(f32[8,8,128]{2,1,0:T(8,128)} %squares.1), calls=%async_computation.6 | async-start | bytes 65536 | tf_op jit(solution)/shard_map/all_to_all | solution.py:975
  190.7 2.1 %collect.3 = bf16[4,4,64,512]{3,2,1,0:T(8,128)(2,1)} custom-call(s32[9]{0:T(128)S(1)} %copy-done.4, bf16[2,64,512]{2,1,0:T(8,128)(2,1)S(1)} %copy-done.21, bf16[2,64,512]{2,1,0:T(8,128)(2,1)S(1)} %copy-done.9, bf16[2,64,512]{2,1,0:T(8,128)(2,1)S(1)} %copy-done.11, bf16[2,64,512]{2,1,0:T(8,128)(2,1)} %collective-permute-done.19.refs_3_, ...), custom_call_target="tpu_custom_call" | custom-call | flops 1000000000 | bytes 2000000 | tf_op jit(solution)/shard_map/collect/pallas_call | solution.py:806
  192.8 4.5 %all-to-all-done.6.squares = f32[8,8,128]{2,1,0:T(8,128)S(1)} async-done(((f32[8,8,128]{2,1,0:T(8,128)}), f32[8,8,128]{2,1,0:T(8,128)S(1)}, u32[]{:S(2)}, u32[]{:S(2)}) %all-to-all-start.6) | async-done | bytes 32800 | tf_op jit(solution)/shard_map/all_to_all | solution.py:975
  197.9 6.0 %adam.1 = (f32[1,1]{1,0:T(1,128)}, f32[64,2048]{1,0:T(8,128)}, f32[64,2048]{1,0:T(8,128)}, f32[64,2048]{1,0:T(8,128)}, f32[2,64,2048]{2,1,0:T(8,128)}, /*index=5...) custom-call(s32[9]{0:T(128)} %stack.41.place, ...), custom_call_target="tpu_custom_call" | custom-call | flops 3000000000 | bytes 6000000 | tf_op jit(solution)/shard_map/adam/pallas_call | solution.py:978
  (174 shorter events, 12.8 us)
Async XLA Ops:
  3.4 10.3 %copy-start.29 = (f32[2,64,2048]{2,1,0:T(8,128)S(1)}, f32[2,64,2048]{2,1,0:T(8,128)}, u32[]{:S(2)}) copy-start(f32[2,64,2048]{2,1,0:T(8,128)} %mlp_w.1) | copy-start | bytes 3145732
  3.4 18.8 %all-to-all-start = ((bf16[4,32,1664]{2,1,0:T(8,128)(2,1)}), bf16[4,32,1664]{2,1,0:T(8,128)(2,1)S(1)}, u32[]{:S(2)}, u32[]{:S(2)}) async-start(bf16[4,32,1664]{2,1,0:T(8,128)(2,1)} %broadcast_in_dim.6), calls=%async_computation | async-start | bytes 851968 | tf_op jit(solution)/shard_map/all_to_all | solution.py:581
  10.7 8.5 %collective-permute-start.2 = (bf16[4,64,512]{2,1,0:T(8,128)(2,1)S(1)}, bf16[4,64,512]{2,1,0:T(8,128)(2,1)S(1)}, u32[]{:S(2)}, u32[]{:S(2)}) collective-permute-start(bf16[4,64,512]{2,1,0:T(8,128)(2,1)S(1)} %get-tuple-element.214), channel_id=1, source_target_pairs={{0,3},{1,2},{2,1},{3,0},{4,7},{5,6},{6,5},{7,4},{8,11},{9,10},{10,... | collective-permute-start | bytes 786440 | tf_op jit(solution)/shard_map/ppermute | solution.py:574
  11.3 24.1 %collective-permute-start = (bf16[4,64,512]{2,1,0:T(8,128)(2,1)S(1)}, bf16[4,64,512]{2,1,0:T(8,128)(2,1)}, u32[]{:S(2)}, u32[]{:S(2)}) collective-permute-start(bf16[4,64,512]{2,1,0:T(8,128)(2,1)S(1)} %get-tuple-element.215), channel_id=1, source_target_pairs={{0,1},{1,0},{2,3},{3,2},{4,5},{5,4},{6,7},{7,6},{8,9},{9,8},{10,11... | collective-permute-start | bytes 786440 | tf_op jit(solution)/shard_map/ppermute | solution.py:574
  12.3 23.2 %collective-permute-start.1 = (bf16[4,64,512]{2,1,0:T(8,128)(2,1)S(1)}, bf16[4,64,512]{2,1,0:T(8,128)(2,1)}, u32[]{:S(2)}, u32[]{:S(2)}) collective-permute-start(bf16[4,64,512]{2,1,0:T(8,128)(2,1)S(1)} %get-tuple-element.217), channel_id=1, source_target_pairs={{0,2},{1,3},{2,0},{3,1},{4,6},{5,7},{6,4},{7,5},{8,10},{9,11},{10,... | collective-permute-start | bytes 786440 | tf_op jit(solution)/shard_map/ppermute | solution.py:574
  22.2 10.8 %copy-start.28 = (bf16[4,32,1664]{2,1,0:T(8,128)(2,1)}, bf16[4,32,1664]{2,1,0:T(8,128)(2,1)S(1)}, u32[]{:S(2)}) copy-start(bf16[4,32,1664]{2,1,0:T(8,128)(2,1)S(1)} %all-to-all-done.p0) | copy-start | bytes 1277956
  22.2 10.8 %collective-permute-start.3 = (bf16[4,32,1664]{2,1,0:T(8,128)(2,1)S(1)}, bf16[4,32,1664]{2,1,0:T(8,128)(2,1)S(1)}, u32[]{:S(2)}, u32[]{:S(2)}) collective-permute-start(bf16[4,32,1664]{2,1,0:T(8,128)(2,1)S(1)} %all-to-all-done.p0), channel_id=1, source_target_pairs={{0,4},{4,0},{1,5},{5,1},{2,6},{6,2},{3,7},{7,3},{8,12},{12,8},{9,1... | collective-permute-start | bytes 1277960 | tf_op jit(solution)/shard_map/ppermute | solution.py:562
  24.7 23.0 %all-to-all-start.1 = ((bf16[4,32,3072]{2,1,0:T(8,128)(2,1)}), bf16[4,32,3072]{2,1,0:T(8,128)(2,1)S(1)}, u32[]{:S(2)}, u32[]{:S(2)}) async-start(bf16[4,32,3072]{2,1,0:T(8,128)(2,1)} %broadcast_in_dim.7), calls=%async_computation.1 | async-start | bytes 1572864 | tf_op jit(solution)/shard_map/all_to_all | solution.py:581
  28.2 7.3 %collective-permute-start.4 = (bf16[4,32,1664]{2,1,0:T(8,128)(2,1)S(1)}, bf16[4,32,1664]{2,1,0:T(8,128)(2,1)S(1)}, u32[]{:S(2)}, u32[]{:S(2)}) collective-permute-start(bf16[4,32,1664]{2,1,0:T(8,128)(2,1)S(1)} %all-to-all-done.p0), channel_id=1, source_target_pairs={{0,1},{1,0},{2,3},{3,2},{4,5},{5,4},{6,7},{7,6},{8,9},{9,8},{10,11... | collective-permute-start | bytes 1277960 | tf_op jit(solution)/shard_map/ppermute | solution.py:562
  33.0 2.5 %collective-permute-start.5 = (bf16[4,32,1664]{2,1,0:T(8,128)(2,1)S(1)}, bf16[4,32,1664]{2,1,0:T(8,128)(2,1)S(1)}, u32[]{:S(2)}, u32[]{:S(2)}) collective-permute-start(bf16[4,32,1664]{2,1,0:T(8,128)(2,1)S(1)} %collective-permute-done.3.p1), channel_id=1, source_target_pairs={{0,1},{1,0},{2,3},{3,2},{4,5},{5,4},{6,7},{7,6},{8,9},{9,8},{10,11... | collective-permute-start | bytes 1277960 | tf_op jit(solution)/shard_map/ppermute | solution.py:562
  33.3 10.0 %collective-permute-start.12 = (bf16[32,1536]{1,0:T(8,128)(2,1)S(1)}, bf16[32,1536]{1,0:T(8,128)(2,1)S(1)}, u32[]{:S(2)}, u32[]{:S(2)}) collective-permute-start(bf16[32,1536]{1,0:T(8,128)(2,1)S(1)} %fusion.4), channel_id=1, source_target_pairs={{0,4},{4,0},{1,5},{5,1},{2,6},{6,2},{3,7},{7,3},{8,12},{12,8},{9,1... | collective-permute-start | bytes 294920 | tf_op jit(solution)/shard_map/ppermute | solution.py:562
  43.2 9.6 %copy-start.2 = (s32[9]{0:T(128)S(1)}, s32[9]{0:T(128)}, u32[]{:S(2)}) copy-start(s32[9]{0:T(128)} %stack.41.place) | copy-start | bytes 112
  43.2 9.6 %copy-start.33 = (s32[4,4]{1,0:T(4,128)S(1)}, s32[4,4]{1,0:T(4,128)}, u32[]{:S(2)}) copy-start(s32[4,4]{1,0:T(4,128)} %param.20) | copy-start | bytes 196
  43.3 9.8 %copy-start.25 = (bf16[4,4,64,512]{3,2,1,0:T(8,128)(2,1)S(1)}, bf16[4,4,64,512]{3,2,1,0:T(8,128)(2,1)}, u32[]{:S(2)}) copy-start(bf16[4,4,64,512]{3,2,1,0:T(8,128)(2,1)} %param.19) | copy-start | bytes 3145732
  48.7 24.8 %all-to-all-start.2 = ((bf16[4,2,32,1536]{3,2,1,0:T(8,128)(2,1)}), bf16[4,2,32,1536]{3,2,1,0:T(8,128)(2,1)S(1)}, u32[]{:S(2)}, u32[]{:S(2)}) async-start(bf16[4,2,32,1536]{3,2,1,0:T(8,128)(2,1)} %broadcast_in_dim.8), calls=%async_computation.2 | async-start | bytes 1572864 | tf_op jit(solution)/shard_map/all_to_all | solution.py:581
  52.2 18.7 %collective-permute-start.6 = (bf16[4,32,3072]{2,1,0:T(8,128)(2,1)S(1)}, bf16[4,32,3072]{2,1,0:T(8,128)(2,1)}, u32[]{:S(2)}, u32[]{:S(2)}) collective-permute-start(bf16[4,32,3072]{2,1,0:T(8,128)(2,1)S(1)} %all-to-all-done.1.b0), channel_id=1, source_target_pairs={{0,4},{4,0},{1,5},{5,1},{2,6},{6,2},{3,7},{7,3},{8,12},{12,8},{9,1... | collective-permute-start | bytes 2359304 | tf_op jit(solution)/shard_map/ppermute | solution.py:562
  53.0 17.9 %copy-start.17 = (s32[4]{0:T(128)}, s32[4]{0:T(128)S(1)}, u32[]{:S(2)}) copy-start(s32[4]{0:T(128)S(1)} %dynamic_slice.52.lengths) | copy-start | bytes 52
  53.8 8.0 %collective-permute-start.7 = (bf16[4,64,512]{2,1,0:T(8,128)(2,1)S(1)}, bf16[4,64,512]{2,1,0:T(8,128)(2,1)S(1)}, u32[]{:S(2)}, u32[]{:S(2)}) collective-permute-start(bf16[4,64,512]{2,1,0:T(8,128)(2,1)S(1)} %get-tuple-element.212), channel_id=1, source_target_pairs={{0,1},{1,0},{2,3},{3,2},{4,5},{5,4},{6,7},{7,6},{8,9},{9,8},{10,11... | collective-permute-start | bytes 786440 | tf_op jit(solution)/shard_map/ppermute | solution.py:574
  53.8 9.1 %collective-permute-start.8 = (bf16[4,64,512]{2,1,0:T(8,128)(2,1)S(1)}, bf16[4,64,512]{2,1,0:T(8,128)(2,1)S(1)}, u32[]{:S(2)}, u32[]{:S(2)}) collective-permute-start(bf16[4,64,512]{2,1,0:T(8,128)(2,1)S(1)} %get-tuple-element.211), channel_id=1, source_target_pairs={{0,2},{1,3},{2,0},{3,1},{4,6},{5,7},{6,4},{7,5},{8,10},{9,11},{10,... | collective-permute-start | bytes 786440 | tf_op jit(solution)/shard_map/ppermute | solution.py:574
  55.1 12.7 %collective-permute-start.9 = (bf16[4,64,512]{2,1,0:T(8,128)(2,1)S(1)}, bf16[4,64,512]{2,1,0:T(8,128)(2,1)S(1)}, u32[]{:S(2)}, u32[]{:S(2)}) collective-permute-start(bf16[4,64,512]{2,1,0:T(8,128)(2,1)S(1)} %get-tuple-element.210), channel_id=1, source_target_pairs={{0,3},{1,2},{2,1},{3,0},{4,7},{5,6},{6,5},{7,4},{8,11},{9,10},{10,... | collective-permute-start | bytes 786440 | tf_op jit(solution)/shard_map/ppermute | solution.py:574
  55.7 18.4 %collective-permute-start.10 = (bf16[4,32,3072]{2,1,0:T(8,128)(2,1)S(1)}, bf16[4,32,3072]{2,1,0:T(8,128)(2,1)}, u32[]{:S(2)}, u32[]{:S(2)}) collective-permute-start(bf16[4,32,3072]{2,1,0:T(8,128)(2,1)S(1)} %all-to-all-done.1.b0), channel_id=1, source_target_pairs={{0,1},{1,0},{2,3},{3,2},{4,5},{5,4},{6,7},{7,6},{8,9},{9,8},{10,11... | collective-permute-start | bytes 2359304 | tf_op jit(solution)/shard_map/ppermute | solution.py:562
  70.9 3.6 %collective-permute-start.11 = (bf16[4,32,3072]{2,1,0:T(8,128)(2,1)}, bf16[4,32,3072]{2,1,0:T(8,128)(2,1)}, u32[]{:S(2)}, u32[]{:S(2)}) collective-permute-start(bf16[4,32,3072]{2,1,0:T(8,128)(2,1)} %collective-permute-done.6.b1), channel_id=1, source_target_pairs={{0,1},{1,0},{2,3},{3,2},{4,5},{5,4},{6,7},{7,6},{8,9},{9,8},{10,11... | collective-permute-start | bytes 2359304 | tf_op jit(solution)/shard_map/ppermute | solution.py:562
  73.6 30.0 %copy-start.23 = (f32[4,8,256]{2,1,0:T(8,128)}, f32[4,8,256]{2,1,0:T(8,128)S(1)}, u32[]{:S(2)}) copy-start(f32[4,8,256]{2,1,0:T(8,128)S(1)} %get-tuple-element.159.lse) | copy-start | bytes 98308
  73.6 30.6 %copy-start.3 = (s32[9]{0:T(128)S(1)}, s32[9]{0:T(128)}, u32[]{:S(2)}) copy-start(s32[9]{0:T(128)} %stack.41.place) | copy-start | bytes 112
  73.6 2.6 %collective-permute-start.13 = (bf16[4,2,32,1536]{3,2,1,0:T(8,128)(2,1)S(1)}, bf16[4,2,32,1536]{3,2,1,0:T(8,128)(2,1)}, u32[]{:S(2)}, u32[]{:S(2)}) collective-permute-start(bf16[4,2,32,1536]{3,2,1,0:T(8,128)(2,1)S(1)} %all-to-all-done.2.c0), channel_id=1, source_target_pairs={{0,1},{1,0},{2,3},{3,2},{4,5},{5,4},{6,7},{7,6},{8,9},{9,8},{10,11... | collective-permute-start | bytes 2359304 | tf_op jit(solution)/shard_map/ppermute | solution.py:562
  103.6 12.6 %collective-permute-start.20 = (bf16[2,2,4,64,640]{4,3,2,1,0:T(8,128)(2,1)}, bf16[2,2,4,64,640]{4,3,2,1,0:T(8,128)(2,1)}, u32[]{:S(2)}, u32[]{:S(2)}) collective-permute-start(bf16[2,2,4,64,640]{4,3,2,1,0:T(8,128)(2,1)} %get-tuple-element.156), channel_id=1, source_target_pairs={{0,1},{1,0},{2,3},{3,2},{4,5},{5,4},{6,7},{7,6},{8,9},{9,8},{10,11... | collective-permute-start | bytes 3932168 | tf_op jit(solution)/shard_map/ppermute | solution.py:562
  104.0 12.2 %collective-permute-start.21 = (bf16[2,2,4,64,512]{4,3,2,1,0:T(8,128)(2,1)}, bf16[2,2,4,64,512]{4,3,2,1,0:T(8,128)(2,1)}, u32[]{:S(2)}, u32[]{:S(2)}) collective-permute-start(bf16[2,2,4,64,512]{4,3,2,1,0:T(8,128)(2,1)} %get-tuple-element.157), channel_id=1, source_target_pairs={{0,1},{1,0},{2,3},{3,2},{4,5},{5,4},{6,7},{7,6},{8,9},{9,8},{10,11... | collective-permute-start | bytes 3145736 | tf_op jit(solution)/shard_map/ppermute | solution.py:562
  104.2 10.1 %copy-start.40 = (s32[9]{0:T(128)}, s32[9]{0:T(128)S(1)}, u32[]{:S(2)}) copy-start(s32[9]{0:T(128)S(1)} %constant_dynamic-update-slice_fusion.place) | copy-start | bytes 112
  104.2 10.2 %collective-permute-start.14 = (bf16[4,64,512]{2,1,0:T(8,128)(2,1)}, bf16[4,64,512]{2,1,0:T(8,128)(2,1)S(1)}, u32[]{:S(2)}, u32[]{:S(2)}) collective-permute-start(bf16[4,64,512]{2,1,0:T(8,128)(2,1)} %get-tuple-element.153), channel_id=1, source_target_pairs={{0,1},{1,0},{2,3},{3,2},{4,5},{5,4},{6,7},{7,6},{8,9},{9,8},{10,11... | collective-permute-start | bytes 786440 | tf_op jit(solution)/shard_map/ppermute | solution.py:574
  104.6 10.5 %collective-permute-start.15 = (bf16[4,64,512]{2,1,0:T(8,128)(2,1)}, bf16[4,64,512]{2,1,0:T(8,128)(2,1)S(1)}, u32[]{:S(2)}, u32[]{:S(2)}) collective-permute-start(bf16[4,64,512]{2,1,0:T(8,128)(2,1)} %get-tuple-element.154), channel_id=1, source_target_pairs={{0,2},{1,3},{2,0},{3,1},{4,6},{5,7},{6,4},{7,5},{8,10},{9,11},{10,... | collective-permute-start | bytes 786440 | tf_op jit(solution)/shard_map/ppermute | solution.py:574
  114.3 11.8 %collective-permute-start.17 = (bf16[2,64,512]{2,1,0:T(8,128)(2,1)}, bf16[2,64,512]{2,1,0:T(8,128)(2,1)S(1)}, u32[]{:S(2)}, u32[]{:S(2)}) collective-permute-start(bf16[2,64,512]{2,1,0:T(8,128)(2,1)} %get-tuple-element.164), channel_id=1, source_target_pairs={{0,1},{1,0},{2,3},{3,2},{4,5},{5,4},{6,7},{7,6},{8,9},{9,8},{10,11... | collective-permute-start | bytes 393224 | tf_op jit(solution)/shard_map/ppermute | solution.py:574
  114.4 26.0 %collective-permute-start.18 = (bf16[2,64,512]{2,1,0:T(8,128)(2,1)}, bf16[2,64,512]{2,1,0:T(8,128)(2,1)S(1)}, u32[]{:S(2)}, u32[]{:S(2)}) collective-permute-start(bf16[2,64,512]{2,1,0:T(8,128)(2,1)} %get-tuple-element.165), channel_id=1, source_target_pairs={{0,2},{1,3},{2,0},{3,1},{4,6},{5,7},{6,4},{7,5},{8,10},{9,11},{10,... | collective-permute-start | bytes 393224 | tf_op jit(solution)/shard_map/ppermute | solution.py:574
  115.2 25.2 %collective-permute-start.19 = (bf16[2,64,512]{2,1,0:T(8,128)(2,1)}, bf16[2,64,512]{2,1,0:T(8,128)(2,1)}, u32[]{:S(2)}, u32[]{:S(2)}) collective-permute-start(bf16[2,64,512]{2,1,0:T(8,128)(2,1)} %get-tuple-element.166), channel_id=1, source_target_pairs={{0,3},{1,2},{2,1},{3,0},{4,7},{5,6},{6,5},{7,4},{8,11},{9,10},{10,... | collective-permute-start | bytes 393224 | tf_op jit(solution)/shard_map/ppermute | solution.py:574
  120.1 20.3 %collective-permute-start.25 = (bf16[4,64,640]{2,1,0:T(8,128)(2,1)}, bf16[4,64,640]{2,1,0:T(8,128)(2,1)}, u32[]{:S(2)}, u32[]{:S(2)}) collective-permute-start(bf16[4,64,640]{2,1,0:T(8,128)(2,1)} %get-tuple-element.176), channel_id=1, source_target_pairs={{0,4},{2,6},{4,0},{6,2},{1,5},{3,7},{5,1},{7,3},{8,12},{10,14},{12... | collective-permute-start | bytes 983048 | tf_op jit(solution)/shard_map/ppermute | solution.py:869
  120.6 19.8 %collective-permute-start.26 = (bf16[4,64,640]{2,1,0:T(8,128)(2,1)}, bf16[4,64,640]{2,1,0:T(8,128)(2,1)}, u32[]{:S(2)}, u32[]{:S(2)}) collective-permute-start(bf16[4,64,640]{2,1,0:T(8,128)(2,1)} %get-tuple-element.175), channel_id=1, source_target_pairs={{0,2},{2,0},{4,6},{6,4},{1,3},{3,1},{5,7},{7,5},{8,10},{10,8},{12,... | collective-permute-start | bytes 983048 | tf_op jit(solution)/shard_map/ppermute | solution.py:869
  121.3 30.5 %all-to-all-start.4 = ((bf16[4,4,64,512]{3,2,1,0:T(8,128)(2,1)}), bf16[4,4,64,512]{3,2,1,0:T(8,128)(2,1)}, u32[]{:S(2)}, u32[]{:S(2)}) async-start(bf16[4,4,64,512]{3,2,1,0:T(8,128)(2,1)} %get-tuple-element.178), calls=%async_computation.4 | async-start | bytes 2097152 | tf_op jit(solution)/shard_map/all_to_all | solution.py:893
  126.1 14.3 %copy-start.8 = (bf16[2,64,512]{2,1,0:T(8,128)(2,1)}, bf16[2,64,512]{2,1,0:T(8,128)(2,1)S(1)}, u32[]{:S(2)}) copy-start(bf16[2,64,512]{2,1,0:T(8,128)(2,1)S(1)} %collective-permute-done.17.refs_1_) | copy-start | bytes 393220
  126.1 14.4 %collective-permute-start.27 = (bf16[4,64,640]{2,1,0:T(8,128)(2,1)}, bf16[4,64,640]{2,1,0:T(8,128)(2,1)}, u32[]{:S(2)}, u32[]{:S(2)}) collective-permute-start(bf16[4,64,640]{2,1,0:T(8,128)(2,1)} %get-tuple-element.177), channel_id=1, source_target_pairs={{0,6},{2,4},{4,2},{6,0},{1,7},{3,5},{5,3},{7,1},{8,14},{10,12},{12... | collective-permute-start | bytes 983048 | tf_op jit(solution)/shard_map/ppermute | solution.py:869
  140.4 2.9 %collective-permute-start.28 = (bf16[2,2,4,64,384]{4,3,2,1,0:T(8,128)(2,1)}, bf16[2,2,4,64,384]{4,3,2,1,0:T(8,128)(2,1)}, u32[]{:S(2)}, u32[]{:S(2)}) collective-permute-start(bf16[2,2,4,64,384]{4,3,2,1,0:T(8,128)(2,1)} %get-tuple-element.187), channel_id=1, source_target_pairs={{0,1},{1,0},{2,3},{3,2},{4,5},{5,4},{6,7},{7,6},{8,9},{9,8},{10,11... | collective-permute-start | bytes 2359304 | tf_op jit(solution)/shard_map/ppermute | solution.py:562
  140.5 6.4 %collective-permute-start.22 = (bf16[2,64,512]{2,1,0:T(8,128)(2,1)}, bf16[2,64,512]{2,1,0:T(8,128)(2,1)S(1)}, u32[]{:S(2)}, u32[]{:S(2)}) collective-permute-start(bf16[2,64,512]{2,1,0:T(8,128)(2,1)} %get-tuple-element.182), channel_id=1, source_target_pairs={{0,1},{1,0},{2,3},{3,2},{4,5},{5,4},{6,7},{7,6},{8,9},{9,8},{10,11... | collective-permute-start | bytes 393224 | tf_op jit(solution)/shard_map/ppermute | solution.py:574
  141.0 15.5 %collective-permute-start.23 = (bf16[2,64,512]{2,1,0:T(8,128)(2,1)}, bf16[2,64,512]{2,1,0:T(8,128)(2,1)}, u32[]{:S(2)}, u32[]{:S(2)}) collective-permute-start(bf16[2,64,512]{2,1,0:T(8,128)(2,1)} %get-tuple-element.183), channel_id=1, source_target_pairs={{0,2},{1,3},{2,0},{3,1},{4,6},{5,7},{6,4},{7,5},{8,10},{9,11},{10,... | collective-permute-start | bytes 393224 | tf_op jit(solution)/shard_map/ppermute | solution.py:574
  141.7 14.8 %collective-permute-start.24 = (bf16[2,64,512]{2,1,0:T(8,128)(2,1)}, bf16[2,64,512]{2,1,0:T(8,128)(2,1)}, u32[]{:S(2)}, u32[]{:S(2)}) collective-permute-start(bf16[2,64,512]{2,1,0:T(8,128)(2,1)} %get-tuple-element.184), channel_id=1, source_target_pairs={{0,3},{1,2},{2,1},{3,0},{4,7},{5,6},{6,5},{7,4},{8,11},{9,10},{10,... | collective-permute-start | bytes 393224 | tf_op jit(solution)/shard_map/ppermute | solution.py:574
  145.7 10.8 %collective-permute-start.35 = (bf16[4,80,384]{2,1,0:T(8,128)(2,1)}, bf16[4,80,384]{2,1,0:T(8,128)(2,1)S(1)}, u32[]{:S(2)}, u32[]{:S(2)}) collective-permute-start(bf16[4,80,384]{2,1,0:T(8,128)(2,1)} %get-tuple-element.191), channel_id=1, source_target_pairs={{0,4},{2,6},{4,0},{6,2},{1,5},{3,7},{5,1},{7,3},{8,12},{10,14},{12... | collective-permute-start | bytes 737288 | tf_op jit(solution)/shard_map/ppermute | solution.py:869
  146.2 14.1 %collective-permute-start.36 = (bf16[4,80,384]{2,1,0:T(8,128)(2,1)}, bf16[4,80,384]{2,1,0:T(8,128)(2,1)S(1)}, u32[]{:S(2)}, u32[]{:S(2)}) collective-permute-start(bf16[4,80,384]{2,1,0:T(8,128)(2,1)} %get-tuple-element.190), channel_id=1, source_target_pairs={{0,2},{2,0},{4,6},{6,4},{1,3},{3,1},{5,7},{7,5},{8,10},{10,8},{12,... | collective-permute-start | bytes 737288 | tf_op jit(solution)/shard_map/ppermute | solution.py:869
  147.0 14.8 %copy-start.12 = (bf16[2,64,512]{2,1,0:T(8,128)(2,1)}, bf16[2,64,512]{2,1,0:T(8,128)(2,1)S(1)}, u32[]{:S(2)}) copy-start(bf16[2,64,512]{2,1,0:T(8,128)(2,1)S(1)} %collective-permute-done.22.refs_5_) | copy-start | bytes 393220
  147.0 13.4 %collective-permute-start.37 = (bf16[4,80,384]{2,1,0:T(8,128)(2,1)}, bf16[4,80,384]{2,1,0:T(8,128)(2,1)S(1)}, u32[]{:S(2)}, u32[]{:S(2)}) collective-permute-start(bf16[4,80,384]{2,1,0:T(8,128)(2,1)} %get-tuple-element.192), channel_id=1, source_target_pairs={{0,6},{2,4},{4,2},{6,0},{1,7},{3,5},{5,3},{7,1},{8,14},{10,12},{12... | collective-permute-start | bytes 737288 | tf_op jit(solution)/shard_map/ppermute | solution.py:869
  151.3 14.0 %copy-start.30 = (bf16[4,80,384]{2,1,0:T(8,128)(2,1)S(1)}, bf16[4,80,384]{2,1,0:T(8,128)(2,1)}, u32[]{:S(2)}) copy-start(bf16[4,80,384]{2,1,0:T(8,128)(2,1)} %get-tuple-element.194) | copy-start | bytes 737284
  151.8 14.4 %all-to-all-start.3 = ((bf16[4,64,640]{2,1,0:T(8,128)(2,1)}), bf16[4,64,640]{2,1,0:T(8,128)(2,1)S(1)}, u32[]{:S(2)}, u32[]{:S(2)}) async-start(bf16[4,64,640]{2,1,0:T(8,128)(2,1)} %add_convert_fusion), calls=%async_computation.3 | async-start | bytes 655360 | tf_op jit(solution)/shard_map/all_to_all | solution.py:930
  156.5 20.0 %collective-permute-start.16 = (bf16[4,64,512]{2,1,0:T(8,128)(2,1)}, bf16[4,64,512]{2,1,0:T(8,128)(2,1)S(1)}, u32[]{:S(2)}, u32[]{:S(2)}) collective-permute-start(bf16[4,64,512]{2,1,0:T(8,128)(2,1)} %get-tuple-element.155), channel_id=1, source_target_pairs={{0,3},{1,2},{2,1},{3,0},{4,7},{5,6},{6,5},{7,4},{8,11},{9,10},{10,... | collective-permute-start | bytes 786440 | tf_op jit(solution)/shard_map/ppermute | solution.py:574
  161.7 14.8 %copy-start.4 = (s32[9]{0:T(128)S(1)}, s32[9]{0:T(128)}, u32[]{:S(2)}) copy-start(s32[9]{0:T(128)} %stack.41.place) | copy-start | bytes 112
  161.8 14.8 %copy-start.20 = (bf16[4,64,512]{2,1,0:T(8,128)(2,1)S(1)}, bf16[4,64,512]{2,1,0:T(8,128)(2,1)}, u32[]{:S(2)}) copy-start(bf16[4,64,512]{2,1,0:T(8,128)(2,1)} %get-tuple-element.152.refs_0_) | copy-start | bytes 786436
  161.8 9.4 %collective-permute-start.29 = (bf16[64,512]{1,0:T(8,128)(2,1)S(1)}, bf16[64,512]{1,0:T(8,128)(2,1)S(1)}, u32[]{:S(2)}, u32[]{:S(2)}) collective-permute-start(bf16[64,512]{1,0:T(8,128)(2,1)S(1)} %get-tuple-element.220), channel_id=1, source_target_pairs={{0,4},{2,6},{4,0},{6,2},{1,5},{3,7},{5,1},{7,3},{8,12},{10,14},{12... | collective-permute-start | bytes 196616 | tf_op jit(solution)/shard_map/ppermute | solution.py:869
  163.0 8.2 %collective-permute-start.30 = (bf16[64,512]{1,0:T(8,128)(2,1)S(1)}, bf16[64,512]{1,0:T(8,128)(2,1)S(1)}, u32[]{:S(2)}, u32[]{:S(2)}) collective-permute-start(bf16[64,512]{1,0:T(8,128)(2,1)S(1)} %get-tuple-element.222), channel_id=1, source_target_pairs={{0,2},{2,0},{4,6},{6,4},{1,3},{3,1},{5,7},{7,5},{8,10},{10,8},{12,... | collective-permute-start | bytes 196616 | tf_op jit(solution)/shard_map/ppermute | solution.py:869
  163.4 7.8 %collective-permute-start.31 = (bf16[64,512]{1,0:T(8,128)(2,1)S(1)}, bf16[64,512]{1,0:T(8,128)(2,1)S(1)}, u32[]{:S(2)}, u32[]{:S(2)}) collective-permute-start(bf16[64,512]{1,0:T(8,128)(2,1)S(1)} %get-tuple-element.221), channel_id=1, source_target_pairs={{0,6},{2,4},{4,2},{6,0},{1,7},{3,5},{5,3},{7,1},{8,14},{10,12},{12... | collective-permute-start | bytes 196616 | tf_op jit(solution)/shard_map/ppermute | solution.py:869
  166.3 11.8 %all-to-all-start.5 = ((bf16[4,80,384]{2,1,0:T(8,128)(2,1)}), bf16[4,80,384]{2,1,0:T(8,128)(2,1)S(1)}, u32[]{:S(2)}, u32[]{:S(2)}) async-start(bf16[4,80,384]{2,1,0:T(8,128)(2,1)} %add_convert_fusion.1), calls=%async_computation.5 | async-start | bytes 491520 | tf_op jit(solution)/shard_map/all_to_all | solution.py:934
  171.3 5.2 %collective-permute-start.32 = (bf16[64,1152]{1,0:T(8,128)(2,1)S(1)}, bf16[64,1152]{1,0:T(8,128)(2,1)S(1)}, u32[]{:S(2)}, u32[]{:S(2)}) collective-permute-start(bf16[64,1152]{1,0:T(8,128)(2,1)S(1)} %pad_maximum_fusion.2.m0), channel_id=1, source_target_pairs={{0,2},{2,0},{1,3},{3,1},{4,6},{6,4},{5,7},{7,5},{8,10},{10,8},{9,1... | collective-permute-start | bytes 442376 | tf_op jit(solution)/shard_map/ppermute | solution.py:562
  171.9 6.3 %collective-permute-start.33 = (bf16[64,1152]{1,0:T(8,128)(2,1)S(1)}, bf16[64,1152]{1,0:T(8,128)(2,1)S(1)}, u32[]{:S(2)}, u32[]{:S(2)}) collective-permute-start(bf16[64,1152]{1,0:T(8,128)(2,1)S(1)} %pad_maximum_fusion.2.m0), channel_id=1, source_target_pairs={{0,1},{1,0},{2,3},{3,2},{4,5},{5,4},{6,7},{7,6},{8,9},{9,8},{10,11... | collective-permute-start | bytes 442376 | tf_op jit(solution)/shard_map/ppermute | solution.py:562
  176.5 1.7 collective-permute-start.34
  178.2 4.9 %collective-permute-start.38 = (bf16[80,384]{1,0:T(8,128)(2,1)S(1)}, bf16[80,384]{1,0:T(8,128)(2,1)S(1)}, u32[]{:S(2)}, u32[]{:S(2)}) collective-permute-start(bf16[80,384]{1,0:T(8,128)(2,1)S(1)} %reduce_sum.38.a0), channel_id=1, source_target_pairs={{0,2},{1,3},{2,0},{3,1},{4,6},{5,7},{6,4},{7,5},{8,10},{9,11},{10,... | collective-permute-start | bytes 184328 | tf_op jit(solution)/shard_map/ppermute | solution.py:613
  178.8 4.3 %collective-permute-start.39 = (bf16[80,384]{1,0:T(8,128)(2,1)S(1)}, bf16[80,384]{1,0:T(8,128)(2,1)S(1)}, u32[]{:S(2)}, u32[]{:S(2)}) collective-permute-start(bf16[80,384]{1,0:T(8,128)(2,1)S(1)} %reduce_sum.38.a0), channel_id=1, source_target_pairs={{0,1},{1,0},{2,3},{3,2},{4,5},{5,4},{6,7},{7,6},{8,9},{9,8},{10,11... | collective-permute-start | bytes 184328 | tf_op jit(solution)/shard_map/ppermute | solution.py:613
  179.0 4.6 %collective-permute-start.40 = (bf16[80,384]{1,0:T(8,128)(2,1)S(1)}, bf16[80,384]{1,0:T(8,128)(2,1)S(1)}, u32[]{:S(2)}, u32[]{:S(2)}) collective-permute-start(bf16[80,384]{1,0:T(8,128)(2,1)S(1)} %reduce_sum.38.a0), channel_id=1, source_target_pairs={{0,3},{1,2},{2,1},{3,0},{4,7},{5,6},{6,5},{7,4},{8,11},{9,10},{10,... | collective-permute-start | bytes 184328 | tf_op jit(solution)/shard_map/ppermute | solution.py:613
  183.1 9.7 %copy-start.14 = (bf16[80,384]{1,0:T(8,128)(2,1)}, bf16[80,384]{1,0:T(8,128)(2,1)S(1)}, u32[]{:S(2)}) copy-start(bf16[80,384]{1,0:T(8,128)(2,1)S(1)} %collective-permute-done.38.a1) | copy-start | bytes 184324
  183.1 9.7 %copy-start.15 = (bf16[80,384]{1,0:T(8,128)(2,1)}, bf16[80,384]{1,0:T(8,128)(2,1)S(1)}, u32[]{:S(2)}) copy-start(bf16[80,384]{1,0:T(8,128)(2,1)S(1)} %collective-permute-done.39.a2) | copy-start | bytes 184324
  184.9 12.4 %all-to-all-start.6 = ((f32[8,8,128]{2,1,0:T(8,128)}), f32[8,8,128]{2,1,0:T(8,128)S(1)}, u32[]{:S(2)}, u32[]{:S(2)}) async-start(f32[8,8,128]{2,1,0:T(8,128)} %squares.1), calls=%async_computation.6 | async-start | bytes 65536 | tf_op jit(solution)/shard_map/all_to_all | solution.py:975
  (25 other events, 132.5 us)
